TPU v7x, 32 devices: a whole 2x2x4 slice. The times are simulated.
32 devices in a mesh: dp: 8 (over z, y), blk: 2 (over core), uly: 2 (over x).
Axes of the slice: x: 2, y: 2, z: 4, core: 2. Of those that a mesh axis runs over, the one named last changes fastest.
Arguments:
- inputs: bfloat16 [16, 1024, 768], P('dp', ('blk', 'uly')), may hold values from -6 to 6
- cotangent: bfloat16 [16, 1024, 768], P('dp', ('blk', 'uly')), may hold values from -6 to 6
- first_gain: bfloat16 [2, 768], P(None, 'dp'), may hold values from 0.5 to 1.5
- first_shift: bfloat16 [2, 768], P(None, 'dp'), may hold values from -1 to 1
- in_weight: bfloat16 [2, 768, 2304], P(None, 'dp'), may hold values from -0.21875 to 0.21875
- query_bias: bfloat16 [2, 768], P(None, 'dp'), may hold values from -1 to 1
- value_bias: bfloat16 [2, 768], P(None, 'dp'), may hold values from -1 to 1
- out_weight: bfloat16 [2, 768, 768], P(None, 'dp'), may hold values from -0.875 to 0.875
- out_bias: bfloat16 [2, 768], P(None, 'dp'), may hold values from -1 to 1
- second_gain: bfloat16 [2, 768], P(None, 'dp'), may hold values from 0.5 to 1.5
- second_shift: bfloat16 [2, 768], P(None, 'dp'), may hold values from -1 to 1
- up_weight: bfloat16 [2, 768, 3072], P(None, 'dp'), may hold values from -0.21875 to 0.21875
- up_bias: bfloat16 [2, 3072], P(None, 'dp'), may hold values from -1 to 1
- down_weight: bfloat16 [2, 3072, 768], P(None, 'dp'), may hold values from -0.109375 to 0.109375
- down_bias: bfloat16 [2, 768], P(None, 'dp'), may hold values from -1 to 1
Outputs:
- outputs: float32 [16, 1024, 768], P('dp', ('blk', 'uly'))
- input_gradient: float32 [16, 1024, 768], P('dp', ('blk', 'uly'))
- first_gain_gradient: float32 [2, 768], P(None, 'dp')
- first_shift_gradient: float32 [2, 768], P(None, 'dp')
- in_weight_gradient: float32 [2, 768, 2304], P(None, 'dp')
- query_bias_gradient: float32 [2, 768], P(None, 'dp')
- value_bias_gradient: float32 [2, 768], P(None, 'dp')
- out_weight_gradient: float32 [2, 768, 768], P(None, 'dp')
- out_bias_gradient: float32 [2, 768], P(None, 'dp')
- second_gain_gradient: float32 [2, 768], P(None, 'dp')
- second_shift_gradient: float32 [2, 768], P(None, 'dp')
- up_weight_gradient: float32 [2, 768, 3072], P(None, 'dp')
- up_bias_gradient: float32 [2, 3072], P(None, 'dp')
- down_weight_gradient: float32 [2, 3072, 768], P(None, 'dp')
- down_bias_gradient: float32 [2, 768], P(None, 'dp')
All inputs are finite; a program needn't handle non-finite values.
Results may differ from a plain program's by a relative error of at most 0.017.
Values may be sent and summed in bfloat16 or wider, within the bound.
No kernel may reach another device: no remote copies, remote signals or barrier semaphores. Data moves between devices by JAX's collectives and lax.ppermute only.
A program may use at most 256 MiB of HBM per device.

v0:
```python
from functools import partial

import jax
import jax.numpy as jnp
from jax import lax
from jax.sharding import PartitionSpec as P

HDIM = 64


EPSILON = 1e-05
NEGATIVE = -1e30


def normalize(residual, gain, shift):
    average = jnp.mean(residual, axis=-1, keepdims=True)
    centred = residual - average
    variance = jnp.mean(centred * centred, axis=-1, keepdims=True)
    return centred * lax.rsqrt(variance + EPSILON) * gain + shift


def matmul(left, right):
    return jnp.dot(left, right, preferred_element_type=jnp.float32)


def contract(left, right):
    return jnp.einsum("std,ste->de", left, right, preferred_element_type=jnp.float32)


def transposed(left, right):
    return jnp.einsum("ste,de->std", left, right, preferred_element_type=jnp.float32)


def causal_mask(first, count, length):
    query_rows = first + lax.broadcasted_iota(jnp.int32, (count, length), 0)
    key_rows = lax.broadcasted_iota(jnp.int32, (count, length), 1)
    return key_rows <= query_rows


def scores_for(queries, keys, first):
    scores = jnp.einsum(
        "qhd,khd->hqk", queries, keys, preferred_element_type=jnp.float32
    ) * HDIM ** (-0.5)
    allowed = causal_mask(first, queries.shape[0], keys.shape[0])
    return jnp.where(allowed[None], scores, NEGATIVE)


def attend_block(queries, keys, values, first):
    count = queries.shape[0]
    length = keys.shape[0]
    queries = queries.reshape(count, -1, HDIM)
    keys = keys.reshape(length, -1, HDIM)
    values = values.reshape(length, -1, HDIM)
    scores = scores_for(queries, keys, first)
    top = jnp.max(scores, axis=-1, keepdims=True)
    raised = jnp.exp(scores - top)
    total = jnp.sum(raised, axis=-1, keepdims=True)
    shares = (raised / total).astype(jnp.bfloat16)
    mixed = jnp.einsum("hqk,khd->qhd", shares, values, preferred_element_type=jnp.float32)
    return (mixed.astype(jnp.bfloat16).reshape(count, -1), (top + jnp.log(total))[..., 0])


def attend_back(queries, keys, values, logsum, upstream, first):
    count = queries.shape[0]
    length = keys.shape[0]
    queries = queries.reshape(count, -1, HDIM)
    keys = keys.reshape(length, -1, HDIM)
    values = values.reshape(length, -1, HDIM)
    upstream = upstream.reshape(count, -1, HDIM)
    scale = HDIM ** (-0.5)
    shares = jnp.exp(scores_for(queries, keys, first) - logsum[..., None])
    against = jnp.einsum("qhd,khd->hqk", upstream, values, preferred_element_type=jnp.float32)
    inner = jnp.sum(shares * against, axis=-1, keepdims=True)
    slopes = (shares * (against - inner)).astype(jnp.bfloat16)
    query_slope = (
        jnp.einsum("hqk,khd->qhd", slopes, keys, preferred_element_type=jnp.float32) * scale
    )
    key_slope = (
        jnp.einsum("hqk,qhd->khd", slopes, queries, preferred_element_type=jnp.float32) * scale
    )
    value_slope = jnp.einsum(
        "hqk,qhd->khd", shares.astype(jnp.bfloat16), upstream, preferred_element_type=jnp.float32
    )
    paired = jnp.stack([key_slope.reshape(length, -1), value_slope.reshape(length, -1)], axis=1)
    return (query_slope.reshape(count, -1), paired)


def attention_forward(residual, weights):
    gain, shift, in_weight, query_bias, value_bias, out_weight, out_bias = weights
    width = out_weight.shape[0]
    sequences, rows = (residual.shape[0], residual.shape[1])
    groups = lax.axis_size("uly")
    block_rows = rows * groups
    normed = normalize(residual, gain.astype(jnp.float32), shift.astype(jnp.float32)).astype(
        jnp.bfloat16
    )
    project = matmul(normed, in_weight)
    queries = (project[..., :width] + query_bias.astype(jnp.float32)).astype(jnp.bfloat16)
    keys = project[..., width : 2 * width].astype(jnp.bfloat16)
    values = (project[..., 2 * width :] + value_bias.astype(jnp.float32)).astype(jnp.bfloat16)
    packed = jnp.stack([queries, keys, values], axis=2).reshape(
        sequences, rows, 3, groups, width // groups
    )
    headed = lax.all_to_all(packed, "uly", split_axis=3, concat_axis=1, tiled=True)
    head_queries = headed[:, :, 0, 0]
    all_keys, all_values = (
        lax.all_gather(headed[:, :, 1, 0], "blk", axis=1, tiled=True),
        lax.all_gather(headed[:, :, 2, 0], "blk", axis=1, tiled=True),
    )
    index = lax.axis_index("blk")
    first = index * block_rows

    def single(items):
        return attend_block(items[0], items[1], items[2], first)

    mixed, logsum = lax.map(single, (head_queries, all_keys, all_values))
    returned = lax.all_to_all(
        mixed.reshape(sequences, block_rows, 1, -1), "uly", split_axis=1, concat_axis=2, tiled=True
    )
    returned = returned.reshape(sequences, rows, width)
    middle = residual + matmul(returned, out_weight) + out_bias.astype(jnp.float32)
    return (middle, (normed, head_queries, all_keys, all_values, logsum, returned))


def feed_forward(residual, weights):
    gain, shift, up_weight, up_bias, down_weight, down_bias = weights
    normed = normalize(residual, gain.astype(jnp.float32), shift.astype(jnp.float32)).astype(
        jnp.bfloat16
    )
    hidden = matmul(normed, up_weight) + up_bias.astype(jnp.float32)
    active = jax.nn.gelu(hidden, approximate=True).astype(jnp.bfloat16)
    result = residual + matmul(active, down_weight) + down_bias.astype(jnp.float32)
    return (result, (normed, hidden, active))


def norm_backward(residual, gain, shift, slope):
    unused, pullback = jax.vjp(
        normalize, residual, gain.astype(jnp.float32), shift.astype(jnp.float32)
    )
    return pullback(slope)


def feed_backward(residual, upstream, weights, record):
    gain, shift, up_weight, up_bias, down_weight, down_bias = weights
    normed, hidden, active = record
    down_bias_slope = jnp.sum(upstream, axis=(0, 1))
    low_upstream = upstream.astype(jnp.bfloat16)
    down_weight_slope = contract(active, low_upstream)
    active_slope = transposed(low_upstream, down_weight)
    unused, pullback = jax.vjp(partial(jax.nn.gelu, approximate=True), hidden)
    hidden_slope = pullback(active_slope)[0]
    up_bias_slope = jnp.sum(hidden_slope, axis=(0, 1))
    low_hidden = hidden_slope.astype(jnp.bfloat16)
    up_weight_slope = contract(normed, low_hidden)
    norm_slope = transposed(low_hidden, up_weight)
    residual_slope, gain_slope, shift_slope = norm_backward(residual, gain, shift, norm_slope)
    return (
        upstream + residual_slope,
        (
            gain_slope,
            shift_slope,
            up_weight_slope,
            up_bias_slope,
            down_weight_slope,
            down_bias_slope,
        ),
    )


def attention_backward(residual, upstream, weights, record):
    gain, shift, in_weight, query_bias, value_bias, out_weight, out_bias = weights
    normed, head_queries, all_keys, all_values, logsum, returned = record
    width = out_weight.shape[0]
    sequences, rows = (residual.shape[0], residual.shape[1])
    groups = lax.axis_size("uly")
    block_rows = rows * groups
    out_bias_slope = jnp.sum(upstream, axis=(0, 1))
    low_upstream = upstream.astype(jnp.bfloat16)
    out_weight_slope = contract(returned, low_upstream)
    mixed_slope = transposed(low_upstream, out_weight).astype(jnp.bfloat16)
    head_slope = lax.all_to_all(
        mixed_slope.reshape(sequences, rows, groups, -1),
        "uly",
        split_axis=2,
        concat_axis=1,
        tiled=True,
    )
    head_slope = head_slope.reshape(sequences, block_rows, -1)
    index = lax.axis_index("blk")
    first = index * block_rows

    def single(items):
        return attend_back(items[0], items[1], items[2], items[3], items[4], first)

    query_slope, pair_slope = lax.map(
        single, (head_queries, all_keys, all_values, logsum, head_slope)
    )
    pair_slope = lax.psum_scatter(
        pair_slope.astype(jnp.bfloat16), "blk", scatter_dimension=1, tiled=True
    ).astype(jnp.float32)
    stacked = jnp.concatenate(
        [query_slope.astype(jnp.bfloat16)[:, :, None], pair_slope.astype(jnp.bfloat16)], axis=2
    )
    project_slope = lax.all_to_all(
        stacked[:, :, :, None], "uly", split_axis=1, concat_axis=3, tiled=True
    )
    project_slope = project_slope.reshape(sequences, rows, 3 * width)
    query_bias_slope = jnp.sum(project_slope[..., :width].astype(jnp.float32), axis=(0, 1))
    value_bias_slope = jnp.sum(project_slope[..., 2 * width :].astype(jnp.float32), axis=(0, 1))
    in_weight_slope = contract(normed, project_slope)
    first_slope = transposed(project_slope, in_weight)
    residual_slope, gain_slope, shift_slope = norm_backward(residual, gain, shift, first_slope)
    return (
        upstream + residual_slope,
        (
            gain_slope,
            shift_slope,
            in_weight_slope,
            query_bias_slope,
            value_bias_slope,
            out_weight_slope,
            out_bias_slope,
        ),
    )


def shards(
    inputs,
    cotangent,
    first_gain,
    first_shift,
    in_weight,
    query_bias,
    value_bias,
    out_weight,
    out_bias,
    second_gain,
    second_shift,
    up_weight,
    up_bias,
    down_weight,
    down_bias,
):
    layers = in_weight.shape[0]
    residual = inputs.astype(jnp.float32)
    records = []
    for layer in range(layers):
        attention_full = (
            lax.all_gather(first_gain[layer], "dp", axis=0, tiled=True),
            lax.all_gather(first_shift[layer], "dp", axis=0, tiled=True),
            lax.all_gather(in_weight[layer], "dp", axis=0, tiled=True),
            lax.all_gather(query_bias[layer], "dp", axis=0, tiled=True),
            lax.all_gather(value_bias[layer], "dp", axis=0, tiled=True),
            lax.all_gather(out_weight[layer], "dp", axis=0, tiled=True),
            lax.all_gather(out_bias[layer], "dp", axis=0, tiled=True),
        )
        entry = residual
        residual, attention_record = attention_forward(residual, attention_full)
        middle = residual
        feed_full = (
            lax.all_gather(second_gain[layer], "dp", axis=0, tiled=True),
            lax.all_gather(second_shift[layer], "dp", axis=0, tiled=True),
            lax.all_gather(up_weight[layer], "dp", axis=0, tiled=True),
            lax.all_gather(up_bias[layer], "dp", axis=0, tiled=True),
            lax.all_gather(down_weight[layer], "dp", axis=0, tiled=True),
            lax.all_gather(down_bias[layer], "dp", axis=0, tiled=True),
        )
        residual, feed_record = feed_forward(residual, feed_full)
        records.append((entry, attention_record, middle, feed_record, attention_full, feed_full))
    upstream = cotangent.astype(jnp.float32)
    summed_layers = [None] * layers
    for layer in reversed(range(layers)):
        entry, attention_record, middle, feed_record, attention_held, feed_held = records[layer]
        feed_full = (
            lax.all_gather(second_gain[layer], "dp", axis=0, tiled=True),
            lax.all_gather(second_shift[layer], "dp", axis=0, tiled=True),
            lax.all_gather(up_weight[layer], "dp", axis=0, tiled=True),
            lax.all_gather(up_bias[layer], "dp", axis=0, tiled=True),
            lax.all_gather(down_weight[layer], "dp", axis=0, tiled=True),
            lax.all_gather(down_bias[layer], "dp", axis=0, tiled=True),
        )
        upstream, feed_slopes = feed_backward(middle, upstream, feed_full, feed_record)
        attention_full = (
            lax.all_gather(first_gain[layer], "dp", axis=0, tiled=True),
            lax.all_gather(first_shift[layer], "dp", axis=0, tiled=True),
            lax.all_gather(in_weight[layer], "dp", axis=0, tiled=True),
            lax.all_gather(query_bias[layer], "dp", axis=0, tiled=True),
            lax.all_gather(value_bias[layer], "dp", axis=0, tiled=True),
            lax.all_gather(out_weight[layer], "dp", axis=0, tiled=True),
            lax.all_gather(out_bias[layer], "dp", axis=0, tiled=True),
        )
        upstream, attention_slopes = attention_backward(
            entry, upstream, attention_full, attention_record
        )
        every = attention_slopes + feed_slopes
        shares = (
            lax.psum_scatter(every[0], ("dp", "blk", "uly"), scatter_dimension=0, tiled=True),
            lax.psum_scatter(every[1], ("dp", "blk", "uly"), scatter_dimension=0, tiled=True),
            lax.psum_scatter(every[2], ("dp", "blk", "uly"), scatter_dimension=0, tiled=True),
            lax.psum_scatter(every[3], ("dp", "blk", "uly"), scatter_dimension=0, tiled=True),
            lax.psum_scatter(every[4], ("dp", "blk", "uly"), scatter_dimension=0, tiled=True),
            lax.psum_scatter(every[5], ("dp", "blk", "uly"), scatter_dimension=0, tiled=True),
            lax.psum_scatter(every[6], ("dp", "blk", "uly"), scatter_dimension=0, tiled=True),
            lax.psum_scatter(every[7], ("dp", "blk", "uly"), scatter_dimension=0, tiled=True),
            lax.psum_scatter(every[8], ("dp", "blk", "uly"), scatter_dimension=0, tiled=True),
            lax.psum_scatter(every[9], ("dp", "blk", "uly"), scatter_dimension=0, tiled=True),
            lax.psum_scatter(every[10], ("dp", "blk", "uly"), scatter_dimension=0, tiled=True),
            lax.psum_scatter(every[11], ("dp", "blk", "uly"), scatter_dimension=0, tiled=True),
            lax.psum_scatter(every[12], ("dp", "blk", "uly"), scatter_dimension=0, tiled=True),
        )
        summed = (
            lax.all_gather(
                shares[0].astype(jnp.bfloat16), ("blk", "uly"), axis=0, tiled=True
            ).astype(jnp.float32),
            lax.all_gather(
                shares[1].astype(jnp.bfloat16), ("blk", "uly"), axis=0, tiled=True
            ).astype(jnp.float32),
            lax.all_gather(
                shares[2].astype(jnp.bfloat16), ("blk", "uly"), axis=0, tiled=True
            ).astype(jnp.float32),
            lax.all_gather(
                shares[3].astype(jnp.bfloat16), ("blk", "uly"), axis=0, tiled=True
            ).astype(jnp.float32),
            lax.all_gather(
                shares[4].astype(jnp.bfloat16), ("blk", "uly"), axis=0, tiled=True
            ).astype(jnp.float32),
            lax.all_gather(
                shares[5].astype(jnp.bfloat16), ("blk", "uly"), axis=0, tiled=True
            ).astype(jnp.float32),
            lax.all_gather(
                shares[6].astype(jnp.bfloat16), ("blk", "uly"), axis=0, tiled=True
            ).astype(jnp.float32),
            lax.all_gather(
                shares[7].astype(jnp.bfloat16), ("blk", "uly"), axis=0, tiled=True
            ).astype(jnp.float32),
            lax.all_gather(
                shares[8].astype(jnp.bfloat16), ("blk", "uly"), axis=0, tiled=True
            ).astype(jnp.float32),
            lax.all_gather(
                shares[9].astype(jnp.bfloat16), ("blk", "uly"), axis=0, tiled=True
            ).astype(jnp.float32),
            lax.all_gather(
                shares[10].astype(jnp.bfloat16), ("blk", "uly"), axis=0, tiled=True
            ).astype(jnp.float32),
            lax.all_gather(
                shares[11].astype(jnp.bfloat16), ("blk", "uly"), axis=0, tiled=True
            ).astype(jnp.float32),
            lax.all_gather(
                shares[12].astype(jnp.bfloat16), ("blk", "uly"), axis=0, tiled=True
            ).astype(jnp.float32),
        )
        summed_layers[layer] = summed
    stacked = tuple(
        (jnp.stack([summed_layers[layer][index] for layer in range(layers)]) for index in range(13))
    )
    return (residual, upstream) + stacked


def solution(mesh):
    in_specs = (
        P("dp", ("blk", "uly"), None),
        P("dp", ("blk", "uly"), None),
        P(None, "dp"),
        P(None, "dp"),
        P(None, "dp", None),
        P(None, "dp"),
        P(None, "dp"),
        P(None, "dp", None),
        P(None, "dp"),
        P(None, "dp"),
        P(None, "dp"),
        P(None, "dp", None),
        P(None, "dp"),
        P(None, "dp", None),
        P(None, "dp"),
    )
    out_specs = (
        P("dp", ("blk", "uly"), None),
        P("dp", ("blk", "uly"), None),
        P(None, "dp"),
        P(None, "dp"),
        P(None, "dp", None),
        P(None, "dp"),
        P(None, "dp"),
        P(None, "dp", None),
        P(None, "dp"),
        P(None, "dp"),
        P(None, "dp"),
        P(None, "dp", None),
        P(None, "dp"),
        P(None, "dp", None),
        P(None, "dp"),
    )
    return jax.shard_map(shards, mesh=mesh, in_specs=in_specs, out_specs=out_specs, check_vma=False)
```

profile of v0, /device:TPU:0, one launch (start us, length us, event | category | flops | bytes accessed | tf_op | source)
XLA Modules:
  0.0 2095.6 jit_solution(17031126188441576071)
XLA Ops:
  34.3 40.1 %all-reduce.55 = (bf16[768]{0:T(1024)(128)(2,1)S(1)}, bf16[768]{0:T(1024)(128)(2,1)S(1)}, bf16[768]{0:T(1024)(128)(2,1)S(1)}, bf16[768]{0:T(1024)(128)(2,1)S(1)}...) all-reduce(bf16[768]{0:T(1024)(128)(2,1)} %dynamic-update-slice.1, ...), channel_id=3, replica_groups=mesh['dp'=8,'blk'=2,'uly'=2] {'dp'}, use_global_device_ids=true, to_apply=%add.1 | all-reduce | flops 12288 | bytes 49152
  85.2 29.3 %all_to_all.126 = bf16[2,256,3,2,384]{4,1,0,2,3:T(8,128)(2,1)S(1)} all-to-all(bf16[2,256,3,2,384]{4,1,0,2,3:T(8,128)(2,1)S(1)} %pad_maximum_fusion), channel_id=1, replica_groups=mesh['dp'=8,'blk'=2,'uly'=2] {'uly'}, dimensions={3} | all-to-all | bytes 4718592 | tf_op jit(solution)/shard_map/all_to_all | solution.py:104
  127.1 11.4 all-gather.47.cloned.1.call-done
  141.1 25.8 %while.48 = (s32[]{:T(128)}, bf16[2,512,384]{1,2,0:T(8,128)(2,1)}, f32[2,6,512]{2,1,0:T(8,128)S(1)}, bf16[2,1024,384]{1,2,0:T(8,128)(2,1)S(1)}, s32[]{:T(128)}, ...) while((s32[]{:T(128)}, bf16[2,512,384]{1,2,0:T(8,128)(2,1)}, ...), condition=%wide.region_5.6_spmd, body=%wide.region_2.5_spmd.sunk | while | flops 843773440 | bytes 53330088 | solution.py:116
  175.2 26.8 %all-gather.12 = bf16[1,3072]{1,0:T(2,128)(2,1)S(1)} all-gather(bf16[1,384]{1,0:T(2,128)(2,1)S(1)} %get-tuple-element.439), channel_id=14, replica_groups=mesh['dp'=8,'blk'=2,'uly'=2] {'dp'}, dimensions={1}, use_global_device_ids=true | all-gather | bytes 6912 | tf_op jit(solution)/shard_map/all_gather | solution.py:264
  210.5 53.7 %all-gather.51.cloned.1.call-done = bf16[1,768,3072]{2,1,0:T(8,128)(2,1)} async-done(((bf16[1,96,3072]{2,1,0:T(8,128)(2,1)}), bf16[1,768,3072]{2,1,0:T(8,128)(2,1)}) %all-gather.51.cloned.1.call-update) | async-done | bytes 4718608 | tf_op jit(solution)/shard_map/all_gather | solution.py:263
  264.2 6.9 fusion.50
  271.1 73.7 %all-gather.53.cloned.1.call-done = bf16[1,3072,768]{2,1,0:T(8,128)(2,1)} async-done(((bf16[1,384,768]{2,1,0:T(8,128)(2,1)}), bf16[1,3072,768]{2,1,0:T(8,128)(2,1)}) %all-gather.53.cloned.1.call-update) | async-done | bytes 4718608 | tf_op jit(solution)/shard_map/all_gather | solution.py:265
  344.9 7.6 fusion.121
  352.8 57.6 %all-gather.55.cloned.1.call-done = bf16[1,768,2304]{2,1,0:T(8,128)(2,1)} async-done(((bf16[1,96,2304]{2,1,0:T(8,128)(2,1)}), bf16[1,768,2304]{2,1,0:T(8,128)(2,1)}) %all-gather.55.cloned.1.call-update) | async-done | bytes 3538960 | tf_op jit(solution)/shard_map/all_gather | solution.py:251
  426.7 29.5 %all_to_all.127 = bf16[2,256,3,2,384]{4,1,0,2,3:T(8,128)(2,1)S(1)} all-to-all(bf16[2,256,3,2,384]{4,1,0,2,3:T(8,128)(2,1)S(1)} %pad_maximum_fusion.1), channel_id=1, replica_groups=mesh['dp'=8,'blk'=2,'uly'=2] {'uly'}, dimensions={3} | all-to-all | bytes 4718592 | tf_op jit(solution)/shard_map/all_to_all | solution.py:104
  468.2 11.4 all-gather.59.cloned.1.call-done
  483.2 28.0 %while.49 = (s32[]{:T(128)}, bf16[2,512,384]{1,2,0:T(8,128)(2,1)}, f32[2,6,512]{2,1,0:T(8,128)S(1)}, bf16[2,1024,384]{1,2,0:T(8,128)(2,1)S(1)}, s32[]{:T(128)}, ...) while((s32[]{:T(128)}, bf16[2,512,384]{1,2,0:T(8,128)(2,1)}, ...), condition=%wide.region_13.14_spmd, body=%wide.region_10.13_spmd.sunk | while | flops 843773440 | bytes 53330088 | solution.py:116
  518.7 26.5 %all-gather.27 = bf16[1,3072]{1,0:T(2,128)(2,1)S(1)} all-gather(bf16[1,384]{1,0:T(2,128)(2,1)S(1)} %copy-done.104), channel_id=29, replica_groups=mesh['dp'=8,'blk'=2,'uly'=2] {'dp'}, dimensions={1}, use_global_device_ids=true | all-gather | bytes 6912 | tf_op jit(solution)/shard_map/all_gather | solution.py:264
  555.0 50.3 %all-gather.63.cloned.1.call-done = bf16[1,768,3072]{2,1,0:T(8,128)(2,1)} async-done(((bf16[1,96,3072]{2,1,0:T(8,128)(2,1)}), bf16[1,768,3072]{2,1,0:T(8,128)(2,1)}) %all-gather.63.cloned.1.call-update) | async-done | bytes 4718608 | tf_op jit(solution)/shard_map/all_gather | solution.py:263
  605.3 8.2 fusion.42
  613.5 72.5 %all-gather.65.cloned.1.call-done = bf16[1,3072,768]{2,1,0:T(8,128)(2,1)} async-done(((bf16[1,384,768]{2,1,0:T(8,128)(2,1)}), bf16[1,3072,768]{2,1,0:T(8,128)(2,1)}) %all-gather.65.cloned.1.call-update) | async-done | bytes 4718608 | tf_op jit(solution)/shard_map/all_gather | solution.py:265
  686.0 9.7 fusion.123
  707.6 9.6 all-to-all-done.4
  722.3 94.1 %while.50 = (s32[]{:T(128)}, bf16[2,512,384]{2,1,0:T(8,128)(2,1)}, bf16[2,1024,2,384]{3,2,0,1:T(2,128)(2,1)}, bf16[2,1024,384]{1,2,0:T(8,128)(2,1)}, s32[]{:T(12...) while((s32[]{:T(128)}, bf16[2,512,384]{2,1,0:T(8,128)(2,1)}, ...), condition=%wide.region_20.21_spmd, body=%wide.region_18.20_spmd.sunk | while | flops 2062939648 | bytes 222781888 | solution.py:195
  733.1 11.4 multiply_reduce_fusion.13
  745.7 6.9 multiply_convert_fusion.10
  756.3 7.0 fusion.226
  773.0 6.4 fusion.225
  780.1 11.4 multiply_reduce_fusion.13
  792.7 6.9 multiply_convert_fusion.10
  803.3 7.0 fusion.226
  819.5 18.7 all-reduce.60.cloned.1.call-done
  846.4 30.9 %all_to_all.128 = bf16[2,512,3,1,384]{4,0,3,2,1:T(2,128)(2,1)S(1)} all-to-all(bf16[2,512,3,1,384]{4,0,3,2,1:T(2,128)(2,1)S(1)} %copy.145), channel_id=1, replica_groups=mesh['dp'=8,'blk'=2,'uly'=2] {'uly'}, dimensions={1} | all-to-all | bytes 4718592 | tf_op jit(solution)/shard_map/all_to_all | solution.py:204
  896.3 10.4 fusion.124
  913.7 12.9 all_to_all.129
  931.8 92.1 %while.51 = (s32[]{:T(128)}, bf16[2,512,384]{2,1,0:T(8,128)(2,1)}, bf16[2,1024,2,384]{3,2,0,1:T(2,128)(2,1)}, bf16[2,1024,384]{1,2,0:T(8,128)(2,1)}, s32[]{:T(12...) while((s32[]{:T(128)}, bf16[2,512,384]{2,1,0:T(8,128)(2,1)}, ...), condition=%wide.region_28.29_spmd, body=%wide.region_26.28_spmd.sunk | while | flops 2062939648 | bytes 210198912 | solution.py:195
  934.7 6.4 fusion.237
  941.8 11.4 multiply_reduce_fusion.14
  954.4 6.9 multiply_convert_fusion.11
  965.0 7.0 fusion.238
  987.7 11.4 multiply_reduce_fusion.14
  1000.3 6.9 multiply_convert_fusion.11
  1010.9 7.0 fusion.238
  1032.9 7.5 convolution_bitcast_fusion.4
  1041.5 10.7 convolution_bitcast_fusion.2
  1053.6 6.7 convolution_bitcast_fusion
  1061.8 7.3 convolution_bitcast_fusion.5
  1070.5 10.2 convolution_bitcast_fusion.3
  1091.5 33.0 %all_to_all.130 = bf16[2,512,3,1,384]{4,0,3,2,1:T(2,128)(2,1)S(1)} all-to-all(bf16[2,512,3,1,384]{4,0,3,2,1:T(2,128)(2,1)S(1)} %copy.156), channel_id=1, replica_groups=mesh['dp'=8,'blk'=2,'uly'=2] {'uly'}, dimensions={1} | all-to-all | bytes 4718592 | tf_op jit(solution)/shard_map/all_to_all | solution.py:204
  1134.6 6.7 convolution_bitcast_fusion.1
  1143.9 9.7 add_add_fusion.7
  1158.3 9.8 all_gather.221
  1168.2 93.2 %reduce-scatter.13.cloned.1.call-done = f32[24,768]{1,0:T(8,128)} async-done(((f32[768,768]{1,0:T(8,128)}), f32[24,768]{1,0:T(8,128)}) %reduce-scatter.13.cloned.1.call-update) | async-done | bytes 73744 | tf_op jit(solution)/shard_map/reduce_scatter | solution.py:302
  1262.5 10.0 all_gather.220
  1281.4 42.4 %all-reduce.54 = (bf16[768]{0:T(1024)(128)(2,1)S(1)}, bf16[768]{0:T(1024)(128)(2,1)S(1)}, bf16[768]{0:T(1024)(128)(2,1)S(1)}, bf16[768]{0:T(1024)(128)(2,1)S(1)}...) all-reduce(f32[768]{0:T(1024)S(1)} %copy-done.86, ...), channel_id=35, replica_groups=mesh['dp'=8,'blk'=2,'uly'=2] {'dp','blk','uly'}, use_global_device_ids=true, to_apply=%region_35.36.clone | all-reduce | flops 18432 | bytes 110592
  1329.1 13.3 all-reduce.56
  1350.8 51.1 %reduce-scatter.19.cloned.1.call-done = f32[24,3072]{1,0:T(8,128)} async-done(((f32[768,3072]{1,0:T(8,128)}), f32[24,3072]{1,0:T(8,128)}) %reduce-scatter.19.cloned.1.call-update) | async-done | bytes 294928 | tf_op jit(solution)/shard_map/reduce_scatter | solution.py:306
  1402.9 140.4 %reduce-scatter.23.cloned.1.call-done = f32[96,768]{1,0:T(8,128)} async-done(((f32[3072,768]{1,0:T(8,128)}), f32[96,768]{1,0:T(8,128)}) %reduce-scatter.23.cloned.1.call-update) | async-done | bytes 294928 | tf_op jit(solution)/shard_map/reduce_scatter | solution.py:308
  1544.3 13.4 all_gather.229
  1557.7 13.1 all_gather.233
  1570.8 96.2 %reduce-scatter.11.cloned.1.call-done = f32[24,2304]{1,0:T(8,128)} async-done(((f32[768,2304]{1,0:T(8,128)}), f32[24,2304]{1,0:T(8,128)}) %reduce-scatter.11.cloned.1.call-update) | async-done | bytes 221200 | tf_op jit(solution)/shard_map/reduce_scatter | solution.py:299
  1668.0 12.2 all_gather.215
  1680.2 128.4 %reduce-scatter.17.cloned.1.call-done = f32[24,3072]{1,0:T(8,128)} async-done(((f32[768,3072]{1,0:T(8,128)}), f32[24,3072]{1,0:T(8,128)}) %reduce-scatter.17.cloned.1.call-update) | async-done | bytes 294928 | tf_op jit(solution)/shard_map/reduce_scatter | solution.py:306
  1809.6 139.6 %reduce-scatter.21.cloned.1.call-done = f32[96,768]{1,0:T(8,128)} async-done(((f32[3072,768]{1,0:T(8,128)}), f32[96,768]{1,0:T(8,128)}) %reduce-scatter.21.cloned.1.call-update) | async-done | bytes 294928 | tf_op jit(solution)/shard_map/reduce_scatter | solution.py:308
  1950.2 13.5 all_gather.232
  1965.2 13.1 all_gather.228
  1979.9 94.1 %reduce-scatter.9.cloned.1.call-done = f32[24,2304]{1,0:T(8,128)} async-done(((f32[768,2304]{1,0:T(8,128)}), f32[24,2304]{1,0:T(8,128)}) %reduce-scatter.9.cloned.1.call-update) | async-done | bytes 221200 | tf_op jit(solution)/shard_map/reduce_scatter | solution.py:299
  2075.0 12.2 all_gather.214
  (730 shorter events, 375.7 us)
Async XLA Ops:
  7.2 67.3 %copy-start.16 = (bf16[2,256,768]{2,1,0:T(8,128)(2,1)S(1)}, bf16[2,256,768]{2,1,0:T(8,128)(2,1)}, u32[]{:S(2)}) copy-start(bf16[2,256,768]{2,1,0:T(8,128)(2,1)} %param.23) | copy-start | bytes 2359300
  7.2 72.3 %all-gather.43.cloned.1.call-start = ((), (), s32[]{:S(2)}) async-start(), calls=%async_computation.24 | async-start | bytes 3981312 | tf_op jit(solution)/shard_map/all_gather | solution.py:251
  9.4 115.9 %all-gather.45.cloned.1.call-start = ((), (), s32[]{:S(2)}) async-start(), calls=%async_computation.25 | async-start | bytes 2359296 | tf_op jit(solution)/shard_map/all_gather | solution.py:108
  116.3 22.2 %all-gather.47.cloned.1.call-start = ((), (), s32[]{:S(2)}) async-start(), calls=%async_computation.26 | async-start | bytes 2359296 | tf_op jit(solution)/shard_map/all_gather | solution.py:107
  117.0 90.5 %all-gather.49.cloned.1.call-start = ((), (), s32[]{:S(2)}) async-start(), calls=%async_computation.27 | async-start | bytes 1327104 | tf_op jit(solution)/shard_map/all_gather | solution.py:254
  117.8 146.3 %all-gather.51.cloned.1.call-start = ((), (), s32[]{:S(2)}) async-start(), calls=%async_computation.28 | async-start | bytes 5308416 | tf_op jit(solution)/shard_map/all_gather | solution.py:263
  119.0 225.8 %all-gather.53.cloned.1.call-start = ((), (), s32[]{:S(2)}) async-start(), calls=%async_computation.29 | async-start | bytes 5308416 | tf_op jit(solution)/shard_map/all_gather | solution.py:265
  120.2 290.2 %all-gather.55.cloned.1.call-start = ((), (), s32[]{:S(2)}) async-start(), calls=%async_computation.30 | async-start | bytes 3981312 | tf_op jit(solution)/shard_map/all_gather | solution.py:251
  166.9 38.1 %copy-start.2 = (bf16[2,1024,384]{1,2,0:T(8,128)(2,1)}, bf16[2,1024,384]{1,2,0:T(8,128)(2,1)S(1)}, u32[]{:S(2)}) copy-start(bf16[2,1024,384]{1,2,0:T(8,128)(2,1)S(1)} %get-tuple-element.834) | copy-start | bytes 4718596
  166.9 38.1 %copy-start.3 = (bf16[2,1024,384]{1,2,0:T(8,128)(2,1)}, bf16[2,1024,384]{1,2,0:T(8,128)(2,1)S(1)}, u32[]{:S(2)}) copy-start(bf16[2,1024,384]{1,2,0:T(8,128)(2,1)S(1)} %get-tuple-element.835) | copy-start | bytes 4718596
  166.9 38.1 %copy-start.47 = (f32[2,6,512]{2,1,0:T(8,128)}, f32[2,6,512]{2,1,0:T(8,128)S(1)}, u32[]{:S(2)}) copy-start(f32[2,6,512]{2,1,0:T(8,128)S(1)} %get-tuple-element.788) | copy-start | bytes 73732
  170.2 32.0 %all-to-all-start.1 = ((bf16[2,512,1,384]{3,0,2,1:T(2,128)(2,1)}), bf16[2,512,1,384]{3,0,2,1:T(2,128)(2,1)}, u32[]{:S(2)}, u32[]{:S(2)}) async-start(bf16[2,512,1,384]{3,0,2,1:T(2,128)(2,1)} %bitcast.462), calls=%async_computation.1 | async-start | bytes 1572864 | tf_op jit(solution)/shard_map/all_to_all | solution.py:117
  174.5 292.0 %all-gather.57.cloned.1.call-start = ((), (), s32[]{:S(2)}) async-start(), calls=%async_computation.31 | async-start | bytes 2359296 | tf_op jit(solution)/shard_map/all_gather | solution.py:108
  174.6 89.6 %copy-start.111 = (f32[768]{0:T(1024)}, f32[768]{0:T(1024)S(1)}, u32[]{:S(2)}) copy-start(f32[768]{0:T(1024)S(1)} %convert_element_type.375) | copy-start | bytes 9220
  174.6 89.5 %copy-start.52 = (f32[768]{0:T(1024)}, f32[768]{0:T(1024)S(1)}, u32[]{:S(2)}) copy-start(f32[768]{0:T(1024)S(1)} %convert_element_type.374) | copy-start | bytes 9220
  202.1 142.8 %copy-start.94 = (f32[1,3072]{1,0:T(1,128)}, f32[1,3072]{1,0:T(1,128)S(1)}, u32[]{:S(2)}) copy-start(f32[1,3072]{1,0:T(1,128)S(1)} %convert_element_type.358) | copy-start | bytes 36868
  202.1 208.3 %copy-start.113 = (f32[768]{0:T(1024)}, f32[768]{0:T(1024)S(1)}, u32[]{:S(2)}) copy-start(f32[768]{0:T(1024)S(1)} %convert_element_type.378) | copy-start | bytes 9220
  202.1 208.3 %copy-start.55 = (f32[768]{0:T(1024)}, f32[768]{0:T(1024)S(1)}, u32[]{:S(2)}) copy-start(f32[768]{0:T(1024)S(1)} %convert_element_type.377) | copy-start | bytes 9220
  210.1 134.7 %copy-start.6 = (f32[2,256,768]{2,1,0:T(8,128)}, f32[2,256,768]{2,1,0:T(8,128)S(1)}, u32[]{:S(2)}) copy-start(f32[2,256,768]{2,1,0:T(8,128)S(1)} %get-tuple-element.457) | copy-start | bytes 4718596
  210.2 60.9 %copy-start.60 = (f32[2,256]{1,0:T(2,128)}, f32[2,256]{1,0:T(2,128)S(1)}, u32[]{:S(2)}) copy-start(f32[2,256]{1,0:T(2,128)S(1)} %broadcast_multiply_fusion.2) | copy-start | bytes 6148
  210.5 60.6 %copy-start.78 = (f32[2,256]{1,0:T(2,128)}, f32[2,256]{1,0:T(2,128)S(1)}, u32[]{:S(2)}) copy-start(f32[2,256]{1,0:T(2,128)S(1)} %multiply_reduce_fusion.10) | copy-start | bytes 6148
  210.5 60.6 %copy-start.68 = (f32[2,256]{1,0:T(2,128)}, f32[2,256]{1,0:T(2,128)S(1)}, u32[]{:S(2)}) copy-start(f32[2,256]{1,0:T(2,128)S(1)} %fusion.104) | copy-start | bytes 6148
  352.4 198.7 %copy-start.9 = (f32[2,256,768]{2,1,0:T(8,128)}, f32[2,256,768]{2,1,0:T(8,128)S(1)}, u32[]{:S(2)}) copy-start(f32[2,256,768]{2,1,0:T(8,128)S(1)} %get-tuple-element.459) | copy-start | bytes 4718596
  352.4 62.1 %copy-start.63 = (f32[2,256]{1,0:T(2,128)}, f32[2,256]{1,0:T(2,128)S(1)}, u32[]{:S(2)}) copy-start(f32[2,256]{1,0:T(2,128)S(1)} %broadcast_multiply_fusion.1) | copy-start | bytes 6148
  352.8 61.8 %copy-start.80 = (f32[2,256]{1,0:T(2,128)}, f32[2,256]{1,0:T(2,128)S(1)}, u32[]{:S(2)}) copy-start(f32[2,256]{1,0:T(2,128)S(1)} %multiply_reduce_fusion.9) | copy-start | bytes 6148
  352.8 61.8 %copy-start.71 = (f32[2,256]{1,0:T(2,128)}, f32[2,256]{1,0:T(2,128)S(1)}, u32[]{:S(2)}) copy-start(f32[2,256]{1,0:T(2,128)S(1)} %fusion.105) | copy-start | bytes 6148
  457.9 21.8 %all-gather.59.cloned.1.call-start = ((), (), s32[]{:S(2)}) async-start(), calls=%async_computation.32 | async-start | bytes 2359296 | tf_op jit(solution)/shard_map/all_gather | solution.py:107
  458.6 92.5 %all-gather.61.cloned.1.call-start = ((), (), s32[]{:S(2)}) async-start(), calls=%async_computation.33 | async-start | bytes 1327104 | tf_op jit(solution)/shard_map/all_gather | solution.py:254
  459.2 146.1 %all-gather.63.cloned.1.call-start = ((), (), s32[]{:S(2)}) async-start(), calls=%async_computation.34 | async-start | bytes 5308416 | tf_op jit(solution)/shard_map/all_gather | solution.py:263
  460.0 226.0 %all-gather.65.cloned.1.call-start = ((), (), s32[]{:S(2)}) async-start(), calls=%async_computation.35 | async-start | bytes 5308416 | tf_op jit(solution)/shard_map/all_gather | solution.py:265
  514.3 30.9 %all-to-all-start.3 = ((bf16[2,512,1,384]{3,0,2,1:T(2,128)(2,1)}), bf16[2,512,1,384]{3,0,2,1:T(2,128)(2,1)}, u32[]{:S(2)}, u32[]{:S(2)}) async-start(bf16[2,512,1,384]{3,0,2,1:T(2,128)(2,1)} %bitcast.463), calls=%async_computation.3 | async-start | bytes 1572864 | tf_op jit(solution)/shard_map/all_to_all | solution.py:117
  518.6 86.7 %copy-start.115 = (f32[768]{0:T(1024)}, f32[768]{0:T(1024)S(1)}, u32[]{:S(2)}) copy-start(f32[768]{0:T(1024)S(1)} %convert_element_type.383) | copy-start | bytes 9220
  518.7 180.6 %copy-start.92 = (f32[768]{0:T(1024)}, f32[768]{0:T(1024)S(1)}, u32[]{:S(2)}) copy-start(f32[768]{0:T(1024)S(1)} %convert_element_type.382) | copy-start | bytes 9220
  545.2 140.8 %copy-start.97 = (f32[1,3072]{1,0:T(1,128)}, f32[1,3072]{1,0:T(1,128)S(1)}, u32[]{:S(2)}) copy-start(f32[1,3072]{1,0:T(1,128)S(1)} %convert_element_type.367) | copy-start | bytes 36868
  553.6 145.7 %copy-start.74 = (f32[2,256]{1,0:T(2,128)}, f32[2,256]{1,0:T(2,128)S(1)}, u32[]{:S(2)}) copy-start(f32[2,256]{1,0:T(2,128)S(1)} %broadcast_multiply_fusion) | copy-start | bytes 6148
  555.0 144.3 %copy-start.101 = (f32[2,256]{1,0:T(2,128)}, f32[2,256]{1,0:T(2,128)S(1)}, u32[]{:S(2)}) copy-start(f32[2,256]{1,0:T(2,128)S(1)} %fusion.106) | copy-start | bytes 6148
  555.0 131.0 %copy-start.30 = (bf16[2,256,768]{2,1,0:T(8,128)(2,1)S(1)}, bf16[2,256,768]{2,1,0:T(8,128)(2,1)}, u32[]{:S(2)}) copy-start(bf16[2,256,768]{2,1,0:T(8,128)(2,1)} %param.24) | copy-start | bytes 2359300
  703.6 13.6 all-to-all-start.4
  707.1 131.1 %all-reduce.60.cloned.1.call-start = ((), (), s32[]{:S(2)}) async-start(), calls=%async_computation.36 | async-start | bytes 6291456
  733.0 11.4 slice-start
  733.1 11.4 slice-start.1
  733.1 12.6 slice-start.2
  780.1 11.4 slice-start
  780.1 11.4 slice-start.1
  780.1 12.6 slice-start.2
  816.4 266.8 %all-reduce.62.cloned.1.call-start = ((), (), s32[]{:S(2)}) async-start(), calls=%async_computation.37 | async-start | bytes 6291456
  894.8 11.9 slice-start.10
  896.2 15.2 copy-start.26
  896.2 10.4 copy-start.61
  941.8 11.4 slice-start.3
  941.8 11.4 slice-start.4
  941.8 12.6 slice-start.5
  987.6 11.4 slice-start.3
  987.6 11.4 slice-start.4
  987.7 12.6 slice-start.5
  1023.9 133.5 %reduce-scatter.15.cloned.1.call-start = ((), (), s32[]{:S(2)}) async-start(), calls=%async_computation.19 | async-start | bytes 2433024 | tf_op jit(solution)/shard_map/reduce_scatter | solution.py:302
  1027.6 233.9 %reduce-scatter.13.cloned.1.call-start = ((), (), s32[]{:S(2)}) async-start(), calls=%async_computation.18 | async-start | bytes 2433024 | tf_op jit(solution)/shard_map/reduce_scatter | solution.py:302
  1031.5 370.4 %reduce-scatter.19.cloned.1.call-start = ((), (), s32[]{:S(2)}) async-start(), calls=%async_computation.21 | async-start | bytes 9732096 | tf_op jit(solution)/shard_map/reduce_scatter | solution.py:306
  1040.4 502.9 %reduce-scatter.23.cloned.1.call-start = ((), (), s32[]{:S(2)}) async-start(), calls=%async_computation.23 | async-start | bytes 9732096 | tf_op jit(solution)/shard_map/reduce_scatter | solution.py:308
  1052.3 614.8 %reduce-scatter.11.cloned.1.call-start = ((), (), s32[]{:S(2)}) async-start(), calls=%async_computation.17 | async-start | bytes 7299072 | tf_op jit(solution)/shard_map/reduce_scatter | solution.py:299
  1060.4 748.3 %reduce-scatter.17.cloned.1.call-start = ((), (), s32[]{:S(2)}) async-start(), calls=%async_computation.20 | async-start | bytes 9732096 | tf_op jit(solution)/shard_map/reduce_scatter | solution.py:306
  1069.1 880.1 %reduce-scatter.21.cloned.1.call-start = ((), (), s32[]{:S(2)}) async-start(), calls=%async_computation.22 | async-start | bytes 9732096 | tf_op jit(solution)/shard_map/reduce_scatter | solution.py:308
  1080.7 993.3 %reduce-scatter.9.cloned.1.call-start = ((), (), s32[]{:S(2)}) async-start(), calls=%async_computation.16 | async-start | bytes 7299072 | tf_op jit(solution)/shard_map/reduce_scatter | solution.py:299
  1261.4 13.6 copy-start.20
  (125 other events, 447.6 us)
Sparse Core Ops, SparseCore 0:
  10.8 68.6 all-gather.42
  116.4 8.9 all-gather.44
  127.5 10.9 all-gather.46
  140.5 42.3 all-gather.48
  185.5 78.6 all-gather.50
  266.8 78.0 all-gather.52
  347.0 63.3 all-gather.54
  458.0 8.4 all-gather.56
  468.7 10.9 all-gather.58
  481.7 42.0 all-gather.60
  526.6 78.7 all-gather.62
  607.9 78.0 all-gather.64
  816.5 21.5 all-reduce.59
  1024.0 23.7 all-reduce.61
  1053.0 104.4 reduce-scatter.14
  1163.4 97.9 reduce-scatter.12
  1267.2 134.6 reduce-scatter.18
  1408.7 134.5 reduce-scatter.22
  1549.0 118.0 reduce-scatter.10
  1673.8 134.7 reduce-scatter.16
  1814.6 134.6 reduce-scatter.20
  1955.8 118.1 reduce-scatter.8
where the time goes:
time: 2110 us; the launch traced here: 2100 us
  waiting for transfers between devices  1120 us (53%)
  blocking collectives  382 us (18%)
  matrix products  277 us (13%)
  local copies, waits for them, and re-layouts  194 us (9%)
  other arithmetic  86.2 us (4%)
    reduce_scatter x2, waiting for transfers between devices, shards(): lax.psum_scatter(every[11], ('dp', 'blk', 'uly'), scatter_dimension=0, ti...  280 us
    reduce_scatter x2, waiting for transfers between devices, shards(): lax.psum_scatter(every[2], ('dp', 'blk', 'uly'), scatter_dimension=0, til...  190 us
    reduce_scatter x2, waiting for transfers between devices, shards(): lax.psum_scatter(every[9], ('dp', 'blk', 'uly'), scatter_dimension=0, til...  179 us
    all_gather x2, waiting for transfers between devices, shards(): lax.all_gather(down_weight[layer], 'dp', axis=0, tiled=True)  146 us
    all_gather x2, waiting for transfers between devices, shards(): lax.all_gather(up_weight[layer], 'dp', axis=0, tiled=True)  104 us
    reduce_scatter x2, waiting for transfers between devices, shards(): lax.psum_scatter(every[5], ('dp', 'blk', 'uly'), scatter_dimension=0, til...  97 us
    unnamed x3, blocking collectives  95.8 us
    all_to_all x2, blocking collectives, attention_backward(): lax.all_to_all(stacked[:, :, :, None], 'uly', split_axis=1, concat_axis=3...  63.9 us
  transfers between devices with their start and end apart: 25, of which 20 were waited for; matrix products, arithmetic and copies ran while one was open for 12% of the time, Pallas kernels for 0%

commit v1 on v0

v1 whole, which is shorter than its diff:
```python
from functools import partial

import jax
import jax.numpy as jnp
from jax import lax
from jax.sharding import PartitionSpec as P

HDIM = 64
EPSILON = 1e-05
NEGATIVE = -1e30
LOW = jnp.bfloat16
FULL = jnp.float32


def normalize(residual, gain, shift):
    average = jnp.mean(residual, axis=-1, keepdims=True)
    centred = residual - average
    variance = jnp.mean(centred * centred, axis=-1, keepdims=True)
    return centred * lax.rsqrt(variance + EPSILON) * gain + shift


def norm_backward(residual, gain, shift, slope):
    unused, pullback = jax.vjp(normalize, residual, gain, shift)
    return pullback(slope)


def matmul(left, right):
    return jnp.dot(left, right, preferred_element_type=FULL)


def contract(left, right):
    return jnp.einsum("std,ste->de", left, right, preferred_element_type=FULL)


def transposed(left, right):
    return jnp.einsum("ste,de->std", left, right, preferred_element_type=FULL)


def swap(item, axis, mask=1):
    count = lax.axis_size(axis)
    return lax.ppermute(item, axis, [(i, i ^ mask) for i in range(count)])


def bit_of(axis, mask=1):
    return (lax.axis_index(axis) & mask) != 0


def ordered(own, other, bit, axis):
    low = jnp.where(bit, other, own)
    high = jnp.where(bit, own, other)
    return jnp.stack([low, high], axis=axis)


def masks_of(axis):
    count = lax.axis_size(axis)
    masks = []
    mask = 1
    while mask < count:
        masks.append(mask)
        mask *= 2
    return masks


def gather_rows(piece):
    held = piece[None]
    for mask in reversed(masks_of("dp")):
        other = swap(held, "dp", mask)
        held = ordered(held, other, bit_of("dp", mask), 1)
        held = held.reshape((-1,) + piece.shape)
    return held


def gather_axis(piece, axis):
    return ordered(piece, swap(piece, axis), bit_of(axis), 0)


def added(left, right, dtype=LOW):
    return (left.astype(FULL) + right.astype(FULL)).astype(dtype)


def halve(held, axis, mask, position):
    index = bit_of(axis, mask).astype(jnp.int32)
    keep = lax.dynamic_index_in_dim(held, index, position, keepdims=False)
    send = lax.dynamic_index_in_dim(held, 1 - index, position, keepdims=False)
    return added(keep, swap(send, axis, mask), held.dtype)


def reduce_rows(held):
    for mask in masks_of("dp"):
        held = held.reshape((-1, 2) + held.shape[1:])
        held = halve(held, "dp", mask, 1)
    return held[0]


def gather_quarters(block):
    quarter = 2 * lax.axis_index("blk") + lax.axis_index("uly")
    width = block.shape[1] // 4
    piece = lax.dynamic_slice_in_dim(block, quarter * width, width, 1)
    rows = gather_rows(piece).reshape(-1, width)
    pair = gather_axis(rows, "uly")
    return gather_axis(pair, "blk").reshape(4, -1, width)


def reduce_quarters(slopes):
    count = lax.axis_size("dp")
    four, rows, width = slopes.shape
    held = halve(slopes.reshape(2, 2, rows, width), "blk", 1, 0)
    held = halve(held, "uly", 1, 0)
    held = reduce_rows(held.reshape(count, rows // count, width))
    pair = gather_axis(held, "uly")
    every = gather_axis(pair, "blk").reshape(4, rows // count, width)
    return every.astype(FULL)


def gather_halves(block):
    width = block.shape[1] // 2
    piece = lax.dynamic_slice_in_dim(block, lax.axis_index("blk") * width, width, 1)
    rows = gather_rows(piece).reshape(-1, width)
    return rows, swap(rows, "blk")


def reduce_halves(own, other):
    count = lax.axis_size("dp")
    rows, width = own.shape
    held = added(own, swap(other, "blk"))
    held = reduce_rows(held.reshape(count, rows // count, width))
    held = added(held, swap(held, "uly"))
    pair = gather_axis(held, "blk")
    return jnp.concatenate([pair[0], pair[1]], axis=1).astype(FULL)


def reduce_small(terms):
    count = lax.axis_size("dp")
    kinds, width = terms.shape
    held = terms.reshape(kinds, count, width // count).transpose(1, 0, 2)
    held = held + swap(held, "blk")
    held = held + swap(held, "uly")
    return reduce_rows(held)


def causal_mask(length):
    query_rows = lax.broadcasted_iota(jnp.int32, (length, length), 0)
    key_rows = lax.broadcasted_iota(jnp.int32, (length, length), 1)
    return key_rows <= query_rows


def scores_for(queries, keys):
    scores = jnp.einsum("qhd,khd->hqk", queries, keys, preferred_element_type=FULL) * HDIM ** (-0.5)
    return jnp.where(causal_mask(queries.shape[0])[None], scores, NEGATIVE)


def attend(queries, keys, values):
    count = queries.shape[0]
    queries, keys, values = (item.reshape(count, -1, HDIM) for item in (queries, keys, values))
    scores = scores_for(queries, keys)
    top = jnp.max(scores, axis=-1, keepdims=True)
    raised = jnp.exp(scores - top)
    total = jnp.sum(raised, axis=-1, keepdims=True)
    shares = (raised / total).astype(LOW)
    mixed = jnp.einsum("hqk,khd->qhd", shares, values, preferred_element_type=FULL)
    return mixed.astype(LOW).reshape(count, -1), (top + jnp.log(total))[..., 0]


def attend_back(queries, keys, values, logsum, upstream):
    count = queries.shape[0]
    queries, keys, values, upstream = (
        item.reshape(count, -1, HDIM) for item in (queries, keys, values, upstream)
    )
    scale = HDIM ** (-0.5)
    shares = jnp.exp(scores_for(queries, keys) - logsum[..., None])
    against = jnp.einsum("qhd,khd->hqk", upstream, values, preferred_element_type=FULL)
    inner = jnp.sum(shares * against, axis=-1, keepdims=True)
    slopes = (shares * (against - inner)).astype(LOW)
    query_slope = jnp.einsum("hqk,khd->qhd", slopes, keys, preferred_element_type=FULL) * scale
    key_slope = jnp.einsum("hqk,qhd->khd", slopes, queries, preferred_element_type=FULL) * scale
    value_slope = jnp.einsum(
        "hqk,qhd->khd", shares.astype(LOW), upstream, preferred_element_type=FULL
    )
    return tuple(
        item.astype(LOW).reshape(count, -1) for item in (query_slope, key_slope, value_slope)
    )


def to_heads(parts):
    core = lax.axis_index("blk")
    half = parts[0].shape[-1] // 2
    mine = jnp.stack([lax.dynamic_slice_in_dim(p, core * half, half, 2) for p in parts])
    theirs = jnp.stack([lax.dynamic_slice_in_dim(p, (1 - core) * half, half, 2) for p in parts])
    joined = ordered(mine, swap(theirs, "blk"), bit_of("blk"), 2)
    joined = joined.reshape(joined.shape[:2] + (-1, half))
    return tuple(joined[i] for i in range(len(parts)))


def to_tokens(parts):
    core = lax.axis_index("blk")
    rows = parts[0].shape[1] // 2
    mine = jnp.stack([lax.dynamic_slice_in_dim(p, core * rows, rows, 1) for p in parts])
    theirs = jnp.stack([lax.dynamic_slice_in_dim(p, (1 - core) * rows, rows, 1) for p in parts])
    other = swap(theirs, "blk")
    bit = bit_of("blk")
    low = jnp.where(bit, other, mine)
    high = jnp.where(bit, mine, other)
    joined = jnp.concatenate([low, high], axis=-1)
    return tuple(joined[i] for i in range(len(parts)))


def to_sequences(local):
    place = lax.axis_index("uly")
    count, rows, width = local.shape
    paired = local.reshape(2, count // 2, rows, width)
    keep = lax.dynamic_index_in_dim(paired, place, 0, keepdims=False)
    send = lax.dynamic_index_in_dim(paired, 1 - place, 0, keepdims=False)
    joined = ordered(keep, swap(send, "uly"), bit_of("uly"), 1)
    return joined.reshape(count // 2, 2 * rows, width)


def from_sequences(held):
    place = lax.axis_index("uly")
    count, rows, width = held.shape
    paired = held.reshape(count, 2, rows // 2, width)
    keep = lax.dynamic_index_in_dim(paired, place, 1, keepdims=False)
    send = lax.dynamic_index_in_dim(paired, 1 - place, 1, keepdims=False)
    other = swap(send.astype(LOW), "uly").astype(FULL)
    joined = ordered(keep, other, bit_of("uly"), 0)
    return joined.reshape(2 * count, rows // 2, width)


def token_sum(item):
    return jnp.sum(item.astype(FULL), axis=(0, 1))


def attention_forward(residual, weights, small):
    first_gain, first_shift, query_bias, value_bias, out_bias = small[:5]
    normed = normalize(residual, first_gain, first_shift).astype(LOW)
    queries = (matmul(normed, weights[0]) + query_bias).astype(LOW)
    keys = matmul(normed, weights[1]).astype(LOW)
    values = (matmul(normed, weights[2]) + value_bias).astype(LOW)
    headed = to_heads((queries, keys, values))
    mixed, logsum = lax.map(lambda items: attend(*items), headed)
    (returned,) = to_tokens((mixed,))
    middle = residual + matmul(returned, weights[3]) + out_bias
    return middle, (normed, headed, logsum, returned)


def feed_forward(residual, up, down, small):
    second_gain, second_shift, down_bias = small[5:8]
    up_bias = small[8:12].reshape(-1)
    own, other = down
    normed = normalize(residual, second_gain, second_shift).astype(LOW)
    width = up.shape[2]
    hidden = [
        matmul(normed, up[i]) + up_bias[i * width : (i + 1) * width] for i in range(up.shape[0])
    ]
    active = jnp.concatenate(
        [jax.nn.gelu(item, approximate=True).astype(LOW) for item in hidden], axis=-1
    )
    left, right = matmul(active, own), matmul(active, other)
    bit = bit_of("blk")
    joined = jnp.concatenate([jnp.where(bit, right, left), jnp.where(bit, left, right)], axis=-1)
    return residual + joined + down_bias, (normed, hidden, active)


def feed_backward(residual, upstream, up, down, small, record):
    second_gain, second_shift = small[5:7]
    own, other = down
    normed, hidden, active = record
    down_bias_slope = token_sum(upstream)
    low_upstream = upstream.astype(LOW)
    half = own.shape[1]
    core = lax.axis_index("blk")
    mine = lax.dynamic_slice_in_dim(low_upstream, core * half, half, 2)
    theirs = lax.dynamic_slice_in_dim(low_upstream, (1 - core) * half, half, 2)
    down_slope = reduce_halves(
        contract(active, mine).astype(LOW), contract(active, theirs).astype(LOW)
    )
    active_slope = transposed(mine, own) + transposed(theirs, other)
    width = up.shape[2]
    up_bias_slopes = []
    up_slopes = []
    norm_slope = 0.0
    for i, item in enumerate(hidden):
        unused, pullback = jax.vjp(partial(jax.nn.gelu, approximate=True), item)
        hidden_slope = pullback(active_slope[..., i * width : (i + 1) * width])[0]
        up_bias_slopes.append(token_sum(hidden_slope))
        low_hidden = hidden_slope.astype(LOW)
        up_slopes.append(contract(normed, low_hidden).astype(LOW))
        norm_slope = norm_slope + transposed(low_hidden, up[i])
    up_slope = reduce_quarters(jnp.stack(up_slopes))
    residual_slope, gain_slope, shift_slope = norm_backward(
        residual, second_gain, second_shift, norm_slope
    )
    up_bias_slope = jnp.concatenate(up_bias_slopes)
    return (
        upstream + residual_slope,
        up_slope,
        down_slope,
        (gain_slope, shift_slope, down_bias_slope, up_bias_slope),
    )


def attention_backward(residual, upstream, weights, small, record):
    first_gain, first_shift = small[:2]
    normed, headed, logsum, returned = record
    out_bias_slope = token_sum(upstream)
    low_upstream = upstream.astype(LOW)
    out_slope = contract(returned, low_upstream).astype(LOW)
    mixed_slope = transposed(low_upstream, weights[3]).astype(LOW)
    (head_slope,) = to_heads((mixed_slope,))
    slopes = lax.map(lambda items: attend_back(*items), headed + (logsum, head_slope))
    parts = to_tokens(slopes)
    query_bias_slope = token_sum(parts[0])
    value_bias_slope = token_sum(parts[2])
    weight_slopes = [contract(normed, part).astype(LOW) for part in parts]
    first_slope = sum(transposed(parts[i], weights[i]) for i in range(3))
    summed = reduce_quarters(jnp.stack(weight_slopes + [out_slope]))
    residual_slope, gain_slope, shift_slope = norm_backward(
        residual, first_gain, first_shift, first_slope
    )
    return (
        upstream + residual_slope,
        summed,
        (gain_slope, shift_slope, query_bias_slope, value_bias_slope, out_bias_slope),
    )


def shards(
    inputs,
    cotangent,
    first_gain,
    first_shift,
    in_weight,
    query_bias,
    value_bias,
    out_weight,
    out_bias,
    second_gain,
    second_shift,
    up_weight,
    up_bias,
    down_weight,
    down_bias,
):
    layers, rows = in_weight.shape[0], in_weight.shape[1]
    width = out_weight.shape[2]
    vectors = jnp.stack(
        [
            first_gain,
            first_shift,
            query_bias,
            value_bias,
            out_bias,
            second_gain,
            second_shift,
            down_bias,
        ],
        axis=1,
    )
    vectors = jnp.concatenate([vectors, up_bias.reshape(layers, -1, rows)], axis=1)
    kinds = vectors.shape[1]
    gathered = gather_rows(vectors.reshape(layers * kinds, rows))
    gathered = gathered.reshape(-1, layers, kinds, rows).astype(FULL)
    straight = gathered.transpose(1, 2, 0, 3).reshape(layers, kinds, width)
    biases = gathered[:, :, 8:].transpose(1, 0, 2, 3).reshape(layers, kinds - 8, width)
    small = jnp.concatenate([straight[:, :8], biases], axis=1)

    residual = to_sequences(inputs).astype(FULL)
    records = []
    for layer in range(layers):
        weights = gather_quarters(jnp.concatenate([in_weight[layer], out_weight[layer]], axis=1))
        up = gather_quarters(up_weight[layer])
        down = gather_halves(down_weight[layer])
        entry = residual
        middle, attention_record = attention_forward(entry, weights, small[layer])
        residual, feed_record = feed_forward(middle, up, down, small[layer])
        records.append((entry, attention_record, middle, feed_record, weights, up, down))
    outputs = from_sequences(residual)
    upstream = to_sequences(cotangent).astype(FULL)
    found = [None] * layers
    for layer in reversed(range(layers)):
        entry, attention_record, middle, feed_record, weights, up, down = records[layer]
        upstream, up_slope, down_slope, feed_small = feed_backward(
            middle, upstream, up, down, small[layer], feed_record
        )
        upstream, summed, attention_small = attention_backward(
            entry, upstream, weights, small[layer], attention_record
        )
        count = lax.axis_size("dp")
        up_terms = feed_small[3].reshape(count, kinds - 8, rows).transpose(1, 0, 2)
        terms = jnp.concatenate(
            [jnp.stack(attention_small + feed_small[:3]), up_terms.reshape(kinds - 8, width)]
        )
        vectors = reduce_small(terms)
        across = summed.transpose(1, 0, 2)
        found[layer] = (
            vectors[0],
            vectors[1],
            across[:, :3].reshape(rows, 3 * width),
            vectors[2],
            vectors[3],
            across[:, 3],
            vectors[4],
            vectors[5],
            vectors[6],
            up_slope.transpose(1, 0, 2).reshape(rows, -1),
            vectors[8:].reshape(-1),
            down_slope,
            vectors[7],
        )
    input_gradient = from_sequences(upstream)
    stacked = tuple(jnp.stack([item[index] for item in found]) for index in range(13))
    return (outputs, input_gradient) + stacked


def solution(mesh):
    token = P("dp", ("blk", "uly"), None)
    vector = P(None, "dp")
    matrix = P(None, "dp", None)
    params = (
        vector,
        vector,
        matrix,
        vector,
        vector,
        matrix,
        vector,
        vector,
        vector,
        matrix,
        vector,
        matrix,
        vector,
    )
    specs = (token, token) + params
    return jax.shard_map(shards, mesh=mesh, in_specs=specs, out_specs=specs, check_vma=False)
```

time: 2110 us -> 955 us (0.45)
  waiting for transfers between devices: 1120 us -> 272 us
  blocking collectives: 382 us -> 0 us
  other arithmetic: 86.2 us -> 188 us
  starting transfers between devices: 14.4 us -> 75.4 us
  local copies, waits for them, and re-layouts: 194 us -> 136 us
    reduce_scatter x8 -> x0, waiting for transfers between devices: 747 us -> none  [the longest x2 280 us: shards(): lax.psum_scatter(every[11], ('dp', 'blk', 'uly'), scatter_dimension=0, ti...]
    all_gather x12 -> x0, waiting for transfers between devices: 343 us -> none  [the longest x2 146 us: shards(): lax.all_gather(down_weight[layer], 'dp', axis=0, tiled=True)]
    ppermute x0 -> x93, waiting for transfers between devices: none -> 272 us  [swap(): return lax.ppermute(item, axis, [(i, i ^ mask) for i in range(count)])]
    all_gather x10 -> x0, blocking collectives: 151 us -> none  [the longest x2 53.3 us: shards(): lax.all_gather(up_bias[layer], 'dp', axis=0, tiled=True)]
    all_to_all x5 -> x0, blocking collectives: 136 us -> none  [the longest x2 63.9 us: attention_backward(): lax.all_to_all(stacked[:, :, :, None], 'uly', split_axis=1, concat_axis=3...]
    unnamed x3 -> x0, blocking collectives: 95.8 us -> none
    ppermute x0 -> x93, starting transfers between devices: none -> 75.4 us  [swap(): return lax.ppermute(item, axis, [(i, i ^ mask) for i in range(count)])]
    another operation x15 -> x101, other arithmetic: 12.2 us -> 71.3 us  [the longest x80 44.5 us: ordered(): return jnp.stack([low, high], axis=axis)]
  transfers between devices with their start and end apart: 25 -> 93, of which waited for: 20 -> 44; matrix products, arithmetic and copies ran while one was open for 12% -> 48% of each run, Pallas kernels for 0% -> 0%
where the time goes in v1:
time: 955 us; the launch traced here: 943 us
  waiting for transfers between devices  272 us (28%)
  matrix products  267 us (28%)
  other arithmetic  188 us (20%)
  local copies, waits for them, and re-layouts  136 us (14%)
  starting transfers between devices  75.4 us (8%)
    ppermute x93, waiting for transfers between devices, swap(): return lax.ppermute(item, axis, [(i, i ^ mask) for i in range(count)])  272 us
    ppermute x93, starting transfers between devices, swap(): return lax.ppermute(item, axis, [(i, i ^ mask) for i in range(count)])  75.4 us
    dot_general x20, matrix products, transposed(): return jnp.einsum('ste,de->std', left, right, preferred_element_type=FULL)  56.1 us
    dot_general x20, matrix products, contract(): return jnp.einsum('std,ste->de', left, right, preferred_element_type=FULL)  47.5 us
    another operation x80, other arithmetic, ordered(): return jnp.stack([low, high], axis=axis)  44.5 us
    dot_general x20, matrix products, matmul(): return jnp.dot(left, right, preferred_element_type=FULL)  40.1 us
    convert_element_type x2, other arithmetic, attend_back(): slopes = (shares * (against - inner)).astype(LOW)  37.9 us
    dot_general x2, matrix products, attend_back(): jnp.einsum('qhd,khd->hqk', upstream, values, preferred_element_type=FULL)  31.8 us
  transfers between devices with their start and end apart: 93, of which 44 were waited for; matrix products, arithmetic and copies ran while one was open for 48% of the time, Pallas kernels for 0%

profile of v1, /device:TPU:0, one launch (start us, length us, event | category | flops | bytes accessed | tf_op | source)
XLA Modules:
  0.0 943.3 jit_solution(14864755886984155193)
XLA Ops:
  6.9 4.1 collective-permute-start.1
  39.5 13.1 %collective-permute-done.11 = bf16[1,96,768]{2,1,0:T(8,128)(2,1)} collective-permute-done((bf16[1,96,768]{2,1,0:T(8,128)(2,1)}, bf16[1,96,768]{2,1,0:T(8,128)(2,1)}, u32[]{:S(2)}, u32[]{:S(2)}) %collective-permute-start.11) | collective-permute-done | bytes 147488 | tf_op jit(solution)/shard_map/ppermute | solution.py:41
  59.4 10.6 %collective-permute-done.32 = bf16[1,384,384]{2,1,0:T(8,128)(2,1)S(1)} collective-permute-done((bf16[1,384,384]{2,1,0:T(8,128)(2,1)}, bf16[1,384,384]{2,1,0:T(8,128)(2,1)S(1)}, u32[]{:S(2)}, u32[]{:S(2)}) %collective-permute-start.32) | collective-permute-done | bytes 294944 | tf_op jit(solution)/shard_map/ppermute | solution.py:41
  89.9 3.8 collective-permute-done.28
  96.5 20.7 %collective-permute-done.33 = bf16[2,384,384]{2,1,0:T(8,128)(2,1)S(1)} collective-permute-done((bf16[2,384,384]{2,1,0:T(8,128)(2,1)S(1)}, bf16[2,384,384]{2,1,0:T(8,128)(2,1)S(1)}, u32[]{:S(2)}, u32[]{:S(2)}) %collective-permute-start.33) | collective-permute-done | bytes 589856 | tf_op jit(solution)/shard_map/ppermute | solution.py:41
  126.9 12.1 %collective-permute-done.13 = bf16[4,96,768]{2,1,0:T(8,128)(2,1)S(1)} collective-permute-done((bf16[4,96,768]{2,1,0:T(8,128)(2,1)S(1)}, bf16[4,96,768]{2,1,0:T(8,128)(2,1)S(1)}, u32[]{:S(2)}, u32[]{:S(2)}) %collective-permute-start.13) | collective-permute-done | bytes 589856 | tf_op jit(solution)/shard_map/ppermute | solution.py:41
  141.4 10.5 %collective-permute-done.7 = bf16[768,768]{1,0:T(8,128)(2,1)S(1)} collective-permute-done((bf16[768,768]{1,0:T(8,128)(2,1)S(1)}, bf16[768,768]{1,0:T(8,128)(2,1)S(1)}, u32[]{:S(2)}, u32[]{:S(2)}) %collective-permute-start.7) | collective-permute-done | bytes 1179680 | tf_op jit(solution)/shard_map/ppermute | solution.py:41
  153.9 10.4 %collective-permute-done.34 = bf16[4,384,384]{2,1,0:T(8,128)(2,1)S(1)} collective-permute-done((bf16[4,384,384]{2,1,0:T(8,128)(2,1)S(1)}, bf16[4,384,384]{2,1,0:T(8,128)(2,1)S(1)}, u32[]{:S(2)}, u32[]{:S(2)}) %collective-permute-start.34) | collective-permute-done | bytes 1179680 | tf_op jit(solution)/shard_map/ppermute | solution.py:41
  164.7 21.3 %collective-permute-done.18 = bf16[4,384,384]{2,1,0:T(8,128)(2,1)S(1)} collective-permute-done((bf16[4,384,384]{2,1,0:T(8,128)(2,1)S(1)}, bf16[4,384,384]{2,1,0:T(8,128)(2,1)S(1)}, u32[]{:S(2)}, u32[]{:S(2)}) %collective-permute-start.18) | collective-permute-done | bytes 1179680 | tf_op jit(solution)/shard_map/ppermute | solution.py:41
  190.2 6.3 fusion.208
  197.5 27.0 %collective-permute-done.23 = bf16[768,768]{1,0:T(8,128)(2,1)S(1)} collective-permute-done((bf16[768,768]{1,0:T(8,128)(2,1)S(1)}, bf16[768,768]{1,0:T(8,128)(2,1)S(1)}, u32[]{:S(2)}, u32[]{:S(2)}) %collective-permute-start.23) | collective-permute-done | bytes 1179680 | tf_op jit(solution)/shard_map/ppermute | solution.py:41
  246.7 3.2 reshape.2113
  251.3 10.5 %fusion.323 = (f32[6,1024]{1,0:T(8,128)S(1)}, f32[6,1024,1024]{1,2,0:T(8,128)}) fusion(bf16[1024,6,64]{0,2,1:T(8,128)(2,1)S(1)} %reshape.2114, bf16[1024,6,64]{0,2,1:T(8,128)(2,1)S(1)} %reshape.2115, pred[1024,1024]{0,1:T(8,128)(4,1)S(1)} %iota_compare_fusion), kind=kOutput, calls=%fused_computation.839 | convolution fusion | flops 824174592 | bytes 27811840 | tf_op jit(solution)/shard_map/while/body/eval_jaxpr/qhd,khd->hqk/dot_general | solution.py:148
  261.8 10.3 %fusion = f32[6,1024]{1,0:T(8,128)S(1)} fusion(f32[6,1024,1024]{1,2,0:T(8,128)} %get-tuple-element.374, f32[6,1024]{1,0:T(8,128)S(1)} %get-tuple-element.373), kind=kLoop, calls=%fused_computation.12 | loop fusion | flops 12576768 | bytes 25214976 | tf_op jit(solution)/shard_map/while/body/eval_jaxpr/reduce_sum | solution.py:158
  272.1 10.9 %fusion.132 = bf16[6,64,1024]{2,1,0:T(8,128)(2,1)S(1)} fusion(bf16[1024,6,64]{0,2,1:T(8,128)(2,1)S(1)} %copy-done.57, f32[6,1024,1024]{1,2,0:T(8,128)} %get-tuple-element.374, f32[6,1024]{1,0:T(8,128)S(1)} %fusion, f32[6,1024]{1,0:T(8,128)S(1)} %get-tuple-element.373), kind=kOutput, calls=%fused_computation.324 | convolution fusion | flops 824573952 | bytes 26787840 | tf_op jit(solution)/shard_map/while/body/eval_jaxpr/hqk,khd->qhd/dot_general | solution.py:160
  286.0 4.4 pad_maximum_fusion.1
  305.7 3.8 fusion.291
  309.5 3.5 broadcast_select_fusion.7
  318.5 6.2 add_bitcast_fusion.1
  334.5 3.2 reshape.2129
  340.7 3.2 reshape.2127
  347.0 3.2 reshape.2128
  350.2 11.7 %fusion.325 = (f32[6,1024]{1,0:T(8,128)S(1)}, f32[6,1024,1024]{1,2,0:T(8,128)}) fusion(bf16[1024,6,64]{0,2,1:T(8,128)(2,1)} %reshape.2128, bf16[1024,6,64]{0,2,1:T(8,128)(2,1)} %reshape.2129, pred[1024,1024]{0,1:T(8,128)(4,1)S(1)} %iota_compare_fusion), kind=kOutput, calls=%fused_computation.841 | convolution fusion | flops 824174592 | bytes 27811840 | tf_op jit(solution)/shard_map/while/body/eval_jaxpr/qhd,khd->hqk/dot_general | solution.py:148
  362.0 10.3 %fusion.1 = f32[6,1024]{1,0:T(8,128)S(1)} fusion(f32[6,1024,1024]{1,2,0:T(8,128)} %get-tuple-element.378, f32[6,1024]{1,0:T(8,128)S(1)} %get-tuple-element.377), kind=kLoop, calls=%fused_computation.13 | loop fusion | flops 12576768 | bytes 25214976 | tf_op jit(solution)/shard_map/while/body/eval_jaxpr/reduce_sum | solution.py:158
  372.2 10.7 %fusion.131 = bf16[6,64,1024]{2,1,0:T(8,128)(2,1)S(1)} fusion(bf16[1024,6,64]{0,2,1:T(8,128)(2,1)S(1)} %copy-done.58, f32[6,1024,1024]{1,2,0:T(8,128)} %get-tuple-element.378, f32[6,1024]{1,0:T(8,128)S(1)} %fusion.1, f32[6,1024]{1,0:T(8,128)S(1)} %get-tuple-element.377), kind=kOutput, calls=%fused_computation.323 | convolution fusion | flops 824573952 | bytes 26787840 | tf_op jit(solution)/shard_map/while/body/eval_jaxpr/hqk,khd->qhd/dot_general | solution.py:160
  394.2 8.6 fusion.311
  407.1 4.7 fusion.289
  411.8 4.2 convolution_convert_fusion
  416.3 3.3 fusion.124
  424.1 3.7 multiply_reduce_fusion.2
  428.5 4.5 broadcast_select_fusion.5
  452.8 11.4 %fusion.125 = bf16[6,64,1024]{2,1,0:T(8,128)(2,1)} fusion(bf16[1024,6,64]{0,2,1:T(8,128)(2,1)S(1)} %reshape.2146, f32[6,1024,1024]{1,2,0:T(8,128)} %get-tuple-element.378, f32[6,1024]{1,0:T(8,128)S(1)} %log_add_fusion.1), kind=kOutput, calls=%fused_computation.321 | convolution fusion | flops 818282496 | bytes 26763264 | tf_op jit(solution)/shard_map/while/body/eval_jaxpr/hqk,qhd->khd/dot_general | solution.py:176
  464.2 15.9 %multiply_reduce_fusion.1 = (f32[6,1024]{1,0:T(8,128)S(1)}, f32[6,1024,1024]{1,2,0:T(8,128)}) fusion(f32[6,1024,1024]{1,2,0:T(8,128)} %get-tuple-element.378, f32[6,1024]{1,0:T(8,128)S(1)} %log_add_fusion.1, bf16[1024,6,64]{0,2,1:T(8,128)(2,1)S(1)} %reshape.2146, bf16[1024,6,64]{0,2,1:T(8,128)(2,1)} %reshape.2127), kind=kOutput, calls=%fused_computation.4 | convolution fusion | flops 824174592 | bytes 51953664 | tf_op jit(solution)/shard_map/while/body/eval_jaxpr/qhd,khd->hqk/dot_general | solution.py:171
  480.0 16.8 %multiply_convert_fusion.1 = bf16[6,1024,1024]{1,2,0:T(8,128)(2,1)S(1)} fusion(f32[6,1024,1024]{1,2,0:T(8,128)} %get-tuple-element.384, f32[6,1024,1024]{1,2,0:T(8,128)} %get-tuple-element.378, f32[6,1024]{1,0:T(8,128)S(1)} %get-tuple-element.383, f32[6,1024]{1,0:T(8,128)S(1)} %log_add_fusion.1), kind=kLoop, calls=%fused_computation.3 | loop fusion | flops 25165824 | bytes 62963712 | tf_op jit(solution)/shard_map/while/body/eval_jaxpr/convert_element_type | solution.py:173
  496.8 6.0 multiply_convert_fusion.4
  502.8 4.4 multiply_convert_fusion.5
  543.9 3.7 convolution_convert_fusion.2
  547.6 3.5 fusion.233
  551.2 3.8 add_bitcast_fusion
  555.0 5.5 fusion.300
  588.0 3.2 multiply_reduce_fusion.4
  594.5 3.1 convolution_convert_fusion.20
  606.5 3.3 collective-permute-done.51
  617.9 15.9 %multiply_reduce_fusion = (f32[6,1024]{1,0:T(8,128)S(1)}, f32[6,1024,1024]{1,2,0:T(8,128)}) fusion(f32[6,1024,1024]{1,2,0:T(8,128)} %get-tuple-element.374, f32[6,1024]{1,0:T(8,128)S(1)} %copy-done.139, bf16[1024,6,64]{0,2,1:T(8,128)(2,1)S(1)} %reshape.2154, bf16[1024,6,64]{0,2,1:T(8,128)(2,1)} %reshape.2113), kind=kOutput, calls=%fused_computation.1 | convolution fusion | flops 824174592 | bytes 51953664 | tf_op jit(solution)/shard_map/while/body/eval_jaxpr/qhd,khd->hqk/dot_general | solution.py:171
  633.9 21.1 %multiply_convert_fusion = bf16[6,1024,1024]{1,2,0:T(8,128)(2,1)} fusion(f32[6,1024,1024]{1,2,0:T(8,128)} %get-tuple-element.388, f32[6,1024,1024]{1,2,0:T(8,128)} %get-tuple-element.374, f32[6,1024]{1,0:T(8,128)S(1)} %get-tuple-element.387, f32[6,1024]{1,0:T(8,128)S(1)} %copy-done.139), kind=kLoop, calls=%fused_computation | loop fusion | flops 25165824 | bytes 62963712 | tf_op jit(solution)/shard_map/while/body/eval_jaxpr/convert_element_type | solution.py:173
  655.0 10.7 %fusion.128 = bf16[6,64,1024]{2,1,0:T(8,128)(2,1)S(1)} fusion(bf16[1024,6,64]{0,2,1:T(8,128)(2,1)S(1)} %reshape.2154, f32[6,1024,1024]{1,2,0:T(8,128)} %get-tuple-element.374, f32[6,1024]{1,0:T(8,128)S(1)} %copy-done.139), kind=kOutput, calls=%fused_computation.322 | convolution fusion | flops 818282496 | bytes 26763264 | tf_op jit(solution)/shard_map/while/body/eval_jaxpr/hqk,qhd->khd/dot_general | solution.py:176
  669.8 6.9 multiply_convert_fusion.3
  679.6 8.5 multiply_convert_fusion.2
  693.2 4.1 add_convert_fusion
  716.7 3.9 fusion.293
  726.7 3.9 collective-permute-done.44
  758.1 13.3 %collective-permute-done.75 = bf16[768,768]{1,0:T(8,128)(2,1)} collective-permute-done((bf16[768,768]{1,0:T(8,128)(2,1)S(1)}, bf16[768,768]{1,0:T(8,128)(2,1)}, u32[]{:S(2)}, u32[]{:S(2)}) %collective-permute-start.75) | collective-permute-done | bytes 1179680 | tf_op jit(solution)/shard_map/ppermute | solution.py:41
  783.7 4.4 add_convert_fusion.1
  794.1 6.6 collective-permute-done.77
  806.1 11.7 %collective-permute-done.78 = bf16[1,96,768]{2,1,0:T(8,128)(2,1)S(1)} collective-permute-done((bf16[1,96,768]{2,1,0:T(8,128)(2,1)S(1)}, bf16[1,96,768]{2,1,0:T(8,128)(2,1)S(1)}, u32[]{:S(2)}, u32[]{:S(2)}) %collective-permute-start.78) | collective-permute-done | bytes 147488 | tf_op jit(solution)/shard_map/ppermute | solution.py:41
  820.1 4.6 collective-permute-done.79
  837.4 17.2 %collective-permute-done.68 = bf16[768,768]{1,0:T(8,128)(2,1)} collective-permute-done((bf16[768,768]{1,0:T(8,128)(2,1)}, bf16[768,768]{1,0:T(8,128)(2,1)}, u32[]{:S(2)}, u32[]{:S(2)}) %collective-permute-start.68) | collective-permute-done | bytes 1179680 | tf_op jit(solution)/shard_map/ppermute | solution.py:41
  862.7 6.1 collective-permute-done.69
  869.0 6.6 collective-permute-done.63
  880.9 7.1 collective-permute-done.64
  899.2 12.2 %collective-permute-done.55 = bf16[4,96,768]{2,1,0:T(8,128)(2,1)S(1)} collective-permute-done((bf16[4,96,768]{2,1,0:T(8,128)(2,1)S(1)}, bf16[4,96,768]{2,1,0:T(8,128)(2,1)S(1)}, u32[]{:S(2)}, u32[]{:S(2)}) %collective-permute-start.55) | collective-permute-done | bytes 589856 | tf_op jit(solution)/shard_map/ppermute | solution.py:41
  913.3 7.8 collective-permute-done.56
  923.8 6.2 collective-permute-done.57
  931.7 3.9 collective-permute-done.58
  (1047 shorter events, 411.4 us)
Async XLA Ops:
  6.9 15.8 %collective-permute-start.1 = (bf16[1,24,96]{2,1,0:T(8,128)(2,1)S(1)}, bf16[1,24,96]{2,1,0:T(8,128)(2,1)S(1)}, u32[]{:S(2)}, u32[]{:S(2)}) collective-permute-start(bf16[1,24,96]{2,1,0:T(8,128)(2,1)S(1)} %broadcast_in_dim_reshape.3), channel_id=1, source_target_pairs={{0,16},{4,20},{8,24},{12,28},{16,0},{20,4},{24,8},{28,12},{1,17},{... | collective-permute-start | bytes 13832 | tf_op jit(solution)/shard_map/ppermute | solution.py:41
  12.7 64.1 %collective-permute-start.37 = (bf16[1,256,768]{2,1,0:T(8,128)(2,1)}, bf16[1,256,768]{2,1,0:T(8,128)(2,1)}, u32[]{:S(2)}, u32[]{:S(2)}) collective-permute-start(bf16[1,256,768]{2,1,0:T(8,128)(2,1)} %constant_dynamic-slice_fusion.30), channel_id=1, source_target_pairs={{0,1},{1,0},{2,3},{3,2},{4,5},{5,4},{6,7},{7,6},{8,9},{9,8},{10,11... | collective-permute-start | bytes 1179656 | tf_op jit(solution)/shard_map/ppermute | solution.py:41
  16.0 58.1 %collective-permute-start = (bf16[1,256,768]{2,1,0:T(8,128)(2,1)}, bf16[1,256,768]{2,1,0:T(8,128)(2,1)}, u32[]{:S(2)}, u32[]{:S(2)}) collective-permute-start(bf16[1,256,768]{2,1,0:T(8,128)(2,1)} %constant_dynamic-slice_fusion.39), channel_id=1, source_target_pairs={{0,1},{1,0},{2,3},{3,2},{4,5},{5,4},{6,7},{7,6},{8,9},{9,8},{10,11... | collective-permute-start | bytes 1179656 | tf_op jit(solution)/shard_map/ppermute | solution.py:41
  16.7 17.8 %collective-permute-start.4 = (bf16[1,96,768]{2,1,0:T(8,128)(2,1)S(1)}, bf16[1,96,768]{2,1,0:T(8,128)(2,1)}, u32[]{:S(2)}, u32[]{:S(2)}) collective-permute-start(bf16[1,96,768]{2,1,0:T(8,128)(2,1)S(1)} %fusion.248), channel_id=1, source_target_pairs={{0,16},{4,20},{8,24},{12,28},{16,0},{20,4},{24,8},{28,12},{1,17},{... | collective-permute-start | bytes 442376 | tf_op jit(solution)/shard_map/ppermute | solution.py:41
  16.9 20.6 %collective-permute-start.20 = (bf16[1,96,768]{2,1,0:T(8,128)(2,1)S(1)}, bf16[1,96,768]{2,1,0:T(8,128)(2,1)}, u32[]{:S(2)}, u32[]{:S(2)}) collective-permute-start(bf16[1,96,768]{2,1,0:T(8,128)(2,1)S(1)} %fusion.246), channel_id=1, source_target_pairs={{0,16},{4,20},{8,24},{12,28},{16,0},{20,4},{24,8},{28,12},{1,17},{... | collective-permute-start | bytes 442376 | tf_op jit(solution)/shard_map/ppermute | solution.py:41
  30.4 22.1 %collective-permute-start.11 = (bf16[1,96,768]{2,1,0:T(8,128)(2,1)}, bf16[1,96,768]{2,1,0:T(8,128)(2,1)}, u32[]{:S(2)}, u32[]{:S(2)}) collective-permute-start(bf16[1,96,768]{2,1,0:T(8,128)(2,1)} %constant_dynamic-slice_fusion.36), channel_id=1, source_target_pairs={{0,16},{4,20},{8,24},{12,28},{16,0},{20,4},{24,8},{28,12},{1,17},{... | collective-permute-start | bytes 442376 | tf_op jit(solution)/shard_map/ppermute | solution.py:41
  34.5 21.1 %collective-permute-start.27 = (bf16[1,96,768]{2,1,0:T(8,128)(2,1)S(1)}, bf16[1,96,768]{2,1,0:T(8,128)(2,1)S(1)}, u32[]{:S(2)}, u32[]{:S(2)}) collective-permute-start(bf16[1,96,768]{2,1,0:T(8,128)(2,1)S(1)} %constant_dynamic-slice_fusion.32), channel_id=1, source_target_pairs={{0,16},{4,20},{8,24},{12,28},{16,0},{20,4},{24,8},{28,12},{1,17},{... | collective-permute-start | bytes 442376 | tf_op jit(solution)/shard_map/ppermute | solution.py:41
  37.4 33.6 %collective-permute-start.16 = (bf16[1,384,384]{2,1,0:T(8,128)(2,1)}, bf16[1,384,384]{2,1,0:T(8,128)(2,1)S(1)}, u32[]{:S(2)}, u32[]{:S(2)}) collective-permute-start(bf16[1,384,384]{2,1,0:T(8,128)(2,1)} %constant_dynamic-slice_fusion.35), channel_id=1, source_target_pairs={{0,16},{4,20},{8,24},{12,28},{16,0},{20,4},{24,8},{28,12},{1,17},{... | collective-permute-start | bytes 884744 | tf_op jit(solution)/shard_map/ppermute | solution.py:41
  52.5 17.4 %collective-permute-start.32 = (bf16[1,384,384]{2,1,0:T(8,128)(2,1)}, bf16[1,384,384]{2,1,0:T(8,128)(2,1)S(1)}, u32[]{:S(2)}, u32[]{:S(2)}) collective-permute-start(bf16[1,384,384]{2,1,0:T(8,128)(2,1)} %constant_dynamic-slice_fusion.31), channel_id=1, source_target_pairs={{0,16},{4,20},{8,24},{12,28},{16,0},{20,4},{24,8},{28,12},{1,17},{... | collective-permute-start | bytes 884744 | tf_op jit(solution)/shard_map/ppermute | solution.py:41
  55.6 29.2 %collective-permute-start.5 = (bf16[2,96,768]{2,1,0:T(8,128)(2,1)}, bf16[2,96,768]{2,1,0:T(8,128)(2,1)}, u32[]{:S(2)}, u32[]{:S(2)}) collective-permute-start(bf16[2,96,768]{2,1,0:T(8,128)(2,1)} %maximum_bitcast_fusion.12), channel_id=1, source_target_pairs={{0,8},{4,12},{8,0},{12,4},{16,24},{20,28},{24,16},{28,20},{1,9},{5... | collective-permute-start | bytes 884744 | tf_op jit(solution)/shard_map/ppermute | solution.py:41
  69.9 13.2 %collective-permute-start.21 = (bf16[2,96,768]{2,1,0:T(8,128)(2,1)}, bf16[2,96,768]{2,1,0:T(8,128)(2,1)}, u32[]{:S(2)}, u32[]{:S(2)}) collective-permute-start(bf16[2,96,768]{2,1,0:T(8,128)(2,1)} %maximum_bitcast_fusion.14), channel_id=1, source_target_pairs={{0,8},{4,12},{8,0},{12,4},{16,24},{20,28},{24,16},{28,20},{1,9},{5... | collective-permute-start | bytes 884744 | tf_op jit(solution)/shard_map/ppermute | solution.py:41
  71.0 16.4 %collective-permute-start.12 = (bf16[2,96,768]{2,1,0:T(8,128)(2,1)}, bf16[2,96,768]{2,1,0:T(8,128)(2,1)}, u32[]{:S(2)}, u32[]{:S(2)}) collective-permute-start(bf16[2,96,768]{2,1,0:T(8,128)(2,1)} %maximum_bitcast_fusion.13), channel_id=1, source_target_pairs={{0,8},{4,12},{8,0},{12,4},{16,24},{20,28},{24,16},{28,20},{1,9},{5... | collective-permute-start | bytes 884744 | tf_op jit(solution)/shard_map/ppermute | solution.py:41
  74.1 19.6 %collective-permute-start.28 = (bf16[2,96,768]{2,1,0:T(8,128)(2,1)}, bf16[2,96,768]{2,1,0:T(8,128)(2,1)}, u32[]{:S(2)}, u32[]{:S(2)}) collective-permute-start(bf16[2,96,768]{2,1,0:T(8,128)(2,1)} %maximum_bitcast_fusion.15), channel_id=1, source_target_pairs={{0,8},{4,12},{8,0},{12,4},{16,24},{20,28},{24,16},{28,20},{1,9},{5... | collective-permute-start | bytes 884744 | tf_op jit(solution)/shard_map/ppermute | solution.py:41
  77.0 42.2 %collective-permute-start.17 = (bf16[2,384,384]{2,1,0:T(8,128)(2,1)}, bf16[2,384,384]{2,1,0:T(8,128)(2,1)}, u32[]{:S(2)}, u32[]{:S(2)}) collective-permute-start(bf16[2,384,384]{2,1,0:T(8,128)(2,1)} %maximum_bitcast_fusion.6), channel_id=1, source_target_pairs={{0,8},{4,12},{8,0},{12,4},{16,24},{20,28},{24,16},{28,20},{1,9},{5... | collective-permute-start | bytes 1769480 | tf_op jit(solution)/shard_map/ppermute | solution.py:41
  83.2 34.0 %collective-permute-start.33 = (bf16[2,384,384]{2,1,0:T(8,128)(2,1)S(1)}, bf16[2,384,384]{2,1,0:T(8,128)(2,1)S(1)}, u32[]{:S(2)}, u32[]{:S(2)}) collective-permute-start(bf16[2,384,384]{2,1,0:T(8,128)(2,1)S(1)} %copy-done.138), channel_id=1, source_target_pairs={{0,8},{4,12},{8,0},{12,4},{16,24},{20,28},{24,16},{28,20},{1,9},{5... | collective-permute-start | bytes 1769480 | tf_op jit(solution)/shard_map/ppermute | solution.py:41
  84.8 38.2 %collective-permute-start.22 = (bf16[4,96,768]{2,1,0:T(8,128)(2,1)S(1)}, bf16[4,96,768]{2,1,0:T(8,128)(2,1)S(1)}, u32[]{:S(2)}, u32[]{:S(2)}) collective-permute-start(bf16[4,96,768]{2,1,0:T(8,128)(2,1)S(1)} %bitcast.1351), channel_id=1, source_target_pairs={{0,4},{4,0},{8,12},{12,8},{16,20},{20,16},{24,28},{28,24},{1,5},{5... | collective-permute-start | bytes 1769480 | tf_op jit(solution)/shard_map/ppermute | solution.py:41
  87.4 33.6 %collective-permute-start.6 = (bf16[4,96,768]{2,1,0:T(8,128)(2,1)S(1)}, bf16[4,96,768]{2,1,0:T(8,128)(2,1)S(1)}, u32[]{:S(2)}, u32[]{:S(2)}) collective-permute-start(bf16[4,96,768]{2,1,0:T(8,128)(2,1)S(1)} %bitcast.1353), channel_id=1, source_target_pairs={{0,4},{4,0},{8,12},{12,8},{16,20},{20,16},{24,28},{28,24},{1,5},{5... | collective-permute-start | bytes 1769480 | tf_op jit(solution)/shard_map/ppermute | solution.py:41
  94.9 31.4 %collective-permute-start.29 = (bf16[4,96,768]{2,1,0:T(8,128)(2,1)S(1)}, bf16[4,96,768]{2,1,0:T(8,128)(2,1)S(1)}, u32[]{:S(2)}, u32[]{:S(2)}) collective-permute-start(bf16[4,96,768]{2,1,0:T(8,128)(2,1)S(1)} %bitcast.1354), channel_id=1, source_target_pairs={{0,4},{4,0},{8,12},{12,8},{16,20},{20,16},{24,28},{28,24},{1,5},{5... | collective-permute-start | bytes 1769480 | tf_op jit(solution)/shard_map/ppermute | solution.py:41
  117.2 21.8 %collective-permute-start.13 = (bf16[4,96,768]{2,1,0:T(8,128)(2,1)S(1)}, bf16[4,96,768]{2,1,0:T(8,128)(2,1)S(1)}, u32[]{:S(2)}, u32[]{:S(2)}) collective-permute-start(bf16[4,96,768]{2,1,0:T(8,128)(2,1)S(1)} %bitcast.1352), channel_id=1, source_target_pairs={{0,4},{4,0},{8,12},{12,8},{16,20},{20,16},{24,28},{28,24},{1,5},{5... | collective-permute-start | bytes 1769480 | tf_op jit(solution)/shard_map/ppermute | solution.py:41
  119.2 45.1 %collective-permute-start.34 = (bf16[4,384,384]{2,1,0:T(8,128)(2,1)S(1)}, bf16[4,384,384]{2,1,0:T(8,128)(2,1)S(1)}, u32[]{:S(2)}, u32[]{:S(2)}) collective-permute-start(bf16[4,384,384]{2,1,0:T(8,128)(2,1)S(1)} %bitcast.1324), channel_id=1, source_target_pairs={{0,4},{4,0},{8,12},{12,8},{16,20},{20,16},{24,28},{28,24},{1,5},{5... | collective-permute-start | bytes 3538952 | tf_op jit(solution)/shard_map/ppermute | solution.py:41
  121.1 64.8 %collective-permute-start.18 = (bf16[4,384,384]{2,1,0:T(8,128)(2,1)S(1)}, bf16[4,384,384]{2,1,0:T(8,128)(2,1)S(1)}, u32[]{:S(2)}, u32[]{:S(2)}) collective-permute-start(bf16[4,384,384]{2,1,0:T(8,128)(2,1)S(1)} %bitcast.1325), channel_id=1, source_target_pairs={{0,4},{4,0},{8,12},{12,8},{16,20},{20,16},{24,28},{28,24},{1,5},{5... | collective-permute-start | bytes 3538952 | tf_op jit(solution)/shard_map/ppermute | solution.py:41
  123.0 29.0 %collective-permute-start.7 = (bf16[768,768]{1,0:T(8,128)(2,1)S(1)}, bf16[768,768]{1,0:T(8,128)(2,1)S(1)}, u32[]{:S(2)}, u32[]{:S(2)}) collective-permute-start(bf16[768,768]{1,0:T(8,128)(2,1)S(1)} %bitcast.1328), channel_id=1, source_target_pairs={{0,1},{1,0},{2,3},{3,2},{4,5},{5,4},{6,7},{7,6},{8,9},{9,8},{10,11... | collective-permute-start | bytes 3538952 | tf_op jit(solution)/shard_map/ppermute | solution.py:41
  139.4 57.1 %collective-permute-start.14 = (bf16[768,768]{1,0:T(8,128)(2,1)S(1)}, bf16[768,768]{1,0:T(8,128)(2,1)S(1)}, u32[]{:S(2)}, u32[]{:S(2)}) collective-permute-start(bf16[768,768]{1,0:T(8,128)(2,1)S(1)} %bitcast.1327), channel_id=1, source_target_pairs={{0,1},{1,0},{2,3},{3,2},{4,5},{5,4},{6,7},{7,6},{8,9},{9,8},{10,11... | collective-permute-start | bytes 3538952 | tf_op jit(solution)/shard_map/ppermute | solution.py:41
  140.9 89.5 %collective-permute-start.30 = (bf16[768,768]{1,0:T(8,128)(2,1)S(1)}, bf16[768,768]{1,0:T(8,128)(2,1)}, u32[]{:S(2)}, u32[]{:S(2)}) collective-permute-start(bf16[768,768]{1,0:T(8,128)(2,1)S(1)} %bitcast.1323), channel_id=1, source_target_pairs={{0,1},{1,0},{2,3},{3,2},{4,5},{5,4},{6,7},{7,6},{8,9},{9,8},{10,11... | collective-permute-start | bytes 3538952 | tf_op jit(solution)/shard_map/ppermute | solution.py:41
  152.0 72.5 %collective-permute-start.23 = (bf16[768,768]{1,0:T(8,128)(2,1)S(1)}, bf16[768,768]{1,0:T(8,128)(2,1)S(1)}, u32[]{:S(2)}, u32[]{:S(2)}) collective-permute-start(bf16[768,768]{1,0:T(8,128)(2,1)S(1)} %bitcast.1326), channel_id=1, source_target_pairs={{0,1},{1,0},{2,3},{3,2},{4,5},{5,4},{6,7},{7,6},{8,9},{9,8},{10,11... | collective-permute-start | bytes 3538952 | tf_op jit(solution)/shard_map/ppermute | solution.py:41
  164.3 60.6 %collective-permute-start.8 = (bf16[2,768,768]{2,1,0:T(8,128)(2,1)S(1)}, bf16[2,768,768]{2,1,0:T(8,128)(2,1)S(1)}, u32[]{:S(2)}, u32[]{:S(2)}) collective-permute-start(bf16[2,768,768]{2,1,0:T(8,128)(2,1)S(1)} %pad_maximum_fusion.8), channel_id=1, source_target_pairs={{0,2},{2,0},{1,3},{3,1},{4,6},{6,4},{5,7},{7,5},{8,10},{10,8},{9,1... | collective-permute-start | bytes 7077896 | tf_op jit(solution)/shard_map/ppermute | solution.py:41
  190.2 127.8 %collective-permute-start.35 = (bf16[3072,384]{1,0:T(8,128)(2,1)}, bf16[3072,384]{1,0:T(8,128)(2,1)}, u32[]{:S(2)}, u32[]{:S(2)}) collective-permute-start(bf16[3072,384]{1,0:T(8,128)(2,1)} %bitcast.160), channel_id=1, source_target_pairs={{0,2},{2,0},{1,3},{3,1},{4,6},{6,4},{5,7},{7,5},{8,10},{10,8},{9,1... | collective-permute-start | bytes 7077896 | tf_op jit(solution)/shard_map/ppermute | solution.py:41
  196.5 113.0 %collective-permute-start.19 = (bf16[3072,384]{1,0:T(8,128)(2,1)}, bf16[3072,384]{1,0:T(8,128)(2,1)}, u32[]{:S(2)}, u32[]{:S(2)}) collective-permute-start(bf16[3072,384]{1,0:T(8,128)(2,1)} %bitcast.93), channel_id=1, source_target_pairs={{0,2},{2,0},{1,3},{3,1},{4,6},{6,4},{5,7},{7,5},{8,10},{10,8},{9,1... | collective-permute-start | bytes 7077896 | tf_op jit(solution)/shard_map/ppermute | solution.py:41
  224.9 12.1 %collective-permute-start.24 = (bf16[2,768,768]{2,1,0:T(8,128)(2,1)S(1)}, bf16[2,768,768]{2,1,0:T(8,128)(2,1)S(1)}, u32[]{:S(2)}, u32[]{:S(2)}) collective-permute-start(bf16[2,768,768]{2,1,0:T(8,128)(2,1)S(1)} %pad_maximum_fusion.11), channel_id=1, source_target_pairs={{0,2},{2,0},{1,3},{3,1},{4,6},{6,4},{5,7},{7,5},{8,10},{10,8},{9,1... | collective-permute-start | bytes 7077896 | tf_op jit(solution)/shard_map/ppermute | solution.py:41
  234.1 90.5 %collective-permute-start.31 = (bf16[2,768,768]{2,1,0:T(8,128)(2,1)}, bf16[2,768,768]{2,1,0:T(8,128)(2,1)}, u32[]{:S(2)}, u32[]{:S(2)}) collective-permute-start(bf16[2,768,768]{2,1,0:T(8,128)(2,1)} %pad_maximum_fusion.12), channel_id=1, source_target_pairs={{0,2},{2,0},{1,3},{3,1},{4,6},{6,4},{5,7},{7,5},{8,10},{10,8},{9,1... | collective-permute-start | bytes 7077896 | tf_op jit(solution)/shard_map/ppermute | solution.py:41
  317.5 12.1 %collective-permute-start.25 = (bf16[3,1,512,384]{3,2,0,1:T(8,128)(2,1)S(1)}, bf16[3,1,512,384]{3,2,0,1:T(8,128)(2,1)S(1)}, u32[]{:S(2)}, u32[]{:S(2)}) collective-permute-start(bf16[3,1,512,384]{3,2,0,1:T(8,128)(2,1)S(1)} %pad_maximum_fusion.21), channel_id=1, source_target_pairs={{0,2},{2,0},{1,3},{3,1},{4,6},{6,4},{5,7},{7,5},{8,10},{10,8},{9,1... | collective-permute-start | bytes 3538952 | tf_op jit(solution)/shard_map/ppermute | solution.py:41
  439.5 86.0 %collective-permute-start.36 = (bf16[1,256,768]{2,1,0:T(8,128)(2,1)}, bf16[1,256,768]{2,1,0:T(8,128)(2,1)}, u32[]{:S(2)}, u32[]{:S(2)}) collective-permute-start(bf16[1,256,768]{2,1,0:T(8,128)(2,1)} %fusion.199), channel_id=1, source_target_pairs={{0,1},{1,0},{2,3},{3,2},{4,5},{5,4},{6,7},{7,6},{8,9},{9,8},{10,11... | collective-permute-start | bytes 1179656 | tf_op jit(solution)/shard_map/ppermute | solution.py:41
  443.9 248.9 %collective-permute-start.87 = (bf16[3072,384]{1,0:T(8,128)(2,1)}, bf16[3072,384]{1,0:T(8,128)(2,1)}, u32[]{:S(2)}, u32[]{:S(2)}) collective-permute-start(bf16[3072,384]{1,0:T(8,128)(2,1)} %convolution_convert_fusion), channel_id=1, source_target_pairs={{0,2},{2,0},{1,3},{3,1},{4,6},{6,4},{5,7},{7,5},{8,10},{10,8},{9,1... | collective-permute-start | bytes 7077896 | tf_op jit(solution)/shard_map/ppermute | solution.py:41
  516.1 12.2 %collective-permute-start.39 = (bf16[3,1,512,384]{3,2,0,1:T(8,128)(2,1)}, bf16[3,1,512,384]{3,2,0,1:T(8,128)(2,1)}, u32[]{:S(2)}, u32[]{:S(2)}) collective-permute-start(bf16[3,1,512,384]{3,2,0,1:T(8,128)(2,1)} %pad_maximum_fusion.25), channel_id=1, source_target_pairs={{0,2},{2,0},{1,3},{3,1},{4,6},{6,4},{5,7},{7,5},{8,10},{10,8},{9,1... | collective-permute-start | bytes 3538952 | tf_op jit(solution)/shard_map/ppermute | solution.py:41
  522.3 176.4 %collective-permute-start.74 = (bf16[2,768,768]{2,1,0:T(8,128)(2,1)}, bf16[2,768,768]{2,1,0:T(8,128)(2,1)}, u32[]{:S(2)}, u32[]{:S(2)}) collective-permute-start(bf16[2,768,768]{2,1,0:T(8,128)(2,1)} %dynamic-slice_bitcast_fusion), channel_id=1, source_target_pairs={{0,2},{2,0},{1,3},{3,1},{4,6},{6,4},{5,7},{7,5},{8,10},{10,8},{9,1... | collective-permute-start | bytes 7077896 | tf_op jit(solution)/shard_map/ppermute | solution.py:41
  579.4 18.3 %collective-permute-start.48 = (f32[8,12,96]{2,1,0:T(8,128)}, f32[8,12,96]{2,1,0:T(8,128)S(1)}, u32[]{:S(2)}, u32[]{:S(2)}) collective-permute-start(f32[8,12,96]{2,1,0:T(8,128)} %bitcast.1393), channel_id=1, source_target_pairs={{0,2},{2,0},{1,3},{3,1},{4,6},{6,4},{5,7},{7,5},{8,10},{10,8},{9,1... | collective-permute-start | bytes 110600 | tf_op jit(solution)/shard_map/ppermute | solution.py:41
  585.5 192.2 %collective-permute-start.60 = (bf16[2,768,768]{2,1,0:T(8,128)(2,1)}, bf16[2,768,768]{2,1,0:T(8,128)(2,1)}, u32[]{:S(2)}, u32[]{:S(2)}) collective-permute-start(bf16[2,768,768]{2,1,0:T(8,128)(2,1)} %dynamic-slice_bitcast_fusion.2), channel_id=1, source_target_pairs={{0,2},{2,0},{1,3},{3,1},{4,6},{6,4},{5,7},{7,5},{8,10},{10,8},{9,1... | collective-permute-start | bytes 7077896 | tf_op jit(solution)/shard_map/ppermute | solution.py:41
  585.7 197.1 %collective-permute-start.81 = (bf16[3072,384]{1,0:T(8,128)(2,1)}, bf16[3072,384]{1,0:T(8,128)(2,1)}, u32[]{:S(2)}, u32[]{:S(2)}) collective-permute-start(bf16[3072,384]{1,0:T(8,128)(2,1)} %convolution_convert_fusion.2), channel_id=1, source_target_pairs={{0,2},{2,0},{1,3},{3,1},{4,6},{6,4},{5,7},{7,5},{8,10},{10,8},{9,1... | collective-permute-start | bytes 7077896 | tf_op jit(solution)/shard_map/ppermute | solution.py:41
  616.2 185.7 %collective-permute-start.67 = (bf16[2,768,768]{2,1,0:T(8,128)(2,1)}, bf16[2,768,768]{2,1,0:T(8,128)(2,1)}, u32[]{:S(2)}, u32[]{:S(2)}) collective-permute-start(bf16[2,768,768]{2,1,0:T(8,128)(2,1)} %dynamic-slice_bitcast_fusion.1), channel_id=1, source_target_pairs={{0,2},{2,0},{1,3},{3,1},{4,6},{6,4},{5,7},{7,5},{8,10},{10,8},{9,1... | collective-permute-start | bytes 7077896 | tf_op jit(solution)/shard_map/ppermute | solution.py:41
  692.8 10.0 %collective-permute-start.41 = (bf16[3,1,512,384]{3,2,0,1:T(8,128)(2,1)S(1)}, bf16[3,1,512,384]{3,2,0,1:T(8,128)(2,1)S(1)}, u32[]{:S(2)}, u32[]{:S(2)}) collective-permute-start(bf16[3,1,512,384]{3,2,0,1:T(8,128)(2,1)S(1)} %pad_maximum_fusion.27), channel_id=1, source_target_pairs={{0,2},{2,0},{1,3},{3,1},{4,6},{6,4},{5,7},{7,5},{8,10},{10,8},{9,1... | collective-permute-start | bytes 3538952 | tf_op jit(solution)/shard_map/ppermute | solution.py:41
  698.7 56.1 %collective-permute-start.88 = (bf16[4,384,384]{2,1,0:T(8,128)(2,1)}, bf16[4,384,384]{2,1,0:T(8,128)(2,1)}, u32[]{:S(2)}, u32[]{:S(2)}) collective-permute-start(bf16[4,384,384]{2,1,0:T(8,128)(2,1)} %dynamic-slice_bitcast_fusion.4), channel_id=1, source_target_pairs={{0,4},{4,0},{8,12},{12,8},{16,20},{20,16},{24,28},{28,24},{1,5},{5... | collective-permute-start | bytes 3538952 | tf_op jit(solution)/shard_map/ppermute | solution.py:41
  743.0 28.4 %collective-permute-start.75 = (bf16[768,768]{1,0:T(8,128)(2,1)S(1)}, bf16[768,768]{1,0:T(8,128)(2,1)}, u32[]{:S(2)}, u32[]{:S(2)}) collective-permute-start(bf16[768,768]{1,0:T(8,128)(2,1)S(1)} %copy-done.102), channel_id=1, source_target_pairs={{0,1},{1,0},{2,3},{3,2},{4,5},{5,4},{6,7},{7,6},{8,9},{9,8},{10,11... | collective-permute-start | bytes 3538952 | tf_op jit(solution)/shard_map/ppermute | solution.py:41
  754.8 20.8 %collective-permute-start.42 = (bf16[1,256,768]{2,1,0:T(8,128)(2,1)}, bf16[1,256,768]{2,1,0:T(8,128)(2,1)S(1)}, u32[]{:S(2)}, u32[]{:S(2)}) collective-permute-start(bf16[1,256,768]{2,1,0:T(8,128)(2,1)} %fusion.200), channel_id=1, source_target_pairs={{0,1},{1,0},{2,3},{3,2},{4,5},{5,4},{6,7},{7,6},{8,9},{9,8},{10,11... | collective-permute-start | bytes 1179656 | tf_op jit(solution)/shard_map/ppermute | solution.py:41
  771.4 85.5 %collective-permute-start.53 = (bf16[2,768,768]{2,1,0:T(8,128)(2,1)}, bf16[2,768,768]{2,1,0:T(8,128)(2,1)}, u32[]{:S(2)}, u32[]{:S(2)}) collective-permute-start(bf16[2,768,768]{2,1,0:T(8,128)(2,1)} %dynamic-slice_bitcast_fusion.3), channel_id=1, source_target_pairs={{0,2},{2,0},{1,3},{3,1},{4,6},{6,4},{5,7},{7,5},{8,10},{10,8},{9,1... | collective-permute-start | bytes 7077896 | tf_op jit(solution)/shard_map/ppermute | solution.py:41
  775.5 17.1 %collective-permute-start.89 = (bf16[2,384,384]{2,1,0:T(8,128)(2,1)S(1)}, bf16[2,384,384]{2,1,0:T(8,128)(2,1)S(1)}, u32[]{:S(2)}, u32[]{:S(2)}) collective-permute-start(bf16[2,384,384]{2,1,0:T(8,128)(2,1)S(1)} %dynamic-slice_bitcast_fusion.10), channel_id=1, source_target_pairs={{0,8},{4,12},{8,0},{12,4},{16,24},{20,28},{24,16},{28,20},{1,9},{5... | collective-permute-start | bytes 1769480 | tf_op jit(solution)/shard_map/ppermute | solution.py:41
  777.7 13.2 %collective-permute-start.76 = (bf16[4,96,768]{2,1,0:T(8,128)(2,1)S(1)}, bf16[4,96,768]{2,1,0:T(8,128)(2,1)S(1)}, u32[]{:S(2)}, u32[]{:S(2)}) collective-permute-start(bf16[4,96,768]{2,1,0:T(8,128)(2,1)S(1)} %dynamic-slice_bitcast_fusion.12), channel_id=1, source_target_pairs={{0,4},{4,0},{8,12},{12,8},{16,20},{20,16},{24,28},{28,24},{1,5},{5... | collective-permute-start | bytes 1769480 | tf_op jit(solution)/shard_map/ppermute | solution.py:41
  782.8 49.9 %collective-permute-start.61 = (bf16[768,768]{1,0:T(8,128)(2,1)}, bf16[768,768]{1,0:T(8,128)(2,1)}, u32[]{:S(2)}, u32[]{:S(2)}) collective-permute-start(bf16[768,768]{1,0:T(8,128)(2,1)} %dynamic-slice_bitcast_fusion.8), channel_id=1, source_target_pairs={{0,1},{1,0},{2,3},{3,2},{4,5},{5,4},{6,7},{7,6},{8,9},{9,8},{10,11... | collective-permute-start | bytes 3538952 | tf_op jit(solution)/shard_map/ppermute | solution.py:41
  790.9 44.2 %collective-permute-start.82 = (bf16[4,384,384]{2,1,0:T(8,128)(2,1)}, bf16[4,384,384]{2,1,0:T(8,128)(2,1)}, u32[]{:S(2)}, u32[]{:S(2)}) collective-permute-start(bf16[4,384,384]{2,1,0:T(8,128)(2,1)} %dynamic-slice_bitcast_fusion.5), channel_id=1, source_target_pairs={{0,4},{4,0},{8,12},{12,8},{16,20},{20,16},{24,28},{28,24},{1,5},{5... | collective-permute-start | bytes 3538952 | tf_op jit(solution)/shard_map/ppermute | solution.py:41
  800.7 17.8 %collective-permute-start.90 = (bf16[1,384,384]{2,1,0:T(8,128)(2,1)S(1)}, bf16[1,384,384]{2,1,0:T(8,128)(2,1)S(1)}, u32[]{:S(2)}, u32[]{:S(2)}) collective-permute-start(bf16[1,384,384]{2,1,0:T(8,128)(2,1)S(1)} %constant_dynamic-slice_fusion), channel_id=1, source_target_pairs={{0,16},{4,20},{8,24},{12,28},{16,0},{20,4},{24,8},{28,12},{1,17},{... | collective-permute-start | bytes 884744 | tf_op jit(solution)/shard_map/ppermute | solution.py:41
  801.9 15.9 %collective-permute-start.78 = (bf16[1,96,768]{2,1,0:T(8,128)(2,1)S(1)}, bf16[1,96,768]{2,1,0:T(8,128)(2,1)S(1)}, u32[]{:S(2)}, u32[]{:S(2)}) collective-permute-start(bf16[1,96,768]{2,1,0:T(8,128)(2,1)S(1)} %constant_dynamic-slice_fusion.2), channel_id=1, source_target_pairs={{0,16},{4,20},{8,24},{12,28},{16,0},{20,4},{24,8},{28,12},{1,17},{... | collective-permute-start | bytes 442376 | tf_op jit(solution)/shard_map/ppermute | solution.py:41
  818.5 9.8 %collective-permute-start.91 = (bf16[384,384]{1,0:T(8,128)(2,1)S(1)}, bf16[384,384]{1,0:T(8,128)(2,1)S(1)}, u32[]{:S(2)}, u32[]{:S(2)}) collective-permute-start(bf16[384,384]{1,0:T(8,128)(2,1)S(1)} %fusion.240), channel_id=1, source_target_pairs={{0,1},{1,0},{2,3},{3,2},{4,5},{5,4},{6,7},{7,6},{8,9},{9,8},{10,11... | collective-permute-start | bytes 884744 | tf_op jit(solution)/shard_map/ppermute | solution.py:41
  828.3 26.3 %collective-permute-start.68 = (bf16[768,768]{1,0:T(8,128)(2,1)}, bf16[768,768]{1,0:T(8,128)(2,1)}, u32[]{:S(2)}, u32[]{:S(2)}) collective-permute-start(bf16[768,768]{1,0:T(8,128)(2,1)} %dynamic-slice_bitcast_fusion.7), channel_id=1, source_target_pairs={{0,1},{1,0},{2,3},{3,2},{4,5},{5,4},{6,7},{7,6},{8,9},{9,8},{10,11... | collective-permute-start | bytes 3538952 | tf_op jit(solution)/shard_map/ppermute | solution.py:41
  834.6 25.2 %collective-permute-start.62 = (bf16[4,96,768]{2,1,0:T(8,128)(2,1)S(1)}, bf16[4,96,768]{2,1,0:T(8,128)(2,1)S(1)}, u32[]{:S(2)}, u32[]{:S(2)}) collective-permute-start(bf16[4,96,768]{2,1,0:T(8,128)(2,1)S(1)} %dynamic-slice_bitcast_fusion.14), channel_id=1, source_target_pairs={{0,4},{4,0},{8,12},{12,8},{16,20},{20,16},{24,28},{28,24},{1,5},{5... | collective-permute-start | bytes 1769480 | tf_op jit(solution)/shard_map/ppermute | solution.py:41
  837.4 22.7 %collective-permute-start.83 = (bf16[2,384,384]{2,1,0:T(8,128)(2,1)S(1)}, bf16[2,384,384]{2,1,0:T(8,128)(2,1)S(1)}, u32[]{:S(2)}, u32[]{:S(2)}) collective-permute-start(bf16[2,384,384]{2,1,0:T(8,128)(2,1)S(1)} %dynamic-slice_bitcast_fusion.11), channel_id=1, source_target_pairs={{0,8},{4,12},{8,0},{12,4},{16,24},{20,28},{24,16},{28,20},{1,9},{5... | collective-permute-start | bytes 1769480 | tf_op jit(solution)/shard_map/ppermute | solution.py:41
  856.3 12.5 %collective-permute-start.69 = (bf16[4,96,768]{2,1,0:T(8,128)(2,1)S(1)}, bf16[4,96,768]{2,1,0:T(8,128)(2,1)S(1)}, u32[]{:S(2)}, u32[]{:S(2)}) collective-permute-start(bf16[4,96,768]{2,1,0:T(8,128)(2,1)S(1)} %dynamic-slice_bitcast_fusion.13), channel_id=1, source_target_pairs={{0,4},{4,0},{8,12},{12,8},{16,20},{20,16},{24,28},{28,24},{1,5},{5... | collective-permute-start | bytes 1769480 | tf_op jit(solution)/shard_map/ppermute | solution.py:41
  859.2 36.0 %collective-permute-start.54 = (bf16[768,768]{1,0:T(8,128)(2,1)S(1)}, bf16[768,768]{1,0:T(8,128)(2,1)S(1)}, u32[]{:S(2)}, u32[]{:S(2)}) collective-permute-start(bf16[768,768]{1,0:T(8,128)(2,1)S(1)} %dynamic-slice_bitcast_fusion.9), channel_id=1, source_target_pairs={{0,1},{1,0},{2,3},{3,2},{4,5},{5,4},{6,7},{7,6},{8,9},{9,8},{10,11... | collective-permute-start | bytes 3538952 | tf_op jit(solution)/shard_map/ppermute | solution.py:41
  860.0 15.6 %collective-permute-start.63 = (bf16[2,96,768]{2,1,0:T(8,128)(2,1)S(1)}, bf16[2,96,768]{2,1,0:T(8,128)(2,1)S(1)}, u32[]{:S(2)}, u32[]{:S(2)}) collective-permute-start(bf16[2,96,768]{2,1,0:T(8,128)(2,1)S(1)} %dynamic-slice_bitcast_fusion.32), channel_id=1, source_target_pairs={{0,8},{4,12},{8,0},{12,4},{16,24},{20,28},{24,16},{28,20},{1,9},{5... | collective-permute-start | bytes 884744 | tf_op jit(solution)/shard_map/ppermute | solution.py:41
  860.3 15.5 %collective-permute-start.84 = (bf16[1,384,384]{2,1,0:T(8,128)(2,1)S(1)}, bf16[1,384,384]{2,1,0:T(8,128)(2,1)S(1)}, u32[]{:S(2)}, u32[]{:S(2)}) collective-permute-start(bf16[1,384,384]{2,1,0:T(8,128)(2,1)S(1)} %constant_dynamic-slice_fusion.1), channel_id=1, source_target_pairs={{0,16},{4,20},{8,24},{12,28},{16,0},{20,4},{24,8},{28,12},{1,17},{... | collective-permute-start | bytes 884744 | tf_op jit(solution)/shard_map/ppermute | solution.py:41
  869.0 10.9 %collective-permute-start.70 = (bf16[2,96,768]{2,1,0:T(8,128)(2,1)S(1)}, bf16[2,96,768]{2,1,0:T(8,128)(2,1)S(1)}, u32[]{:S(2)}, u32[]{:S(2)}) collective-permute-start(bf16[2,96,768]{2,1,0:T(8,128)(2,1)S(1)} %dynamic-slice_bitcast_fusion.31), channel_id=1, source_target_pairs={{0,8},{4,12},{8,0},{12,4},{16,24},{20,28},{24,16},{28,20},{1,9},{5... | collective-permute-start | bytes 884744 | tf_op jit(solution)/shard_map/ppermute | solution.py:41
  875.7 12.2 %collective-permute-start.64 = (bf16[1,96,768]{2,1,0:T(8,128)(2,1)S(1)}, bf16[1,96,768]{2,1,0:T(8,128)(2,1)S(1)}, u32[]{:S(2)}, u32[]{:S(2)}) collective-permute-start(bf16[1,96,768]{2,1,0:T(8,128)(2,1)S(1)} %constant_dynamic-slice_fusion.4), channel_id=1, source_target_pairs={{0,16},{4,20},{8,24},{12,28},{16,0},{20,4},{24,8},{28,12},{1,17},{... | collective-permute-start | bytes 442376 | tf_op jit(solution)/shard_map/ppermute | solution.py:41
  875.9 17.0 %collective-permute-start.85 = (bf16[384,384]{1,0:T(8,128)(2,1)S(1)}, bf16[384,384]{1,0:T(8,128)(2,1)S(1)}, u32[]{:S(2)}, u32[]{:S(2)}) collective-permute-start(bf16[384,384]{1,0:T(8,128)(2,1)S(1)} %fusion.239), channel_id=1, source_target_pairs={{0,1},{1,0},{2,3},{3,2},{4,5},{5,4},{6,7},{7,6},{8,9},{9,8},{10,11... | collective-permute-start | bytes 884744 | tf_op jit(solution)/shard_map/ppermute | solution.py:41
  895.2 35.5 %collective-permute-start.66 = (bf16[2,96,768]{2,1,0:T(8,128)(2,1)S(1)}, bf16[2,96,768]{2,1,0:T(8,128)(2,1)}, u32[]{:S(2)}, u32[]{:S(2)}) collective-permute-start(bf16[2,96,768]{2,1,0:T(8,128)(2,1)S(1)} %pad_maximum_fusion.47), channel_id=1, source_target_pairs={{0,2},{2,0},{1,3},{3,1},{4,6},{6,4},{5,7},{7,5},{8,10},{10,8},{9,1... | collective-permute-start | bytes 884744 | tf_op jit(solution)/shard_map/ppermute | solution.py:41
  895.6 15.8 %collective-permute-start.55 = (bf16[4,96,768]{2,1,0:T(8,128)(2,1)S(1)}, bf16[4,96,768]{2,1,0:T(8,128)(2,1)S(1)}, u32[]{:S(2)}, u32[]{:S(2)}) collective-permute-start(bf16[4,96,768]{2,1,0:T(8,128)(2,1)S(1)} %dynamic-slice_bitcast_fusion.15), channel_id=1, source_target_pairs={{0,4},{4,0},{8,12},{12,8},{16,20},{20,16},{24,28},{28,24},{1,5},{5... | collective-permute-start | bytes 1769480 | tf_op jit(solution)/shard_map/ppermute | solution.py:41
  897.3 15.0 %collective-permute-start.73 = (bf16[2,96,768]{2,1,0:T(8,128)(2,1)S(1)}, bf16[2,96,768]{2,1,0:T(8,128)(2,1)S(1)}, u32[]{:S(2)}, u32[]{:S(2)}) collective-permute-start(bf16[2,96,768]{2,1,0:T(8,128)(2,1)S(1)} %pad_maximum_fusion.48), channel_id=1, source_target_pairs={{0,2},{2,0},{1,3},{3,1},{4,6},{6,4},{5,7},{7,5},{8,10},{10,8},{9,1... | collective-permute-start | bytes 884744 | tf_op jit(solution)/shard_map/ppermute | solution.py:41
  (255 other events, 1501.2 us)

commit v2 on v1

v2 whole, which is shorter than its diff:
```python
import jax
import jax.numpy as jnp
from jax import lax
from jax.experimental import pallas as pl
from jax.experimental.pallas import tpu as pltpu
from jax.sharding import PartitionSpec as P

HDIM = 64
EPSILON = 1e-05
NEGATIVE = -1e30
LOW = jnp.bfloat16
FULL = jnp.float32
SCALE = HDIM**-0.5
TILE = 256
MIB = 2**20


def dot_nt(left, right):
    return lax.dot_general(left, right, (((1,), (1,)), ((), ())), preferred_element_type=FULL)


def dot_nn(left, right):
    return lax.dot_general(left, right, (((1,), (0,)), ((), ())), preferred_element_type=FULL)


def head_lanes(item, head):
    lane = lax.broadcasted_iota(jnp.int32, item.shape, 1)
    return jnp.where((lane // HDIM) == head, item, jnp.zeros_like(item))


def keep_diagonal(scores):
    keys = lax.broadcasted_iota(jnp.int32, scores.shape, 0)
    rows = lax.broadcasted_iota(jnp.int32, scores.shape, 1)
    return jnp.where(keys <= rows, scores, NEGATIVE)


def join(core, mine, theirs, whole):
    half = mine.shape[0]

    @pl.when(core == 0)
    def _():
        whole[:half] = mine[...]
        whole[half:] = theirs[...]

    @pl.when(core != 0)
    def _():
        whole[:half] = theirs[...]
        whole[half:] = mine[...]


def part(core, whole, mine, theirs):
    half = mine.shape[0]

    @pl.when(core == 0)
    def _():
        mine[...] = whole[:half].astype(mine.dtype)
        theirs[...] = whole[half:].astype(theirs.dtype)

    @pl.when(core != 0)
    def _():
        theirs[...] = whole[:half].astype(theirs.dtype)
        mine[...] = whole[half:].astype(mine.dtype)


def attend_kernel(core_ref, mine_ref, theirs_ref, mixed_mine, mixed_theirs, logsum_ref, qkv, mixed_ref):
    core = core_ref[0]
    for kind in range(3):
        join(core, mine_ref.at[kind, 0], theirs_ref.at[kind, 0], qkv.at[kind])
    length = qkv.shape[1]
    values_t = qkv[2].T
    for start in range(0, length, TILE):
        rows = slice(start, start + TILE)
        queries = qkv[0, rows] * jnp.asarray(SCALE, LOW)
        outs = []
        for head in range(2):
            own = head_lanes(queries, head)
            scores = keep_diagonal(dot_nt(qkv[1, rows], own))
            top = jnp.max(scores, axis=0, keepdims=True)
            if start:
                early = dot_nt(qkv[1, :start], own)
                top = jnp.maximum(top, jnp.max(early, axis=0, keepdims=True))
            raised = jnp.exp(scores - top)
            total = jnp.sum(raised, axis=0, keepdims=True)
            mixed = dot_nn(values_t[:, rows], raised.astype(LOW))
            if start:
                raised = jnp.exp(early - top)
                total = total + jnp.sum(raised, axis=0, keepdims=True)
                mixed = mixed + dot_nn(values_t[:, :start], raised.astype(LOW))
            outs.append((mixed / total)[head * HDIM : (head + 1) * HDIM])
            logsum_ref[0, 0, head : head + 1, rows] = top + jnp.log(total)
        mixed_ref[rows] = jnp.concatenate(outs, axis=0).T.astype(LOW)
    part(core, mixed_ref, mixed_mine.at[0], mixed_theirs.at[0])


def attend(core, mine, theirs):
    three, count, rows, width = mine.shape
    pairs = width // 128
    wide = pl.BlockSpec((3, 1, rows, 128), lambda s, p, core: (0, s, 0, p))
    thin = pl.BlockSpec((1, rows, 128), lambda s, p, core: (s, 0, p))
    return pl.pallas_call(
        attend_kernel,
        grid_spec=pltpu.PrefetchScalarGridSpec(
            num_scalar_prefetch=1,
            grid=(count, pairs),
            in_specs=[wide, wide],
            out_specs=[
                thin,
                thin,
                pl.BlockSpec((1, 1, 8, 2 * rows), lambda s, p, core: (s, p, 0, 0)),
            ],
            scratch_shapes=[pltpu.VMEM((3, 2 * rows, 128), LOW), pltpu.VMEM((2 * rows, 128), LOW)],
        ),
        out_shape=[
            jax.ShapeDtypeStruct((count, rows, width), LOW),
            jax.ShapeDtypeStruct((count, rows, width), LOW),
            jax.ShapeDtypeStruct((count, pairs, 8, 2 * rows), FULL),
        ],
        compiler_params=pltpu.CompilerParams(vmem_limit_bytes=32 * MIB),
        name="attend",
    )(core, mine, theirs)


def attend_back_kernel(
    core_ref,
    mine_ref,
    theirs_ref,
    logsum_ref,
    mixed_mine,
    mixed_theirs,
    slope_mine,
    slope_theirs,
    out_mine,
    out_theirs,
    qkv,
    mixed_ref,
    slope_ref,
    grads,
):
    core = core_ref[0]
    for kind in range(3):
        join(core, mine_ref.at[kind, 0], theirs_ref.at[kind, 0], qkv.at[kind])
    join(core, mixed_mine.at[0], mixed_theirs.at[0], mixed_ref)
    join(core, slope_mine.at[0], slope_theirs.at[0], slope_ref)
    length = qkv.shape[1]
    keys_t = qkv[1].T * jnp.asarray(SCALE, LOW)
    product = (mixed_ref[...].astype(FULL) * slope_ref[...].astype(FULL)).T
    inner = [
        jnp.sum(product[h * HDIM : (h + 1) * HDIM], axis=0, keepdims=True) for h in range(2)
    ]
    for start in range(0, length, TILE):
        rows = slice(start, start + TILE)
        queries = qkv[0, rows] * jnp.asarray(SCALE, LOW)
        slope = slope_ref[rows]
        query_slopes = []
        for head in range(2):
            own = head_lanes(queries, head)
            own_slope = head_lanes(slope, head)
            logsum = logsum_ref[0, 0, head : head + 1, rows]
            query_slope = None
            for first in range(0, start + TILE, TILE):
                span = slice(first, first + TILE)
                scores = dot_nt(qkv[1, span], own)
                if first == start:
                    scores = keep_diagonal(scores)
                shares = jnp.exp(scores - logsum)
                against = dot_nt(qkv[2, span], own_slope)
                slopes = (shares * (against - inner[head][:, rows])).astype(LOW)
                value_slope = dot_nn(shares.astype(LOW), own_slope)
                key_slope = dot_nn(slopes, own)
                if first == start and head == 0:
                    grads[2, span] = value_slope
                    grads[1, span] = key_slope
                else:
                    grads[2, span] += value_slope
                    grads[1, span] += key_slope
                piece = dot_nn(keys_t[:, span], slopes)
                query_slope = piece if query_slope is None else query_slope + piece
            query_slopes.append(query_slope[head * HDIM : (head + 1) * HDIM])
        grads[0, rows] = jnp.concatenate(query_slopes, axis=0).T
    for kind in range(3):
        part(core, grads.at[kind], out_mine.at[kind, 0], out_theirs.at[kind, 0])


def attend_back(core, mine, theirs, logsum, mixed, slope):
    three, count, rows, width = mine.shape
    pairs = width // 128
    wide = pl.BlockSpec((3, 1, rows, 128), lambda s, p, core: (0, s, 0, p))
    thin = pl.BlockSpec((1, rows, 128), lambda s, p, core: (s, 0, p))
    sums = pl.BlockSpec((1, 1, 8, 2 * rows), lambda s, p, core: (s, p, 0, 0))
    return pl.pallas_call(
        attend_back_kernel,
        grid_spec=pltpu.PrefetchScalarGridSpec(
            num_scalar_prefetch=1,
            grid=(count, pairs),
            in_specs=[wide, wide, sums, thin, thin, thin, thin],
            out_specs=[wide, wide],
            scratch_shapes=[
                pltpu.VMEM((3, 2 * rows, 128), LOW),
                pltpu.VMEM((2 * rows, 128), LOW),
                pltpu.VMEM((2 * rows, 128), LOW),
                pltpu.VMEM((3, 2 * rows, 128), FULL),
            ],
        ),
        out_shape=[jax.ShapeDtypeStruct(mine.shape, LOW)] * 2,
        compiler_params=pltpu.CompilerParams(vmem_limit_bytes=32 * MIB),
        name="attend_back",
    )(core, mine, theirs, logsum, *mixed, *slope)


def normalize(residual, gain, shift):
    average = jnp.mean(residual, axis=-1, keepdims=True)
    centred = residual - average
    variance = jnp.mean(centred * centred, axis=-1, keepdims=True)
    return centred * lax.rsqrt(variance + EPSILON) * gain + shift


def norm_backward(residual, gain, shift, slope):
    unused, pullback = jax.vjp(normalize, residual, gain, shift)
    return pullback(slope)


def gelu(hidden):
    return jax.nn.gelu(hidden, approximate=True)


def matmul(left, right):
    return jnp.dot(left, right, preferred_element_type=FULL)


def contract(left, right):
    return jnp.einsum("std,ste->de", left, right, preferred_element_type=FULL).astype(LOW)


def transposed(left, right):
    return jnp.einsum("ste,de->std", left, right, preferred_element_type=FULL)


def swap(item, axis, mask=1):
    count = lax.axis_size(axis)
    return lax.ppermute(item, axis, [(i, i ^ mask) for i in range(count)])


def bit_of(axis, mask=1):
    return (lax.axis_index(axis) & mask) != 0


def masks_of(axis):
    count = lax.axis_size(axis)
    masks = []
    mask = 1
    while mask < count:
        masks.append(mask)
        mask *= 2
    return masks


def ordered(own, other, bit, axis):
    low = jnp.where(bit, other, own)
    high = jnp.where(bit, own, other)
    return jnp.stack([low, high], axis=axis)


def side_by_side(own, other, bit):
    low = jnp.where(bit, other, own)
    high = jnp.where(bit, own, other)
    return jnp.concatenate([low, high], axis=-1)


def chosen(item, bit, axis):
    return lax.dynamic_index_in_dim(item, bit.astype(jnp.int32), axis, keepdims=False)


def added(left, right):
    return (left.astype(FULL) + right.astype(FULL)).astype(LOW)


class Flow:
    def __init__(self, steps):
        self.steps = steps
        self.result = None
        self.done = False
        self.flying = None
        self.waiting = None
        self.advance(None)

    def advance(self, arrived):
        try:
            self.waiting = self.steps.send(arrived)
        except StopIteration as stop:
            self.done = True
            self.waiting = None
            self.result = stop.value

    def launch(self):
        if not self.done:
            self.flying = [swap(*send) for send in self.waiting]
            self.waiting = None


def cut(live, *flows):
    flows = [flow for flow in flows if not flow.done]
    sends = [
        flow.flying if flow.flying is not None else [item[0] for item in flow.waiting]
        for flow in flows
    ]
    live, sends = lax.optimization_barrier((live, sends))
    for flow, arrays in zip(flows, sends):
        if flow.flying is not None:
            flow.flying = None
            flow.advance(arrays)
        else:
            flow.waiting = [(a,) + item[1:] for a, item in zip(arrays, flow.waiting)]
        flow.launch()
    return live


def drain(live, *flows):
    while not all(flow.done for flow in flows):
        live = cut(live, *flows)
    return live


def grown(held, other, mask, flip=None):
    bit = bit_of("dp", mask)
    if flip is not None:
        bit = bit ^ flip
    joined = ordered(held, other, bit, -3)
    return joined.reshape(held.shape[:-3] + (-1,) + held.shape[-2:])


def gather_small(piece):
    held = piece[None]
    for mask in reversed(masks_of("dp")):
        (other,) = yield [(held, "dp", mask)]
        held = grown(held, other, mask)
    return held


def rows_of(held):
    return held.reshape(held.shape[:-3] + (-1, held.shape[-1]))


def quarter_of(block):
    width = block.shape[1] // 4
    start = (2 * lax.axis_index("uly") + lax.axis_index("blk")) * width
    return lax.dynamic_slice_in_dim(block, start, width, 1)


def gather_attention(first, second):
    held = jnp.stack([quarter_of(first), quarter_of(second)])[:, None]
    masks = masks_of("dp")
    for mask in reversed(masks[1:]):
        (other,) = yield [(held, "dp", mask)]
        held = grown(held, other, mask)
    left, right = held[0], held[1]
    place = bit_of("uly")
    other_left, other_right = yield [(left, "dp", masks[0]), (right, "uly", 1)]
    left = grown(left, other_left, masks[0])
    right = ordered(right, other_right, place, 0)
    other_left, other_right = yield [(left, "uly", 1), (right, "dp", masks[0])]
    left = rows_of(ordered(left, other_left, place, 0))
    right = rows_of(grown(right, other_right, masks[0]))
    other = yield [(left, "blk", 1), (right, "blk", 1)]
    return (left, right), tuple(other)


def gather_up(block):
    width = block.shape[1] // 4
    start = (2 * lax.axis_index("blk") + lax.axis_index("uly")) * width
    held = lax.dynamic_slice_in_dim(block, start, width, 1)[None]
    for mask in reversed(masks_of("dp")):
        (other,) = yield [(held, "dp", mask)]
        held = grown(held, other, mask)
    rows = rows_of(held)
    (other,) = yield [(rows, "uly", 1)]
    own = ordered(rows, other, bit_of("uly"), 0)
    (other,) = yield [(own, "blk", 1)]
    return own, other


def gather_down(block):
    width = block.shape[1] // 2
    held = lax.dynamic_slice_in_dim(block, lax.axis_index("blk") * width, width, 1)[None]
    masks = masks_of("dp")
    for mask in reversed(masks):
        (other,) = yield [(held, "dp", mask)]
        held = grown(held, other, mask, bit_of("blk") if mask == masks[-1] else None)
    own = held.reshape(2, -1, width)
    (other,) = yield [(own, "blk", 1)]
    return own, other


def halved(held, bit):
    return chosen(held, bit, -3), chosen(held, ~bit, -3)


def split_rows(held):
    return held.reshape(held.shape[:-3] + (-1, 2) + held.shape[-2:])


def reduce_attention(own, other):
    count = lax.axis_size("dp")
    masks = masks_of("dp")
    place = bit_of("uly")
    arrived = yield [(other[0], "blk", 1), (other[1], "blk", 1)]
    left, right = added(own[0], arrived[0]), added(own[1], arrived[1])
    two, rows, width = left.shape
    left = left.reshape(2, count, rows // count, width)
    right = right.reshape(2, count, rows // count, width)
    keep_left, send_left = chosen(left, place, 0), chosen(left, ~place, 0)
    bit = bit_of("dp", masks[0])
    keep_right, send_right = halved(split_rows(right), bit)
    arrived = yield [(send_left, "uly", 1), (send_right, "dp", masks[0])]
    left, right = added(keep_left, arrived[0]), added(keep_right, arrived[1])
    keep_left, send_left = halved(split_rows(left), bit)
    keep_right, send_right = chosen(right, place, 0), chosen(right, ~place, 0)
    arrived = yield [(send_left, "dp", masks[0]), (send_right, "uly", 1)]
    held = jnp.stack([added(keep_left, arrived[0]), added(keep_right, arrived[1])])
    for mask in masks[1:]:
        keep, send = halved(split_rows(held), bit_of("dp", mask))
        (other,) = yield [(send, "dp", mask)]
        held = added(keep, other)
    held = held[:, 0]
    (other,) = yield [(held, "uly", 1)]
    held = ordered(held, other, place, 1)
    (other,) = yield [(held, "blk", 1)]
    return ordered(held, other, bit_of("blk"), 1)


def reduce_up(own, other):
    count = lax.axis_size("dp")
    place = bit_of("uly")
    (arrived,) = yield [(other, "blk", 1)]
    held = added(own, arrived)
    two, rows, width = held.shape
    keep, send = chosen(held, place, 0), chosen(held, ~place, 0)
    (arrived,) = yield [(send, "uly", 1)]
    held = added(keep, arrived).reshape(count, rows // count, width)
    for mask in masks_of("dp"):
        keep, send = halved(split_rows(held), bit_of("dp", mask))
        (arrived,) = yield [(send, "dp", mask)]
        held = added(keep, arrived)
    held = held[0]
    (arrived,) = yield [(held, "uly", 1)]
    held = ordered(held, arrived, place, 0)
    (arrived,) = yield [(held, "blk", 1)]
    every = ordered(held, arrived, bit_of("blk"), 0)
    return jnp.concatenate([every[i, j] for i in range(2) for j in range(2)], axis=-1)


def reduce_down(own, other):
    count = lax.axis_size("dp")
    masks = masks_of("dp")
    (arrived,) = yield [(other, "blk", 1)]
    held = added(own, jnp.stack([arrived[1], arrived[0]]))
    width = held.shape[2]
    held = held.reshape(count, -1, width)
    for mask in masks:
        bit = bit_of("dp", mask)
        if mask == masks[-1]:
            bit = bit ^ bit_of("blk")
        keep, send = halved(split_rows(held), bit)
        (arrived,) = yield [(send, "dp", mask)]
        held = added(keep, arrived)
    held = held[0]
    (arrived,) = yield [(held, "uly", 1)]
    held = added(held, arrived)
    (arrived,) = yield [(held, "blk", 1)]
    return side_by_side(held, arrived, bit_of("blk"))


def to_sequences(local):
    place = bit_of("uly")
    count, rows, width = local.shape
    paired = local.reshape(2, count // 2, rows, width)
    (arrived,) = yield [(chosen(paired, ~place, 0), "uly", 1)]
    joined = ordered(chosen(paired, place, 0), arrived, place, 1)
    return joined.reshape(count // 2, 2 * rows, width)


def from_sequences(held):
    place = bit_of("uly")
    count, rows, width = held.shape
    paired = held.reshape(count, 2, rows // 2, width)
    (arrived,) = yield [(chosen(paired, ~place, 1).astype(LOW), "uly", 1)]
    joined = ordered(chosen(paired, place, 1), arrived.astype(FULL), place, 0)
    return joined.reshape(2 * count, rows // 2, width)


def token_sum(item):
    return jnp.sum(item.astype(FULL), axis=(0, 1))


def halves_of(item):
    half = item.shape[-1] // 2
    core = lax.axis_index("blk")
    axis = item.ndim - 1
    return (
        lax.dynamic_slice_in_dim(item, core * half, half, axis),
        lax.dynamic_slice_in_dim(item, (1 - core) * half, half, axis),
    )


def layer_forward(residual, small, flows, coming, core):
    attention, up_flow, down_flow = flows
    first_gain, first_shift, query_bias, value_bias, out_bias = small[:5]
    second_gain, second_shift, down_bias = small[5:8]
    up_bias = small[8:].reshape(-1)
    bit = bit_of("blk")
    next_attention, next_up, next_down = coming if coming else (None, None, None)

    def with_next(*items):
        return [item for item in items if item is not None]

    own, other = attention.result
    normed = normalize(residual, first_gain, first_shift).astype(LOW)
    normed = cut(normed, up_flow, down_flow)
    query_biases, value_biases = halves_of(query_bias), halves_of(value_bias)

    def project(weights, i):
        (query, key), (value, unused) = weights
        return jnp.stack(
            [
                (matmul(normed, query) + query_biases[i]).astype(LOW),
                matmul(normed, key).astype(LOW),
                (matmul(normed, value) + value_biases[i]).astype(LOW),
            ]
        )

    away = swap(project(other, 1), "blk")
    mine = project(own, 0)
    mine, away = cut((mine, away), up_flow, down_flow, *with_next(next_attention))
    mixed_mine, mixed_theirs, logsum = attend(core, mine, away)
    mixed_mine, mixed_theirs = cut((mixed_mine, mixed_theirs), *with_next(next_attention))
    arrived = swap(mixed_theirs, "blk")
    mixed = side_by_side(mixed_mine, arrived, bit)
    columns = side_by_side(matmul(mixed, own[1][1]), matmul(mixed, other[1][1]), bit)
    middle = residual + columns + out_bias
    normed_two = normalize(middle, second_gain, second_shift).astype(LOW)
    middle, normed_two = cut(
        (middle, normed_two), up_flow, down_flow, *with_next(next_attention)
    )
    middle, normed_two = drain((middle, normed_two), up_flow)
    up_biases = halves_of(up_bias)
    width = up_flow.result[0].shape[2]
    hidden = []
    active = []
    for weights, bias in zip(up_flow.result, up_biases):
        parts = [
            matmul(normed_two, weights[i]) + bias[i * width : (i + 1) * width] for i in range(2)
        ]
        hidden.append(parts)
        active.append(jnp.concatenate([gelu(item).astype(LOW) for item in parts], axis=-1))
    active, middle = cut(
        (active, middle), down_flow, *with_next(next_attention, next_up)
    )
    active, middle = drain((active, middle), down_flow)
    down_own, down_other = down_flow.result
    left = matmul(active[0], down_own[0]) + matmul(active[1], down_own[1])
    right = matmul(active[0], down_other[1]) + matmul(active[1], down_other[0])
    result = middle + side_by_side(left, right, bit) + down_bias
    if coming:
        result = cut(result, next_attention, next_up, next_down)
        result = cut(result, next_attention)
    record = (residual, normed, mine, away, logsum, mixed_mine, mixed_theirs, mixed)
    return result, record + (middle, normed_two, hidden, active)


def layer_backward(upstream, small, weights, record, core, before):
    (own, other), (up_own, up_other), (down_own, down_other) = weights
    first_gain, first_shift = small[:2]
    second_gain, second_shift = small[5:7]
    residual, normed, mine, away, logsum, mixed_mine, mixed_theirs, mixed = record[:8]
    middle, normed_two, hidden, active = record[8:]
    bit = bit_of("blk")

    down_bias_slope = token_sum(upstream)
    low_own, low_other = halves_of(upstream.astype(LOW))
    down_slopes = [
        jnp.stack([contract(active[i], low_other) for i in range(2)]),
        jnp.stack([contract(active[i], low_own) for i in range(2)]),
    ]
    down_flow = Flow(reduce_down(down_slopes[1], down_slopes[0]))
    low_own, low_other, upstream = cut((low_own, low_other, upstream), down_flow, *before)
    active_slopes = [
        transposed(low_own, down_own[0]) + transposed(low_other, down_other[1]),
        transposed(low_own, down_own[1]) + transposed(low_other, down_other[0]),
    ]
    low_hidden = []
    bias_slopes = []
    for slope, parts in zip(active_slopes, hidden):
        width = parts[0].shape[-1]
        for i, item in enumerate(parts):
            unused, pullback = jax.vjp(gelu, item)
            hidden_slope = pullback(slope[..., i * width : (i + 1) * width])[0]
            bias_slopes.append(token_sum(hidden_slope))
            low_hidden.append(hidden_slope.astype(LOW))
    low_hidden = cut(low_hidden, down_flow, *before)
    up_bias_slope = side_by_side(
        jnp.concatenate(bias_slopes[:2]), jnp.concatenate(bias_slopes[2:]), bit
    )
    up_slopes = [
        jnp.stack([contract(normed_two, low_hidden[2 + i]) for i in range(2)]),
        jnp.stack([contract(normed_two, low_hidden[i]) for i in range(2)]),
    ]
    up_flow = Flow(reduce_up(up_slopes[1], up_slopes[0]))
    low_hidden = cut(low_hidden, up_flow)
    norm_slope = (
        transposed(low_hidden[0], up_own[0])
        + transposed(low_hidden[1], up_own[1])
        + transposed(low_hidden[2], up_other[0])
        + transposed(low_hidden[3], up_other[1])
    )
    through, second_gain_slope, second_shift_slope = norm_backward(
        middle, second_gain, second_shift, norm_slope
    )
    middle_slope = upstream + through
    middle_slope = cut(middle_slope, up_flow, *before)

    out_bias_slope = token_sum(middle_slope)
    low_own, low_other = halves_of(middle_slope.astype(LOW))
    mixed_slope = transposed(low_own, own[1][1]) + transposed(low_other, other[1][1])
    slope_own, slope_other = halves_of(mixed_slope.astype(LOW))
    slope_away = swap(slope_other, "blk")
    out_slopes = contract(mixed, low_own), contract(mixed, low_other)
    slope_own, slope_away, out_slopes = cut((slope_own, slope_away, out_slopes), *before)
    grads_mine, grads_theirs = attend_back(
        core, mine, away, logsum, (mixed_mine, mixed_theirs), (slope_own, slope_away)
    )
    grads_mine, grads_theirs, middle_slope = cut(
        (grads_mine, grads_theirs, middle_slope), down_flow, up_flow, *before
    )
    grads_away = swap(grads_theirs, "blk")
    first, second = [], []
    for grads, out_slope in zip((grads_mine, grads_away), out_slopes):
        slopes = [contract(normed, grads[i]) for i in range(3)]
        first.append(jnp.stack(slopes[:2]))
        second.append(jnp.stack([slopes[2], out_slope]))
    attention_flow = Flow(reduce_attention((first[0], second[0]), (first[1], second[1])))
    grads_mine, grads_away, middle_slope = cut(
        (grads_mine, grads_away, middle_slope), attention_flow, *before
    )
    query_bias_slope = side_by_side(token_sum(grads_mine[0]), token_sum(grads_away[0]), bit)
    value_bias_slope = side_by_side(token_sum(grads_mine[2]), token_sum(grads_away[2]), bit)
    first_slope = 0.0
    for grads, (pair, last) in ((grads_mine, own), (grads_away, other)):
        first_slope = (
            first_slope
            + transposed(grads[0], pair[0])
            + transposed(grads[1], pair[1])
            + transposed(grads[2], last[0])
        )
    through, first_gain_slope, first_shift_slope = norm_backward(
        residual, first_gain, first_shift, first_slope
    )
    upstream = middle_slope + through
    upstream = cut(upstream, attention_flow, up_flow, down_flow, *before)
    vectors = [
        first_gain_slope,
        first_shift_slope,
        query_bias_slope,
        value_bias_slope,
        out_bias_slope,
        second_gain_slope,
        second_shift_slope,
        down_bias_slope,
    ]
    terms = jnp.concatenate([jnp.stack(vectors), up_bias_slope.reshape(-1, middle.shape[-1])])
    return upstream, terms, (attention_flow, up_flow, down_flow)


def shards(
    inputs,
    cotangent,
    first_gain,
    first_shift,
    in_weight,
    query_bias,
    value_bias,
    out_weight,
    out_bias,
    second_gain,
    second_shift,
    up_weight,
    up_bias,
    down_weight,
    down_bias,
):
    layers, rows = in_weight.shape[0], in_weight.shape[1]
    width = out_weight.shape[2]
    core = lax.axis_index("blk").astype(jnp.int32).reshape(1)
    vectors = jnp.stack(
        [
            first_gain,
            first_shift,
            query_bias,
            value_bias,
            out_bias,
            second_gain,
            second_shift,
            down_bias,
        ],
        axis=1,
    )
    vectors = jnp.concatenate([vectors, up_bias.reshape(layers, -1, rows)], axis=1)
    kinds = vectors.shape[1]

    flows = []
    for layer in range(layers):
        first = in_weight[layer][:, : 2 * width]
        second = jnp.concatenate([in_weight[layer][:, 2 * width :], out_weight[layer]], axis=1)
        flows.append(
            (
                Flow(gather_attention(first, second)),
                Flow(gather_up(up_weight[layer])),
                Flow(gather_down(down_weight[layer])),
            )
        )
    attention, up_flow, down_flow = flows[0]
    entering = Flow(to_sequences(inputs))
    vector_flow = Flow(gather_small(vectors.reshape(layers * kinds, rows)))
    cut((), attention, entering, vector_flow)
    cut((), attention, entering, vector_flow)
    residual = entering.result.astype(FULL)
    residual = cut(residual, attention, vector_flow, up_flow)
    residual = cut(residual, attention, vector_flow, up_flow, down_flow)
    residual = drain(residual, vector_flow)
    gathered = vector_flow.result.reshape(-1, layers, kinds, rows).astype(FULL)
    straight = gathered.transpose(1, 2, 0, 3).reshape(layers, kinds, width)
    biases = gathered[:, :, 8:].transpose(1, 0, 2, 3).reshape(layers, kinds - 8, width)
    small = jnp.concatenate([straight[:, :8], biases], axis=1)
    residual = cut(residual, attention)
    leaving = Flow(to_sequences(cotangent))
    records = []
    for layer in range(layers):
        residual = drain(residual, flows[layer][0])
        coming = flows[layer + 1] if layer + 1 < layers else None
        if coming is None:
            residual = cut(residual, leaving)
        residual, record = layer_forward(residual, small[layer], flows[layer], coming, core)
        records.append(record)
    residual = drain(residual, leaving)
    outgoing = Flow(from_sequences(residual))
    upstream = leaving.result.astype(FULL)
    upstream = cut(upstream, outgoing)
    found = [None] * layers
    terms = [None] * layers
    before = ()
    for layer in reversed(range(layers)):
        weights = tuple(flow.result for flow in flows[layer])
        upstream, terms[layer], after = layer_backward(
            upstream, small[layer], weights, records[layer], core, before
        )
        upstream = drain(upstream, *before)
        before = after
        found[layer] = after
    gradient = Flow(from_sequences(upstream))
    drain((), *before, gradient, outgoing)

    sums = lax.psum(jnp.stack(terms), ("dp", "blk", "uly"))
    place = lax.axis_index("dp")
    sliced = lax.dynamic_slice_in_dim(sums, place * rows, rows, 2)
    long = kinds - 8
    up_sums = lax.dynamic_slice_in_dim(
        sums[:, 8:].reshape(layers, -1), place * long * rows, long * rows, 1
    )
    matrices = [[], [], [], []]
    for layer in range(layers):
        attention, up_flow, down_flow = found[layer]
        pairs = attention.result
        whole = [
            jnp.concatenate([pairs[block, 0, kind], pairs[block, 1, kind]], axis=-1)
            for block in range(2)
            for kind in range(2)
        ]
        matrices[0].append(jnp.concatenate(whole[:3], axis=-1))
        matrices[1].append(whole[3])
        matrices[2].append(up_flow.result)
        matrices[3].append(down_flow.result)
    in_sum, out_sum, up_sum, down_sum = (jnp.stack(item).astype(FULL) for item in matrices)
    return (
        outgoing.result,
        gradient.result,
        sliced[:, 0],
        sliced[:, 1],
        in_sum,
        sliced[:, 2],
        sliced[:, 3],
        out_sum,
        sliced[:, 4],
        sliced[:, 5],
        sliced[:, 6],
        up_sum,
        up_sums,
        down_sum,
        sliced[:, 7],
    )


def solution(mesh):
    token = P("dp", ("blk", "uly"), None)
    vector = P(None, "dp")
    matrix = P(None, "dp", None)
    params = (
        vector,
        vector,
        matrix,
        vector,
        vector,
        matrix,
        vector,
        vector,
        vector,
        matrix,
        vector,
        matrix,
        vector,
    )
    specs = (token, token) + params
    return jax.shard_map(shards, mesh=mesh, in_specs=specs, out_specs=specs, check_vma=False)
```

time: 955 us -> 828 us (0.87)
  matrix products: 267 us -> 122 us
  Pallas kernels: 0 us -> 56.4 us
  other arithmetic: 188 us -> 133 us
  between operations: 4.96 us -> 19.2 us
  local copies, waits for them, and re-layouts: 136 us -> 122 us
  starting transfers between devices: 75.4 us -> 87.6 us
    dot_general x32, matrix products: 171 us -> 36.3 us  [contract(): jnp.einsum('std,ste->de', left, right, preferred_element_type=FULL)]
    psum x0 -> x1, waiting for transfers between devices: none -> 111 us  [shards(): sums = lax.psum(jnp.stack(terms), ('dp', 'blk', 'uly'))]
    ppermute x93 -> x95, waiting for transfers between devices: 272 us -> 165 us  [swap(): return lax.ppermute(item, axis, [(i, i ^ mask) for i in range(count)])]
    pallas_call x0 -> x4, Pallas kernels: none -> 56.4 us  [the longest x2 33 us: attend_back(): pl.pallas_call(attend_back_kernel, grid_spec=pltpu.PrefetchScalarGridSpec...]
    reduce_sum x5 -> x0, other arithmetic: 23.6 us -> none  [the longest x2 20.5 us: attend(): total = jnp.sum(raised, axis=-1, keepdims=True)]
    convert_element_type x38 -> x49, other arithmetic: 64.7 us -> 43.6 us  [the longest x30 29.9 us: added(): return (left.astype(FULL) + right.astype(FULL)).astype(LOW)]
    unnamed x457 -> x479, local copies, waits for them, and re-layouts: 22.7 us -> 41.1 us
    another operation x80 -> x69, other arithmetic: 44.5 us -> 26.4 us  [ordered(): return jnp.stack([low, high], axis=axis)]
  transfers between devices with their start and end apart: 93 -> 96, of which waited for: 44 -> 35; matrix products, arithmetic and copies ran while one was open for 48% -> 33% of each run, Pallas kernels for 0% -> 5%
where the time goes in v2:
time: 828 us; the launch traced here: 816 us
  waiting for transfers between devices  276 us (33%)
  other arithmetic  133 us (16%)
  local copies, waits for them, and re-layouts  122 us (15%)
  matrix products  122 us (15%)
  starting transfers between devices  87.6 us (11%)
  Pallas kernels  56.4 us (7%)
  between operations  19.2 us (2%)
    ppermute x95, waiting for transfers between devices, swap(): return lax.ppermute(item, axis, [(i, i ^ mask) for i in range(count)])  165 us
    psum x1, waiting for transfers between devices, shards(): sums = lax.psum(jnp.stack(terms), ('dp', 'blk', 'uly'))  111 us
    ppermute x95, starting transfers between devices, swap(): return lax.ppermute(item, axis, [(i, i ^ mask) for i in range(count)])  87.5 us
    dot_general x32, matrix products, matmul(): return jnp.dot(left, right, preferred_element_type=FULL)  45.4 us
    unnamed x479, local copies, waits for them, and re-layouts  41.1 us
    dot_general x32, matrix products, transposed(): return jnp.einsum('ste,de->std', left, right, preferred_element_type=FULL)  40.3 us
    dot_general x32, matrix products, contract(): jnp.einsum('std,ste->de', left, right, preferred_element_type=FULL)  36.3 us
    pallas_call x2, Pallas kernels, attend_back(): pl.pallas_call(attend_back_kernel, grid_spec=pltpu.PrefetchScalarGridSpec...  33 us
  transfers between devices with their start and end apart: 96, of which 35 were waited for; matrix products, arithmetic and copies ran while one was open for 33% of the time, Pallas kernels for 5%

profile of v2, /device:TPU:0, one launch (start us, length us, event | category | flops | bytes accessed | tf_op | source)
XLA Modules:
  0.0 815.9 jit_solution(3285001111893788381)
XLA Ops:
  7.3 2.0 slice_bitcast_fusion
  13.3 4.0 collective-permute-start.2
  22.0 4.9 collective-permute-done
  32.7 6.0 collective-permute-done.3
  43.0 2.7 collective-permute-start.8
  47.0 2.6 collective-permute-done.7
  57.0 9.1 %collective-permute-done.10 = bf16[2,4,96,384]{3,2,1,0:T(8,128)(2,1)} collective-permute-done((bf16[2,4,96,384]{3,2,1,0:T(8,128)(2,1)}, bf16[2,4,96,384]{3,2,1,0:T(8,128)(2,1)}, u32[]{:S(2)}, u32[]{:S(2)}) %collective-permute-start.10) | collective-permute-done | bytes 589856 | tf_op jit(solution)/shard_map/ppermute | solution.py:240
  75.5 3.1 collective-permute-start.14
  84.3 6.3 collective-permute-done.13
  104.7 9.8 %collective-permute-done.17 = bf16[2,384,384]{2,1,0:T(8,128)(2,1)S(1)} collective-permute-done((bf16[2,384,384]{2,1,0:T(8,128)(2,1)S(1)}, bf16[2,384,384]{2,1,0:T(8,128)(2,1)S(1)}, u32[]{:S(2)}, u32[]{:S(2)}) %collective-permute-start.17) | collective-permute-done | bytes 589856 | tf_op jit(solution)/shard_map/ppermute | solution.py:240
  115.7 2.6 collective-permute-start.18
  118.7 11.6 %attend.2 = (bf16[1,512,384]{2,1,0:T(8,128)(2,1)S(1)}, bf16[1,512,384]{2,1,0:T(8,128)(2,1)S(1)}, f32[1,3,8,1024]{3,2,1,0:T(8,128)S(1)}) custom-call(s32[1]{0:T(128)} %bitcast.50.core_ref, bf16[3,1,512,384]{3,2,1,0:T(8,128)(2,1)S(1)} %pad_maximum_fusion.15.mine_ref, bf16[3,1,512,384]{3,2,1,0:T(8,128)(2,1)S(1)} %collective-permute-done.15.theirs_ref), custom_call_target="tpu_custom_call" | custom-call | tf_op jit(solution)/shard_map/attend/pallas_call | solution.py:100
  137.9 4.1 collective-permute-done.22
  142.0 17.3 %collective-permute-done.21 = bf16[4,384,384]{2,1,0:T(8,128)(2,1)S(1)} collective-permute-done((bf16[4,384,384]{2,1,0:T(8,128)(2,1)S(1)}, bf16[4,384,384]{2,1,0:T(8,128)(2,1)S(1)}, u32[]{:S(2)}, u32[]{:S(2)}) %collective-permute-start.21) | collective-permute-done | bytes 1179680 | tf_op jit(solution)/shard_map/ppermute | solution.py:240
  173.4 2.1 convolution_add_fusion.8
  176.0 2.1 convolution_add_fusion.9
  188.4 9.7 %fusion.116 = f32[512,384]{0,1:T(8,128)S(1)} fusion(bf16[1,512,1536]{2,1,0:T(8,128)(2,1)S(1)} %pad_maximum_fusion.9, bf16[2,1536,384]{2,1,0:T(8,128)(2,1)S(1)} %collective-permute-done.24), kind=kOutput, calls=%fused_computation.218 | convolution fusion | flops 603979776 | bytes 3538944 | tf_op jit(solution)/shard_map/dot_general | solution.py:227
  209.2 11.0 %collective-permute-done.32 = bf16[2,96,768]{2,1,0:T(8,128)(2,1)} collective-permute-done((bf16[2,96,768]{2,1,0:T(8,128)(2,1)}, bf16[2,96,768]{2,1,0:T(8,128)(2,1)}, u32[]{:S(2)}, u32[]{:S(2)}) %collective-permute-start.32) | collective-permute-done | bytes 294944 | tf_op jit(solution)/shard_map/ppermute | solution.py:240
  220.2 2.2 collective-permute-done.33
  234.5 11.4 %collective-permute-done.36 = bf16[2,384,384]{2,1,0:T(8,128)(2,1)S(1)} collective-permute-done((bf16[2,384,384]{2,1,0:T(8,128)(2,1)S(1)}, bf16[2,384,384]{2,1,0:T(8,128)(2,1)S(1)}, u32[]{:S(2)}, u32[]{:S(2)}) %collective-permute-start.36) | collective-permute-done | bytes 589856 | tf_op jit(solution)/shard_map/ppermute | solution.py:240
  246.2 11.8 %attend.3 = (bf16[1,512,384]{2,1,0:T(8,128)(2,1)S(1)}, bf16[1,512,384]{2,1,0:T(8,128)(2,1)S(1)}, f32[1,3,8,1024]{3,2,1,0:T(8,128)S(1)}) custom-call(s32[1]{0:T(128)} %bitcast.50.core_ref, bf16[3,1,512,384]{3,2,1,0:T(8,128)(2,1)S(1)} %pad_maximum_fusion.20.mine_ref, bf16[3,1,512,384]{3,2,1,0:T(8,128)(2,1)S(1)} %collective-permute-done.34.theirs_ref), custom_call_target="tpu_custom_call" | custom-call | tf_op jit(solution)/shard_map/attend/pallas_call | solution.py:100
  265.6 21.4 %collective-permute-done.39 = bf16[4,384,384]{2,1,0:T(8,128)(2,1)S(1)} collective-permute-done((bf16[4,384,384]{2,1,0:T(8,128)(2,1)S(1)}, bf16[4,384,384]{2,1,0:T(8,128)(2,1)S(1)}, u32[]{:S(2)}, u32[]{:S(2)}) %collective-permute-start.39) | collective-permute-done | bytes 1179680 | tf_op jit(solution)/shard_map/ppermute | solution.py:240
  301.1 2.1 convolution_add_fusion.4
  303.6 2.1 convolution_add_fusion.5
  318.7 2.0 fusion.540
  322.1 3.1 copy.256
  325.2 3.1 reshape.1482
  328.3 3.0 constant_dynamic-slice_fusion.22
  331.3 2.8 copy.282
  334.1 2.8 fusion.537
  348.6 2.9 fusion.523
  351.5 2.9 fusion.527
  362.1 2.1 fusion.195
  364.3 2.2 fusion.192
  381.5 3.1 copy.220
  393.8 2.7 convolution_convert_fusion.31
  397.4 17.0 %attend_back.2 = (bf16[3,1,512,384]{3,2,1,0:T(8,128)(2,1)S(1)}, bf16[3,1,512,384]{3,2,1,0:T(8,128)(2,1)S(1)}) custom-call(s32[1]{0:T(128)} %bitcast.50.core_ref, bf16[3,1,512,384]{3,2,1,0:T(8,128)(2,1)S(1)} %pad_maximum_fusion.20.mine_ref, bf16[3,1,512,384]{3,2,1,0:T(8,128)(2,1)S(1)} %collective-permute-done.34.theirs_ref, f32[1,3,8,1024]{3,2,1,0:T(8,128)S(1)} %copy-done.11, ...), custom_call_target="tpu_custom_call" | custom-call | tf_op jit(solution)/shard_map/attend_back/pallas_call | solution.py:190
  438.0 2.1 fusion.90
  460.6 2.5 fusion.11
  463.7 2.1 fusion.10
  468.0 4.9 collective-permute-done.53
  485.2 3.1 fusion.515
  488.4 3.2 fusion.519
  507.5 2.1 fusion.207
  509.6 2.2 fusion.204
  516.1 2.0 fusion.533
  518.4 2.0 add_convert_fusion.1
  536.9 2.2 add_convert_fusion
  545.3 16.0 %attend_back.3 = (bf16[3,1,512,384]{3,2,1,0:T(8,128)(2,1)S(1)}, bf16[3,1,512,384]{3,2,1,0:T(8,128)(2,1)S(1)}) custom-call(s32[1]{0:T(128)} %bitcast.50.core_ref, bf16[3,1,512,384]{3,2,1,0:T(8,128)(2,1)S(1)} %copy-done.1, bf16[3,1,512,384]{3,2,1,0:T(8,128)(2,1)S(1)} %copy-done.3, f32[1,3,8,1024]{3,2,1,0:T(8,128)S(1)} %copy-done.9, ...), custom_call_target="tpu_custom_call" | custom-call | tf_op jit(solution)/shard_map/attend_back/pallas_call | solution.py:190
  561.3 12.2 %collective-permute-done.71 = bf16[2,96,384]{2,1,0:T(8,128)(2,1)S(1)} collective-permute-done((bf16[2,96,384]{2,1,0:T(8,128)(2,1)S(1)}, bf16[2,96,384]{2,1,0:T(8,128)(2,1)S(1)}, u32[]{:S(2)}, u32[]{:S(2)}) %collective-permute-start.71) | collective-permute-done | bytes 147488 | tf_op jit(solution)/shard_map/ppermute | solution.py:240
  597.6 2.2 fusion.80
  603.6 2.7 concatenate.121
  610.0 3.1 add_add_fusion.4
  613.1 111.0 %all-reduce.2.cloned.1.call-done = f32[2,12,768]{2,0,1:T(2,128)} async-done(((f32[2,12,768]{2,0,1:T(2,128)}), f32[2,12,768]{2,0,1:T(2,128)}) %all-reduce.2.cloned.1.call-update) | async-done | bytes 73744 | tf_op jit(solution)/shard_map/psum | solution.py:760
  737.8 3.9 collective-permute-start.80
  748.6 4.1 collective-permute-done.80
  752.7 2.8 collective-permute-done.81
  767.2 3.4 collective-permute-done.84
  770.6 5.8 collective-permute-done.86
  776.5 5.7 collective-permute-done.87
  787.7 4.2 collective-permute-done.88
  792.1 3.3 collective-permute-start.91
  797.2 2.0 collective-permute-done.91
  801.0 3.5 collective-permute-done.93
  (1080 shorter events, 371.0 us)
Async XLA Ops:
  7.3 716.9 %all-reduce.2.cloned.1.call-start = ((), (), s32[]{:S(2)}) async-start(), calls=%async_computation | async-start | bytes 147456 | tf_op jit(solution)/shard_map/psum | solution.py:760
  17.3 10.8 %collective-permute-start.1 = (bf16[1,256,768]{2,1,0:T(8,128)(2,1)}, bf16[1,256,768]{2,1,0:T(8,128)(2,1)S(1)}, u32[]{:S(2)}, u32[]{:S(2)}) collective-permute-start(bf16[1,256,768]{2,1,0:T(8,128)(2,1)} %get-tuple-element.209), channel_id=1, source_target_pairs={{0,1},{1,0},{2,3},{3,2},{4,5},{5,4},{6,7},{7,6},{8,9},{9,8},{10,11... | collective-permute-start | bytes 1179656 | tf_op jit(solution)/shard_map/ppermute | solution.py:240
  39.9 10.8 %collective-permute-start.5 = (bf16[4,96,384]{2,1,0:T(8,128)(2,1)S(1)}, bf16[4,96,384]{2,1,0:T(8,128)(2,1)S(1)}, u32[]{:S(2)}, u32[]{:S(2)}) collective-permute-start(bf16[4,96,384]{2,1,0:T(8,128)(2,1)S(1)} %bitcast.1631), channel_id=1, source_target_pairs={{0,4},{4,0},{8,12},{12,8},{16,20},{20,16},{24,28},{28,24},{1,5},{5... | collective-permute-start | bytes 884744 | tf_op jit(solution)/shard_map/ppermute | solution.py:240
  55.1 11.0 %collective-permute-start.10 = (bf16[2,4,96,384]{3,2,1,0:T(8,128)(2,1)}, bf16[2,4,96,384]{3,2,1,0:T(8,128)(2,1)}, u32[]{:S(2)}, u32[]{:S(2)}) collective-permute-start(bf16[2,4,96,384]{3,2,1,0:T(8,128)(2,1)} %pad_maximum_fusion.31), channel_id=1, source_target_pairs={{0,4},{4,0},{8,12},{12,8},{16,20},{20,16},{24,28},{28,24},{1,5},{5... | collective-permute-start | bytes 1769480 | tf_op jit(solution)/shard_map/ppermute | solution.py:240
  55.6 10.5 %collective-permute-start.9 = (bf16[8,96,384]{2,1,0:T(8,128)(2,1)S(1)}, bf16[8,96,384]{2,1,0:T(8,128)(2,1)}, u32[]{:S(2)}, u32[]{:S(2)}) collective-permute-start(bf16[8,96,384]{2,1,0:T(8,128)(2,1)S(1)} %bitcast.1607), channel_id=1, source_target_pairs={{0,1},{1,0},{2,3},{3,2},{4,5},{5,4},{6,7},{7,6},{8,9},{9,8},{10,11... | collective-permute-start | bytes 1769480 | tf_op jit(solution)/shard_map/ppermute | solution.py:240
  71.4 12.1 %collective-permute-start.11 = (bf16[2,768,384]{2,1,0:T(8,128)(2,1)}, bf16[2,768,384]{2,1,0:T(8,128)(2,1)}, u32[]{:S(2)}, u32[]{:S(2)}) collective-permute-start(bf16[2,768,384]{2,1,0:T(8,128)(2,1)} %pad_maximum_fusion.14), channel_id=1, source_target_pairs={{0,2},{2,0},{1,3},{3,1},{4,6},{6,4},{5,7},{7,5},{8,10},{10,8},{9,1... | collective-permute-start | bytes 3538952 | tf_op jit(solution)/shard_map/ppermute | solution.py:240
  71.4 12.1 %collective-permute-start.12 = (bf16[2,768,384]{2,1,0:T(8,128)(2,1)}, bf16[2,768,384]{2,1,0:T(8,128)(2,1)}, u32[]{:S(2)}, u32[]{:S(2)}) collective-permute-start(bf16[2,768,384]{2,1,0:T(8,128)(2,1)} %bitcast.40), channel_id=1, source_target_pairs={{0,2},{2,0},{1,3},{3,1},{4,6},{6,4},{5,7},{7,5},{8,10},{10,8},{9,1... | collective-permute-start | bytes 3538952 | tf_op jit(solution)/shard_map/ppermute | solution.py:240
  75.3 15.3 %collective-permute-start.13 = (bf16[2,96,768]{2,1,0:T(8,128)(2,1)}, bf16[2,96,768]{2,1,0:T(8,128)(2,1)}, u32[]{:S(2)}, u32[]{:S(2)}) collective-permute-start(bf16[2,96,768]{2,1,0:T(8,128)(2,1)} %maximum_bitcast_fusion.11), channel_id=1, source_target_pairs={{0,8},{4,12},{8,0},{12,4},{16,24},{20,28},{24,16},{28,20},{1,9},{5... | collective-permute-start | bytes 884744 | tf_op jit(solution)/shard_map/ppermute | solution.py:240
  75.5 16.7 %collective-permute-start.14 = (bf16[1,384,384]{2,1,0:T(8,128)(2,1)}, bf16[1,384,384]{2,1,0:T(8,128)(2,1)}, u32[]{:S(2)}, u32[]{:S(2)}) collective-permute-start(bf16[1,384,384]{2,1,0:T(8,128)(2,1)} %constant_dynamic-slice_fusion.34), channel_id=1, source_target_pairs={{0,16},{4,20},{8,24},{12,28},{16,0},{20,4},{24,8},{28,12},{1,17},{... | collective-permute-start | bytes 884744 | tf_op jit(solution)/shard_map/ppermute | solution.py:240
  97.5 18.3 %collective-permute-start.15 = (bf16[3,1,512,384]{3,2,1,0:T(8,128)(2,1)S(1)}, bf16[3,1,512,384]{3,2,1,0:T(8,128)(2,1)S(1)}, u32[]{:S(2)}, u32[]{:S(2)}) collective-permute-start(bf16[3,1,512,384]{3,2,1,0:T(8,128)(2,1)S(1)} %pad_maximum_fusion.16), channel_id=1, source_target_pairs={{0,2},{2,0},{1,3},{3,1},{4,6},{6,4},{5,7},{7,5},{8,10},{10,8},{9,1... | collective-permute-start | bytes 3538952 | tf_op jit(solution)/shard_map/ppermute | solution.py:240
  99.5 15.0 %collective-permute-start.17 = (bf16[2,384,384]{2,1,0:T(8,128)(2,1)S(1)}, bf16[2,384,384]{2,1,0:T(8,128)(2,1)S(1)}, u32[]{:S(2)}, u32[]{:S(2)}) collective-permute-start(bf16[2,384,384]{2,1,0:T(8,128)(2,1)S(1)} %maximum_bitcast_fusion.4), channel_id=1, source_target_pairs={{0,8},{4,12},{8,0},{12,4},{16,24},{20,28},{24,16},{28,20},{1,9},{5... | collective-permute-start | bytes 1769480 | tf_op jit(solution)/shard_map/ppermute | solution.py:240
  101.0 14.7 %collective-permute-start.16 = (bf16[4,96,768]{2,1,0:T(8,128)(2,1)S(1)}, bf16[4,96,768]{2,1,0:T(8,128)(2,1)S(1)}, u32[]{:S(2)}, u32[]{:S(2)}) collective-permute-start(bf16[4,96,768]{2,1,0:T(8,128)(2,1)S(1)} %bitcast.1610), channel_id=1, source_target_pairs={{0,4},{4,0},{8,12},{12,8},{16,20},{20,16},{24,28},{28,24},{1,5},{5... | collective-permute-start | bytes 1769480 | tf_op jit(solution)/shard_map/ppermute | solution.py:240
  115.7 14.7 %collective-permute-start.18 = (bf16[2,1,96,384]{3,2,0,1:T(8,128)(2,1)S(1)}, bf16[2,1,96,384]{3,2,0,1:T(8,128)(2,1)S(1)}, u32[]{:S(2)}, u32[]{:S(2)}) collective-permute-start(bf16[2,1,96,384]{3,2,0,1:T(8,128)(2,1)S(1)} %copy-done.194), channel_id=1, source_target_pairs={{0,16},{4,20},{8,24},{12,28},{16,0},{20,4},{24,8},{28,12},{1,17},{... | collective-permute-start | bytes 442376 | tf_op jit(solution)/shard_map/ppermute | solution.py:240
  131.2 28.1 %collective-permute-start.21 = (bf16[4,384,384]{2,1,0:T(8,128)(2,1)S(1)}, bf16[4,384,384]{2,1,0:T(8,128)(2,1)S(1)}, u32[]{:S(2)}, u32[]{:S(2)}) collective-permute-start(bf16[4,384,384]{2,1,0:T(8,128)(2,1)S(1)} %bitcast.1570), channel_id=1, source_target_pairs={{0,4},{4,0},{8,12},{12,8},{16,20},{20,16},{24,28},{28,24},{1,5},{5... | collective-permute-start | bytes 3538952 | tf_op jit(solution)/shard_map/ppermute | solution.py:240
  132.8 27.7 %collective-permute-start.20 = (bf16[768,768]{1,0:T(8,128)(2,1)S(1)}, bf16[768,768]{1,0:T(8,128)(2,1)S(1)}, u32[]{:S(2)}, u32[]{:S(2)}) collective-permute-start(bf16[768,768]{1,0:T(8,128)(2,1)S(1)} %bitcast.1576), channel_id=1, source_target_pairs={{0,1},{1,0},{2,3},{3,2},{4,5},{5,4},{6,7},{7,6},{8,9},{9,8},{10,11... | collective-permute-start | bytes 3538952 | tf_op jit(solution)/shard_map/ppermute | solution.py:240
  168.7 15.4 %collective-permute-start.25 = (bf16[4,96,384]{2,1,0:T(8,128)(2,1)S(1)}, bf16[4,96,384]{2,1,0:T(8,128)(2,1)S(1)}, u32[]{:S(2)}, u32[]{:S(2)}) collective-permute-start(bf16[4,96,384]{2,1,0:T(8,128)(2,1)S(1)} %bitcast.1629), channel_id=1, source_target_pairs={{0,4},{4,0},{8,12},{12,8},{16,20},{20,16},{24,28},{28,24},{1,5},{5... | collective-permute-start | bytes 884744 | tf_op jit(solution)/shard_map/ppermute | solution.py:240
  169.9 14.2 %collective-permute-start.26 = (bf16[4,96,384]{2,1,0:T(8,128)(2,1)S(1)}, bf16[4,96,384]{2,1,0:T(8,128)(2,1)S(1)}, u32[]{:S(2)}, u32[]{:S(2)}) collective-permute-start(bf16[4,96,384]{2,1,0:T(8,128)(2,1)S(1)} %bitcast.1628), channel_id=1, source_target_pairs={{0,1},{1,0},{2,3},{3,2},{4,5},{5,4},{6,7},{7,6},{8,9},{9,8},{10,11... | collective-permute-start | bytes 884744 | tf_op jit(solution)/shard_map/ppermute | solution.py:240
  171.8 12.3 %collective-permute-start.24 = (bf16[2,1536,384]{2,1,0:T(8,128)(2,1)S(1)}, bf16[2,1536,384]{2,1,0:T(8,128)(2,1)S(1)}, u32[]{:S(2)}, u32[]{:S(2)}) collective-permute-start(bf16[2,1536,384]{2,1,0:T(8,128)(2,1)S(1)} %bitcast.1611), channel_id=1, source_target_pairs={{0,2},{2,0},{1,3},{3,1},{4,6},{6,4},{5,7},{7,5},{8,10},{10,8},{9,1... | collective-permute-start | bytes 7077896 | tf_op jit(solution)/shard_map/ppermute | solution.py:240
  185.2 16.4 %collective-permute-start.29 = (bf16[1,96,768]{2,1,0:T(8,128)(2,1)S(1)}, bf16[1,96,768]{2,1,0:T(8,128)(2,1)S(1)}, u32[]{:S(2)}, u32[]{:S(2)}) collective-permute-start(bf16[1,96,768]{2,1,0:T(8,128)(2,1)S(1)} %copy-done.195), channel_id=1, source_target_pairs={{0,16},{4,20},{8,24},{12,28},{16,0},{20,4},{24,8},{28,12},{1,17},{... | collective-permute-start | bytes 442376 | tf_op jit(solution)/shard_map/ppermute | solution.py:240
  186.0 15.6 %collective-permute-start.28 = (bf16[2,4,96,384]{3,2,1,0:T(8,128)(2,1)S(1)}, bf16[2,4,96,384]{3,2,1,0:T(8,128)(2,1)S(1)}, u32[]{:S(2)}, u32[]{:S(2)}) collective-permute-start(bf16[2,4,96,384]{3,2,1,0:T(8,128)(2,1)S(1)} %pad_maximum_fusion.34), channel_id=1, source_target_pairs={{0,4},{4,0},{8,12},{12,8},{16,20},{20,16},{24,28},{28,24},{1,5},{5... | collective-permute-start | bytes 1769480 | tf_op jit(solution)/shard_map/ppermute | solution.py:240
  187.0 14.6 %collective-permute-start.27 = (bf16[8,96,384]{2,1,0:T(8,128)(2,1)S(1)}, bf16[8,96,384]{2,1,0:T(8,128)(2,1)S(1)}, u32[]{:S(2)}, u32[]{:S(2)}) collective-permute-start(bf16[8,96,384]{2,1,0:T(8,128)(2,1)S(1)} %bitcast.1608), channel_id=1, source_target_pairs={{0,1},{1,0},{2,3},{3,2},{4,5},{5,4},{6,7},{7,6},{8,9},{9,8},{10,11... | collective-permute-start | bytes 1769480 | tf_op jit(solution)/shard_map/ppermute | solution.py:240
  204.8 15.4 %collective-permute-start.32 = (bf16[2,96,768]{2,1,0:T(8,128)(2,1)}, bf16[2,96,768]{2,1,0:T(8,128)(2,1)}, u32[]{:S(2)}, u32[]{:S(2)}) collective-permute-start(bf16[2,96,768]{2,1,0:T(8,128)(2,1)} %maximum_bitcast_fusion.13), channel_id=1, source_target_pairs={{0,8},{4,12},{8,0},{12,4},{16,24},{20,28},{24,16},{28,20},{1,9},{5... | collective-permute-start | bytes 884744 | tf_op jit(solution)/shard_map/ppermute | solution.py:240
  206.1 16.3 %collective-permute-start.33 = (bf16[1,384,384]{2,1,0:T(8,128)(2,1)}, bf16[1,384,384]{2,1,0:T(8,128)(2,1)}, u32[]{:S(2)}, u32[]{:S(2)}) collective-permute-start(bf16[1,384,384]{2,1,0:T(8,128)(2,1)} %constant_dynamic-slice_fusion.28), channel_id=1, source_target_pairs={{0,16},{4,20},{8,24},{12,28},{16,0},{20,4},{24,8},{28,12},{1,17},{... | collective-permute-start | bytes 884744 | tf_op jit(solution)/shard_map/ppermute | solution.py:240
  228.7 17.3 %collective-permute-start.34 = (bf16[3,1,512,384]{3,2,1,0:T(8,128)(2,1)S(1)}, bf16[3,1,512,384]{3,2,1,0:T(8,128)(2,1)S(1)}, u32[]{:S(2)}, u32[]{:S(2)}) collective-permute-start(bf16[3,1,512,384]{3,2,1,0:T(8,128)(2,1)S(1)} %pad_maximum_fusion.21), channel_id=1, source_target_pairs={{0,2},{2,0},{1,3},{3,1},{4,6},{6,4},{5,7},{7,5},{8,10},{10,8},{9,1... | collective-permute-start | bytes 3538952 | tf_op jit(solution)/shard_map/ppermute | solution.py:240
  230.9 14.9 %collective-permute-start.36 = (bf16[2,384,384]{2,1,0:T(8,128)(2,1)S(1)}, bf16[2,384,384]{2,1,0:T(8,128)(2,1)S(1)}, u32[]{:S(2)}, u32[]{:S(2)}) collective-permute-start(bf16[2,384,384]{2,1,0:T(8,128)(2,1)S(1)} %maximum_bitcast_fusion.5), channel_id=1, source_target_pairs={{0,8},{4,12},{8,0},{12,4},{16,24},{20,28},{24,16},{28,20},{1,9},{5... | collective-permute-start | bytes 1769480 | tf_op jit(solution)/shard_map/ppermute | solution.py:240
  231.3 14.6 %collective-permute-start.35 = (bf16[4,96,768]{2,1,0:T(8,128)(2,1)S(1)}, bf16[4,96,768]{2,1,0:T(8,128)(2,1)S(1)}, u32[]{:S(2)}, u32[]{:S(2)}) collective-permute-start(bf16[4,96,768]{2,1,0:T(8,128)(2,1)S(1)} %bitcast.1609), channel_id=1, source_target_pairs={{0,4},{4,0},{8,12},{12,8},{16,20},{20,16},{24,28},{28,24},{1,5},{5... | collective-permute-start | bytes 1769480 | tf_op jit(solution)/shard_map/ppermute | solution.py:240
  258.8 28.2 %collective-permute-start.39 = (bf16[4,384,384]{2,1,0:T(8,128)(2,1)S(1)}, bf16[4,384,384]{2,1,0:T(8,128)(2,1)S(1)}, u32[]{:S(2)}, u32[]{:S(2)}) collective-permute-start(bf16[4,384,384]{2,1,0:T(8,128)(2,1)S(1)} %bitcast.1569), channel_id=1, source_target_pairs={{0,4},{4,0},{8,12},{12,8},{16,20},{20,16},{24,28},{28,24},{1,5},{5... | collective-permute-start | bytes 3538952 | tf_op jit(solution)/shard_map/ppermute | solution.py:240
  259.9 27.9 %collective-permute-start.38 = (bf16[768,768]{1,0:T(8,128)(2,1)S(1)}, bf16[768,768]{1,0:T(8,128)(2,1)S(1)}, u32[]{:S(2)}, u32[]{:S(2)}) collective-permute-start(bf16[768,768]{1,0:T(8,128)(2,1)S(1)} %bitcast.1571), channel_id=1, source_target_pairs={{0,1},{1,0},{2,3},{3,2},{4,5},{5,4},{6,7},{7,6},{8,9},{9,8},{10,11... | collective-permute-start | bytes 3538952 | tf_op jit(solution)/shard_map/ppermute | solution.py:240
  295.1 25.6 %collective-permute-start.42 = (bf16[1,256,768]{2,1,0:T(8,128)(2,1)S(1)}, bf16[1,256,768]{2,1,0:T(8,128)(2,1)S(1)}, u32[]{:S(2)}, u32[]{:S(2)}) collective-permute-start(bf16[1,256,768]{2,1,0:T(8,128)(2,1)S(1)} %copy-done.187), channel_id=1, source_target_pairs={{0,1},{1,0},{2,3},{3,2},{4,5},{5,4},{6,7},{7,6},{8,9},{9,8},{10,11... | collective-permute-start | bytes 1179656 | tf_op jit(solution)/shard_map/ppermute | solution.py:240
  299.5 15.0 %collective-permute-start.41 = (bf16[2,1536,384]{2,1,0:T(8,128)(2,1)S(1)}, bf16[2,1536,384]{2,1,0:T(8,128)(2,1)S(1)}, u32[]{:S(2)}, u32[]{:S(2)}) collective-permute-start(bf16[2,1536,384]{2,1,0:T(8,128)(2,1)S(1)} %bitcast.1612), channel_id=1, source_target_pairs={{0,2},{2,0},{1,3},{3,1},{4,6},{6,4},{5,7},{7,5},{8,10},{10,8},{9,1... | collective-permute-start | bytes 7077896 | tf_op jit(solution)/shard_map/ppermute | solution.py:240
  361.1 53.3 %collective-permute-start.46 = (bf16[4,384,384]{2,1,0:T(8,128)(2,1)}, bf16[4,384,384]{2,1,0:T(8,128)(2,1)}, u32[]{:S(2)}, u32[]{:S(2)}) collective-permute-start(bf16[4,384,384]{2,1,0:T(8,128)(2,1)} %dynamic-slice_bitcast_fusion.3), channel_id=1, source_target_pairs={{0,4},{4,0},{8,12},{12,8},{16,20},{20,16},{24,28},{28,24},{1,5},{5... | collective-permute-start | bytes 3538952 | tf_op jit(solution)/shard_map/ppermute | solution.py:240
  375.5 38.9 %collective-permute-start.47 = (bf16[768,768]{1,0:T(8,128)(2,1)}, bf16[768,768]{1,0:T(8,128)(2,1)}, u32[]{:S(2)}, u32[]{:S(2)}) collective-permute-start(bf16[768,768]{1,0:T(8,128)(2,1)} %dynamic-slice_bitcast_fusion.2), channel_id=1, source_target_pairs={{0,1},{1,0},{2,3},{3,2},{4,5},{5,4},{6,7},{7,6},{8,9},{9,8},{10,11... | collective-permute-start | bytes 3538952 | tf_op jit(solution)/shard_map/ppermute | solution.py:240
  379.2 17.9 %collective-permute-start.45 = (bf16[1,512,384]{2,1,0:T(8,128)(2,1)}, bf16[1,512,384]{2,1,0:T(8,128)(2,1)}, u32[]{:S(2)}, u32[]{:S(2)}) collective-permute-start(bf16[1,512,384]{2,1,0:T(8,128)(2,1)} %get-tuple-element.543), channel_id=1, source_target_pairs={{0,2},{2,0},{1,3},{3,1},{4,6},{6,4},{5,7},{7,5},{8,10},{10,8},{9,1... | collective-permute-start | bytes 1179656 | tf_op jit(solution)/shard_map/ppermute | solution.py:240
  414.4 12.6 %collective-permute-start.48 = (bf16[3,1,512,384]{3,2,1,0:T(8,128)(2,1)S(1)}, bf16[3,1,512,384]{3,2,1,0:T(8,128)(2,1)S(1)}, u32[]{:S(2)}, u32[]{:S(2)}) collective-permute-start(bf16[3,1,512,384]{3,2,1,0:T(8,128)(2,1)S(1)} %get-tuple-element.316), channel_id=1, source_target_pairs={{0,2},{2,0},{1,3},{3,1},{4,6},{6,4},{5,7},{7,5},{8,10},{10,8},{9,1... | collective-permute-start | bytes 3538952 | tf_op jit(solution)/shard_map/ppermute | solution.py:240
  417.5 26.7 %collective-permute-start.52 = (bf16[2,384,384]{2,1,0:T(8,128)(2,1)}, bf16[2,384,384]{2,1,0:T(8,128)(2,1)}, u32[]{:S(2)}, u32[]{:S(2)}) collective-permute-start(bf16[2,384,384]{2,1,0:T(8,128)(2,1)} %dynamic-slice_bitcast_fusion.10), channel_id=1, source_target_pairs={{0,8},{4,12},{8,0},{12,4},{16,24},{20,28},{24,16},{28,20},{1,9},{5... | collective-permute-start | bytes 1769480 | tf_op jit(solution)/shard_map/ppermute | solution.py:240
  421.8 22.4 %collective-permute-start.51 = (bf16[4,96,768]{2,1,0:T(8,128)(2,1)}, bf16[4,96,768]{2,1,0:T(8,128)(2,1)}, u32[]{:S(2)}, u32[]{:S(2)}) collective-permute-start(bf16[4,96,768]{2,1,0:T(8,128)(2,1)} %dynamic-slice_bitcast_fusion.11), channel_id=1, source_target_pairs={{0,4},{4,0},{8,12},{12,8},{16,20},{20,16},{24,28},{28,24},{1,5},{5... | collective-permute-start | bytes 1769480 | tf_op jit(solution)/shard_map/ppermute | solution.py:240
  451.6 16.2 %collective-permute-start.56 = (bf16[1,384,384]{2,1,0:T(8,128)(2,1)S(1)}, bf16[1,384,384]{2,1,0:T(8,128)(2,1)S(1)}, u32[]{:S(2)}, u32[]{:S(2)}) collective-permute-start(bf16[1,384,384]{2,1,0:T(8,128)(2,1)S(1)} %constant_dynamic-slice_fusion.17), channel_id=1, source_target_pairs={{0,16},{4,20},{8,24},{12,28},{16,0},{20,4},{24,8},{28,12},{1,17},{... | collective-permute-start | bytes 884744 | tf_op jit(solution)/shard_map/ppermute | solution.py:240
  452.9 15.0 %collective-permute-start.55 = (bf16[2,96,768]{2,1,0:T(8,128)(2,1)S(1)}, bf16[2,96,768]{2,1,0:T(8,128)(2,1)S(1)}, u32[]{:S(2)}, u32[]{:S(2)}) collective-permute-start(bf16[2,96,768]{2,1,0:T(8,128)(2,1)S(1)} %dynamic-slice_bitcast_fusion.21), channel_id=1, source_target_pairs={{0,8},{4,12},{8,0},{12,4},{16,24},{20,28},{24,16},{28,20},{1,9},{5... | collective-permute-start | bytes 884744 | tf_op jit(solution)/shard_map/ppermute | solution.py:240
  458.0 14.8 %collective-permute-start.53 = (bf16[8,96,384]{2,1,0:T(8,128)(2,1)S(1)}, bf16[8,96,384]{2,1,0:T(8,128)(2,1)S(1)}, u32[]{:S(2)}, u32[]{:S(2)}) collective-permute-start(bf16[8,96,384]{2,1,0:T(8,128)(2,1)S(1)} %dynamic-slice_bitcast_fusion.9), channel_id=1, source_target_pairs={{0,1},{1,0},{2,3},{3,2},{4,5},{5,4},{6,7},{7,6},{8,9},{9,8},{10,11... | collective-permute-start | bytes 1769480 | tf_op jit(solution)/shard_map/ppermute | solution.py:240
  459.6 14.5 %collective-permute-start.54 = (bf16[2,4,96,384]{3,2,1,0:T(8,128)(2,1)S(1)}, bf16[2,4,96,384]{3,2,1,0:T(8,128)(2,1)S(1)}, u32[]{:S(2)}, u32[]{:S(2)}) collective-permute-start(bf16[2,4,96,384]{3,2,1,0:T(8,128)(2,1)S(1)} %dynamic-slice_bitcast_fusion.8), channel_id=1, source_target_pairs={{0,4},{4,0},{8,12},{12,8},{16,20},{20,16},{24,28},{28,24},{1,5},{5... | collective-permute-start | bytes 1769480 | tf_op jit(solution)/shard_map/ppermute | solution.py:240
  477.2 15.6 %collective-permute-start.60 = (bf16[1,96,768]{2,1,0:T(8,128)(2,1)}, bf16[1,96,768]{2,1,0:T(8,128)(2,1)}, u32[]{:S(2)}, u32[]{:S(2)}) collective-permute-start(bf16[1,96,768]{2,1,0:T(8,128)(2,1)} %constant_dynamic-slice_fusion.16), channel_id=1, source_target_pairs={{0,16},{4,20},{8,24},{12,28},{16,0},{20,4},{24,8},{28,12},{1,17},{... | collective-permute-start | bytes 442376 | tf_op jit(solution)/shard_map/ppermute | solution.py:240
  479.0 14.3 %collective-permute-start.59 = (bf16[4,96,384]{2,1,0:T(8,128)(2,1)}, bf16[4,96,384]{2,1,0:T(8,128)(2,1)S(1)}, u32[]{:S(2)}, u32[]{:S(2)}) collective-permute-start(bf16[4,96,384]{2,1,0:T(8,128)(2,1)} %dynamic-slice_bitcast_fusion.19), channel_id=1, source_target_pairs={{0,1},{1,0},{2,3},{3,2},{4,5},{5,4},{6,7},{7,6},{8,9},{9,8},{10,11... | collective-permute-start | bytes 884744 | tf_op jit(solution)/shard_map/ppermute | solution.py:240
  479.6 13.8 %collective-permute-start.58 = (bf16[4,96,384]{2,1,0:T(8,128)(2,1)}, bf16[4,96,384]{2,1,0:T(8,128)(2,1)S(1)}, u32[]{:S(2)}, u32[]{:S(2)}) collective-permute-start(bf16[4,96,384]{2,1,0:T(8,128)(2,1)} %dynamic-slice_bitcast_fusion.20), channel_id=1, source_target_pairs={{0,4},{4,0},{8,12},{12,8},{16,20},{20,16},{24,28},{28,24},{1,5},{5... | collective-permute-start | bytes 884744 | tf_op jit(solution)/shard_map/ppermute | solution.py:240
  480.7 12.7 %collective-permute-start.57 = (bf16[2,1536,384]{2,1,0:T(8,128)(2,1)}, bf16[2,1536,384]{2,1,0:T(8,128)(2,1)}, u32[]{:S(2)}, u32[]{:S(2)}) collective-permute-start(bf16[2,1536,384]{2,1,0:T(8,128)(2,1)} %pad_maximum_fusion.6), channel_id=1, source_target_pairs={{0,2},{2,0},{1,3},{3,1},{4,6},{6,4},{5,7},{7,5},{8,10},{10,8},{9,1... | collective-permute-start | bytes 7077896 | tf_op jit(solution)/shard_map/ppermute | solution.py:240
  480.8 12.6 %collective-permute-start.61 = (bf16[384,384]{1,0:T(8,128)(2,1)S(1)}, bf16[384,384]{1,0:T(8,128)(2,1)S(1)}, u32[]{:S(2)}, u32[]{:S(2)}) collective-permute-start(bf16[384,384]{1,0:T(8,128)(2,1)S(1)} %fusion.424), channel_id=1, source_target_pairs={{0,1},{1,0},{2,3},{3,2},{4,5},{5,4},{6,7},{7,6},{8,9},{9,8},{10,11... | collective-permute-start | bytes 884744 | tf_op jit(solution)/shard_map/ppermute | solution.py:240
  492.8 255.8 %collective-permute-start.82 = (bf16[1,256,768]{2,1,0:T(8,128)(2,1)}, bf16[1,256,768]{2,1,0:T(8,128)(2,1)}, u32[]{:S(2)}, u32[]{:S(2)}) collective-permute-start(bf16[1,256,768]{2,1,0:T(8,128)(2,1)} %bitcast.1457), channel_id=1, source_target_pairs={{0,1},{1,0},{2,3},{3,2},{4,5},{5,4},{6,7},{7,6},{8,9},{9,8},{10,11... | collective-permute-start | bytes 1179656 | tf_op jit(solution)/shard_map/ppermute | solution.py:240
  498.9 26.5 %collective-permute-start.64 = (bf16[96,768]{1,0:T(8,128)(2,1)}, bf16[96,768]{1,0:T(8,128)(2,1)}, u32[]{:S(2)}, u32[]{:S(2)}) collective-permute-start(bf16[96,768]{1,0:T(8,128)(2,1)} %fusion.435), channel_id=1, source_target_pairs={{0,1},{1,0},{2,3},{3,2},{4,5},{5,4},{6,7},{7,6},{8,9},{9,8},{10,11... | collective-permute-start | bytes 442376 | tf_op jit(solution)/shard_map/ppermute | solution.py:240
  501.1 25.4 %collective-permute-start.63 = (bf16[2,2,96,384]{3,2,1,0:T(8,128)(2,1)}, bf16[2,2,96,384]{3,2,1,0:T(8,128)(2,1)}, u32[]{:S(2)}, u32[]{:S(2)}) collective-permute-start(bf16[2,2,96,384]{3,2,1,0:T(8,128)(2,1)} %fusion.433), channel_id=1, source_target_pairs={{0,8},{4,12},{8,0},{12,4},{16,24},{20,28},{24,16},{28,20},{1,9},{5... | collective-permute-start | bytes 884744 | tf_op jit(solution)/shard_map/ppermute | solution.py:240
  502.8 23.7 %collective-permute-start.65 = (bf16[384,384]{1,0:T(8,128)(2,1)}, bf16[384,384]{1,0:T(8,128)(2,1)}, u32[]{:S(2)}, u32[]{:S(2)}) collective-permute-start(bf16[384,384]{1,0:T(8,128)(2,1)} %add_convert_fusion.16), channel_id=1, source_target_pairs={{0,2},{2,0},{1,3},{3,1},{4,6},{6,4},{5,7},{7,5},{8,10},{10,8},{9,1... | collective-permute-start | bytes 884744 | tf_op jit(solution)/shard_map/ppermute | solution.py:240
  511.8 14.7 %collective-permute-start.62 = (bf16[2,768,768]{2,1,0:T(8,128)(2,1)}, bf16[2,768,768]{2,1,0:T(8,128)(2,1)}, u32[]{:S(2)}, u32[]{:S(2)}) collective-permute-start(bf16[2,768,768]{2,1,0:T(8,128)(2,1)} %pad_maximum_fusion.7), channel_id=1, source_target_pairs={{0,2},{2,0},{1,3},{3,1},{4,6},{6,4},{5,7},{7,5},{8,10},{10,8},{9,1... | collective-permute-start | bytes 7077896 | tf_op jit(solution)/shard_map/ppermute | solution.py:240
  525.4 35.8 %collective-permute-start.69 = (bf16[4,384,384]{2,1,0:T(8,128)(2,1)S(1)}, bf16[4,384,384]{2,1,0:T(8,128)(2,1)S(1)}, u32[]{:S(2)}, u32[]{:S(2)}) collective-permute-start(bf16[4,384,384]{2,1,0:T(8,128)(2,1)S(1)} %dynamic-slice_bitcast_fusion.1), channel_id=1, source_target_pairs={{0,4},{4,0},{8,12},{12,8},{16,20},{20,16},{24,28},{28,24},{1,5},{5... | collective-permute-start | bytes 3538952 | tf_op jit(solution)/shard_map/ppermute | solution.py:240
  542.0 31.6 %collective-permute-start.70 = (bf16[768,768]{1,0:T(8,128)(2,1)S(1)}, bf16[768,768]{1,0:T(8,128)(2,1)S(1)}, u32[]{:S(2)}, u32[]{:S(2)}) collective-permute-start(bf16[768,768]{1,0:T(8,128)(2,1)S(1)} %dynamic-slice_bitcast_fusion), channel_id=1, source_target_pairs={{0,1},{1,0},{2,3},{3,2},{4,5},{5,4},{6,7},{7,6},{8,9},{9,8},{10,11... | collective-permute-start | bytes 3538952 | tf_op jit(solution)/shard_map/ppermute | solution.py:240
  542.7 30.9 %collective-permute-start.71 = (bf16[2,96,384]{2,1,0:T(8,128)(2,1)S(1)}, bf16[2,96,384]{2,1,0:T(8,128)(2,1)S(1)}, u32[]{:S(2)}, u32[]{:S(2)}) collective-permute-start(bf16[2,96,384]{2,1,0:T(8,128)(2,1)S(1)} %fusion.436), channel_id=1, source_target_pairs={{0,1},{1,0},{2,3},{3,2},{4,5},{5,4},{6,7},{7,6},{8,9},{9,8},{10,11... | collective-permute-start | bytes 442376 | tf_op jit(solution)/shard_map/ppermute | solution.py:240
  574.1 13.7 %collective-permute-start.73 = (bf16[2,2,96,384]{3,2,1,0:T(8,128)(2,1)S(1)}, bf16[2,2,96,384]{3,2,1,0:T(8,128)(2,1)S(1)}, u32[]{:S(2)}, u32[]{:S(2)}) collective-permute-start(bf16[2,2,96,384]{3,2,1,0:T(8,128)(2,1)S(1)} %copy.209), channel_id=1, source_target_pairs={{0,2},{2,0},{1,3},{3,1},{4,6},{6,4},{5,7},{7,5},{8,10},{10,8},{9,1... | collective-permute-start | bytes 884744 | tf_op jit(solution)/shard_map/ppermute | solution.py:240
  575.5 150.0 %collective-permute-start.77 = (bf16[2,384,384]{2,1,0:T(8,128)(2,1)}, bf16[2,384,384]{2,1,0:T(8,128)(2,1)}, u32[]{:S(2)}, u32[]{:S(2)}) collective-permute-start(bf16[2,384,384]{2,1,0:T(8,128)(2,1)} %dynamic-slice_bitcast_fusion.6), channel_id=1, source_target_pairs={{0,8},{4,12},{8,0},{12,4},{16,24},{20,28},{24,16},{28,20},{1,9},{5... | collective-permute-start | bytes 1769480 | tf_op jit(solution)/shard_map/ppermute | solution.py:240
  578.5 147.0 %collective-permute-start.76 = (bf16[4,96,768]{2,1,0:T(8,128)(2,1)}, bf16[4,96,768]{2,1,0:T(8,128)(2,1)}, u32[]{:S(2)}, u32[]{:S(2)}) collective-permute-start(bf16[4,96,768]{2,1,0:T(8,128)(2,1)} %dynamic-slice_bitcast_fusion.7), channel_id=1, source_target_pairs={{0,4},{4,0},{8,12},{12,8},{16,20},{20,16},{24,28},{28,24},{1,5},{5... | collective-permute-start | bytes 1769480 | tf_op jit(solution)/shard_map/ppermute | solution.py:240
  596.8 128.8 %collective-permute-start.74 = (bf16[2,768,384]{2,1,0:T(8,128)(2,1)}, bf16[2,768,384]{2,1,0:T(8,128)(2,1)}, u32[]{:S(2)}, u32[]{:S(2)}) collective-permute-start(bf16[2,768,384]{2,1,0:T(8,128)(2,1)} %pad_maximum_fusion.26), channel_id=1, source_target_pairs={{0,2},{2,0},{1,3},{3,1},{4,6},{6,4},{5,7},{7,5},{8,10},{10,8},{9,1... | collective-permute-start | bytes 3538952 | tf_op jit(solution)/shard_map/ppermute | solution.py:240
  597.5 128.0 %collective-permute-start.75 = (bf16[2,768,384]{2,1,0:T(8,128)(2,1)}, bf16[2,768,384]{2,1,0:T(8,128)(2,1)}, u32[]{:S(2)}, u32[]{:S(2)}) collective-permute-start(bf16[2,768,384]{2,1,0:T(8,128)(2,1)} %pad_maximum_fusion.27), channel_id=1, source_target_pairs={{0,2},{2,0},{1,3},{3,1},{4,6},{6,4},{5,7},{7,5},{8,10},{10,8},{9,1... | collective-permute-start | bytes 3538952 | tf_op jit(solution)/shard_map/ppermute | solution.py:240
  733.9 21.6 %collective-permute-start.78 = (bf16[8,96,384]{2,1,0:T(8,128)(2,1)}, bf16[8,96,384]{2,1,0:T(8,128)(2,1)}, u32[]{:S(2)}, u32[]{:S(2)}) collective-permute-start(bf16[8,96,384]{2,1,0:T(8,128)(2,1)} %dynamic-slice_bitcast_fusion.5), channel_id=1, source_target_pairs={{0,1},{1,0},{2,3},{3,2},{4,5},{5,4},{6,7},{7,6},{8,9},{9,8},{10,11... | collective-permute-start | bytes 1769480 | tf_op jit(solution)/shard_map/ppermute | solution.py:240
  735.3 20.1 %collective-permute-start.79 = (bf16[2,4,96,384]{3,2,1,0:T(8,128)(2,1)}, bf16[2,4,96,384]{3,2,1,0:T(8,128)(2,1)}, u32[]{:S(2)}, u32[]{:S(2)}) collective-permute-start(bf16[2,4,96,384]{3,2,1,0:T(8,128)(2,1)} %dynamic-slice_bitcast_fusion.4), channel_id=1, source_target_pairs={{0,4},{4,0},{8,12},{12,8},{16,20},{20,16},{24,28},{28,24},{1,5},{5... | collective-permute-start | bytes 1769480 | tf_op jit(solution)/shard_map/ppermute | solution.py:240
  737.8 14.9 %collective-permute-start.80 = (bf16[2,96,768]{2,1,0:T(8,128)(2,1)}, bf16[2,96,768]{2,1,0:T(8,128)(2,1)}, u32[]{:S(2)}, u32[]{:S(2)}) collective-permute-start(bf16[2,96,768]{2,1,0:T(8,128)(2,1)} %dynamic-slice_bitcast_fusion.18), channel_id=1, source_target_pairs={{0,8},{4,12},{8,0},{12,4},{16,24},{20,28},{24,16},{28,20},{1,9},{5... | collective-permute-start | bytes 884744 | tf_op jit(solution)/shard_map/ppermute | solution.py:240
  741.7 13.7 %collective-permute-start.81 = (bf16[1,384,384]{2,1,0:T(8,128)(2,1)}, bf16[1,384,384]{2,1,0:T(8,128)(2,1)}, u32[]{:S(2)}, u32[]{:S(2)}) collective-permute-start(bf16[1,384,384]{2,1,0:T(8,128)(2,1)} %constant_dynamic-slice_fusion.14), channel_id=1, source_target_pairs={{0,16},{4,20},{8,24},{12,28},{16,0},{20,4},{24,8},{28,12},{1,17},{... | collective-permute-start | bytes 884744 | tf_op jit(solution)/shard_map/ppermute | solution.py:240
  762.7 13.7 %collective-permute-start.86 = (bf16[384,384]{1,0:T(8,128)(2,1)S(1)}, bf16[384,384]{1,0:T(8,128)(2,1)S(1)}, u32[]{:S(2)}, u32[]{:S(2)}) collective-permute-start(bf16[384,384]{1,0:T(8,128)(2,1)S(1)} %fusion.425), channel_id=1, source_target_pairs={{0,1},{1,0},{2,3},{3,2},{4,5},{5,4},{6,7},{7,6},{8,9},{9,8},{10,11... | collective-permute-start | bytes 884744 | tf_op jit(solution)/shard_map/ppermute | solution.py:240
  764.2 18.0 %collective-permute-start.87 = (bf16[1,256,768]{2,1,0:T(8,128)(2,1)S(1)}, bf16[1,256,768]{2,1,0:T(8,128)(2,1)S(1)}, u32[]{:S(2)}, u32[]{:S(2)}) collective-permute-start(bf16[1,256,768]{2,1,0:T(8,128)(2,1)S(1)} %bitcast.1640), channel_id=1, source_target_pairs={{0,1},{1,0},{2,3},{3,2},{4,5},{5,4},{6,7},{7,6},{8,9},{9,8},{10,11... | collective-permute-start | bytes 1179656 | tf_op jit(solution)/shard_map/ppermute | solution.py:240
  (266 other events, 1742.3 us)
Sparse Core Ops, SparseCore 0:
  608.0 116.1 all-reduce.1

commit v3 on v2

--- a/solution.py
+++ b/solution.py
@@ -214,9 +214,26 @@
     return centred * lax.rsqrt(variance + EPSILON) * gain + shift
 
 
-def norm_backward(residual, gain, shift, slope):
-    unused, pullback = jax.vjp(normalize, residual, gain, shift)
-    return pullback(slope)
+def norm_backward(residual, gain, slope):
+    average = jnp.mean(residual, axis=-1, keepdims=True)
+    centred = residual - average
+    scale = lax.rsqrt(jnp.mean(centred * centred, axis=-1, keepdims=True) + EPSILON)
+    unit = centred * scale
+    raised = slope * gain
+    along = jnp.mean(raised * unit, axis=-1, keepdims=True)
+    level = jnp.mean(raised, axis=-1, keepdims=True)
+    return scale * (raised - level - unit * along), token_sum(slope * unit), token_sum(slope)
+
+
+def sum_small(held):
+    arrived = yield [(held, "blk", 1)]
+    held = held + arrived[0]
+    arrived = yield [(held, "uly", 1)]
+    held = held + arrived[0]
+    for mask in masks_of("dp"):
+        arrived = yield [(held, "dp", mask)]
+        held = held + arrived[0]
+    return held
 
 
 def gelu(hidden):
@@ -488,24 +505,20 @@
 
 
 def token_sum(item):
-    return jnp.sum(item.astype(FULL), axis=(0, 1))
+    return jnp.sum(item.astype(FULL), axis=(0, 1))[None]
 
 
 def halves_of(item):
     half = item.shape[-1] // 2
-    core = lax.axis_index("blk")
-    axis = item.ndim - 1
-    return (
-        lax.dynamic_slice_in_dim(item, core * half, half, axis),
-        lax.dynamic_slice_in_dim(item, (1 - core) * half, half, axis),
-    )
+    low, high = item[..., :half], item[..., half:]
+    bit = bit_of("blk")
+    return jnp.where(bit, high, low), jnp.where(bit, low, high)
 
 
 def layer_forward(residual, small, flows, coming, core):
     attention, up_flow, down_flow = flows
-    first_gain, first_shift, query_bias, value_bias, out_bias = small[:5]
-    second_gain, second_shift, down_bias = small[5:8]
-    up_bias = small[8:].reshape(-1)
+    first_gain, first_shift, query_bias, value_bias, out_bias = (small[i : i + 1] for i in range(5))
+    second_gain, second_shift, down_bias = (small[i : i + 1] for i in range(5, 8))
     bit = bit_of("blk")
     next_attention, next_up, next_down = coming if coming else (None, None, None)
 
@@ -514,7 +527,7 @@
 
     own, other = attention.result
     normed = normalize(residual, first_gain, first_shift).astype(LOW)
-    normed = cut(normed, up_flow, down_flow)
+    normed = cut(normed, up_flow, down_flow, *with_next(next_attention))
     query_biases, value_biases = halves_of(query_bias), halves_of(value_bias)
 
     def project(weights, i):
@@ -529,30 +542,34 @@
 
     away = swap(project(other, 1), "blk")
     mine = project(own, 0)
-    mine, away = cut((mine, away), up_flow, down_flow, *with_next(next_attention))
+    mine, away = cut((mine, away), *([next_attention] if coming else [down_flow]))
     mixed_mine, mixed_theirs, logsum = attend(core, mine, away)
-    mixed_mine, mixed_theirs = cut((mixed_mine, mixed_theirs), *with_next(next_attention))
+    mixed_mine, mixed_theirs = cut(
+        (mixed_mine, mixed_theirs),
+        up_flow,
+        *([down_flow, next_attention, next_up] if coming else []),
+    )
     arrived = swap(mixed_theirs, "blk")
     mixed = side_by_side(mixed_mine, arrived, bit)
     columns = side_by_side(matmul(mixed, own[1][1]), matmul(mixed, other[1][1]), bit)
     middle = residual + columns + out_bias
     normed_two = normalize(middle, second_gain, second_shift).astype(LOW)
     middle, normed_two = cut(
-        (middle, normed_two), up_flow, down_flow, *with_next(next_attention)
+        (middle, normed_two), up_flow, down_flow, *with_next(next_attention, next_up)
     )
     middle, normed_two = drain((middle, normed_two), up_flow)
-    up_biases = halves_of(up_bias)
-    width = up_flow.result[0].shape[2]
+    low_biases, high_biases = small[8:10], small[10:12]
+    up_biases = jnp.where(bit, high_biases, low_biases), jnp.where(bit, low_biases, high_biases)
     hidden = []
     active = []
     for weights, bias in zip(up_flow.result, up_biases):
         parts = [
-            matmul(normed_two, weights[i]) + bias[i * width : (i + 1) * width] for i in range(2)
+            matmul(normed_two, weights[i]) + bias[i : i + 1] for i in range(2)
         ]
         hidden.append(parts)
         active.append(jnp.concatenate([gelu(item).astype(LOW) for item in parts], axis=-1))
     active, middle = cut(
-        (active, middle), down_flow, *with_next(next_attention, next_up)
+        (active, middle), down_flow, *with_next(next_attention, next_up, next_down)
     )
     active, middle = drain((active, middle), down_flow)
     down_own, down_other = down_flow.result
@@ -560,7 +577,6 @@
     right = matmul(active[0], down_other[1]) + matmul(active[1], down_other[0])
     result = middle + side_by_side(left, right, bit) + down_bias
     if coming:
-        result = cut(result, next_attention, next_up, next_down)
         result = cut(result, next_attention)
     record = (residual, normed, mine, away, logsum, mixed_mine, mixed_theirs, mixed)
     return result, record + (middle, normed_two, hidden, active)
@@ -568,8 +584,7 @@
 
 def layer_backward(upstream, small, weights, record, core, before):
     (own, other), (up_own, up_other), (down_own, down_other) = weights
-    first_gain, first_shift = small[:2]
-    second_gain, second_shift = small[5:7]
+    first_gain, second_gain = small[0:1], small[5:6]
     residual, normed, mine, away, logsum, mixed_mine, mixed_theirs, mixed = record[:8]
     middle, normed_two, hidden, active = record[8:]
     bit = bit_of("blk")
@@ -596,9 +611,8 @@
             bias_slopes.append(token_sum(hidden_slope))
             low_hidden.append(hidden_slope.astype(LOW))
     low_hidden = cut(low_hidden, down_flow, *before)
-    up_bias_slope = side_by_side(
-        jnp.concatenate(bias_slopes[:2]), jnp.concatenate(bias_slopes[2:]), bit
-    )
+    low_biases = [jnp.where(bit, bias_slopes[2 + i], bias_slopes[i]) for i in range(2)]
+    high_biases = [jnp.where(bit, bias_slopes[i], bias_slopes[2 + i]) for i in range(2)]
     up_slopes = [
         jnp.stack([contract(normed_two, low_hidden[2 + i]) for i in range(2)]),
         jnp.stack([contract(normed_two, low_hidden[i]) for i in range(2)]),
@@ -611,9 +625,7 @@
         + transposed(low_hidden[2], up_other[0])
         + transposed(low_hidden[3], up_other[1])
     )
-    through, second_gain_slope, second_shift_slope = norm_backward(
-        middle, second_gain, second_shift, norm_slope
-    )
+    through, second_gain_slope, second_shift_slope = norm_backward(middle, second_gain, norm_slope)
     middle_slope = upstream + through
     middle_slope = cut(middle_slope, up_flow, *before)
 
@@ -650,9 +662,7 @@
             + transposed(grads[1], pair[1])
             + transposed(grads[2], last[0])
         )
-    through, first_gain_slope, first_shift_slope = norm_backward(
-        residual, first_gain, first_shift, first_slope
-    )
+    through, first_gain_slope, first_shift_slope = norm_backward(residual, first_gain, first_slope)
     upstream = middle_slope + through
     upstream = cut(upstream, attention_flow, up_flow, down_flow, *before)
     vectors = [
@@ -665,7 +675,7 @@
         second_shift_slope,
         down_bias_slope,
     ]
-    terms = jnp.concatenate([jnp.stack(vectors), up_bias_slope.reshape(-1, middle.shape[-1])])
+    terms = jnp.concatenate(vectors + low_biases + high_biases)
     return upstream, terms, (attention_flow, up_flow, down_flow)
 
 
@@ -729,7 +739,7 @@
     straight = gathered.transpose(1, 2, 0, 3).reshape(layers, kinds, width)
     biases = gathered[:, :, 8:].transpose(1, 0, 2, 3).reshape(layers, kinds - 8, width)
     small = jnp.concatenate([straight[:, :8], biases], axis=1)
-    residual = cut(residual, attention)
+    residual = cut(residual, attention, up_flow, down_flow)
     leaving = Flow(to_sequences(cotangent))
     records = []
     for layer in range(layers):
@@ -755,9 +765,10 @@
         before = after
         found[layer] = after
     gradient = Flow(from_sequences(upstream))
-    drain((), *before, gradient, outgoing)
-
-    sums = lax.psum(jnp.stack(terms), ("dp", "blk", "uly"))
+    totals = Flow(sum_small(jnp.concatenate(terms)))
+    drain((), *before, gradient, totals, outgoing)
+
+    sums = totals.result.reshape(layers, kinds, width)
     place = lax.axis_index("dp")
     sliced = lax.dynamic_slice_in_dim(sums, place * rows, rows, 2)
     long = kinds - 8

time: 828 us -> 594 us (0.72)
  waiting for transfers between devices: 276 us -> 167 us
  local copies, waits for them, and re-layouts: 122 us -> 68.3 us
  other arithmetic: 133 us -> 99.7 us
  matrix products: 122 us -> 102 us
  between operations: 19.2 us -> 5.86 us
    psum x1 -> x0, waiting for transfers between devices: 111 us -> none  [shards(): sums = lax.psum(jnp.stack(terms), ('dp', 'blk', 'uly'))]
    convert_element_type x30, other arithmetic: 29.9 us -> 12.3 us  [added(): return (left.astype(FULL) + right.astype(FULL)).astype(LOW)]
    unnamed x479 -> x379, local copies, waits for them, and re-layouts: 41.1 us -> 25.9 us
    another operation x20 -> x0, local copies, waits for them, and re-layouts: 12.5 us -> none  [the longest x16 8.43 us: layer_backward(): jnp.stack(vectors)]
    dynamic_slice x14 -> x0, local copies, waits for them, and re-layouts: 12.1 us -> none  [the longest x6 9.75 us: chosen(): lax.dynamic_index_in_dim(item, bit.astype(jnp.int32), axis, keepdims=False)]
    squeeze x25, local copies, waits for them, and re-layouts: 14.5 us -> 3.91 us  [chosen(): lax.dynamic_index_in_dim(item, bit.astype(jnp.int32), axis, keepdims=False)]
    dot_general x32, matrix products: 45.4 us -> 35.5 us  [matmul(): return jnp.dot(left, right, preferred_element_type=FULL)]
    ppermute x95 -> x100, starting transfers between devices: 87.5 us -> 85.5 us  [swap(): return lax.ppermute(item, axis, [(i, i ^ mask) for i in range(count)])]
  transfers between devices with their start and end apart: 96 -> 100, of which waited for: 35 -> 39; matrix products, arithmetic and copies ran while one was open for 33% -> 33% of each run, Pallas kernels for 5% -> 9%
where the time goes in v3:
time: 594 us; the launch traced here: 584 us
  waiting for transfers between devices  167 us (28%)
  matrix products  102 us (17%)
  other arithmetic  99.7 us (17%)
  starting transfers between devices  85.5 us (14%)
  local copies, waits for them, and re-layouts  68.3 us (11%)
  Pallas kernels  55.3 us (9%)
    ppermute x100, waiting for transfers between devices, swap(): return lax.ppermute(item, axis, [(i, i ^ mask) for i in range(count)])  167 us
    ppermute x100, starting transfers between devices, swap(): return lax.ppermute(item, axis, [(i, i ^ mask) for i in range(count)])  85.5 us
    dot_general x32, matrix products, transposed(): return jnp.einsum('ste,de->std', left, right, preferred_element_type=FULL)  38.3 us
    dot_general x32, matrix products, matmul(): return jnp.dot(left, right, preferred_element_type=FULL)  35.5 us
    pallas_call x2, Pallas kernels, attend_back(): pl.pallas_call(attend_back_kernel, grid_spec=pltpu.PrefetchScalarGridSpec...  32 us
    dot_general x32, matrix products, contract(): jnp.einsum('std,ste->de', left, right, preferred_element_type=FULL)  28.1 us
    unnamed x379, local copies, waits for them, and re-layouts  25.9 us
    another operation x69, other arithmetic, ordered(): return jnp.stack([low, high], axis=axis)  25.5 us
  transfers between devices with their start and end apart: 100, of which 39 were waited for; matrix products, arithmetic and copies ran while one was open for 33% of the time, Pallas kernels for 9%

profile of v3, /device:TPU:0, one launch (start us, length us, event | category | flops | bytes accessed | tf_op | source)
XLA Modules:
  0.0 583.5 jit_solution(13372627032175685259)
XLA Ops:
  3.8 1.7 slice_bitcast_fusion.22
  8.1 4.0 collective-permute-start.2
  12.1 1.8 collective-permute-start.1
  18.6 3.2 collective-permute-done
  23.1 1.7 collective-permute-start.4
  27.7 5.2 collective-permute-done.3
  36.2 2.7 collective-permute-start.8
  40.1 2.6 collective-permute-done.7
  43.9 1.8 select_bitcast_fusion.68
  51.4 3.0 collective-permute-start.12
  56.9 4.3 collective-permute-done.11
  68.2 1.8 fusion.459
  72.2 1.7 collective-permute-start.15
  76.7 10.0 %collective-permute-done.16 = bf16[2,384,384]{2,1,0:T(8,128)(2,1)} collective-permute-done((bf16[2,384,384]{2,1,0:T(8,128)(2,1)}, bf16[2,384,384]{2,1,0:T(8,128)(2,1)}, u32[]{:S(2)}, u32[]{:S(2)}) %collective-permute-start.16) | collective-permute-done | bytes 589856 | tf_op jit(solution)/shard_map/ppermute | solution.py:257
  87.7 2.7 collective-permute-start.18
  98.5 1.8 collective-permute-start.20
  105.6 11.7 %attend.2 = (bf16[1,512,384]{2,1,0:T(8,128)(2,1)S(1)}, bf16[1,512,384]{2,1,0:T(8,128)(2,1)S(1)}, f32[1,3,8,1024]{3,2,1,0:T(8,128)S(1)}) custom-call(s32[1]{0:T(128)} %bitcast.62.core_ref, bf16[3,1,512,384]{3,2,1,0:T(8,128)(2,1)S(1)} %pad_maximum_fusion.15.mine_ref, bf16[3,1,512,384]{3,2,1,0:T(8,128)(2,1)S(1)} %collective-permute-done.17.theirs_ref), custom_call_target="tpu_custom_call" | custom-call | tf_op jit(solution)/shard_map/attend/pallas_call | solution.py:100
  117.4 9.6 %collective-permute-done.20 = bf16[4,384,384]{2,1,0:T(8,128)(2,1)S(1)} collective-permute-done((bf16[4,384,384]{2,1,0:T(8,128)(2,1)S(1)}, bf16[4,384,384]{2,1,0:T(8,128)(2,1)S(1)}, u32[]{:S(2)}, u32[]{:S(2)}) %collective-permute-start.20) | collective-permute-done | bytes 1179680 | tf_op jit(solution)/shard_map/ppermute | solution.py:257
  140.9 2.6 collective-permute-done.26
  145.9 1.8 collective-permute-start.30
  147.7 1.7 collective-permute-start.29
  158.8 3.3 collective-permute-done.29
  180.1 2.3 collective-permute-done.34
  194.6 1.8 collective-permute-start.36
  198.8 10.6 %collective-permute-done.36 = bf16[2,384,384]{2,1,0:T(8,128)(2,1)S(1)} collective-permute-done((bf16[2,384,384]{2,1,0:T(8,128)(2,1)S(1)}, bf16[2,384,384]{2,1,0:T(8,128)(2,1)S(1)}, u32[]{:S(2)}, u32[]{:S(2)}) %collective-permute-start.36) | collective-permute-done | bytes 589856 | tf_op jit(solution)/shard_map/ppermute | solution.py:257
  209.4 11.6 %attend.3 = (bf16[1,512,384]{2,1,0:T(8,128)(2,1)S(1)}, bf16[1,512,384]{2,1,0:T(8,128)(2,1)S(1)}, f32[1,3,8,1024]{3,2,1,0:T(8,128)S(1)}) custom-call(s32[1]{0:T(128)} %bitcast.62.core_ref, bf16[3,1,512,384]{3,2,1,0:T(8,128)(2,1)S(1)} %pad_maximum_fusion.20.mine_ref, bf16[3,1,512,384]{3,2,1,0:T(8,128)(2,1)S(1)} %collective-permute-done.35.theirs_ref), custom_call_target="tpu_custom_call" | custom-call | tf_op jit(solution)/shard_map/attend/pallas_call | solution.py:100
  224.7 1.8 select_bitcast_fusion.7
  227.9 22.6 %collective-permute-done.40 = bf16[4,384,384]{2,1,0:T(8,128)(2,1)S(1)} collective-permute-done((bf16[4,384,384]{2,1,0:T(8,128)(2,1)S(1)}, bf16[4,384,384]{2,1,0:T(8,128)(2,1)S(1)}, u32[]{:S(2)}, u32[]{:S(2)}) %collective-permute-start.40) | collective-permute-done | bytes 1179680 | tf_op jit(solution)/shard_map/ppermute | solution.py:257
  266.5 2.9 fusion.112
  272.2 2.4 select_bitcast_fusion.5
  281.2 2.5 fusion.1
  283.7 2.3 fusion.487
  287.6 2.5 fusion
  290.1 2.5 fusion.485
  314.3 1.7 fusion.152
  318.7 16.0 %attend_back.2 = (bf16[3,1,512,384]{3,2,1,0:T(8,128)(2,1)S(1)}, bf16[3,1,512,384]{3,2,1,0:T(8,128)(2,1)S(1)}) custom-call(s32[1]{0:T(128)} %bitcast.62.core_ref, bf16[3,1,512,384]{3,2,1,0:T(8,128)(2,1)S(1)} %pad_maximum_fusion.20.mine_ref, bf16[3,1,512,384]{3,2,1,0:T(8,128)(2,1)S(1)} %collective-permute-done.35.theirs_ref, ...), custom_call_target="tpu_custom_call" | custom-call | tf_op jit(solution)/shard_map/attend_back/pallas_call | solution.py:190
  334.7 6.4 %collective-permute-done.47 = bf16[768,768]{1,0:T(8,128)(2,1)S(1)} collective-permute-done((bf16[768,768]{1,0:T(8,128)(2,1)S(1)}, bf16[768,768]{1,0:T(8,128)(2,1)S(1)}, u32[]{:S(2)}, u32[]{:S(2)}) %collective-permute-start.47) | collective-permute-done | bytes 1179680 | tf_op jit(solution)/shard_map/ppermute | solution.py:257
  341.5 1.8 collective-permute-start.52
  352.0 1.7 fusion.323
  353.6 1.8 fusion.326
  356.1 2.4 fusion.77
  373.8 8.1 %collective-permute-done.56 = bf16[1,384,384]{2,1,0:T(8,128)(2,1)S(1)} collective-permute-done((bf16[1,384,384]{2,1,0:T(8,128)(2,1)S(1)}, bf16[1,384,384]{2,1,0:T(8,128)(2,1)S(1)}, u32[]{:S(2)}, u32[]{:S(2)}) %collective-permute-start.56) | collective-permute-done | bytes 294944 | tf_op jit(solution)/shard_map/ppermute | solution.py:257
  394.6 2.3 fusion.495
  396.9 2.7 fusion.493
  404.5 1.8 collective-permute-start.63
  429.1 4.4 collective-permute-done.67
  436.8 16.0 %attend_back.3 = (bf16[3,1,512,384]{3,2,1,0:T(8,128)(2,1)S(1)}, bf16[3,1,512,384]{3,2,1,0:T(8,128)(2,1)S(1)}) custom-call(s32[1]{0:T(128)} %bitcast.62.core_ref, bf16[3,1,512,384]{3,2,1,0:T(8,128)(2,1)S(1)} %copy-done.1, bf16[3,1,512,384]{3,2,1,0:T(8,128)(2,1)S(1)} %copy-done.3, f32[1,3,8,1024]{3,2,1,0:T(8,128)S(1)} %get-tuple-element.239.logsum_ref, ...), custom_call_target="tpu_custom_call" | custom-call | tf_op jit(solution)/shard_map/attend_back/pallas_call | solution.py:190
  452.8 11.7 %collective-permute-done.71 = bf16[2,96,384]{2,1,0:T(8,128)(2,1)S(1)} collective-permute-done((bf16[2,96,384]{2,1,0:T(8,128)(2,1)S(1)}, bf16[2,96,384]{2,1,0:T(8,128)(2,1)S(1)}, u32[]{:S(2)}, u32[]{:S(2)}) %collective-permute-start.71) | collective-permute-done | bytes 147488 | tf_op jit(solution)/shard_map/ppermute | solution.py:257
  482.4 1.8 fusion.337
  485.5 2.4 fusion.79
  491.8 2.3 concatenate.100
  498.5 2.0 fusion.82
  501.9 1.7 add_convert_fusion.4
  503.7 1.7 add_convert_fusion.5
  509.2 2.1 collective-permute-start.80
  511.4 11.6 %collective-permute-done.80 = bf16[2,96,768]{2,1,0:T(8,128)(2,1)S(1)} collective-permute-done((bf16[2,96,768]{2,1,0:T(8,128)(2,1)S(1)}, bf16[2,96,768]{2,1,0:T(8,128)(2,1)S(1)}, u32[]{:S(2)}, u32[]{:S(2)}) %collective-permute-start.80) | collective-permute-done | bytes 294944 | tf_op jit(solution)/shard_map/ppermute | solution.py:257
  523.0 3.7 collective-permute-done.81
  536.1 7.0 %collective-permute-done.85 = bf16[1,96,768]{2,1,0:T(8,128)(2,1)S(1)} collective-permute-done((bf16[1,96,768]{2,1,0:T(8,128)(2,1)S(1)}, bf16[1,96,768]{2,1,0:T(8,128)(2,1)S(1)}, u32[]{:S(2)}, u32[]{:S(2)}) %collective-permute-start.85) | collective-permute-done | bytes 147488 | tf_op jit(solution)/shard_map/ppermute | solution.py:257
  544.5 6.4 %collective-permute-done.87 = bf16[1,256,768]{2,1,0:T(8,128)(2,1)S(1)} collective-permute-done((bf16[1,256,768]{2,1,0:T(8,128)(2,1)S(1)}, bf16[1,256,768]{2,1,0:T(8,128)(2,1)S(1)}, u32[]{:S(2)}, u32[]{:S(2)}) %collective-permute-start.87) | collective-permute-done | bytes 393248 | tf_op jit(solution)/shard_map/ppermute | solution.py:257
  551.7 1.8 collective-permute-start.90
  557.4 4.2 collective-permute-done.89
  566.0 2.9 collective-permute-done.93
  569.6 4.6 collective-permute-done.97
  574.2 2.3 collective-permute-start.99
  (989 shorter events, 294.0 us)
Async XLA Ops:
  8.1 10.5 %collective-permute-start.2 = (bf16[1,24,96]{2,1,0:T(8,128)(2,1)S(1)}, bf16[1,24,96]{2,1,0:T(8,128)(2,1)S(1)}, u32[]{:S(2)}, u32[]{:S(2)}) collective-permute-start(bf16[1,24,96]{2,1,0:T(8,128)(2,1)S(1)} %broadcast_in_dim_reshape.3), channel_id=1, source_target_pairs={{0,16},{4,20},{8,24},{12,28},{16,0},{20,4},{24,8},{28,12},{1,17},{... | collective-permute-start | bytes 13832 | tf_op jit(solution)/shard_map/ppermute | solution.py:257
  12.1 10.9 %collective-permute-start.1 = (bf16[1,256,768]{2,1,0:T(8,128)(2,1)}, bf16[1,256,768]{2,1,0:T(8,128)(2,1)}, u32[]{:S(2)}, u32[]{:S(2)}) collective-permute-start(bf16[1,256,768]{2,1,0:T(8,128)(2,1)} %get-tuple-element.212), channel_id=1, source_target_pairs={{0,1},{1,0},{2,3},{3,2},{4,5},{5,4},{6,7},{7,6},{8,9},{9,8},{10,11... | collective-permute-start | bytes 1179656 | tf_op jit(solution)/shard_map/ppermute | solution.py:257
  33.1 10.8 %collective-permute-start.5 = (bf16[4,96,384]{2,1,0:T(8,128)(2,1)S(1)}, bf16[4,96,384]{2,1,0:T(8,128)(2,1)}, u32[]{:S(2)}, u32[]{:S(2)}) collective-permute-start(bf16[4,96,384]{2,1,0:T(8,128)(2,1)S(1)} %bitcast.1600), channel_id=1, source_target_pairs={{0,4},{4,0},{8,12},{12,8},{16,20},{20,16},{24,28},{28,24},{1,5},{5... | collective-permute-start | bytes 884744 | tf_op jit(solution)/shard_map/ppermute | solution.py:257
  50.0 12.9 %collective-permute-start.10 = (bf16[2,4,96,384]{3,2,1,0:T(8,128)(2,1)}, bf16[2,4,96,384]{3,2,1,0:T(8,128)(2,1)}, u32[]{:S(2)}, u32[]{:S(2)}) collective-permute-start(bf16[2,4,96,384]{3,2,1,0:T(8,128)(2,1)} %pad_maximum_fusion.31), channel_id=1, source_target_pairs={{0,4},{4,0},{8,12},{12,8},{16,20},{20,16},{24,28},{28,24},{1,5},{5... | collective-permute-start | bytes 1769480 | tf_op jit(solution)/shard_map/ppermute | solution.py:257
  50.5 12.4 %collective-permute-start.9 = (bf16[8,96,384]{2,1,0:T(8,128)(2,1)S(1)}, bf16[8,96,384]{2,1,0:T(8,128)(2,1)}, u32[]{:S(2)}, u32[]{:S(2)}) collective-permute-start(bf16[8,96,384]{2,1,0:T(8,128)(2,1)S(1)} %bitcast.1577), channel_id=1, source_target_pairs={{0,1},{1,0},{2,3},{3,2},{4,5},{5,4},{6,7},{7,6},{8,9},{9,8},{10,11... | collective-permute-start | bytes 1769480 | tf_op jit(solution)/shard_map/ppermute | solution.py:257
  51.3 10.0 %collective-permute-start.11 = (bf16[2,96,768]{2,1,0:T(8,128)(2,1)S(1)}, bf16[2,96,768]{2,1,0:T(8,128)(2,1)S(1)}, u32[]{:S(2)}, u32[]{:S(2)}) collective-permute-start(bf16[2,96,768]{2,1,0:T(8,128)(2,1)S(1)} %maximum_bitcast_fusion.11), channel_id=1, source_target_pairs={{0,8},{4,12},{8,0},{12,4},{16,24},{20,28},{24,16},{28,20},{1,9},{5... | collective-permute-start | bytes 884744 | tf_op jit(solution)/shard_map/ppermute | solution.py:257
  51.4 11.5 %collective-permute-start.12 = (bf16[1,384,384]{2,1,0:T(8,128)(2,1)}, bf16[1,384,384]{2,1,0:T(8,128)(2,1)S(1)}, u32[]{:S(2)}, u32[]{:S(2)}) collective-permute-start(bf16[1,384,384]{2,1,0:T(8,128)(2,1)} %constant_dynamic-slice_fusion.17), channel_id=1, source_target_pairs={{0,16},{4,20},{8,24},{12,28},{16,0},{20,4},{24,8},{28,12},{1,17},{... | collective-permute-start | bytes 884744 | tf_op jit(solution)/shard_map/ppermute | solution.py:257
  71.1 15.6 %collective-permute-start.16 = (bf16[2,384,384]{2,1,0:T(8,128)(2,1)}, bf16[2,384,384]{2,1,0:T(8,128)(2,1)}, u32[]{:S(2)}, u32[]{:S(2)}) collective-permute-start(bf16[2,384,384]{2,1,0:T(8,128)(2,1)} %maximum_bitcast_fusion.4), channel_id=1, source_target_pairs={{0,8},{4,12},{8,0},{12,4},{16,24},{20,28},{24,16},{28,20},{1,9},{5... | collective-permute-start | bytes 1769480 | tf_op jit(solution)/shard_map/ppermute | solution.py:257
  72.2 15.4 %collective-permute-start.15 = (bf16[4,96,768]{2,1,0:T(8,128)(2,1)}, bf16[4,96,768]{2,1,0:T(8,128)(2,1)}, u32[]{:S(2)}, u32[]{:S(2)}) collective-permute-start(bf16[4,96,768]{2,1,0:T(8,128)(2,1)} %bitcast.52), channel_id=1, source_target_pairs={{0,4},{4,0},{8,12},{12,8},{16,20},{20,16},{24,28},{28,24},{1,5},{5... | collective-permute-start | bytes 1769480 | tf_op jit(solution)/shard_map/ppermute | solution.py:257
  87.7 15.9 %collective-permute-start.18 = (bf16[2,1,96,384]{3,2,0,1:T(8,128)(2,1)S(1)}, bf16[2,1,96,384]{3,2,0,1:T(8,128)(2,1)S(1)}, u32[]{:S(2)}, u32[]{:S(2)}) collective-permute-start(bf16[2,1,96,384]{3,2,0,1:T(8,128)(2,1)S(1)} %copy-done.138), channel_id=1, source_target_pairs={{0,16},{4,20},{8,24},{12,28},{16,0},{20,4},{24,8},{28,12},{1,17},{... | collective-permute-start | bytes 442376 | tf_op jit(solution)/shard_map/ppermute | solution.py:257
  98.5 28.4 %collective-permute-start.20 = (bf16[4,384,384]{2,1,0:T(8,128)(2,1)S(1)}, bf16[4,384,384]{2,1,0:T(8,128)(2,1)S(1)}, u32[]{:S(2)}, u32[]{:S(2)}) collective-permute-start(bf16[4,384,384]{2,1,0:T(8,128)(2,1)S(1)} %bitcast.1539), channel_id=1, source_target_pairs={{0,4},{4,0},{8,12},{12,8},{16,20},{20,16},{24,28},{28,24},{1,5},{5... | collective-permute-start | bytes 3538952 | tf_op jit(solution)/shard_map/ppermute | solution.py:257
  100.3 28.1 %collective-permute-start.19 = (bf16[768,768]{1,0:T(8,128)(2,1)S(1)}, bf16[768,768]{1,0:T(8,128)(2,1)S(1)}, u32[]{:S(2)}, u32[]{:S(2)}) collective-permute-start(bf16[768,768]{1,0:T(8,128)(2,1)S(1)} %bitcast.1540), channel_id=1, source_target_pairs={{0,1},{1,0},{2,3},{3,2},{4,5},{5,4},{6,7},{7,6},{8,9},{9,8},{10,11... | collective-permute-start | bytes 3538952 | tf_op jit(solution)/shard_map/ppermute | solution.py:257
  103.7 24.7 %collective-permute-start.21 = (bf16[2,2,96,384]{3,2,0,1:T(8,128)(2,1)S(1)}, bf16[2,2,96,384]{3,2,0,1:T(8,128)(2,1)S(1)}, u32[]{:S(2)}, u32[]{:S(2)}) collective-permute-start(bf16[2,2,96,384]{3,2,0,1:T(8,128)(2,1)S(1)} %maximum_bitcast_fusion.12), channel_id=1, source_target_pairs={{0,8},{4,12},{8,0},{12,4},{16,24},{20,28},{24,16},{28,20},{1,9},{5... | collective-permute-start | bytes 884744 | tf_op jit(solution)/shard_map/ppermute | solution.py:257
  129.3 9.9 %collective-permute-start.27 = (bf16[1,96,768]{2,1,0:T(8,128)(2,1)S(1)}, bf16[1,96,768]{2,1,0:T(8,128)(2,1)S(1)}, u32[]{:S(2)}, u32[]{:S(2)}) collective-permute-start(bf16[1,96,768]{2,1,0:T(8,128)(2,1)S(1)} %copy-done.137), channel_id=1, source_target_pairs={{0,16},{4,20},{8,24},{12,28},{16,0},{20,4},{24,8},{28,12},{1,17},{... | collective-permute-start | bytes 442376 | tf_op jit(solution)/shard_map/ppermute | solution.py:257
  130.6 12.9 %collective-permute-start.23 = (bf16[2,768,768]{2,1,0:T(8,128)(2,1)S(1)}, bf16[2,768,768]{2,1,0:T(8,128)(2,1)S(1)}, u32[]{:S(2)}, u32[]{:S(2)}) collective-permute-start(bf16[2,768,768]{2,1,0:T(8,128)(2,1)S(1)} %pad_maximum_fusion.2), channel_id=1, source_target_pairs={{0,2},{2,0},{1,3},{3,1},{4,6},{6,4},{5,7},{7,5},{8,10},{10,8},{9,1... | collective-permute-start | bytes 7077896 | tf_op jit(solution)/shard_map/ppermute | solution.py:257
  131.2 12.4 %collective-permute-start.24 = (bf16[2,1536,384]{2,1,0:T(8,128)(2,1)S(1)}, bf16[2,1536,384]{2,1,0:T(8,128)(2,1)S(1)}, u32[]{:S(2)}, u32[]{:S(2)}) collective-permute-start(bf16[2,1536,384]{2,1,0:T(8,128)(2,1)S(1)} %bitcast.1579), channel_id=1, source_target_pairs={{0,2},{2,0},{1,3},{3,1},{4,6},{6,4},{5,7},{7,5},{8,10},{10,8},{9,1... | collective-permute-start | bytes 7077896 | tf_op jit(solution)/shard_map/ppermute | solution.py:257
  145.9 12.9 %collective-permute-start.30 = (bf16[2,96,768]{2,1,0:T(8,128)(2,1)S(1)}, bf16[2,96,768]{2,1,0:T(8,128)(2,1)S(1)}, u32[]{:S(2)}, u32[]{:S(2)}) collective-permute-start(bf16[2,96,768]{2,1,0:T(8,128)(2,1)S(1)} %maximum_bitcast_fusion.13), channel_id=1, source_target_pairs={{0,8},{4,12},{8,0},{12,4},{16,24},{20,28},{24,16},{28,20},{1,9},{5... | collective-permute-start | bytes 884744 | tf_op jit(solution)/shard_map/ppermute | solution.py:257
  147.7 14.4 %collective-permute-start.29 = (bf16[2,4,96,384]{3,2,1,0:T(8,128)(2,1)S(1)}, bf16[2,4,96,384]{3,2,1,0:T(8,128)(2,1)S(1)}, u32[]{:S(2)}, u32[]{:S(2)}) collective-permute-start(bf16[2,4,96,384]{3,2,1,0:T(8,128)(2,1)S(1)} %pad_maximum_fusion.34), channel_id=1, source_target_pairs={{0,4},{4,0},{8,12},{12,8},{16,20},{20,16},{24,28},{28,24},{1,5},{5... | collective-permute-start | bytes 1769480 | tf_op jit(solution)/shard_map/ppermute | solution.py:257
  149.4 14.0 %collective-permute-start.28 = (bf16[8,96,384]{2,1,0:T(8,128)(2,1)S(1)}, bf16[8,96,384]{2,1,0:T(8,128)(2,1)S(1)}, u32[]{:S(2)}, u32[]{:S(2)}) collective-permute-start(bf16[8,96,384]{2,1,0:T(8,128)(2,1)S(1)} %bitcast.1578), channel_id=1, source_target_pairs={{0,1},{1,0},{2,3},{3,2},{4,5},{5,4},{6,7},{7,6},{8,9},{9,8},{10,11... | collective-permute-start | bytes 1769480 | tf_op jit(solution)/shard_map/ppermute | solution.py:257
  168.2 14.2 %collective-permute-start.34 = (bf16[1,384,384]{2,1,0:T(8,128)(2,1)}, bf16[1,384,384]{2,1,0:T(8,128)(2,1)}, u32[]{:S(2)}, u32[]{:S(2)}) collective-permute-start(bf16[1,384,384]{2,1,0:T(8,128)(2,1)} %constant_dynamic-slice_fusion.15), channel_id=1, source_target_pairs={{0,16},{4,20},{8,24},{12,28},{16,0},{20,4},{24,8},{28,12},{1,17},{... | collective-permute-start | bytes 884744 | tf_op jit(solution)/shard_map/ppermute | solution.py:257
  169.8 13.2 %collective-permute-start.33 = (bf16[4,96,768]{2,1,0:T(8,128)(2,1)}, bf16[4,96,768]{2,1,0:T(8,128)(2,1)}, u32[]{:S(2)}, u32[]{:S(2)}) collective-permute-start(bf16[4,96,768]{2,1,0:T(8,128)(2,1)} %bitcast.132), channel_id=1, source_target_pairs={{0,4},{4,0},{8,12},{12,8},{16,20},{20,16},{24,28},{28,24},{1,5},{5... | collective-permute-start | bytes 1769480 | tf_op jit(solution)/shard_map/ppermute | solution.py:257
  187.8 33.2 %collective-permute-start.37 = (bf16[768,768]{1,0:T(8,128)(2,1)S(1)}, bf16[768,768]{1,0:T(8,128)(2,1)S(1)}, u32[]{:S(2)}, u32[]{:S(2)}) collective-permute-start(bf16[768,768]{1,0:T(8,128)(2,1)S(1)} %bitcast.1541), channel_id=1, source_target_pairs={{0,1},{1,0},{2,3},{3,2},{4,5},{5,4},{6,7},{7,6},{8,9},{9,8},{10,11... | collective-permute-start | bytes 3538952 | tf_op jit(solution)/shard_map/ppermute | solution.py:257
  191.0 18.4 %collective-permute-start.35 = (bf16[3,1,512,384]{3,2,1,0:T(8,128)(2,1)S(1)}, bf16[3,1,512,384]{3,2,1,0:T(8,128)(2,1)S(1)}, u32[]{:S(2)}, u32[]{:S(2)}) collective-permute-start(bf16[3,1,512,384]{3,2,1,0:T(8,128)(2,1)S(1)} %pad_maximum_fusion.21), channel_id=1, source_target_pairs={{0,2},{2,0},{1,3},{3,1},{4,6},{6,4},{5,7},{7,5},{8,10},{10,8},{9,1... | collective-permute-start | bytes 3538952 | tf_op jit(solution)/shard_map/ppermute | solution.py:257
  192.3 83.0 %collective-permute-start.42 = (bf16[1,256,768]{2,1,0:T(8,128)(2,1)}, bf16[1,256,768]{2,1,0:T(8,128)(2,1)}, u32[]{:S(2)}, u32[]{:S(2)}) collective-permute-start(bf16[1,256,768]{2,1,0:T(8,128)(2,1)} %get-tuple-element.289), channel_id=1, source_target_pairs={{0,1},{1,0},{2,3},{3,2},{4,5},{5,4},{6,7},{7,6},{8,9},{9,8},{10,11... | collective-permute-start | bytes 1179656 | tf_op jit(solution)/shard_map/ppermute | solution.py:257
  194.6 14.8 %collective-permute-start.36 = (bf16[2,384,384]{2,1,0:T(8,128)(2,1)S(1)}, bf16[2,384,384]{2,1,0:T(8,128)(2,1)S(1)}, u32[]{:S(2)}, u32[]{:S(2)}) collective-permute-start(bf16[2,384,384]{2,1,0:T(8,128)(2,1)S(1)} %maximum_bitcast_fusion.5), channel_id=1, source_target_pairs={{0,8},{4,12},{8,0},{12,4},{16,24},{20,28},{24,16},{28,20},{1,9},{5... | collective-permute-start | bytes 1769480 | tf_op jit(solution)/shard_map/ppermute | solution.py:257
  221.6 28.9 %collective-permute-start.39 = (bf16[2,768,768]{2,1,0:T(8,128)(2,1)S(1)}, bf16[2,768,768]{2,1,0:T(8,128)(2,1)S(1)}, u32[]{:S(2)}, u32[]{:S(2)}) collective-permute-start(bf16[2,768,768]{2,1,0:T(8,128)(2,1)S(1)} %pad_maximum_fusion.3), channel_id=1, source_target_pairs={{0,2},{2,0},{1,3},{3,1},{4,6},{6,4},{5,7},{7,5},{8,10},{10,8},{9,1... | collective-permute-start | bytes 7077896 | tf_op jit(solution)/shard_map/ppermute | solution.py:257
  222.5 28.0 %collective-permute-start.40 = (bf16[4,384,384]{2,1,0:T(8,128)(2,1)S(1)}, bf16[4,384,384]{2,1,0:T(8,128)(2,1)S(1)}, u32[]{:S(2)}, u32[]{:S(2)}) collective-permute-start(bf16[4,384,384]{2,1,0:T(8,128)(2,1)S(1)} %bitcast.1548), channel_id=1, source_target_pairs={{0,4},{4,0},{8,12},{12,8},{16,20},{20,16},{24,28},{28,24},{1,5},{5... | collective-permute-start | bytes 3538952 | tf_op jit(solution)/shard_map/ppermute | solution.py:257
  253.3 11.7 %collective-permute-start.41 = (bf16[2,1536,384]{2,1,0:T(8,128)(2,1)S(1)}, bf16[2,1536,384]{2,1,0:T(8,128)(2,1)}, u32[]{:S(2)}, u32[]{:S(2)}) collective-permute-start(bf16[2,1536,384]{2,1,0:T(8,128)(2,1)S(1)} %bitcast.1580), channel_id=1, source_target_pairs={{0,2},{2,0},{1,3},{3,1},{4,6},{6,4},{5,7},{7,5},{8,10},{10,8},{9,1... | collective-permute-start | bytes 7077896 | tf_op jit(solution)/shard_map/ppermute | solution.py:257
  286.0 11.0 %collective-permute-start.43 = (bf16[2,1536,384]{2,1,0:T(8,128)(2,1)S(1)}, bf16[2,1536,384]{2,1,0:T(8,128)(2,1)S(1)}, u32[]{:S(2)}, u32[]{:S(2)}) collective-permute-start(bf16[2,1536,384]{2,1,0:T(8,128)(2,1)S(1)} %pad_maximum_fusion.4), channel_id=1, source_target_pairs={{0,2},{2,0},{1,3},{3,1},{4,6},{6,4},{5,7},{7,5},{8,10},{10,8},{9,1... | collective-permute-start | bytes 7077896 | tf_op jit(solution)/shard_map/ppermute | solution.py:257
  302.7 32.0 %collective-permute-start.46 = (bf16[4,384,384]{2,1,0:T(8,128)(2,1)S(1)}, bf16[4,384,384]{2,1,0:T(8,128)(2,1)S(1)}, u32[]{:S(2)}, u32[]{:S(2)}) collective-permute-start(bf16[4,384,384]{2,1,0:T(8,128)(2,1)S(1)} %dynamic-slice_bitcast_fusion.3), channel_id=1, source_target_pairs={{0,4},{4,0},{8,12},{12,8},{16,20},{20,16},{24,28},{28,24},{1,5},{5... | collective-permute-start | bytes 3538952 | tf_op jit(solution)/shard_map/ppermute | solution.py:257
  312.7 28.4 %collective-permute-start.47 = (bf16[768,768]{1,0:T(8,128)(2,1)S(1)}, bf16[768,768]{1,0:T(8,128)(2,1)S(1)}, u32[]{:S(2)}, u32[]{:S(2)}) collective-permute-start(bf16[768,768]{1,0:T(8,128)(2,1)S(1)} %dynamic-slice_bitcast_fusion.2), channel_id=1, source_target_pairs={{0,1},{1,0},{2,3},{3,2},{4,5},{5,4},{6,7},{7,6},{8,9},{9,8},{10,11... | collective-permute-start | bytes 3538952 | tf_op jit(solution)/shard_map/ppermute | solution.py:257
  341.5 20.2 %collective-permute-start.52 = (bf16[2,384,384]{2,1,0:T(8,128)(2,1)S(1)}, bf16[2,384,384]{2,1,0:T(8,128)(2,1)S(1)}, u32[]{:S(2)}, u32[]{:S(2)}) collective-permute-start(bf16[2,384,384]{2,1,0:T(8,128)(2,1)S(1)} %dynamic-slice_bitcast_fusion.10), channel_id=1, source_target_pairs={{0,8},{4,12},{8,0},{12,4},{16,24},{20,28},{24,16},{28,20},{1,9},{5... | collective-permute-start | bytes 1769480 | tf_op jit(solution)/shard_map/ppermute | solution.py:257
  343.7 18.0 %collective-permute-start.51 = (bf16[4,96,768]{2,1,0:T(8,128)(2,1)S(1)}, bf16[4,96,768]{2,1,0:T(8,128)(2,1)S(1)}, u32[]{:S(2)}, u32[]{:S(2)}) collective-permute-start(bf16[4,96,768]{2,1,0:T(8,128)(2,1)S(1)} %dynamic-slice_bitcast_fusion.11), channel_id=1, source_target_pairs={{0,4},{4,0},{8,12},{12,8},{16,20},{20,16},{24,28},{28,24},{1,5},{5... | collective-permute-start | bytes 1769480 | tf_op jit(solution)/shard_map/ppermute | solution.py:257
  365.9 16.0 %collective-permute-start.56 = (bf16[1,384,384]{2,1,0:T(8,128)(2,1)S(1)}, bf16[1,384,384]{2,1,0:T(8,128)(2,1)S(1)}, u32[]{:S(2)}, u32[]{:S(2)}) collective-permute-start(bf16[1,384,384]{2,1,0:T(8,128)(2,1)S(1)} %constant_dynamic-slice_fusion.13), channel_id=1, source_target_pairs={{0,16},{4,20},{8,24},{12,28},{16,0},{20,4},{24,8},{28,12},{1,17},{... | collective-permute-start | bytes 884744 | tf_op jit(solution)/shard_map/ppermute | solution.py:257
  366.9 15.0 %collective-permute-start.55 = (bf16[2,96,768]{2,1,0:T(8,128)(2,1)S(1)}, bf16[2,96,768]{2,1,0:T(8,128)(2,1)S(1)}, u32[]{:S(2)}, u32[]{:S(2)}) collective-permute-start(bf16[2,96,768]{2,1,0:T(8,128)(2,1)S(1)} %dynamic-slice_bitcast_fusion.17), channel_id=1, source_target_pairs={{0,8},{4,12},{8,0},{12,4},{16,24},{20,28},{24,16},{28,20},{1,9},{5... | collective-permute-start | bytes 884744 | tf_op jit(solution)/shard_map/ppermute | solution.py:257
  368.8 14.8 %collective-permute-start.53 = (bf16[8,96,384]{2,1,0:T(8,128)(2,1)S(1)}, bf16[8,96,384]{2,1,0:T(8,128)(2,1)S(1)}, u32[]{:S(2)}, u32[]{:S(2)}) collective-permute-start(bf16[8,96,384]{2,1,0:T(8,128)(2,1)S(1)} %dynamic-slice_bitcast_fusion.9), channel_id=1, source_target_pairs={{0,1},{1,0},{2,3},{3,2},{4,5},{5,4},{6,7},{7,6},{8,9},{9,8},{10,11... | collective-permute-start | bytes 1769480 | tf_op jit(solution)/shard_map/ppermute | solution.py:257
  369.6 14.5 %collective-permute-start.54 = (bf16[2,4,96,384]{3,2,1,0:T(8,128)(2,1)S(1)}, bf16[2,4,96,384]{3,2,1,0:T(8,128)(2,1)S(1)}, u32[]{:S(2)}, u32[]{:S(2)}) collective-permute-start(bf16[2,4,96,384]{3,2,1,0:T(8,128)(2,1)S(1)} %dynamic-slice_bitcast_fusion.8), channel_id=1, source_target_pairs={{0,4},{4,0},{8,12},{12,8},{16,20},{20,16},{24,28},{28,24},{1,5},{5... | collective-permute-start | bytes 1769480 | tf_op jit(solution)/shard_map/ppermute | solution.py:257
  384.5 17.5 %collective-permute-start.60 = (bf16[1,96,768]{2,1,0:T(8,128)(2,1)S(1)}, bf16[1,96,768]{2,1,0:T(8,128)(2,1)S(1)}, u32[]{:S(2)}, u32[]{:S(2)}) collective-permute-start(bf16[1,96,768]{2,1,0:T(8,128)(2,1)S(1)} %constant_dynamic-slice_fusion.12), channel_id=1, source_target_pairs={{0,16},{4,20},{8,24},{12,28},{16,0},{20,4},{24,8},{28,12},{1,17},{... | collective-permute-start | bytes 442376 | tf_op jit(solution)/shard_map/ppermute | solution.py:257
  386.0 17.3 %collective-permute-start.59 = (bf16[4,96,384]{2,1,0:T(8,128)(2,1)S(1)}, bf16[4,96,384]{2,1,0:T(8,128)(2,1)S(1)}, u32[]{:S(2)}, u32[]{:S(2)}) collective-permute-start(bf16[4,96,384]{2,1,0:T(8,128)(2,1)S(1)} %dynamic-slice_bitcast_fusion.15), channel_id=1, source_target_pairs={{0,1},{1,0},{2,3},{3,2},{4,5},{5,4},{6,7},{7,6},{8,9},{9,8},{10,11... | collective-permute-start | bytes 884744 | tf_op jit(solution)/shard_map/ppermute | solution.py:257
  387.3 16.0 %collective-permute-start.58 = (bf16[4,96,384]{2,1,0:T(8,128)(2,1)S(1)}, bf16[4,96,384]{2,1,0:T(8,128)(2,1)S(1)}, u32[]{:S(2)}, u32[]{:S(2)}) collective-permute-start(bf16[4,96,384]{2,1,0:T(8,128)(2,1)S(1)} %dynamic-slice_bitcast_fusion.16), channel_id=1, source_target_pairs={{0,4},{4,0},{8,12},{12,8},{16,20},{20,16},{24,28},{28,24},{1,5},{5... | collective-permute-start | bytes 884744 | tf_op jit(solution)/shard_map/ppermute | solution.py:257
  388.5 14.8 %collective-permute-start.61 = (bf16[384,384]{1,0:T(8,128)(2,1)S(1)}, bf16[384,384]{1,0:T(8,128)(2,1)S(1)}, u32[]{:S(2)}, u32[]{:S(2)}) collective-permute-start(bf16[384,384]{1,0:T(8,128)(2,1)S(1)} %fusion.428), channel_id=1, source_target_pairs={{0,1},{1,0},{2,3},{3,2},{4,5},{5,4},{6,7},{7,6},{8,9},{9,8},{10,11... | collective-permute-start | bytes 884744 | tf_op jit(solution)/shard_map/ppermute | solution.py:257
  389.3 13.9 %collective-permute-start.57 = (bf16[2,1536,384]{2,1,0:T(8,128)(2,1)S(1)}, bf16[2,1536,384]{2,1,0:T(8,128)(2,1)S(1)}, u32[]{:S(2)}, u32[]{:S(2)}) collective-permute-start(bf16[2,1536,384]{2,1,0:T(8,128)(2,1)S(1)} %pad_maximum_fusion.6), channel_id=1, source_target_pairs={{0,2},{2,0},{1,3},{3,1},{4,6},{6,4},{5,7},{7,5},{8,10},{10,8},{9,1... | collective-permute-start | bytes 7077896 | tf_op jit(solution)/shard_map/ppermute | solution.py:257
  402.0 109.4 %collective-permute-start.82 = (bf16[1,256,768]{2,1,0:T(8,128)(2,1)}, bf16[1,256,768]{2,1,0:T(8,128)(2,1)}, u32[]{:S(2)}, u32[]{:S(2)}) collective-permute-start(bf16[1,256,768]{2,1,0:T(8,128)(2,1)} %fusion.356), channel_id=1, source_target_pairs={{0,1},{1,0},{2,3},{3,2},{4,5},{5,4},{6,7},{7,6},{8,9},{9,8},{10,11... | collective-permute-start | bytes 1179656 | tf_op jit(solution)/shard_map/ppermute | solution.py:257
  403.6 15.7 %collective-permute-start.64 = (bf16[96,768]{1,0:T(8,128)(2,1)S(1)}, bf16[96,768]{1,0:T(8,128)(2,1)S(1)}, u32[]{:S(2)}, u32[]{:S(2)}) collective-permute-start(bf16[96,768]{1,0:T(8,128)(2,1)S(1)} %fusion.439), channel_id=1, source_target_pairs={{0,1},{1,0},{2,3},{3,2},{4,5},{5,4},{6,7},{7,6},{8,9},{9,8},{10,11... | collective-permute-start | bytes 442376 | tf_op jit(solution)/shard_map/ppermute | solution.py:257
  404.5 15.8 %collective-permute-start.63 = (bf16[2,2,96,384]{3,2,1,0:T(8,128)(2,1)S(1)}, bf16[2,2,96,384]{3,2,1,0:T(8,128)(2,1)S(1)}, u32[]{:S(2)}, u32[]{:S(2)}) collective-permute-start(bf16[2,2,96,384]{3,2,1,0:T(8,128)(2,1)S(1)} %fusion.437), channel_id=1, source_target_pairs={{0,8},{4,12},{8,0},{12,4},{16,24},{20,28},{24,16},{28,20},{1,9},{5... | collective-permute-start | bytes 884744 | tf_op jit(solution)/shard_map/ppermute | solution.py:257
  406.3 14.0 %collective-permute-start.65 = (bf16[384,384]{1,0:T(8,128)(2,1)S(1)}, bf16[384,384]{1,0:T(8,128)(2,1)S(1)}, u32[]{:S(2)}, u32[]{:S(2)}) collective-permute-start(bf16[384,384]{1,0:T(8,128)(2,1)S(1)} %add_convert_fusion.16), channel_id=1, source_target_pairs={{0,2},{2,0},{1,3},{3,1},{4,6},{6,4},{5,7},{7,5},{8,10},{10,8},{9,1... | collective-permute-start | bytes 884744 | tf_op jit(solution)/shard_map/ppermute | solution.py:257
  419.3 33.5 %collective-permute-start.69 = (bf16[4,384,384]{2,1,0:T(8,128)(2,1)S(1)}, bf16[4,384,384]{2,1,0:T(8,128)(2,1)S(1)}, u32[]{:S(2)}, u32[]{:S(2)}) collective-permute-start(bf16[4,384,384]{2,1,0:T(8,128)(2,1)S(1)} %dynamic-slice_bitcast_fusion.1), channel_id=1, source_target_pairs={{0,4},{4,0},{8,12},{12,8},{16,20},{20,16},{24,28},{28,24},{1,5},{5... | collective-permute-start | bytes 3538952 | tf_op jit(solution)/shard_map/ppermute | solution.py:257
  423.4 10.0 %collective-permute-start.67 = (bf16[2,1,96,384]{3,2,1,0:T(8,128)(2,1)S(1)}, bf16[2,1,96,384]{3,2,1,0:T(8,128)(2,1)S(1)}, u32[]{:S(2)}, u32[]{:S(2)}) collective-permute-start(bf16[2,1,96,384]{3,2,1,0:T(8,128)(2,1)S(1)} %constant_dynamic-slice_fusion.11), channel_id=1, source_target_pairs={{0,16},{4,20},{8,24},{12,28},{16,0},{20,4},{24,8},{28,12},{1,17},{... | collective-permute-start | bytes 442376 | tf_op jit(solution)/shard_map/ppermute | solution.py:257
  424.4 10.3 %collective-permute-start.68 = (bf16[2,96,768]{2,1,0:T(8,128)(2,1)S(1)}, bf16[2,96,768]{2,1,0:T(8,128)(2,1)S(1)}, u32[]{:S(2)}, u32[]{:S(2)}) collective-permute-start(bf16[2,96,768]{2,1,0:T(8,128)(2,1)S(1)} %pad_maximum_fusion.38), channel_id=1, source_target_pairs={{0,2},{2,0},{1,3},{3,1},{4,6},{6,4},{5,7},{7,5},{8,10},{10,8},{9,1... | collective-permute-start | bytes 884744 | tf_op jit(solution)/shard_map/ppermute | solution.py:257
  433.4 31.1 %collective-permute-start.70 = (bf16[768,768]{1,0:T(8,128)(2,1)S(1)}, bf16[768,768]{1,0:T(8,128)(2,1)S(1)}, u32[]{:S(2)}, u32[]{:S(2)}) collective-permute-start(bf16[768,768]{1,0:T(8,128)(2,1)S(1)} %dynamic-slice_bitcast_fusion), channel_id=1, source_target_pairs={{0,1},{1,0},{2,3},{3,2},{4,5},{5,4},{6,7},{7,6},{8,9},{9,8},{10,11... | collective-permute-start | bytes 3538952 | tf_op jit(solution)/shard_map/ppermute | solution.py:257
  434.8 29.8 %collective-permute-start.71 = (bf16[2,96,384]{2,1,0:T(8,128)(2,1)S(1)}, bf16[2,96,384]{2,1,0:T(8,128)(2,1)S(1)}, u32[]{:S(2)}, u32[]{:S(2)}) collective-permute-start(bf16[2,96,384]{2,1,0:T(8,128)(2,1)S(1)} %fusion.440), channel_id=1, source_target_pairs={{0,1},{1,0},{2,3},{3,2},{4,5},{5,4},{6,7},{7,6},{8,9},{9,8},{10,11... | collective-permute-start | bytes 442376 | tf_op jit(solution)/shard_map/ppermute | solution.py:257
  465.1 11.9 %collective-permute-start.73 = (bf16[2,2,96,384]{3,2,1,0:T(8,128)(2,1)S(1)}, bf16[2,2,96,384]{3,2,1,0:T(8,128)(2,1)S(1)}, u32[]{:S(2)}, u32[]{:S(2)}) collective-permute-start(bf16[2,2,96,384]{3,2,1,0:T(8,128)(2,1)S(1)} %copy.188), channel_id=1, source_target_pairs={{0,2},{2,0},{1,3},{3,1},{4,6},{6,4},{5,7},{7,5},{8,10},{10,8},{9,1... | collective-permute-start | bytes 884744 | tf_op jit(solution)/shard_map/ppermute | solution.py:257
  466.5 34.0 %collective-permute-start.77 = (bf16[2,384,384]{2,1,0:T(8,128)(2,1)}, bf16[2,384,384]{2,1,0:T(8,128)(2,1)}, u32[]{:S(2)}, u32[]{:S(2)}) collective-permute-start(bf16[2,384,384]{2,1,0:T(8,128)(2,1)} %dynamic-slice_bitcast_fusion.6), channel_id=1, source_target_pairs={{0,8},{4,12},{8,0},{12,4},{16,24},{20,28},{24,16},{28,20},{1,9},{5... | collective-permute-start | bytes 1769480 | tf_op jit(solution)/shard_map/ppermute | solution.py:257
  467.8 32.8 %collective-permute-start.76 = (bf16[4,96,768]{2,1,0:T(8,128)(2,1)}, bf16[4,96,768]{2,1,0:T(8,128)(2,1)}, u32[]{:S(2)}, u32[]{:S(2)}) collective-permute-start(bf16[4,96,768]{2,1,0:T(8,128)(2,1)} %dynamic-slice_bitcast_fusion.7), channel_id=1, source_target_pairs={{0,4},{4,0},{8,12},{12,8},{16,20},{20,16},{24,28},{28,24},{1,5},{5... | collective-permute-start | bytes 1769480 | tf_op jit(solution)/shard_map/ppermute | solution.py:257
  485.0 15.6 %collective-permute-start.74 = (bf16[2,768,384]{2,1,0:T(8,128)(2,1)}, bf16[2,768,384]{2,1,0:T(8,128)(2,1)}, u32[]{:S(2)}, u32[]{:S(2)}) collective-permute-start(bf16[2,768,384]{2,1,0:T(8,128)(2,1)} %pad_maximum_fusion.26), channel_id=1, source_target_pairs={{0,2},{2,0},{1,3},{3,1},{4,6},{6,4},{5,7},{7,5},{8,10},{10,8},{9,1... | collective-permute-start | bytes 3538952 | tf_op jit(solution)/shard_map/ppermute | solution.py:257
  485.0 15.5 %collective-permute-start.75 = (bf16[2,768,384]{2,1,0:T(8,128)(2,1)}, bf16[2,768,384]{2,1,0:T(8,128)(2,1)}, u32[]{:S(2)}, u32[]{:S(2)}) collective-permute-start(bf16[2,768,384]{2,1,0:T(8,128)(2,1)} %pad_maximum_fusion.27), channel_id=1, source_target_pairs={{0,2},{2,0},{1,3},{3,1},{4,6},{6,4},{5,7},{7,5},{8,10},{10,8},{9,1... | collective-permute-start | bytes 3538952 | tf_op jit(solution)/shard_map/ppermute | solution.py:257
  505.5 21.2 %collective-permute-start.78 = (bf16[8,96,384]{2,1,0:T(8,128)(2,1)S(1)}, bf16[8,96,384]{2,1,0:T(8,128)(2,1)S(1)}, u32[]{:S(2)}, u32[]{:S(2)}) collective-permute-start(bf16[8,96,384]{2,1,0:T(8,128)(2,1)S(1)} %dynamic-slice_bitcast_fusion.5), channel_id=1, source_target_pairs={{0,1},{1,0},{2,3},{3,2},{4,5},{5,4},{6,7},{7,6},{8,9},{9,8},{10,11... | collective-permute-start | bytes 1769480 | tf_op jit(solution)/shard_map/ppermute | solution.py:257
  506.8 19.9 %collective-permute-start.79 = (bf16[2,4,96,384]{3,2,1,0:T(8,128)(2,1)S(1)}, bf16[2,4,96,384]{3,2,1,0:T(8,128)(2,1)S(1)}, u32[]{:S(2)}, u32[]{:S(2)}) collective-permute-start(bf16[2,4,96,384]{3,2,1,0:T(8,128)(2,1)S(1)} %dynamic-slice_bitcast_fusion.4), channel_id=1, source_target_pairs={{0,4},{4,0},{8,12},{12,8},{16,20},{20,16},{24,28},{28,24},{1,5},{5... | collective-permute-start | bytes 1769480 | tf_op jit(solution)/shard_map/ppermute | solution.py:257
  509.2 13.8 %collective-permute-start.80 = (bf16[2,96,768]{2,1,0:T(8,128)(2,1)S(1)}, bf16[2,96,768]{2,1,0:T(8,128)(2,1)S(1)}, u32[]{:S(2)}, u32[]{:S(2)}) collective-permute-start(bf16[2,96,768]{2,1,0:T(8,128)(2,1)S(1)} %dynamic-slice_bitcast_fusion.14), channel_id=1, source_target_pairs={{0,8},{4,12},{8,0},{12,4},{16,24},{20,28},{24,16},{28,20},{1,9},{5... | collective-permute-start | bytes 884744 | tf_op jit(solution)/shard_map/ppermute | solution.py:257
  511.3 15.4 %collective-permute-start.81 = (bf16[1,384,384]{2,1,0:T(8,128)(2,1)S(1)}, bf16[1,384,384]{2,1,0:T(8,128)(2,1)S(1)}, u32[]{:S(2)}, u32[]{:S(2)}) collective-permute-start(bf16[1,384,384]{2,1,0:T(8,128)(2,1)S(1)} %constant_dynamic-slice_fusion.10), channel_id=1, source_target_pairs={{0,16},{4,20},{8,24},{12,28},{16,0},{20,4},{24,8},{28,12},{1,17},{... | collective-permute-start | bytes 884744 | tf_op jit(solution)/shard_map/ppermute | solution.py:257
  529.5 13.7 %collective-permute-start.84 = (bf16[4,96,384]{2,1,0:T(8,128)(2,1)S(1)}, bf16[4,96,384]{2,1,0:T(8,128)(2,1)S(1)}, u32[]{:S(2)}, u32[]{:S(2)}) collective-permute-start(bf16[4,96,384]{2,1,0:T(8,128)(2,1)S(1)} %dynamic-slice_bitcast_fusion.12), channel_id=1, source_target_pairs={{0,1},{1,0},{2,3},{3,2},{4,5},{5,4},{6,7},{7,6},{8,9},{9,8},{10,11... | collective-permute-start | bytes 884744 | tf_op jit(solution)/shard_map/ppermute | solution.py:257
  530.3 12.8 %collective-permute-start.83 = (bf16[4,96,384]{2,1,0:T(8,128)(2,1)S(1)}, bf16[4,96,384]{2,1,0:T(8,128)(2,1)S(1)}, u32[]{:S(2)}, u32[]{:S(2)}) collective-permute-start(bf16[4,96,384]{2,1,0:T(8,128)(2,1)S(1)} %dynamic-slice_bitcast_fusion.13), channel_id=1, source_target_pairs={{0,4},{4,0},{8,12},{12,8},{16,20},{20,16},{24,28},{28,24},{1,5},{5... | collective-permute-start | bytes 884744 | tf_op jit(solution)/shard_map/ppermute | solution.py:257
  531.2 13.3 %collective-permute-start.86 = (bf16[384,384]{1,0:T(8,128)(2,1)S(1)}, bf16[384,384]{1,0:T(8,128)(2,1)S(1)}, u32[]{:S(2)}, u32[]{:S(2)}) collective-permute-start(bf16[384,384]{1,0:T(8,128)(2,1)S(1)} %fusion.429), channel_id=1, source_target_pairs={{0,1},{1,0},{2,3},{3,2},{4,5},{5,4},{6,7},{7,6},{8,9},{9,8},{10,11... | collective-permute-start | bytes 884744 | tf_op jit(solution)/shard_map/ppermute | solution.py:257
  532.5 18.4 %collective-permute-start.87 = (bf16[1,256,768]{2,1,0:T(8,128)(2,1)S(1)}, bf16[1,256,768]{2,1,0:T(8,128)(2,1)S(1)}, u32[]{:S(2)}, u32[]{:S(2)}) collective-permute-start(bf16[1,256,768]{2,1,0:T(8,128)(2,1)S(1)} %fusion.357), channel_id=1, source_target_pairs={{0,1},{1,0},{2,3},{3,2},{4,5},{5,4},{6,7},{7,6},{8,9},{9,8},{10,11... | collective-permute-start | bytes 1179656 | tf_op jit(solution)/shard_map/ppermute | solution.py:257
  (219 other events, 1364.5 us)

commit v4 on v3

--- a/solution.py
+++ b/solution.py
@@ -225,15 +225,46 @@
     return scale * (raised - level - unit * along), token_sum(slope * unit), token_sum(slope)
 
 
+def partners(item):
+    return [(item, "uly", 1), (item, "blk", 1), (item, ("blk", "uly"), 3)]
+
+
+def far_sends(items):
+    near = masks_of("dp")[-2]
+    return [(item, "dp", (i + 1) * near) for i, item in enumerate(items)]
+
+
 def sum_small(held):
-    arrived = yield [(held, "blk", 1)]
-    held = held + arrived[0]
-    arrived = yield [(held, "uly", 1)]
-    held = held + arrived[0]
-    for mask in masks_of("dp"):
+    arrived = yield partners(held)
+    held = total(held, *arrived)
+    for mask in masks_of("dp")[:-2]:
         arrived = yield [(held, "dp", mask)]
-        held = held + arrived[0]
-    return held
+        held = total(held, *arrived)
+    arrived = yield far_sends([held] * 3)
+    return total(held, *arrived)
+
+
+def gather_far(held):
+    near, far = masks_of("dp")[-2:]
+    first, second, both = yield far_sends([held] * 3)
+    low = ordered(held, first, bit_of("dp", near), -3)
+    high = ordered(second, both, bit_of("dp", near), -3)
+    joined = ordered(low, high, bit_of("dp", far), -5)
+    return joined.reshape(held.shape[:-3] + (4,) + held.shape[-2:])
+
+
+def reduce_far(held):
+    place = lax.axis_index("dp") // masks_of("dp")[-2]
+    axis = held.ndim - 3
+    parts = [lax.dynamic_index_in_dim(held, place ^ i, axis, keepdims=False) for i in range(4)]
+    arrived = yield far_sends(parts[1:])
+    return total(parts[0], *arrived)
+
+
+def gather_partners(held):
+    along, across, both = yield partners(held)
+    place = bit_of("uly")
+    return ordered(ordered(held, along, place, 0), ordered(across, both, place, 0), bit_of("blk"), 0)
 
 
 def gelu(hidden):
@@ -253,7 +284,7 @@
 
 
 def swap(item, axis, mask=1):
-    count = lax.axis_size(axis)
+    count = 4 if isinstance(axis, tuple) else lax.axis_size(axis)
     return lax.ppermute(item, axis, [(i, i ^ mask) for i in range(count)])
 
 
@@ -285,6 +316,10 @@
 
 def chosen(item, bit, axis):
     return lax.dynamic_index_in_dim(item, bit.astype(jnp.int32), axis, keepdims=False)
+
+
+def total(*items):
+    return sum(item.astype(FULL) for item in items).astype(items[0].dtype)
 
 
 def added(left, right):
@@ -366,7 +401,8 @@
 def gather_attention(first, second):
     held = jnp.stack([quarter_of(first), quarter_of(second)])[:, None]
     masks = masks_of("dp")
-    for mask in reversed(masks[1:]):
+    held = yield from gather_far(held)
+    for mask in reversed(masks[1:-2]):
         (other,) = yield [(held, "dp", mask)]
         held = grown(held, other, mask)
     left, right = held[0], held[1]
@@ -433,15 +469,12 @@
     keep_right, send_right = chosen(right, place, 0), chosen(right, ~place, 0)
     arrived = yield [(send_left, "dp", masks[0]), (send_right, "uly", 1)]
     held = jnp.stack([added(keep_left, arrived[0]), added(keep_right, arrived[1])])
-    for mask in masks[1:]:
+    for mask in masks[1:-2]:
         keep, send = halved(split_rows(held), bit_of("dp", mask))
         (other,) = yield [(send, "dp", mask)]
         held = added(keep, other)
-    held = held[:, 0]
-    (other,) = yield [(held, "uly", 1)]
-    held = ordered(held, other, place, 1)
-    (other,) = yield [(held, "blk", 1)]
-    return ordered(held, other, bit_of("blk"), 1)
+    held = yield from reduce_far(held)
+    return (yield from gather_partners(held))
 
 
 def reduce_up(own, other):
@@ -457,11 +490,7 @@
         keep, send = halved(split_rows(held), bit_of("dp", mask))
         (arrived,) = yield [(send, "dp", mask)]
         held = added(keep, arrived)
-    held = held[0]
-    (arrived,) = yield [(held, "uly", 1)]
-    held = ordered(held, arrived, place, 0)
-    (arrived,) = yield [(held, "blk", 1)]
-    every = ordered(held, arrived, bit_of("blk"), 0)
+    every = yield from gather_partners(held[0])
     return jnp.concatenate([every[i, j] for i in range(2) for j in range(2)], axis=-1)
 
 
@@ -527,7 +556,7 @@
 
     own, other = attention.result
     normed = normalize(residual, first_gain, first_shift).astype(LOW)
-    normed = cut(normed, up_flow, down_flow, *with_next(next_attention))
+    normed = cut(normed, up_flow, down_flow)
     query_biases, value_biases = halves_of(query_bias), halves_of(value_bias)
 
     def project(weights, i):
@@ -542,12 +571,13 @@
 
     away = swap(project(other, 1), "blk")
     mine = project(own, 0)
-    mine, away = cut((mine, away), *([next_attention] if coming else [down_flow]))
+    mine, away = cut((mine, away), *with_next(next_attention))
     mixed_mine, mixed_theirs, logsum = attend(core, mine, away)
     mixed_mine, mixed_theirs = cut(
         (mixed_mine, mixed_theirs),
         up_flow,
-        *([down_flow, next_attention, next_up] if coming else []),
+        down_flow,
+        *with_next(next_attention, next_up),
     )
     arrived = swap(mixed_theirs, "blk")
     mixed = side_by_side(mixed_mine, arrived, bit)
@@ -555,7 +585,7 @@
     middle = residual + columns + out_bias
     normed_two = normalize(middle, second_gain, second_shift).astype(LOW)
     middle, normed_two = cut(
-        (middle, normed_two), up_flow, down_flow, *with_next(next_attention, next_up)
+        (middle, normed_two), up_flow, down_flow, *with_next(next_attention, next_up, next_down)
     )
     middle, normed_two = drain((middle, normed_two), up_flow)
     low_biases, high_biases = small[8:10], small[10:12]
@@ -582,7 +612,7 @@
     return result, record + (middle, normed_two, hidden, active)
 
 
-def layer_backward(upstream, small, weights, record, core, before):
+def layer_backward(upstream, small, weights, record, core, before, lowest):
     (own, other), (up_own, up_other), (down_own, down_other) = weights
     first_gain, second_gain = small[0:1], small[5:6]
     residual, normed, mine, away, logsum, mixed_mine, mixed_theirs, mixed = record[:8]
@@ -596,7 +626,7 @@
         jnp.stack([contract(active[i], low_own) for i in range(2)]),
     ]
     down_flow = Flow(reduce_down(down_slopes[1], down_slopes[0]))
-    low_own, low_other, upstream = cut((low_own, low_other, upstream), down_flow, *before)
+    low_own, low_other, upstream = cut((low_own, low_other, upstream), down_flow, *before[:2])
     active_slopes = [
         transposed(low_own, down_own[0]) + transposed(low_other, down_other[1]),
         transposed(low_own, down_own[1]) + transposed(low_other, down_other[0]),
@@ -650,7 +680,10 @@
         second.append(jnp.stack([slopes[2], out_slope]))
     attention_flow = Flow(reduce_attention((first[0], second[0]), (first[1], second[1])))
     grads_mine, grads_away, middle_slope = cut(
-        (grads_mine, grads_away, middle_slope), attention_flow, *before
+        (grads_mine, grads_away, middle_slope),
+        attention_flow,
+        *before,
+        *([down_flow] if lowest else []),
     )
     query_bias_slope = side_by_side(token_sum(grads_mine[0]), token_sum(grads_away[0]), bit)
     value_bias_slope = side_by_side(token_sum(grads_mine[2]), token_sum(grads_away[2]), bit)
@@ -662,6 +695,8 @@
             + transposed(grads[1], pair[1])
             + transposed(grads[2], last[0])
         )
+    if lowest:
+        first_slope = cut(first_slope, attention_flow)
     through, first_gain_slope, first_shift_slope = norm_backward(residual, first_gain, first_slope)
     upstream = middle_slope + through
     upstream = cut(upstream, attention_flow, up_flow, down_flow, *before)
@@ -730,9 +765,8 @@
     entering = Flow(to_sequences(inputs))
     vector_flow = Flow(gather_small(vectors.reshape(layers * kinds, rows)))
     cut((), attention, entering, vector_flow)
-    cut((), attention, entering, vector_flow)
+    cut((), attention, entering, vector_flow, up_flow)
     residual = entering.result.astype(FULL)
-    residual = cut(residual, attention, vector_flow, up_flow)
     residual = cut(residual, attention, vector_flow, up_flow, down_flow)
     residual = drain(residual, vector_flow)
     gathered = vector_flow.result.reshape(-1, layers, kinds, rows).astype(FULL)
@@ -759,13 +793,16 @@
     for layer in reversed(range(layers)):
         weights = tuple(flow.result for flow in flows[layer])
         upstream, terms[layer], after = layer_backward(
-            upstream, small[layer], weights, records[layer], core, before
+            upstream, small[layer], weights, records[layer], core, before, layer == 0
         )
         upstream = drain(upstream, *before)
         before = after
         found[layer] = after
     gradient = Flow(from_sequences(upstream))
     totals = Flow(sum_small(jnp.concatenate(terms)))
+    attention, up_flow, down_flow = before
+    cut((), attention, down_flow, up_flow, totals, gradient)
+    cut((), attention, up_flow, totals)
     drain((), *before, gradient, totals, outgoing)
 
     sums = totals.result.reshape(layers, kinds, width)
@@ -780,7 +817,7 @@
         attention, up_flow, down_flow = found[layer]
         pairs = attention.result
         whole = [
-            jnp.concatenate([pairs[block, 0, kind], pairs[block, 1, kind]], axis=-1)
+            jnp.concatenate([pairs[0, kind, block], pairs[1, kind, block]], axis=-1)
             for block in range(2)
             for kind in range(2)
         ]

time: 594 us -> 576 us (0.970)
  starting transfers between devices: 85.5 us -> 106 us
  waiting for transfers between devices: 167 us -> 148 us
  local copies, waits for them, and re-layouts: 68.3 us -> 58.3 us
    ppermute x100 -> x110, starting transfers between devices: 85.5 us -> 106 us  [swap(): return lax.ppermute(item, axis, [(i, i ^ mask) for i in range(count)])]
    ppermute x100 -> x110, waiting for transfers between devices: 167 us -> 148 us  [swap(): return lax.ppermute(item, axis, [(i, i ^ mask) for i in range(count)])]
    dot_general x32, matrix products: 35.5 us -> 42.4 us  [matmul(): return jnp.dot(left, right, preferred_element_type=FULL)]
    convert_element_type x30 -> x24, other arithmetic: 12.3 us -> 8.23 us  [added(): return (left.astype(FULL) + right.astype(FULL)).astype(LOW)]
    another operation x69 -> x64, other arithmetic: 25.5 us -> 26.2 us  [ordered(): return jnp.stack([low, high], axis=axis)]
    unnamed x379 -> x382, local copies, waits for them, and re-layouts: 25.9 us -> 26.1 us
  transfers between devices with their start and end apart: 100 -> 110, of which waited for: 39 -> 39; matrix products, arithmetic and copies ran while one was open for 33% -> 30% of each run, Pallas kernels for 9% -> 10%
where the time goes in v4:
time: 576 us; the launch traced here: 569 us
  waiting for transfers between devices  148 us (26%)
  starting transfers between devices  106 us (18%)
  matrix products  102 us (18%)
  other arithmetic  94.2 us (16%)
  local copies, waits for them, and re-layouts  58.3 us (10%)
  Pallas kernels  55.2 us (10%)
    ppermute x110, waiting for transfers between devices, swap(): return lax.ppermute(item, axis, [(i, i ^ mask) for i in range(count)])  148 us
    ppermute x110, starting transfers between devices, swap(): return lax.ppermute(item, axis, [(i, i ^ mask) for i in range(count)])  106 us
    dot_general x32, matrix products, matmul(): return jnp.dot(left, right, preferred_element_type=FULL)  42.4 us
    dot_general x32, matrix products, transposed(): return jnp.einsum('ste,de->std', left, right, preferred_element_type=FULL)  34.9 us
    pallas_call x2, Pallas kernels, attend_back(): pl.pallas_call(attend_back_kernel, grid_spec=pltpu.PrefetchScalarGridSpec...  32 us
    another operation x64, other arithmetic, ordered(): return jnp.stack([low, high], axis=axis)  26.2 us
    unnamed x382, local copies, waits for them, and re-layouts  26.1 us
    dot_general x32, matrix products, contract(): jnp.einsum('std,ste->de', left, right, preferred_element_type=FULL)  24.8 us
  transfers between devices with their start and end apart: 110, of which 39 were waited for; matrix products, arithmetic and copies ran while one was open for 30% of the time, Pallas kernels for 10%

profile of v4, /device:TPU:0, one launch (start us, length us, event | category | flops | bytes accessed | tf_op | source)
XLA Modules:
  0.0 569.2 jit_solution(15181216260914701956)
XLA Ops:
  3.1 1.7 slice_bitcast_fusion.22
  7.4 4.0 collective-permute-start.4
  13.3 2.5 collective-permute-start.2
  22.0 4.4 collective-permute-done.1
  26.5 2.8 collective-permute-start.7
  36.0 1.8 collective-permute-done.8
  42.4 2.2 collective-permute-start.13
  49.2 5.5 collective-permute-done.12
  54.8 3.2 collective-permute-done.11
  60.4 1.8 select_bitcast_fusion.22
  64.4 1.8 fusion.470
  73.1 11.2 %collective-permute-done.17 = bf16[2,384,384]{2,1,0:T(8,128)(2,1)} collective-permute-done((bf16[2,384,384]{2,1,0:T(8,128)(2,1)}, bf16[2,384,384]{2,1,0:T(8,128)(2,1)}, u32[]{:S(2)}, u32[]{:S(2)}) %collective-permute-start.17) | collective-permute-done | bytes 589856 | tf_op jit(solution)/shard_map/ppermute | solution.py:288
  84.3 3.0 collective-permute-done.16
  90.3 1.7 fusion.175
  102.3 3.2 collective-permute-start.23
  106.1 11.6 %attend.2 = (bf16[1,512,384]{2,1,0:T(8,128)(2,1)S(1)}, bf16[1,512,384]{2,1,0:T(8,128)(2,1)S(1)}, f32[1,3,8,1024]{3,2,1,0:T(8,128)S(1)}) custom-call(s32[1]{0:T(128)} %bitcast.59.core_ref, bf16[3,1,512,384]{3,2,1,0:T(8,128)(2,1)S(1)} %pad_maximum_fusion.15.mine_ref, bf16[3,1,512,384]{3,2,1,0:T(8,128)(2,1)S(1)} %collective-permute-done.18.theirs_ref), custom_call_target="tpu_custom_call" | custom-call | tf_op jit(solution)/shard_map/attend/pallas_call | solution.py:100
  117.8 6.1 %collective-permute-done.20 = bf16[4,384,384]{2,1,0:T(8,128)(2,1)S(1)} collective-permute-done((bf16[4,384,384]{2,1,0:T(8,128)(2,1)S(1)}, bf16[4,384,384]{2,1,0:T(8,128)(2,1)S(1)}, u32[]{:S(2)}, u32[]{:S(2)}) %collective-permute-start.20) | collective-permute-done | bytes 1179680 | tf_op jit(solution)/shard_map/ppermute | solution.py:288
  137.5 3.5 collective-permute-done.28
  143.9 2.4 collective-permute-start.33
  157.9 2.6 collective-permute-done.31
  171.3 9.2 %fusion.120 = f32[512,384]{1,0:T(8,128)S(1)} fusion(bf16[1,512,1536]{2,1,0:T(8,128)(2,1)S(1)} %copy-done.99, bf16[2,1536,384]{2,1,0:T(8,128)(2,1)S(1)} %copy-done.57), kind=kOutput, calls=%fused_computation.219 | convolution fusion | flops 603979776 | bytes 3538944 | tf_op jit(solution)/shard_map/dot_general | solution.py:275
  191.2 1.7 fusion.171
  206.0 11.6 %attend.3 = (bf16[1,512,384]{2,1,0:T(8,128)(2,1)S(1)}, bf16[1,512,384]{2,1,0:T(8,128)(2,1)S(1)}, f32[1,3,8,1024]{3,2,1,0:T(8,128)S(1)}) custom-call(s32[1]{0:T(128)} %bitcast.59.core_ref, bf16[3,1,512,384]{3,2,1,0:T(8,128)(2,1)S(1)} %pad_maximum_fusion.20.mine_ref, bf16[3,1,512,384]{3,2,1,0:T(8,128)(2,1)S(1)} %collective-permute-done.38.theirs_ref), custom_call_target="tpu_custom_call" | custom-call | tf_op jit(solution)/shard_map/attend/pallas_call | solution.py:100
  217.6 10.5 %collective-permute-done.40 = bf16[4,384,384]{2,1,0:T(8,128)(2,1)} collective-permute-done((bf16[4,384,384]{2,1,0:T(8,128)(2,1)}, bf16[4,384,384]{2,1,0:T(8,128)(2,1)}, u32[]{:S(2)}, u32[]{:S(2)}) %collective-permute-start.40) | collective-permute-done | bytes 1179680 | tf_op jit(solution)/shard_map/ppermute | solution.py:288
  228.4 1.8 broadcast_select_fusion.1
  230.3 2.6 select_bitcast_fusion.1
  239.0 1.8 select_bitcast_fusion.7
  253.7 2.9 fusion.106
  270.3 2.3 fusion.497
  275.6 2.5 fusion.495
  295.8 1.7 fusion.148
  300.2 16.0 %attend_back.2 = (bf16[3,1,512,384]{3,2,1,0:T(8,128)(2,1)S(1)}, bf16[3,1,512,384]{3,2,1,0:T(8,128)(2,1)S(1)}) custom-call(s32[1]{0:T(128)} %bitcast.59.core_ref, bf16[3,1,512,384]{3,2,1,0:T(8,128)(2,1)S(1)} %pad_maximum_fusion.20.mine_ref, bf16[3,1,512,384]{3,2,1,0:T(8,128)(2,1)S(1)} %collective-permute-done.38.theirs_ref, ...), custom_call_target="tpu_custom_call" | custom-call | tf_op jit(solution)/shard_map/attend_back/pallas_call | solution.py:190
  316.2 6.2 %collective-permute-done.49 = bf16[768,768]{1,0:T(8,128)(2,1)S(1)} collective-permute-done((bf16[768,768]{1,0:T(8,128)(2,1)S(1)}, bf16[768,768]{1,0:T(8,128)(2,1)S(1)}, u32[]{:S(2)}, u32[]{:S(2)}) %collective-permute-start.49) | collective-permute-done | bytes 1179680 | tf_op jit(solution)/shard_map/ppermute | solution.py:288
  334.3 1.8 fusion.320
  336.8 2.4 fusion.77
  352.5 6.3 %collective-permute-done.57 = bf16[2,96,768]{2,1,0:T(8,128)(2,1)S(1)} collective-permute-done((bf16[2,96,768]{2,1,0:T(8,128)(2,1)S(1)}, bf16[2,96,768]{2,1,0:T(8,128)(2,1)S(1)}, u32[]{:S(2)}, u32[]{:S(2)}) %collective-permute-start.57) | collective-permute-done | bytes 294944 | tf_op jit(solution)/shard_map/ppermute | solution.py:288
  358.8 4.1 collective-permute-done.55
  364.0 2.4 collective-permute-start.61
  373.5 2.3 fusion.505
  375.9 2.7 fusion.503
  394.7 3.1 collective-permute-start.65
  399.4 2.6 collective-permute-done.66
  401.9 2.8 collective-permute-done.64
  404.7 4.5 collective-permute-done.65
  413.4 1.7 fusion.149
  421.2 16.0 %attend_back.3 = (bf16[3,1,512,384]{3,2,1,0:T(8,128)(2,1)S(1)}, bf16[3,1,512,384]{3,2,1,0:T(8,128)(2,1)S(1)}) custom-call(s32[1]{0:T(128)} %bitcast.59.core_ref, bf16[3,1,512,384]{3,2,1,0:T(8,128)(2,1)S(1)} %copy-done.1, bf16[3,1,512,384]{3,2,1,0:T(8,128)(2,1)S(1)} %copy-done.3, f32[1,3,8,1024]{3,2,1,0:T(8,128)S(1)} %get-tuple-element.258.logsum_ref, ...), custom_call_target="tpu_custom_call" | custom-call | tf_op jit(solution)/shard_map/attend_back/pallas_call | solution.py:190
  438.3 8.2 %collective-permute-done.76 = bf16[4,384,384]{2,1,0:T(8,128)(2,1)S(1)} collective-permute-done((bf16[4,384,384]{2,1,0:T(8,128)(2,1)S(1)}, bf16[4,384,384]{2,1,0:T(8,128)(2,1)S(1)}, u32[]{:S(2)}, u32[]{:S(2)}) %collective-permute-start.76) | collective-permute-done | bytes 1179680 | tf_op jit(solution)/shard_map/ppermute | solution.py:288
  453.1 11.4 %collective-permute-done.79 = bf16[2,384,384]{2,1,0:T(8,128)(2,1)S(1)} collective-permute-done((bf16[2,384,384]{2,1,0:T(8,128)(2,1)S(1)}, bf16[2,384,384]{2,1,0:T(8,128)(2,1)S(1)}, u32[]{:S(2)}, u32[]{:S(2)}) %collective-permute-start.79) | collective-permute-done | bytes 589856 | tf_op jit(solution)/shard_map/ppermute | solution.py:288
  471.7 2.0 add_bitcast_fusion
  478.2 5.7 %collective-permute-done.85 = bf16[1,384,384]{2,1,0:T(8,128)(2,1)S(1)} collective-permute-done((bf16[1,384,384]{2,1,0:T(8,128)(2,1)S(1)}, bf16[1,384,384]{2,1,0:T(8,128)(2,1)S(1)}, u32[]{:S(2)}, u32[]{:S(2)}) %collective-permute-start.85) | collective-permute-done | bytes 294944 | tf_op jit(solution)/shard_map/ppermute | solution.py:288
  483.9 6.5 %collective-permute-done.82 = bf16[8,96,384]{2,1,0:T(8,128)(2,1)S(1)} collective-permute-done((bf16[8,96,384]{2,1,0:T(8,128)(2,1)S(1)}, bf16[8,96,384]{2,1,0:T(8,128)(2,1)S(1)}, u32[]{:S(2)}, u32[]{:S(2)}) %collective-permute-start.82) | collective-permute-done | bytes 589856 | tf_op jit(solution)/shard_map/ppermute | solution.py:288
  495.8 1.7 collective-permute-start.89
  502.1 3.3 concatenate.282
  505.6 3.5 collective-permute-done.88
  514.5 2.6 collective-permute-start.93
  518.9 2.7 collective-permute-start.91
  523.8 5.5 collective-permute-done.93
  530.2 6.9 %collective-permute-done.91 = bf16[2,96,384]{2,1,0:T(8,128)(2,1)S(1)} collective-permute-done((bf16[2,96,384]{2,1,0:T(8,128)(2,1)S(1)}, bf16[2,96,384]{2,1,0:T(8,128)(2,1)S(1)}, u32[]{:S(2)}, u32[]{:S(2)}) %collective-permute-start.91) | collective-permute-done | bytes 147488 | tf_op jit(solution)/shard_map/ppermute | solution.py:288
  539.9 3.0 collective-permute-done.105
  546.3 2.8 collective-permute-done.97
  549.1 2.0 collective-permute-done.102
  551.1 3.3 collective-permute-done.100
  554.3 2.4 collective-permute-start.109
  556.7 2.1 collective-permute-start.108
  (998 shorter events, 287.4 us)
Async XLA Ops:
  7.4 14.7 %collective-permute-start.4 = (bf16[1,24,96]{2,1,0:T(8,128)(2,1)S(1)}, bf16[1,24,96]{2,1,0:T(8,128)(2,1)S(1)}, u32[]{:S(2)}, u32[]{:S(2)}) collective-permute-start(bf16[1,24,96]{2,1,0:T(8,128)(2,1)S(1)} %broadcast_in_dim_reshape.3), channel_id=1, source_target_pairs={{0,16},{4,20},{8,24},{12,28},{16,0},{20,4},{24,8},{28,12},{1,17},{... | collective-permute-start | bytes 13832 | tf_op jit(solution)/shard_map/ppermute | solution.py:288
  11.4 10.6 %collective-permute-start = (bf16[2,1,96,384]{3,2,0,1:T(8,128)(2,1)}, bf16[2,1,96,384]{3,2,0,1:T(8,128)(2,1)}, u32[]{:S(2)}, u32[]{:S(2)}) collective-permute-start(bf16[2,1,96,384]{3,2,0,1:T(8,128)(2,1)} %maximum_bitcast_fusion.12), channel_id=1, source_target_pairs={{0,8},{4,12},{8,0},{12,4},{16,24},{20,28},{24,16},{28,20},{1,9},{5... | collective-permute-start | bytes 442376 | tf_op jit(solution)/shard_map/ppermute | solution.py:288
  13.0 13.5 %collective-permute-start.1 = (bf16[2,1,96,384]{3,2,0,1:T(8,128)(2,1)}, bf16[2,1,96,384]{3,2,0,1:T(8,128)(2,1)}, u32[]{:S(2)}, u32[]{:S(2)}) collective-permute-start(bf16[2,1,96,384]{3,2,0,1:T(8,128)(2,1)} %maximum_bitcast_fusion.12), channel_id=1, source_target_pairs={{0,16},{4,20},{8,24},{12,28},{16,0},{20,4},{24,8},{28,12},{1,17},{... | collective-permute-start | bytes 442376 | tf_op jit(solution)/shard_map/ppermute | solution.py:288
  13.3 13.1 %collective-permute-start.2 = (bf16[2,1,96,384]{3,2,0,1:T(8,128)(2,1)}, bf16[2,1,96,384]{3,2,0,1:T(8,128)(2,1)}, u32[]{:S(2)}, u32[]{:S(2)}) collective-permute-start(bf16[2,1,96,384]{3,2,0,1:T(8,128)(2,1)} %maximum_bitcast_fusion.12), channel_id=1, source_target_pairs={{0,24},{4,28},{8,16},{12,20},{16,8},{20,12},{24,0},{28,4},{1,25},{... | collective-permute-start | bytes 442376 | tf_op jit(solution)/shard_map/ppermute | solution.py:288
  15.8 10.7 %collective-permute-start.3 = (bf16[1,256,768]{2,1,0:T(8,128)(2,1)}, bf16[1,256,768]{2,1,0:T(8,128)(2,1)}, u32[]{:S(2)}, u32[]{:S(2)}) collective-permute-start(bf16[1,256,768]{2,1,0:T(8,128)(2,1)} %get-tuple-element.231), channel_id=1, source_target_pairs={{0,1},{1,0},{2,3},{3,2},{4,5},{5,4},{6,7},{7,6},{8,9},{9,8},{10,11... | collective-permute-start | bytes 1179656 | tf_op jit(solution)/shard_map/ppermute | solution.py:288
  41.5 13.2 %collective-permute-start.12 = (bf16[2,96,768]{2,1,0:T(8,128)(2,1)S(1)}, bf16[2,96,768]{2,1,0:T(8,128)(2,1)}, u32[]{:S(2)}, u32[]{:S(2)}) collective-permute-start(bf16[2,96,768]{2,1,0:T(8,128)(2,1)S(1)} %maximum_bitcast_fusion.10), channel_id=1, source_target_pairs={{0,8},{4,12},{8,0},{12,4},{16,24},{20,28},{24,16},{28,20},{1,9},{5... | collective-permute-start | bytes 884744 | tf_op jit(solution)/shard_map/ppermute | solution.py:288
  42.4 12.4 %collective-permute-start.13 = (bf16[1,384,384]{2,1,0:T(8,128)(2,1)}, bf16[1,384,384]{2,1,0:T(8,128)(2,1)}, u32[]{:S(2)}, u32[]{:S(2)}) collective-permute-start(bf16[1,384,384]{2,1,0:T(8,128)(2,1)} %constant_dynamic-slice_fusion.15), channel_id=1, source_target_pairs={{0,16},{4,20},{8,24},{12,28},{16,0},{20,4},{24,8},{28,12},{1,17},{... | collective-permute-start | bytes 884744 | tf_op jit(solution)/shard_map/ppermute | solution.py:288
  45.5 12.5 %collective-permute-start.11 = (bf16[2,4,96,384]{3,2,1,0:T(8,128)(2,1)}, bf16[2,4,96,384]{3,2,1,0:T(8,128)(2,1)}, u32[]{:S(2)}, u32[]{:S(2)}) collective-permute-start(bf16[2,4,96,384]{3,2,1,0:T(8,128)(2,1)} %pad_maximum_fusion.31), channel_id=1, source_target_pairs={{0,4},{4,0},{8,12},{12,8},{16,20},{20,16},{24,28},{28,24},{1,5},{5... | collective-permute-start | bytes 1769480 | tf_op jit(solution)/shard_map/ppermute | solution.py:288
  47.2 12.0 %collective-permute-start.10 = (bf16[8,96,384]{2,1,0:T(8,128)(2,1)S(1)}, bf16[8,96,384]{2,1,0:T(8,128)(2,1)}, u32[]{:S(2)}, u32[]{:S(2)}) collective-permute-start(bf16[8,96,384]{2,1,0:T(8,128)(2,1)S(1)} %bitcast.1549), channel_id=1, source_target_pairs={{0,1},{1,0},{2,3},{3,2},{4,5},{5,4},{6,7},{7,6},{8,9},{9,8},{10,11... | collective-permute-start | bytes 1769480 | tf_op jit(solution)/shard_map/ppermute | solution.py:288
  68.4 15.9 %collective-permute-start.17 = (bf16[2,384,384]{2,1,0:T(8,128)(2,1)}, bf16[2,384,384]{2,1,0:T(8,128)(2,1)}, u32[]{:S(2)}, u32[]{:S(2)}) collective-permute-start(bf16[2,384,384]{2,1,0:T(8,128)(2,1)} %maximum_bitcast_fusion.4), channel_id=1, source_target_pairs={{0,8},{4,12},{8,0},{12,4},{16,24},{20,28},{24,16},{28,20},{1,9},{5... | collective-permute-start | bytes 1769480 | tf_op jit(solution)/shard_map/ppermute | solution.py:288
  71.7 15.6 %collective-permute-start.16 = (bf16[4,96,768]{2,1,0:T(8,128)(2,1)}, bf16[4,96,768]{2,1,0:T(8,128)(2,1)}, u32[]{:S(2)}, u32[]{:S(2)}) collective-permute-start(bf16[4,96,768]{2,1,0:T(8,128)(2,1)} %bitcast.54), channel_id=1, source_target_pairs={{0,4},{4,0},{8,12},{12,8},{16,20},{20,16},{24,28},{28,24},{1,5},{5... | collective-permute-start | bytes 1769480 | tf_op jit(solution)/shard_map/ppermute | solution.py:288
  95.5 28.4 %collective-permute-start.20 = (bf16[4,384,384]{2,1,0:T(8,128)(2,1)S(1)}, bf16[4,384,384]{2,1,0:T(8,128)(2,1)S(1)}, u32[]{:S(2)}, u32[]{:S(2)}) collective-permute-start(bf16[4,384,384]{2,1,0:T(8,128)(2,1)S(1)} %bitcast.1518), channel_id=1, source_target_pairs={{0,4},{4,0},{8,12},{12,8},{16,20},{20,16},{24,28},{28,24},{1,5},{5... | collective-permute-start | bytes 3538952 | tf_op jit(solution)/shard_map/ppermute | solution.py:288
  96.1 28.1 %collective-permute-start.19 = (bf16[768,768]{1,0:T(8,128)(2,1)S(1)}, bf16[768,768]{1,0:T(8,128)(2,1)S(1)}, u32[]{:S(2)}, u32[]{:S(2)}) collective-permute-start(bf16[768,768]{1,0:T(8,128)(2,1)S(1)} %bitcast.1519), channel_id=1, source_target_pairs={{0,1},{1,0},{2,3},{3,2},{4,5},{5,4},{6,7},{7,6},{8,9},{9,8},{10,11... | collective-permute-start | bytes 3538952 | tf_op jit(solution)/shard_map/ppermute | solution.py:288
  101.1 23.1 %collective-permute-start.21 = (bf16[2,1,96,384]{3,2,0,1:T(8,128)(2,1)S(1)}, bf16[2,1,96,384]{3,2,0,1:T(8,128)(2,1)S(1)}, u32[]{:S(2)}, u32[]{:S(2)}) collective-permute-start(bf16[2,1,96,384]{3,2,0,1:T(8,128)(2,1)S(1)} %copy-done.146), channel_id=1, source_target_pairs={{0,8},{4,12},{8,0},{12,4},{16,24},{20,28},{24,16},{28,20},{1,9},{5... | collective-permute-start | bytes 442376 | tf_op jit(solution)/shard_map/ppermute | solution.py:288
  101.7 22.5 %collective-permute-start.22 = (bf16[2,1,96,384]{3,2,0,1:T(8,128)(2,1)S(1)}, bf16[2,1,96,384]{3,2,0,1:T(8,128)(2,1)S(1)}, u32[]{:S(2)}, u32[]{:S(2)}) collective-permute-start(bf16[2,1,96,384]{3,2,0,1:T(8,128)(2,1)S(1)} %copy-done.146), channel_id=1, source_target_pairs={{0,16},{4,20},{8,24},{12,28},{16,0},{20,4},{24,8},{28,12},{1,17},{... | collective-permute-start | bytes 442376 | tf_op jit(solution)/shard_map/ppermute | solution.py:288
  102.3 21.9 %collective-permute-start.23 = (bf16[2,1,96,384]{3,2,0,1:T(8,128)(2,1)S(1)}, bf16[2,1,96,384]{3,2,0,1:T(8,128)(2,1)S(1)}, u32[]{:S(2)}, u32[]{:S(2)}) collective-permute-start(bf16[2,1,96,384]{3,2,0,1:T(8,128)(2,1)S(1)} %copy-done.146), channel_id=1, source_target_pairs={{0,24},{4,28},{8,16},{12,20},{16,8},{20,12},{24,0},{28,4},{1,25},{... | collective-permute-start | bytes 442376 | tf_op jit(solution)/shard_map/ppermute | solution.py:288
  125.1 11.6 %collective-permute-start.29 = (bf16[1,96,768]{2,1,0:T(8,128)(2,1)S(1)}, bf16[1,96,768]{2,1,0:T(8,128)(2,1)S(1)}, u32[]{:S(2)}, u32[]{:S(2)}) collective-permute-start(bf16[1,96,768]{2,1,0:T(8,128)(2,1)S(1)} %copy-done.145), channel_id=1, source_target_pairs={{0,16},{4,20},{8,24},{12,28},{16,0},{20,4},{24,8},{28,12},{1,17},{... | collective-permute-start | bytes 442376 | tf_op jit(solution)/shard_map/ppermute | solution.py:288
  127.2 13.7 %collective-permute-start.25 = (bf16[2,768,768]{2,1,0:T(8,128)(2,1)S(1)}, bf16[2,768,768]{2,1,0:T(8,128)(2,1)S(1)}, u32[]{:S(2)}, u32[]{:S(2)}) collective-permute-start(bf16[2,768,768]{2,1,0:T(8,128)(2,1)S(1)} %pad_maximum_fusion.2), channel_id=1, source_target_pairs={{0,2},{2,0},{1,3},{3,1},{4,6},{6,4},{5,7},{7,5},{8,10},{10,8},{9,1... | collective-permute-start | bytes 7077896 | tf_op jit(solution)/shard_map/ppermute | solution.py:288
  127.8 13.2 %collective-permute-start.26 = (bf16[2,1536,384]{2,1,0:T(8,128)(2,1)S(1)}, bf16[2,1536,384]{2,1,0:T(8,128)(2,1)S(1)}, u32[]{:S(2)}, u32[]{:S(2)}) collective-permute-start(bf16[2,1536,384]{2,1,0:T(8,128)(2,1)S(1)} %bitcast.1550), channel_id=1, source_target_pairs={{0,2},{2,0},{1,3},{3,1},{4,6},{6,4},{5,7},{7,5},{8,10},{10,8},{9,1... | collective-permute-start | bytes 7077896 | tf_op jit(solution)/shard_map/ppermute | solution.py:288
  143.3 14.6 %collective-permute-start.32 = (bf16[2,96,768]{2,1,0:T(8,128)(2,1)S(1)}, bf16[2,96,768]{2,1,0:T(8,128)(2,1)S(1)}, u32[]{:S(2)}, u32[]{:S(2)}) collective-permute-start(bf16[2,96,768]{2,1,0:T(8,128)(2,1)S(1)} %maximum_bitcast_fusion.11), channel_id=1, source_target_pairs={{0,8},{4,12},{8,0},{12,4},{16,24},{20,28},{24,16},{28,20},{1,9},{5... | collective-permute-start | bytes 884744 | tf_op jit(solution)/shard_map/ppermute | solution.py:288
  143.9 14.0 %collective-permute-start.33 = (bf16[1,384,384]{2,1,0:T(8,128)(2,1)S(1)}, bf16[1,384,384]{2,1,0:T(8,128)(2,1)S(1)}, u32[]{:S(2)}, u32[]{:S(2)}) collective-permute-start(bf16[1,384,384]{2,1,0:T(8,128)(2,1)S(1)} %copy-done.141), channel_id=1, source_target_pairs={{0,16},{4,20},{8,24},{12,28},{16,0},{20,4},{24,8},{28,12},{1,17},{... | collective-permute-start | bytes 884744 | tf_op jit(solution)/shard_map/ppermute | solution.py:288
  146.4 14.1 %collective-permute-start.31 = (bf16[2,4,96,384]{3,2,1,0:T(8,128)(2,1)S(1)}, bf16[2,4,96,384]{3,2,1,0:T(8,128)(2,1)S(1)}, u32[]{:S(2)}, u32[]{:S(2)}) collective-permute-start(bf16[2,4,96,384]{3,2,1,0:T(8,128)(2,1)S(1)} %pad_maximum_fusion.34), channel_id=1, source_target_pairs={{0,4},{4,0},{8,12},{12,8},{16,20},{20,16},{24,28},{28,24},{1,5},{5... | collective-permute-start | bytes 1769480 | tf_op jit(solution)/shard_map/ppermute | solution.py:288
  147.1 13.7 %collective-permute-start.30 = (bf16[8,96,384]{2,1,0:T(8,128)(2,1)S(1)}, bf16[8,96,384]{2,1,0:T(8,128)(2,1)S(1)}, u32[]{:S(2)}, u32[]{:S(2)}) collective-permute-start(bf16[8,96,384]{2,1,0:T(8,128)(2,1)S(1)} %bitcast.1548), channel_id=1, source_target_pairs={{0,1},{1,0},{2,3},{3,2},{4,5},{5,4},{6,7},{7,6},{8,9},{9,8},{10,11... | collective-permute-start | bytes 1769480 | tf_op jit(solution)/shard_map/ppermute | solution.py:288
  166.8 21.1 %collective-permute-start.37 = (bf16[2,384,384]{2,1,0:T(8,128)(2,1)}, bf16[2,384,384]{2,1,0:T(8,128)(2,1)}, u32[]{:S(2)}, u32[]{:S(2)}) collective-permute-start(bf16[2,384,384]{2,1,0:T(8,128)(2,1)} %maximum_bitcast_fusion.5), channel_id=1, source_target_pairs={{0,8},{4,12},{8,0},{12,4},{16,24},{20,28},{24,16},{28,20},{1,9},{5... | collective-permute-start | bytes 1769480 | tf_op jit(solution)/shard_map/ppermute | solution.py:288
  168.2 19.7 %collective-permute-start.36 = (bf16[4,96,768]{2,1,0:T(8,128)(2,1)}, bf16[4,96,768]{2,1,0:T(8,128)(2,1)}, u32[]{:S(2)}, u32[]{:S(2)}) collective-permute-start(bf16[4,96,768]{2,1,0:T(8,128)(2,1)} %bitcast.133), channel_id=1, source_target_pairs={{0,4},{4,0},{8,12},{12,8},{16,20},{20,16},{24,28},{28,24},{1,5},{5... | collective-permute-start | bytes 1769480 | tf_op jit(solution)/shard_map/ppermute | solution.py:288
  199.5 28.6 %collective-permute-start.40 = (bf16[4,384,384]{2,1,0:T(8,128)(2,1)}, bf16[4,384,384]{2,1,0:T(8,128)(2,1)}, u32[]{:S(2)}, u32[]{:S(2)}) collective-permute-start(bf16[4,384,384]{2,1,0:T(8,128)(2,1)} %bitcast.157), channel_id=1, source_target_pairs={{0,4},{4,0},{8,12},{12,8},{16,20},{20,16},{24,28},{28,24},{1,5},{5... | collective-permute-start | bytes 3538952 | tf_op jit(solution)/shard_map/ppermute | solution.py:288
  200.1 28.3 %collective-permute-start.39 = (bf16[768,768]{1,0:T(8,128)(2,1)}, bf16[768,768]{1,0:T(8,128)(2,1)}, u32[]{:S(2)}, u32[]{:S(2)}) collective-permute-start(bf16[768,768]{1,0:T(8,128)(2,1)} %bitcast.154), channel_id=1, source_target_pairs={{0,1},{1,0},{2,3},{3,2},{4,5},{5,4},{6,7},{7,6},{8,9},{9,8},{10,11... | collective-permute-start | bytes 3538952 | tf_op jit(solution)/shard_map/ppermute | solution.py:288
  234.2 27.0 %collective-permute-start.44 = (bf16[1,256,768]{2,1,0:T(8,128)(2,1)}, bf16[1,256,768]{2,1,0:T(8,128)(2,1)}, u32[]{:S(2)}, u32[]{:S(2)}) collective-permute-start(bf16[1,256,768]{2,1,0:T(8,128)(2,1)} %get-tuple-element.312), channel_id=1, source_target_pairs={{0,1},{1,0},{2,3},{3,2},{4,5},{5,4},{6,7},{7,6},{8,9},{9,8},{10,11... | collective-permute-start | bytes 1179656 | tf_op jit(solution)/shard_map/ppermute | solution.py:288
  285.8 30.4 %collective-permute-start.48 = (bf16[4,384,384]{2,1,0:T(8,128)(2,1)S(1)}, bf16[4,384,384]{2,1,0:T(8,128)(2,1)S(1)}, u32[]{:S(2)}, u32[]{:S(2)}) collective-permute-start(bf16[4,384,384]{2,1,0:T(8,128)(2,1)S(1)} %dynamic-slice_bitcast_fusion.3), channel_id=1, source_target_pairs={{0,4},{4,0},{8,12},{12,8},{16,20},{20,16},{24,28},{28,24},{1,5},{5... | collective-permute-start | bytes 3538952 | tf_op jit(solution)/shard_map/ppermute | solution.py:288
  294.2 28.2 %collective-permute-start.49 = (bf16[768,768]{1,0:T(8,128)(2,1)S(1)}, bf16[768,768]{1,0:T(8,128)(2,1)S(1)}, u32[]{:S(2)}, u32[]{:S(2)}) collective-permute-start(bf16[768,768]{1,0:T(8,128)(2,1)S(1)} %dynamic-slice_bitcast_fusion.2), channel_id=1, source_target_pairs={{0,1},{1,0},{2,3},{3,2},{4,5},{5,4},{6,7},{7,6},{8,9},{9,8},{10,11... | collective-permute-start | bytes 3538952 | tf_op jit(solution)/shard_map/ppermute | solution.py:288
  322.8 18.3 %collective-permute-start.54 = (bf16[2,384,384]{2,1,0:T(8,128)(2,1)S(1)}, bf16[2,384,384]{2,1,0:T(8,128)(2,1)S(1)}, u32[]{:S(2)}, u32[]{:S(2)}) collective-permute-start(bf16[2,384,384]{2,1,0:T(8,128)(2,1)S(1)} %dynamic-slice_bitcast_fusion.10), channel_id=1, source_target_pairs={{0,8},{4,12},{8,0},{12,4},{16,24},{20,28},{24,16},{28,20},{1,9},{5... | collective-permute-start | bytes 1769480 | tf_op jit(solution)/shard_map/ppermute | solution.py:288
  324.0 17.2 %collective-permute-start.53 = (bf16[4,96,768]{2,1,0:T(8,128)(2,1)S(1)}, bf16[4,96,768]{2,1,0:T(8,128)(2,1)S(1)}, u32[]{:S(2)}, u32[]{:S(2)}) collective-permute-start(bf16[4,96,768]{2,1,0:T(8,128)(2,1)S(1)} %dynamic-slice_bitcast_fusion.11), channel_id=1, source_target_pairs={{0,4},{4,0},{8,12},{12,8},{16,20},{20,16},{24,28},{28,24},{1,5},{5... | collective-permute-start | bytes 1769480 | tf_op jit(solution)/shard_map/ppermute | solution.py:288
  345.4 33.3 %collective-permute-start.62 = (bf16[1,384,384]{2,1,0:T(8,128)(2,1)S(1)}, bf16[1,384,384]{2,1,0:T(8,128)(2,1)S(1)}, u32[]{:S(2)}, u32[]{:S(2)}) collective-permute-start(bf16[1,384,384]{2,1,0:T(8,128)(2,1)S(1)} %constant_dynamic-slice_fusion.10), channel_id=1, source_target_pairs={{0,16},{4,20},{8,24},{12,28},{16,0},{20,4},{24,8},{28,12},{1,17},{... | collective-permute-start | bytes 884744 | tf_op jit(solution)/shard_map/ppermute | solution.py:288
  345.9 12.9 %collective-permute-start.57 = (bf16[2,96,768]{2,1,0:T(8,128)(2,1)S(1)}, bf16[2,96,768]{2,1,0:T(8,128)(2,1)S(1)}, u32[]{:S(2)}, u32[]{:S(2)}) collective-permute-start(bf16[2,96,768]{2,1,0:T(8,128)(2,1)S(1)} %dynamic-slice_bitcast_fusion.17), channel_id=1, source_target_pairs={{0,8},{4,12},{8,0},{12,4},{16,24},{20,28},{24,16},{28,20},{1,9},{5... | collective-permute-start | bytes 884744 | tf_op jit(solution)/shard_map/ppermute | solution.py:288
  348.1 14.8 %collective-permute-start.55 = (bf16[8,96,384]{2,1,0:T(8,128)(2,1)S(1)}, bf16[8,96,384]{2,1,0:T(8,128)(2,1)S(1)}, u32[]{:S(2)}, u32[]{:S(2)}) collective-permute-start(bf16[8,96,384]{2,1,0:T(8,128)(2,1)S(1)} %dynamic-slice_bitcast_fusion.9), channel_id=1, source_target_pairs={{0,1},{1,0},{2,3},{3,2},{4,5},{5,4},{6,7},{7,6},{8,9},{9,8},{10,11... | collective-permute-start | bytes 1769480 | tf_op jit(solution)/shard_map/ppermute | solution.py:288
  349.1 14.5 %collective-permute-start.56 = (bf16[2,4,96,384]{3,2,1,0:T(8,128)(2,1)S(1)}, bf16[2,4,96,384]{3,2,1,0:T(8,128)(2,1)S(1)}, u32[]{:S(2)}, u32[]{:S(2)}) collective-permute-start(bf16[2,4,96,384]{3,2,1,0:T(8,128)(2,1)S(1)} %dynamic-slice_bitcast_fusion.8), channel_id=1, source_target_pairs={{0,4},{4,0},{8,12},{12,8},{16,20},{20,16},{24,28},{28,24},{1,5},{5... | collective-permute-start | bytes 1769480 | tf_op jit(solution)/shard_map/ppermute | solution.py:288
  364.0 14.7 %collective-permute-start.61 = (bf16[1,96,768]{2,1,0:T(8,128)(2,1)S(1)}, bf16[1,96,768]{2,1,0:T(8,128)(2,1)S(1)}, u32[]{:S(2)}, u32[]{:S(2)}) collective-permute-start(bf16[1,96,768]{2,1,0:T(8,128)(2,1)S(1)} %constant_dynamic-slice_fusion.11), channel_id=1, source_target_pairs={{0,16},{4,20},{8,24},{12,28},{16,0},{20,4},{24,8},{28,12},{1,17},{... | collective-permute-start | bytes 442376 | tf_op jit(solution)/shard_map/ppermute | solution.py:288
  366.5 12.2 %collective-permute-start.60 = (bf16[4,96,384]{2,1,0:T(8,128)(2,1)S(1)}, bf16[4,96,384]{2,1,0:T(8,128)(2,1)S(1)}, u32[]{:S(2)}, u32[]{:S(2)}) collective-permute-start(bf16[4,96,384]{2,1,0:T(8,128)(2,1)S(1)} %dynamic-slice_bitcast_fusion.15), channel_id=1, source_target_pairs={{0,1},{1,0},{2,3},{3,2},{4,5},{5,4},{6,7},{7,6},{8,9},{9,8},{10,11... | collective-permute-start | bytes 884744 | tf_op jit(solution)/shard_map/ppermute | solution.py:288
  367.7 11.0 %collective-permute-start.59 = (bf16[4,96,384]{2,1,0:T(8,128)(2,1)S(1)}, bf16[4,96,384]{2,1,0:T(8,128)(2,1)S(1)}, u32[]{:S(2)}, u32[]{:S(2)}) collective-permute-start(bf16[4,96,384]{2,1,0:T(8,128)(2,1)S(1)} %dynamic-slice_bitcast_fusion.16), channel_id=1, source_target_pairs={{0,4},{4,0},{8,12},{12,8},{16,20},{20,16},{24,28},{28,24},{1,5},{5... | collective-permute-start | bytes 884744 | tf_op jit(solution)/shard_map/ppermute | solution.py:288
  368.3 10.4 %collective-permute-start.58 = (bf16[2,1536,384]{2,1,0:T(8,128)(2,1)S(1)}, bf16[2,1536,384]{2,1,0:T(8,128)(2,1)S(1)}, u32[]{:S(2)}, u32[]{:S(2)}) collective-permute-start(bf16[2,1536,384]{2,1,0:T(8,128)(2,1)S(1)} %pad_maximum_fusion.6), channel_id=1, source_target_pairs={{0,2},{2,0},{1,3},{3,1},{4,6},{6,4},{5,7},{7,5},{8,10},{10,8},{9,1... | collective-permute-start | bytes 7077896 | tf_op jit(solution)/shard_map/ppermute | solution.py:288
  378.8 14.6 %collective-permute-start.69 = (bf16[96,768]{1,0:T(8,128)(2,1)S(1)}, bf16[96,768]{1,0:T(8,128)(2,1)S(1)}, u32[]{:S(2)}, u32[]{:S(2)}) collective-permute-start(bf16[96,768]{1,0:T(8,128)(2,1)S(1)} %fusion.436), channel_id=1, source_target_pairs={{0,3},{1,2},{2,1},{3,0},{4,7},{5,6},{6,5},{7,4},{8,11},{9,10},{10,... | collective-permute-start | bytes 442376 | tf_op jit(solution)/shard_map/ppermute | solution.py:288
  380.0 14.0 %collective-permute-start.68 = (bf16[96,768]{1,0:T(8,128)(2,1)S(1)}, bf16[96,768]{1,0:T(8,128)(2,1)S(1)}, u32[]{:S(2)}, u32[]{:S(2)}) collective-permute-start(bf16[96,768]{1,0:T(8,128)(2,1)S(1)} %fusion.436), channel_id=1, source_target_pairs={{0,2},{2,0},{1,3},{3,1},{4,6},{6,4},{5,7},{7,5},{8,10},{10,8},{9,1... | collective-permute-start | bytes 442376 | tf_op jit(solution)/shard_map/ppermute | solution.py:288
  380.0 14.7 %collective-permute-start.67 = (bf16[96,768]{1,0:T(8,128)(2,1)S(1)}, bf16[96,768]{1,0:T(8,128)(2,1)S(1)}, u32[]{:S(2)}, u32[]{:S(2)}) collective-permute-start(bf16[96,768]{1,0:T(8,128)(2,1)S(1)} %fusion.436), channel_id=1, source_target_pairs={{0,1},{1,0},{2,3},{3,2},{4,5},{5,4},{6,7},{7,6},{8,9},{9,8},{10,11... | collective-permute-start | bytes 442376 | tf_op jit(solution)/shard_map/ppermute | solution.py:288
  381.2 28.1 %collective-permute-start.70 = (bf16[384,384]{1,0:T(8,128)(2,1)S(1)}, bf16[384,384]{1,0:T(8,128)(2,1)S(1)}, u32[]{:S(2)}, u32[]{:S(2)}) collective-permute-start(bf16[384,384]{1,0:T(8,128)(2,1)S(1)} %fusion.422), channel_id=1, source_target_pairs={{0,1},{1,0},{2,3},{3,2},{4,5},{5,4},{6,7},{7,6},{8,9},{9,8},{10,11... | collective-permute-start | bytes 884744 | tf_op jit(solution)/shard_map/ppermute | solution.py:288
  390.9 18.3 %collective-permute-start.63 = (bf16[2,768,768]{2,1,0:T(8,128)(2,1)S(1)}, bf16[2,768,768]{2,1,0:T(8,128)(2,1)S(1)}, u32[]{:S(2)}, u32[]{:S(2)}) collective-permute-start(bf16[2,768,768]{2,1,0:T(8,128)(2,1)S(1)} %pad_maximum_fusion.7), channel_id=1, source_target_pairs={{0,2},{2,0},{1,3},{3,1},{4,6},{6,4},{5,7},{7,5},{8,10},{10,8},{9,1... | collective-permute-start | bytes 7077896 | tf_op jit(solution)/shard_map/ppermute | solution.py:288
  394.0 10.7 %collective-permute-start.64 = (bf16[2,96,384]{2,1,0:T(8,128)(2,1)S(1)}, bf16[2,96,384]{2,1,0:T(8,128)(2,1)S(1)}, u32[]{:S(2)}, u32[]{:S(2)}) collective-permute-start(bf16[2,96,384]{2,1,0:T(8,128)(2,1)S(1)} %get-tuple-element.619), channel_id=1, source_target_pairs={{0,8},{4,12},{8,0},{12,4},{16,24},{20,28},{24,16},{28,20},{1,9},{5... | collective-permute-start | bytes 442376 | tf_op jit(solution)/shard_map/ppermute | solution.py:288
  394.7 14.5 %collective-permute-start.65 = (bf16[2,96,384]{2,1,0:T(8,128)(2,1)S(1)}, bf16[2,96,384]{2,1,0:T(8,128)(2,1)S(1)}, u32[]{:S(2)}, u32[]{:S(2)}) collective-permute-start(bf16[2,96,384]{2,1,0:T(8,128)(2,1)S(1)} %get-tuple-element.620), channel_id=1, source_target_pairs={{0,16},{4,20},{8,24},{12,28},{16,0},{20,4},{24,8},{28,12},{1,17},{... | collective-permute-start | bytes 442376 | tf_op jit(solution)/shard_map/ppermute | solution.py:288
  418.4 28.1 %collective-permute-start.76 = (bf16[4,384,384]{2,1,0:T(8,128)(2,1)S(1)}, bf16[4,384,384]{2,1,0:T(8,128)(2,1)S(1)}, u32[]{:S(2)}, u32[]{:S(2)}) collective-permute-start(bf16[4,384,384]{2,1,0:T(8,128)(2,1)S(1)} %dynamic-slice_bitcast_fusion.1), channel_id=1, source_target_pairs={{0,4},{4,0},{8,12},{12,8},{16,20},{20,16},{24,28},{28,24},{1,5},{5... | collective-permute-start | bytes 3538952 | tf_op jit(solution)/shard_map/ppermute | solution.py:288
  419.8 27.7 %collective-permute-start.77 = (bf16[768,768]{1,0:T(8,128)(2,1)S(1)}, bf16[768,768]{1,0:T(8,128)(2,1)S(1)}, u32[]{:S(2)}, u32[]{:S(2)}) collective-permute-start(bf16[768,768]{1,0:T(8,128)(2,1)S(1)} %dynamic-slice_bitcast_fusion), channel_id=1, source_target_pairs={{0,1},{1,0},{2,3},{3,2},{4,5},{5,4},{6,7},{7,6},{8,9},{9,8},{10,11... | collective-permute-start | bytes 3538952 | tf_op jit(solution)/shard_map/ppermute | solution.py:288
  447.8 30.4 %collective-permute-start.84 = (bf16[4,96,768]{2,1,0:T(8,128)(2,1)S(1)}, bf16[4,96,768]{2,1,0:T(8,128)(2,1)S(1)}, u32[]{:S(2)}, u32[]{:S(2)}) collective-permute-start(bf16[4,96,768]{2,1,0:T(8,128)(2,1)S(1)} %dynamic-slice_bitcast_fusion.4), channel_id=1, source_target_pairs={{0,4},{4,0},{8,12},{12,8},{16,20},{20,16},{24,28},{28,24},{1,5},{5... | collective-permute-start | bytes 1769480 | tf_op jit(solution)/shard_map/ppermute | solution.py:288
  449.1 15.5 %collective-permute-start.79 = (bf16[2,384,384]{2,1,0:T(8,128)(2,1)S(1)}, bf16[2,384,384]{2,1,0:T(8,128)(2,1)S(1)}, u32[]{:S(2)}, u32[]{:S(2)}) collective-permute-start(bf16[2,384,384]{2,1,0:T(8,128)(2,1)S(1)} %dynamic-slice_bitcast_fusion.7), channel_id=1, source_target_pairs={{0,8},{4,12},{8,0},{12,4},{16,24},{20,28},{24,16},{28,20},{1,9},{5... | collective-permute-start | bytes 1769480 | tf_op jit(solution)/shard_map/ppermute | solution.py:288
  467.9 16.0 %collective-permute-start.85 = (bf16[1,384,384]{2,1,0:T(8,128)(2,1)S(1)}, bf16[1,384,384]{2,1,0:T(8,128)(2,1)S(1)}, u32[]{:S(2)}, u32[]{:S(2)}) collective-permute-start(bf16[1,384,384]{2,1,0:T(8,128)(2,1)S(1)} %constant_dynamic-slice_fusion.7), channel_id=1, source_target_pairs={{0,16},{4,20},{8,24},{12,28},{16,0},{20,4},{24,8},{28,12},{1,17},{... | collective-permute-start | bytes 884744 | tf_op jit(solution)/shard_map/ppermute | solution.py:288
  475.4 15.1 %collective-permute-start.82 = (bf16[8,96,384]{2,1,0:T(8,128)(2,1)S(1)}, bf16[8,96,384]{2,1,0:T(8,128)(2,1)S(1)}, u32[]{:S(2)}, u32[]{:S(2)}) collective-permute-start(bf16[8,96,384]{2,1,0:T(8,128)(2,1)S(1)} %dynamic-slice_bitcast_fusion.6), channel_id=1, source_target_pairs={{0,1},{1,0},{2,3},{3,2},{4,5},{5,4},{6,7},{7,6},{8,9},{9,8},{10,11... | collective-permute-start | bytes 1769480 | tf_op jit(solution)/shard_map/ppermute | solution.py:288
  476.6 14.8 %collective-permute-start.83 = (bf16[2,4,96,384]{3,2,1,0:T(8,128)(2,1)S(1)}, bf16[2,4,96,384]{3,2,1,0:T(8,128)(2,1)S(1)}, u32[]{:S(2)}, u32[]{:S(2)}) collective-permute-start(bf16[2,4,96,384]{3,2,1,0:T(8,128)(2,1)S(1)} %dynamic-slice_bitcast_fusion.5), channel_id=1, source_target_pairs={{0,4},{4,0},{8,12},{12,8},{16,20},{20,16},{24,28},{28,24},{1,5},{5... | collective-permute-start | bytes 1769480 | tf_op jit(solution)/shard_map/ppermute | solution.py:288
  494.9 10.6 %collective-permute-start.87 = (bf16[4,96,384]{2,1,0:T(8,128)(2,1)}, bf16[4,96,384]{2,1,0:T(8,128)(2,1)}, u32[]{:S(2)}, u32[]{:S(2)}) collective-permute-start(bf16[4,96,384]{2,1,0:T(8,128)(2,1)} %dynamic-slice_bitcast_fusion.13), channel_id=1, source_target_pairs={{0,1},{1,0},{2,3},{3,2},{4,5},{5,4},{6,7},{7,6},{8,9},{9,8},{10,11... | collective-permute-start | bytes 884744 | tf_op jit(solution)/shard_map/ppermute | solution.py:288
  514.5 14.8 %collective-permute-start.93 = (bf16[1,96,768]{2,1,0:T(8,128)(2,1)S(1)}, bf16[1,96,768]{2,1,0:T(8,128)(2,1)S(1)}, u32[]{:S(2)}, u32[]{:S(2)}) collective-permute-start(bf16[1,96,768]{2,1,0:T(8,128)(2,1)S(1)} %constant_dynamic-slice_fusion.6), channel_id=1, source_target_pairs={{0,16},{4,20},{8,24},{12,28},{16,0},{20,4},{24,8},{28,12},{1,17},{... | collective-permute-start | bytes 442376 | tf_op jit(solution)/shard_map/ppermute | solution.py:288
  517.1 12.1 %collective-permute-start.92 = (bf16[2,96,384]{2,1,0:T(8,128)(2,1)S(1)}, bf16[2,96,384]{2,1,0:T(8,128)(2,1)S(1)}, u32[]{:S(2)}, u32[]{:S(2)}) collective-permute-start(bf16[2,96,384]{2,1,0:T(8,128)(2,1)S(1)} %get-tuple-element.615), channel_id=1, source_target_pairs={{0,24},{4,28},{8,16},{12,20},{16,8},{20,12},{24,0},{28,4},{1,25},{... | collective-permute-start | bytes 442376 | tf_op jit(solution)/shard_map/ppermute | solution.py:288
  518.8 11.4 %collective-permute-start.90 = (bf16[2,96,384]{2,1,0:T(8,128)(2,1)S(1)}, bf16[2,96,384]{2,1,0:T(8,128)(2,1)S(1)}, u32[]{:S(2)}, u32[]{:S(2)}) collective-permute-start(bf16[2,96,384]{2,1,0:T(8,128)(2,1)S(1)} %get-tuple-element.616), channel_id=1, source_target_pairs={{0,8},{4,12},{8,0},{12,4},{16,24},{20,28},{24,16},{28,20},{1,9},{5... | collective-permute-start | bytes 442376 | tf_op jit(solution)/shard_map/ppermute | solution.py:288
  518.9 18.2 %collective-permute-start.91 = (bf16[2,96,384]{2,1,0:T(8,128)(2,1)S(1)}, bf16[2,96,384]{2,1,0:T(8,128)(2,1)S(1)}, u32[]{:S(2)}, u32[]{:S(2)}) collective-permute-start(bf16[2,96,384]{2,1,0:T(8,128)(2,1)S(1)} %get-tuple-element.617), channel_id=1, source_target_pairs={{0,16},{4,20},{8,24},{12,28},{16,0},{20,4},{24,8},{28,12},{1,17},{... | collective-permute-start | bytes 442376 | tf_op jit(solution)/shard_map/ppermute | solution.py:288
  522.7 15.7 %collective-permute-start.106 = (bf16[1,256,768]{2,1,0:T(8,128)(2,1)S(1)}, bf16[1,256,768]{2,1,0:T(8,128)(2,1)S(1)}, u32[]{:S(2)}, u32[]{:S(2)}) collective-permute-start(bf16[1,256,768]{2,1,0:T(8,128)(2,1)S(1)} %copy-done.140), channel_id=1, source_target_pairs={{0,1},{1,0},{2,3},{3,2},{4,5},{5,4},{6,7},{7,6},{8,9},{9,8},{10,11... | collective-permute-start | bytes 1179656 | tf_op jit(solution)/shard_map/ppermute | solution.py:288
  529.3 14.7 %collective-permute-start.103 = (bf16[384,384]{1,0:T(8,128)(2,1)S(1)}, bf16[384,384]{1,0:T(8,128)(2,1)S(1)}, u32[]{:S(2)}, u32[]{:S(2)}) collective-permute-start(bf16[384,384]{1,0:T(8,128)(2,1)S(1)} %add_convert_fusion.14), channel_id=1, source_target_pairs={{0,2},{2,0},{1,3},{3,1},{4,6},{6,4},{5,7},{7,5},{8,10},{10,8},{9,1... | collective-permute-start | bytes 884744 | tf_op jit(solution)/shard_map/ppermute | solution.py:288
  529.3 25.1 %collective-permute-start.104 = (bf16[1,256,768]{2,1,0:T(8,128)(2,1)S(1)}, bf16[1,256,768]{2,1,0:T(8,128)(2,1)S(1)}, u32[]{:S(2)}, u32[]{:S(2)}) collective-permute-start(bf16[1,256,768]{2,1,0:T(8,128)(2,1)S(1)} %fusion.351), channel_id=1, source_target_pairs={{0,1},{1,0},{2,3},{3,2},{4,5},{5,4},{6,7},{7,6},{8,9},{9,8},{10,11... | collective-permute-start | bytes 1179656 | tf_op jit(solution)/shard_map/ppermute | solution.py:288
  554.3 13.2 %collective-permute-start.109 = (f32[24,768]{1,0:T(8,128)S(1)}, f32[24,768]{1,0:T(8,128)S(1)}, u32[]{:S(2)}, u32[]{:S(2)}) collective-permute-start(f32[24,768]{1,0:T(8,128)S(1)} %add.1030), channel_id=1, source_target_pairs={{0,24},{4,28},{8,16},{12,20},{16,8},{20,12},{24,0},{28,4},{1,25},{... | collective-permute-start | bytes 221192 | tf_op jit(solution)/shard_map/ppermute | solution.py:288
  556.7 10.9 %collective-permute-start.108 = (f32[24,768]{1,0:T(8,128)S(1)}, f32[24,768]{1,0:T(8,128)S(1)}, u32[]{:S(2)}, u32[]{:S(2)}) collective-permute-start(f32[24,768]{1,0:T(8,128)S(1)} %add.1030), channel_id=1, source_target_pairs={{0,16},{4,20},{8,24},{12,28},{16,0},{20,4},{24,8},{28,12},{1,17},{... | collective-permute-start | bytes 221192 | tf_op jit(solution)/shard_map/ppermute | solution.py:288
  (231 other events, 1486.5 us)

commit v5 on v4

--- a/solution.py
+++ b/solution.py
@@ -556,7 +556,6 @@
 
     own, other = attention.result
     normed = normalize(residual, first_gain, first_shift).astype(LOW)
-    normed = cut(normed, up_flow, down_flow)
     query_biases, value_biases = halves_of(query_bias), halves_of(value_bias)
 
     def project(weights, i):
@@ -569,7 +568,8 @@
             ]
         )
 
-    away = swap(project(other, 1), "blk")
+    theirs, normed = cut((project(other, 1), normed), up_flow, down_flow)
+    away = swap(theirs, "blk")
     mine = project(own, 0)
     mine, away = cut((mine, away), *with_next(next_attention))
     mixed_mine, mixed_theirs, logsum = attend(core, mine, away)
@@ -683,7 +683,6 @@
         (grads_mine, grads_away, middle_slope),
         attention_flow,
         *before,
-        *([down_flow] if lowest else []),
     )
     query_bias_slope = side_by_side(token_sum(grads_mine[0]), token_sum(grads_away[0]), bit)
     value_bias_slope = side_by_side(token_sum(grads_mine[2]), token_sum(grads_away[2]), bit)
@@ -696,7 +695,7 @@
             + transposed(grads[2], last[0])
         )
     if lowest:
-        first_slope = cut(first_slope, attention_flow)
+        first_slope = cut(first_slope, attention_flow, down_flow)
     through, first_gain_slope, first_shift_slope = norm_backward(residual, first_gain, first_slope)
     upstream = middle_slope + through
     upstream = cut(upstream, attention_flow, up_flow, down_flow, *before)

time: 576 us -> 563 us (0.977)
  waiting for transfers between devices: 148 us -> 139 us
    ppermute x110, waiting for transfers between devices: 148 us -> 139 us  [swap(): return lax.ppermute(item, axis, [(i, i ^ mask) for i in range(count)])]
    unnamed x382 -> x380, local copies, waits for them, and re-layouts: 26.1 us -> 27.2 us
  transfers between devices with their start and end apart: 110 -> 110, of which waited for: 39 -> 41; matrix products, arithmetic and copies ran while one was open for 30% -> 32% of each run, Pallas kernels for 10% -> 10%
where the time goes in v5:
time: 563 us; the launch traced here: 557 us
  waiting for transfers between devices  139 us (25%)
  starting transfers between devices  102 us (18%)
  matrix products  102 us (18%)
  other arithmetic  94 us (17%)
  local copies, waits for them, and re-layouts  59.5 us (11%)
  Pallas kernels  55.2 us (10%)
    ppermute x110, waiting for transfers between devices, swap(): return lax.ppermute(item, axis, [(i, i ^ mask) for i in range(count)])  139 us
    ppermute x110, starting transfers between devices, swap(): return lax.ppermute(item, axis, [(i, i ^ mask) for i in range(count)])  102 us
    dot_general x32, matrix products, matmul(): return jnp.dot(left, right, preferred_element_type=FULL)  42.8 us
    dot_general x32, matrix products, transposed(): return jnp.einsum('ste,de->std', left, right, preferred_element_type=FULL)  34.7 us
    pallas_call x2, Pallas kernels, attend_back(): pl.pallas_call(attend_back_kernel, grid_spec=pltpu.PrefetchScalarGridSpec...  32 us
    unnamed x380, local copies, waits for them, and re-layouts  27.2 us
    another operation x64, other arithmetic, ordered(): return jnp.stack([low, high], axis=axis)  25.9 us
    dot_general x32, matrix products, contract(): jnp.einsum('std,ste->de', left, right, preferred_element_type=FULL)  24.8 us
  transfers between devices with their start and end apart: 110, of which 41 were waited for; matrix products, arithmetic and copies ran while one was open for 32% of the time, Pallas kernels for 10%

profile of v5, /device:TPU:0, one launch (start us, length us, event | category | flops | bytes accessed | tf_op | source)
XLA Modules:
  0.0 556.8 jit_solution(17476116312367110633)
XLA Ops:
  3.1 1.7 slice_bitcast_fusion.22
  7.4 4.0 collective-permute-start.4
  13.3 2.5 collective-permute-start.2
  22.1 4.4 collective-permute-done.1
  26.5 2.8 collective-permute-start.7
  36.0 1.8 collective-permute-done.8
  42.4 2.2 collective-permute-start.13
  49.2 5.5 collective-permute-done.12
  54.8 3.2 collective-permute-done.11
  60.4 1.8 select_bitcast_fusion.22
  64.4 1.8 fusion.470
  73.1 1.9 fusion.178
  78.5 5.8 %collective-permute-done.17 = bf16[2,384,384]{2,1,0:T(8,128)(2,1)} collective-permute-done((bf16[2,384,384]{2,1,0:T(8,128)(2,1)}, bf16[2,384,384]{2,1,0:T(8,128)(2,1)}, u32[]{:S(2)}, u32[]{:S(2)}) %collective-permute-start.17) | collective-permute-done | bytes 589856 | tf_op jit(solution)/shard_map/ppermute | solution.py:288
  84.3 3.0 collective-permute-done.16
  97.2 3.2 collective-permute-start.23
  101.0 11.6 %attend.2 = (bf16[1,512,384]{2,1,0:T(8,128)(2,1)S(1)}, bf16[1,512,384]{2,1,0:T(8,128)(2,1)S(1)}, f32[1,3,8,1024]{3,2,1,0:T(8,128)S(1)}) custom-call(s32[1]{0:T(128)} %bitcast.68.core_ref, bf16[3,1,512,384]{3,2,1,0:T(8,128)(2,1)S(1)} %pad_maximum_fusion.16.mine_ref, bf16[3,1,512,384]{3,2,1,0:T(8,128)(2,1)S(1)} %collective-permute-done.18.theirs_ref), custom_call_target="tpu_custom_call" | custom-call | tf_op jit(solution)/shard_map/attend/pallas_call | solution.py:100
  112.6 6.1 %collective-permute-done.20 = bf16[4,384,384]{2,1,0:T(8,128)(2,1)S(1)} collective-permute-done((bf16[4,384,384]{2,1,0:T(8,128)(2,1)S(1)}, bf16[4,384,384]{2,1,0:T(8,128)(2,1)S(1)}, u32[]{:S(2)}, u32[]{:S(2)}) %collective-permute-start.20) | collective-permute-done | bytes 1179680 | tf_op jit(solution)/shard_map/ppermute | solution.py:288
  132.3 3.4 collective-permute-done.28
  138.8 2.4 collective-permute-start.33
  152.8 2.6 collective-permute-done.31
  166.2 9.2 %fusion.120 = f32[512,384]{1,0:T(8,128)S(1)} fusion(bf16[1,512,1536]{2,1,0:T(8,128)(2,1)S(1)} %copy-done.99, bf16[2,1536,384]{2,1,0:T(8,128)(2,1)S(1)} %copy-done.57), kind=kOutput, calls=%fused_computation.219 | convolution fusion | flops 603979776 | bytes 3538944 | tf_op jit(solution)/shard_map/dot_general | solution.py:275
  182.7 1.9 fusion.180
  200.4 11.6 %attend.3 = (bf16[1,512,384]{2,1,0:T(8,128)(2,1)S(1)}, bf16[1,512,384]{2,1,0:T(8,128)(2,1)S(1)}, f32[1,3,8,1024]{3,2,1,0:T(8,128)S(1)}) custom-call(s32[1]{0:T(128)} %bitcast.68.core_ref, bf16[3,1,512,384]{3,2,1,0:T(8,128)(2,1)S(1)} %pad_maximum_fusion.21.mine_ref, bf16[3,1,512,384]{3,2,1,0:T(8,128)(2,1)S(1)} %collective-permute-done.38.theirs_ref), custom_call_target="tpu_custom_call" | custom-call | tf_op jit(solution)/shard_map/attend/pallas_call | solution.py:100
  212.0 11.0 %collective-permute-done.39 = bf16[768,768]{1,0:T(8,128)(2,1)} collective-permute-done((bf16[768,768]{1,0:T(8,128)(2,1)}, bf16[768,768]{1,0:T(8,128)(2,1)}, u32[]{:S(2)}, u32[]{:S(2)}) %collective-permute-start.39) | collective-permute-done | bytes 1179680 | tf_op jit(solution)/shard_map/ppermute | solution.py:288
  224.2 1.8 broadcast_select_fusion.1
  226.1 2.6 select_bitcast_fusion.1
  233.8 1.8 select_bitcast_fusion.7
  248.9 2.9 fusion.106
  265.5 2.3 fusion.497
  270.9 2.5 fusion.495
  291.0 1.7 fusion.148
  295.4 16.0 %attend_back.2 = (bf16[3,1,512,384]{3,2,1,0:T(8,128)(2,1)S(1)}, bf16[3,1,512,384]{3,2,1,0:T(8,128)(2,1)S(1)}) custom-call(s32[1]{0:T(128)} %bitcast.68.core_ref, bf16[3,1,512,384]{3,2,1,0:T(8,128)(2,1)S(1)} %pad_maximum_fusion.21.mine_ref, bf16[3,1,512,384]{3,2,1,0:T(8,128)(2,1)S(1)} %collective-permute-done.38.theirs_ref, ...), custom_call_target="tpu_custom_call" | custom-call | tf_op jit(solution)/shard_map/attend_back/pallas_call | solution.py:190
  311.4 6.2 %collective-permute-done.49 = bf16[768,768]{1,0:T(8,128)(2,1)S(1)} collective-permute-done((bf16[768,768]{1,0:T(8,128)(2,1)S(1)}, bf16[768,768]{1,0:T(8,128)(2,1)S(1)}, u32[]{:S(2)}, u32[]{:S(2)}) %collective-permute-start.49) | collective-permute-done | bytes 1179680 | tf_op jit(solution)/shard_map/ppermute | solution.py:288
  327.1 1.7 fusion.317
  328.8 1.8 fusion.320
  331.2 2.4 fusion.77
  347.6 5.7 %collective-permute-done.57 = bf16[2,96,768]{2,1,0:T(8,128)(2,1)S(1)} collective-permute-done((bf16[2,96,768]{2,1,0:T(8,128)(2,1)S(1)}, bf16[2,96,768]{2,1,0:T(8,128)(2,1)S(1)}, u32[]{:S(2)}, u32[]{:S(2)}) %collective-permute-start.57) | collective-permute-done | bytes 294944 | tf_op jit(solution)/shard_map/ppermute | solution.py:288
  353.3 4.3 collective-permute-done.55
  358.9 2.1 collective-permute-start.61
  368.7 2.3 fusion.505
  371.0 2.7 fusion.503
  389.8 3.3 collective-permute-start.65
  394.6 2.6 collective-permute-done.66
  397.1 2.8 collective-permute-done.64
  399.9 4.6 collective-permute-done.65
  408.7 1.7 fusion.149
  415.7 16.0 %attend_back.3 = (bf16[3,1,512,384]{3,2,1,0:T(8,128)(2,1)S(1)}, bf16[3,1,512,384]{3,2,1,0:T(8,128)(2,1)S(1)}) custom-call(s32[1]{0:T(128)} %bitcast.68.core_ref, bf16[3,1,512,384]{3,2,1,0:T(8,128)(2,1)S(1)} %copy-done.1, bf16[3,1,512,384]{3,2,1,0:T(8,128)(2,1)S(1)} %copy-done.3, f32[1,3,8,1024]{3,2,1,0:T(8,128)S(1)} %get-tuple-element.261.logsum_ref, ...), custom_call_target="tpu_custom_call" | custom-call | tf_op jit(solution)/shard_map/attend_back/pallas_call | solution.py:190
  432.7 9.0 %collective-permute-done.76 = bf16[4,384,384]{2,1,0:T(8,128)(2,1)S(1)} collective-permute-done((bf16[4,384,384]{2,1,0:T(8,128)(2,1)S(1)}, bf16[4,384,384]{2,1,0:T(8,128)(2,1)S(1)}, u32[]{:S(2)}, u32[]{:S(2)}) %collective-permute-start.76) | collective-permute-done | bytes 1179680 | tf_op jit(solution)/shard_map/ppermute | solution.py:288
  452.3 1.7 fusion.328
  453.9 1.7 fusion.331
  455.6 1.9 add_bitcast_fusion
  457.6 2.2 collective-permute-done.81
  465.0 11.5 %collective-permute-done.85 = bf16[1,384,384]{2,1,0:T(8,128)(2,1)S(1)} collective-permute-done((bf16[1,384,384]{2,1,0:T(8,128)(2,1)S(1)}, bf16[1,384,384]{2,1,0:T(8,128)(2,1)S(1)}, u32[]{:S(2)}, u32[]{:S(2)}) %collective-permute-start.85) | collective-permute-done | bytes 294944 | tf_op jit(solution)/shard_map/ppermute | solution.py:288
  487.6 3.3 concatenate.282
  492.2 3.9 collective-permute-done.88
  502.3 1.8 collective-permute-start.92
  505.2 1.8 collective-permute-start.91
  509.5 5.6 %collective-permute-done.93 = bf16[1,96,768]{2,1,0:T(8,128)(2,1)S(1)} collective-permute-done((bf16[1,96,768]{2,1,0:T(8,128)(2,1)S(1)}, bf16[1,96,768]{2,1,0:T(8,128)(2,1)S(1)}, u32[]{:S(2)}, u32[]{:S(2)}) %collective-permute-start.93) | collective-permute-done | bytes 147488 | tf_op jit(solution)/shard_map/ppermute | solution.py:288
  516.2 7.6 %collective-permute-done.91 = bf16[2,96,384]{2,1,0:T(8,128)(2,1)S(1)} collective-permute-done((bf16[2,96,384]{2,1,0:T(8,128)(2,1)S(1)}, bf16[2,96,384]{2,1,0:T(8,128)(2,1)S(1)}, u32[]{:S(2)}, u32[]{:S(2)}) %collective-permute-start.91) | collective-permute-done | bytes 147488 | tf_op jit(solution)/shard_map/ppermute | solution.py:288
  526.3 3.6 collective-permute-done.105
  533.1 3.2 collective-permute-done.97
  537.7 3.7 collective-permute-done.100
  541.4 1.9 collective-permute-start.109
  543.3 3.2 collective-permute-start.108
  (996 shorter events, 286.7 us)
Async XLA Ops:
  7.4 14.7 %collective-permute-start.4 = (bf16[1,24,96]{2,1,0:T(8,128)(2,1)S(1)}, bf16[1,24,96]{2,1,0:T(8,128)(2,1)S(1)}, u32[]{:S(2)}, u32[]{:S(2)}) collective-permute-start(bf16[1,24,96]{2,1,0:T(8,128)(2,1)S(1)} %broadcast_in_dim_reshape.3), channel_id=1, source_target_pairs={{0,16},{4,20},{8,24},{12,28},{16,0},{20,4},{24,8},{28,12},{1,17},{... | collective-permute-start | bytes 13832 | tf_op jit(solution)/shard_map/ppermute | solution.py:288
  11.4 10.6 %collective-permute-start = (bf16[2,1,96,384]{3,2,0,1:T(8,128)(2,1)}, bf16[2,1,96,384]{3,2,0,1:T(8,128)(2,1)}, u32[]{:S(2)}, u32[]{:S(2)}) collective-permute-start(bf16[2,1,96,384]{3,2,0,1:T(8,128)(2,1)} %maximum_bitcast_fusion.12), channel_id=1, source_target_pairs={{0,8},{4,12},{8,0},{12,4},{16,24},{20,28},{24,16},{28,20},{1,9},{5... | collective-permute-start | bytes 442376 | tf_op jit(solution)/shard_map/ppermute | solution.py:288
  13.0 13.5 %collective-permute-start.1 = (bf16[2,1,96,384]{3,2,0,1:T(8,128)(2,1)}, bf16[2,1,96,384]{3,2,0,1:T(8,128)(2,1)}, u32[]{:S(2)}, u32[]{:S(2)}) collective-permute-start(bf16[2,1,96,384]{3,2,0,1:T(8,128)(2,1)} %maximum_bitcast_fusion.12), channel_id=1, source_target_pairs={{0,16},{4,20},{8,24},{12,28},{16,0},{20,4},{24,8},{28,12},{1,17},{... | collective-permute-start | bytes 442376 | tf_op jit(solution)/shard_map/ppermute | solution.py:288
  13.3 13.1 %collective-permute-start.2 = (bf16[2,1,96,384]{3,2,0,1:T(8,128)(2,1)}, bf16[2,1,96,384]{3,2,0,1:T(8,128)(2,1)}, u32[]{:S(2)}, u32[]{:S(2)}) collective-permute-start(bf16[2,1,96,384]{3,2,0,1:T(8,128)(2,1)} %maximum_bitcast_fusion.12), channel_id=1, source_target_pairs={{0,24},{4,28},{8,16},{12,20},{16,8},{20,12},{24,0},{28,4},{1,25},{... | collective-permute-start | bytes 442376 | tf_op jit(solution)/shard_map/ppermute | solution.py:288
  15.8 10.7 %collective-permute-start.3 = (bf16[1,256,768]{2,1,0:T(8,128)(2,1)}, bf16[1,256,768]{2,1,0:T(8,128)(2,1)}, u32[]{:S(2)}, u32[]{:S(2)}) collective-permute-start(bf16[1,256,768]{2,1,0:T(8,128)(2,1)} %get-tuple-element.233), channel_id=1, source_target_pairs={{0,1},{1,0},{2,3},{3,2},{4,5},{5,4},{6,7},{7,6},{8,9},{9,8},{10,11... | collective-permute-start | bytes 1179656 | tf_op jit(solution)/shard_map/ppermute | solution.py:288
  41.5 13.2 %collective-permute-start.12 = (bf16[2,96,768]{2,1,0:T(8,128)(2,1)S(1)}, bf16[2,96,768]{2,1,0:T(8,128)(2,1)}, u32[]{:S(2)}, u32[]{:S(2)}) collective-permute-start(bf16[2,96,768]{2,1,0:T(8,128)(2,1)S(1)} %maximum_bitcast_fusion.10), channel_id=1, source_target_pairs={{0,8},{4,12},{8,0},{12,4},{16,24},{20,28},{24,16},{28,20},{1,9},{5... | collective-permute-start | bytes 884744 | tf_op jit(solution)/shard_map/ppermute | solution.py:288
  42.4 12.4 %collective-permute-start.13 = (bf16[1,384,384]{2,1,0:T(8,128)(2,1)}, bf16[1,384,384]{2,1,0:T(8,128)(2,1)}, u32[]{:S(2)}, u32[]{:S(2)}) collective-permute-start(bf16[1,384,384]{2,1,0:T(8,128)(2,1)} %constant_dynamic-slice_fusion.15), channel_id=1, source_target_pairs={{0,16},{4,20},{8,24},{12,28},{16,0},{20,4},{24,8},{28,12},{1,17},{... | collective-permute-start | bytes 884744 | tf_op jit(solution)/shard_map/ppermute | solution.py:288
  45.5 12.5 %collective-permute-start.11 = (bf16[2,4,96,384]{3,2,1,0:T(8,128)(2,1)}, bf16[2,4,96,384]{3,2,1,0:T(8,128)(2,1)}, u32[]{:S(2)}, u32[]{:S(2)}) collective-permute-start(bf16[2,4,96,384]{3,2,1,0:T(8,128)(2,1)} %pad_maximum_fusion.31), channel_id=1, source_target_pairs={{0,4},{4,0},{8,12},{12,8},{16,20},{20,16},{24,28},{28,24},{1,5},{5... | collective-permute-start | bytes 1769480 | tf_op jit(solution)/shard_map/ppermute | solution.py:288
  47.2 12.0 %collective-permute-start.10 = (bf16[8,96,384]{2,1,0:T(8,128)(2,1)S(1)}, bf16[8,96,384]{2,1,0:T(8,128)(2,1)}, u32[]{:S(2)}, u32[]{:S(2)}) collective-permute-start(bf16[8,96,384]{2,1,0:T(8,128)(2,1)S(1)} %bitcast.1551), channel_id=1, source_target_pairs={{0,1},{1,0},{2,3},{3,2},{4,5},{5,4},{6,7},{7,6},{8,9},{9,8},{10,11... | collective-permute-start | bytes 1769480 | tf_op jit(solution)/shard_map/ppermute | solution.py:288
  68.4 15.9 %collective-permute-start.17 = (bf16[2,384,384]{2,1,0:T(8,128)(2,1)}, bf16[2,384,384]{2,1,0:T(8,128)(2,1)}, u32[]{:S(2)}, u32[]{:S(2)}) collective-permute-start(bf16[2,384,384]{2,1,0:T(8,128)(2,1)} %maximum_bitcast_fusion.4), channel_id=1, source_target_pairs={{0,8},{4,12},{8,0},{12,4},{16,24},{20,28},{24,16},{28,20},{1,9},{5... | collective-permute-start | bytes 1769480 | tf_op jit(solution)/shard_map/ppermute | solution.py:288
  71.7 15.6 %collective-permute-start.16 = (bf16[4,96,768]{2,1,0:T(8,128)(2,1)}, bf16[4,96,768]{2,1,0:T(8,128)(2,1)}, u32[]{:S(2)}, u32[]{:S(2)}) collective-permute-start(bf16[4,96,768]{2,1,0:T(8,128)(2,1)} %bitcast.63), channel_id=1, source_target_pairs={{0,4},{4,0},{8,12},{12,8},{16,20},{20,16},{24,28},{28,24},{1,5},{5... | collective-permute-start | bytes 1769480 | tf_op jit(solution)/shard_map/ppermute | solution.py:288
  90.3 28.4 %collective-permute-start.20 = (bf16[4,384,384]{2,1,0:T(8,128)(2,1)S(1)}, bf16[4,384,384]{2,1,0:T(8,128)(2,1)S(1)}, u32[]{:S(2)}, u32[]{:S(2)}) collective-permute-start(bf16[4,384,384]{2,1,0:T(8,128)(2,1)S(1)} %bitcast.1520), channel_id=1, source_target_pairs={{0,4},{4,0},{8,12},{12,8},{16,20},{20,16},{24,28},{28,24},{1,5},{5... | collective-permute-start | bytes 3538952 | tf_op jit(solution)/shard_map/ppermute | solution.py:288
  91.0 28.1 %collective-permute-start.19 = (bf16[768,768]{1,0:T(8,128)(2,1)S(1)}, bf16[768,768]{1,0:T(8,128)(2,1)S(1)}, u32[]{:S(2)}, u32[]{:S(2)}) collective-permute-start(bf16[768,768]{1,0:T(8,128)(2,1)S(1)} %bitcast.1521), channel_id=1, source_target_pairs={{0,1},{1,0},{2,3},{3,2},{4,5},{5,4},{6,7},{7,6},{8,9},{9,8},{10,11... | collective-permute-start | bytes 3538952 | tf_op jit(solution)/shard_map/ppermute | solution.py:288
  95.9 23.1 %collective-permute-start.21 = (bf16[2,1,96,384]{3,2,0,1:T(8,128)(2,1)S(1)}, bf16[2,1,96,384]{3,2,0,1:T(8,128)(2,1)S(1)}, u32[]{:S(2)}, u32[]{:S(2)}) collective-permute-start(bf16[2,1,96,384]{3,2,0,1:T(8,128)(2,1)S(1)} %copy-done.145), channel_id=1, source_target_pairs={{0,8},{4,12},{8,0},{12,4},{16,24},{20,28},{24,16},{28,20},{1,9},{5... | collective-permute-start | bytes 442376 | tf_op jit(solution)/shard_map/ppermute | solution.py:288
  96.6 22.5 %collective-permute-start.22 = (bf16[2,1,96,384]{3,2,0,1:T(8,128)(2,1)S(1)}, bf16[2,1,96,384]{3,2,0,1:T(8,128)(2,1)S(1)}, u32[]{:S(2)}, u32[]{:S(2)}) collective-permute-start(bf16[2,1,96,384]{3,2,0,1:T(8,128)(2,1)S(1)} %copy-done.145), channel_id=1, source_target_pairs={{0,16},{4,20},{8,24},{12,28},{16,0},{20,4},{24,8},{28,12},{1,17},{... | collective-permute-start | bytes 442376 | tf_op jit(solution)/shard_map/ppermute | solution.py:288
  97.2 21.9 %collective-permute-start.23 = (bf16[2,1,96,384]{3,2,0,1:T(8,128)(2,1)S(1)}, bf16[2,1,96,384]{3,2,0,1:T(8,128)(2,1)S(1)}, u32[]{:S(2)}, u32[]{:S(2)}) collective-permute-start(bf16[2,1,96,384]{3,2,0,1:T(8,128)(2,1)S(1)} %copy-done.145), channel_id=1, source_target_pairs={{0,24},{4,28},{8,16},{12,20},{16,8},{20,12},{24,0},{28,4},{1,25},{... | collective-permute-start | bytes 442376 | tf_op jit(solution)/shard_map/ppermute | solution.py:288
  120.0 11.6 %collective-permute-start.29 = (bf16[1,96,768]{2,1,0:T(8,128)(2,1)S(1)}, bf16[1,96,768]{2,1,0:T(8,128)(2,1)S(1)}, u32[]{:S(2)}, u32[]{:S(2)}) collective-permute-start(bf16[1,96,768]{2,1,0:T(8,128)(2,1)S(1)} %copy-done.144), channel_id=1, source_target_pairs={{0,16},{4,20},{8,24},{12,28},{16,0},{20,4},{24,8},{28,12},{1,17},{... | collective-permute-start | bytes 442376 | tf_op jit(solution)/shard_map/ppermute | solution.py:288
  122.0 13.7 %collective-permute-start.25 = (bf16[2,768,768]{2,1,0:T(8,128)(2,1)S(1)}, bf16[2,768,768]{2,1,0:T(8,128)(2,1)S(1)}, u32[]{:S(2)}, u32[]{:S(2)}) collective-permute-start(bf16[2,768,768]{2,1,0:T(8,128)(2,1)S(1)} %pad_maximum_fusion.2), channel_id=1, source_target_pairs={{0,2},{2,0},{1,3},{3,1},{4,6},{6,4},{5,7},{7,5},{8,10},{10,8},{9,1... | collective-permute-start | bytes 7077896 | tf_op jit(solution)/shard_map/ppermute | solution.py:288
  122.6 13.2 %collective-permute-start.26 = (bf16[2,1536,384]{2,1,0:T(8,128)(2,1)S(1)}, bf16[2,1536,384]{2,1,0:T(8,128)(2,1)S(1)}, u32[]{:S(2)}, u32[]{:S(2)}) collective-permute-start(bf16[2,1536,384]{2,1,0:T(8,128)(2,1)S(1)} %bitcast.1552), channel_id=1, source_target_pairs={{0,2},{2,0},{1,3},{3,1},{4,6},{6,4},{5,7},{7,5},{8,10},{10,8},{9,1... | collective-permute-start | bytes 7077896 | tf_op jit(solution)/shard_map/ppermute | solution.py:288
  138.1 14.6 %collective-permute-start.32 = (bf16[2,96,768]{2,1,0:T(8,128)(2,1)S(1)}, bf16[2,96,768]{2,1,0:T(8,128)(2,1)S(1)}, u32[]{:S(2)}, u32[]{:S(2)}) collective-permute-start(bf16[2,96,768]{2,1,0:T(8,128)(2,1)S(1)} %maximum_bitcast_fusion.11), channel_id=1, source_target_pairs={{0,8},{4,12},{8,0},{12,4},{16,24},{20,28},{24,16},{28,20},{1,9},{5... | collective-permute-start | bytes 884744 | tf_op jit(solution)/shard_map/ppermute | solution.py:288
  138.8 14.0 %collective-permute-start.33 = (bf16[1,384,384]{2,1,0:T(8,128)(2,1)S(1)}, bf16[1,384,384]{2,1,0:T(8,128)(2,1)S(1)}, u32[]{:S(2)}, u32[]{:S(2)}) collective-permute-start(bf16[1,384,384]{2,1,0:T(8,128)(2,1)S(1)} %copy-done.140), channel_id=1, source_target_pairs={{0,16},{4,20},{8,24},{12,28},{16,0},{20,4},{24,8},{28,12},{1,17},{... | collective-permute-start | bytes 884744 | tf_op jit(solution)/shard_map/ppermute | solution.py:288
  141.3 14.1 %collective-permute-start.31 = (bf16[2,4,96,384]{3,2,1,0:T(8,128)(2,1)S(1)}, bf16[2,4,96,384]{3,2,1,0:T(8,128)(2,1)S(1)}, u32[]{:S(2)}, u32[]{:S(2)}) collective-permute-start(bf16[2,4,96,384]{3,2,1,0:T(8,128)(2,1)S(1)} %pad_maximum_fusion.34), channel_id=1, source_target_pairs={{0,4},{4,0},{8,12},{12,8},{16,20},{20,16},{24,28},{28,24},{1,5},{5... | collective-permute-start | bytes 1769480 | tf_op jit(solution)/shard_map/ppermute | solution.py:288
  141.9 13.7 %collective-permute-start.30 = (bf16[8,96,384]{2,1,0:T(8,128)(2,1)S(1)}, bf16[8,96,384]{2,1,0:T(8,128)(2,1)S(1)}, u32[]{:S(2)}, u32[]{:S(2)}) collective-permute-start(bf16[8,96,384]{2,1,0:T(8,128)(2,1)S(1)} %bitcast.1550), channel_id=1, source_target_pairs={{0,1},{1,0},{2,3},{3,2},{4,5},{5,4},{6,7},{7,6},{8,9},{9,8},{10,11... | collective-permute-start | bytes 1769480 | tf_op jit(solution)/shard_map/ppermute | solution.py:288
  161.7 27.5 %collective-permute-start.37 = (bf16[2,384,384]{2,1,0:T(8,128)(2,1)}, bf16[2,384,384]{2,1,0:T(8,128)(2,1)}, u32[]{:S(2)}, u32[]{:S(2)}) collective-permute-start(bf16[2,384,384]{2,1,0:T(8,128)(2,1)} %maximum_bitcast_fusion.5), channel_id=1, source_target_pairs={{0,8},{4,12},{8,0},{12,4},{16,24},{20,28},{24,16},{28,20},{1,9},{5... | collective-permute-start | bytes 1769480 | tf_op jit(solution)/shard_map/ppermute | solution.py:288
  163.1 26.1 %collective-permute-start.36 = (bf16[4,96,768]{2,1,0:T(8,128)(2,1)}, bf16[4,96,768]{2,1,0:T(8,128)(2,1)}, u32[]{:S(2)}, u32[]{:S(2)}) collective-permute-start(bf16[4,96,768]{2,1,0:T(8,128)(2,1)} %bitcast.143), channel_id=1, source_target_pairs={{0,4},{4,0},{8,12},{12,8},{16,20},{20,16},{24,28},{28,24},{1,5},{5... | collective-permute-start | bytes 1769480 | tf_op jit(solution)/shard_map/ppermute | solution.py:288
  194.4 28.6 %collective-permute-start.39 = (bf16[768,768]{1,0:T(8,128)(2,1)}, bf16[768,768]{1,0:T(8,128)(2,1)}, u32[]{:S(2)}, u32[]{:S(2)}) collective-permute-start(bf16[768,768]{1,0:T(8,128)(2,1)} %bitcast.156), channel_id=1, source_target_pairs={{0,1},{1,0},{2,3},{3,2},{4,5},{5,4},{6,7},{7,6},{8,9},{9,8},{10,11... | collective-permute-start | bytes 3538952 | tf_op jit(solution)/shard_map/ppermute | solution.py:288
  195.9 28.3 %collective-permute-start.40 = (bf16[4,384,384]{2,1,0:T(8,128)(2,1)}, bf16[4,384,384]{2,1,0:T(8,128)(2,1)}, u32[]{:S(2)}, u32[]{:S(2)}) collective-permute-start(bf16[4,384,384]{2,1,0:T(8,128)(2,1)} %bitcast.159), channel_id=1, source_target_pairs={{0,4},{4,0},{8,12},{12,8},{16,20},{20,16},{24,28},{28,24},{1,5},{5... | collective-permute-start | bytes 3538952 | tf_op jit(solution)/shard_map/ppermute | solution.py:288
  230.0 26.4 %collective-permute-start.44 = (bf16[1,256,768]{2,1,0:T(8,128)(2,1)}, bf16[1,256,768]{2,1,0:T(8,128)(2,1)}, u32[]{:S(2)}, u32[]{:S(2)}) collective-permute-start(bf16[1,256,768]{2,1,0:T(8,128)(2,1)} %get-tuple-element.316), channel_id=1, source_target_pairs={{0,1},{1,0},{2,3},{3,2},{4,5},{5,4},{6,7},{7,6},{8,9},{9,8},{10,11... | collective-permute-start | bytes 1179656 | tf_op jit(solution)/shard_map/ppermute | solution.py:288
  281.1 30.3 %collective-permute-start.48 = (bf16[4,384,384]{2,1,0:T(8,128)(2,1)S(1)}, bf16[4,384,384]{2,1,0:T(8,128)(2,1)S(1)}, u32[]{:S(2)}, u32[]{:S(2)}) collective-permute-start(bf16[4,384,384]{2,1,0:T(8,128)(2,1)S(1)} %dynamic-slice_bitcast_fusion.3), channel_id=1, source_target_pairs={{0,4},{4,0},{8,12},{12,8},{16,20},{20,16},{24,28},{28,24},{1,5},{5... | collective-permute-start | bytes 3538952 | tf_op jit(solution)/shard_map/ppermute | solution.py:288
  289.3 28.3 %collective-permute-start.49 = (bf16[768,768]{1,0:T(8,128)(2,1)S(1)}, bf16[768,768]{1,0:T(8,128)(2,1)S(1)}, u32[]{:S(2)}, u32[]{:S(2)}) collective-permute-start(bf16[768,768]{1,0:T(8,128)(2,1)S(1)} %dynamic-slice_bitcast_fusion.2), channel_id=1, source_target_pairs={{0,1},{1,0},{2,3},{3,2},{4,5},{5,4},{6,7},{7,6},{8,9},{9,8},{10,11... | collective-permute-start | bytes 3538952 | tf_op jit(solution)/shard_map/ppermute | solution.py:288
  318.0 17.6 %collective-permute-start.54 = (bf16[2,384,384]{2,1,0:T(8,128)(2,1)S(1)}, bf16[2,384,384]{2,1,0:T(8,128)(2,1)S(1)}, u32[]{:S(2)}, u32[]{:S(2)}) collective-permute-start(bf16[2,384,384]{2,1,0:T(8,128)(2,1)S(1)} %dynamic-slice_bitcast_fusion.10), channel_id=1, source_target_pairs={{0,8},{4,12},{8,0},{12,4},{16,24},{20,28},{24,16},{28,20},{1,9},{5... | collective-permute-start | bytes 1769480 | tf_op jit(solution)/shard_map/ppermute | solution.py:288
  319.0 16.6 %collective-permute-start.53 = (bf16[4,96,768]{2,1,0:T(8,128)(2,1)S(1)}, bf16[4,96,768]{2,1,0:T(8,128)(2,1)S(1)}, u32[]{:S(2)}, u32[]{:S(2)}) collective-permute-start(bf16[4,96,768]{2,1,0:T(8,128)(2,1)S(1)} %dynamic-slice_bitcast_fusion.11), channel_id=1, source_target_pairs={{0,4},{4,0},{8,12},{12,8},{16,20},{20,16},{24,28},{28,24},{1,5},{5... | collective-permute-start | bytes 1769480 | tf_op jit(solution)/shard_map/ppermute | solution.py:288
  339.8 34.0 %collective-permute-start.62 = (bf16[1,384,384]{2,1,0:T(8,128)(2,1)S(1)}, bf16[1,384,384]{2,1,0:T(8,128)(2,1)S(1)}, u32[]{:S(2)}, u32[]{:S(2)}) collective-permute-start(bf16[1,384,384]{2,1,0:T(8,128)(2,1)S(1)} %constant_dynamic-slice_fusion.10), channel_id=1, source_target_pairs={{0,16},{4,20},{8,24},{12,28},{16,0},{20,4},{24,8},{28,12},{1,17},{... | collective-permute-start | bytes 884744 | tf_op jit(solution)/shard_map/ppermute | solution.py:288
  340.4 12.9 %collective-permute-start.57 = (bf16[2,96,768]{2,1,0:T(8,128)(2,1)S(1)}, bf16[2,96,768]{2,1,0:T(8,128)(2,1)S(1)}, u32[]{:S(2)}, u32[]{:S(2)}) collective-permute-start(bf16[2,96,768]{2,1,0:T(8,128)(2,1)S(1)} %dynamic-slice_bitcast_fusion.17), channel_id=1, source_target_pairs={{0,8},{4,12},{8,0},{12,4},{16,24},{20,28},{24,16},{28,20},{1,9},{5... | collective-permute-start | bytes 884744 | tf_op jit(solution)/shard_map/ppermute | solution.py:288
  342.7 14.8 %collective-permute-start.55 = (bf16[8,96,384]{2,1,0:T(8,128)(2,1)S(1)}, bf16[8,96,384]{2,1,0:T(8,128)(2,1)S(1)}, u32[]{:S(2)}, u32[]{:S(2)}) collective-permute-start(bf16[8,96,384]{2,1,0:T(8,128)(2,1)S(1)} %dynamic-slice_bitcast_fusion.9), channel_id=1, source_target_pairs={{0,1},{1,0},{2,3},{3,2},{4,5},{5,4},{6,7},{7,6},{8,9},{9,8},{10,11... | collective-permute-start | bytes 1769480 | tf_op jit(solution)/shard_map/ppermute | solution.py:288
  343.9 14.5 %collective-permute-start.56 = (bf16[2,4,96,384]{3,2,1,0:T(8,128)(2,1)S(1)}, bf16[2,4,96,384]{3,2,1,0:T(8,128)(2,1)S(1)}, u32[]{:S(2)}, u32[]{:S(2)}) collective-permute-start(bf16[2,4,96,384]{3,2,1,0:T(8,128)(2,1)S(1)} %dynamic-slice_bitcast_fusion.8), channel_id=1, source_target_pairs={{0,4},{4,0},{8,12},{12,8},{16,20},{20,16},{24,28},{28,24},{1,5},{5... | collective-permute-start | bytes 1769480 | tf_op jit(solution)/shard_map/ppermute | solution.py:288
  358.9 15.0 %collective-permute-start.61 = (bf16[1,96,768]{2,1,0:T(8,128)(2,1)S(1)}, bf16[1,96,768]{2,1,0:T(8,128)(2,1)S(1)}, u32[]{:S(2)}, u32[]{:S(2)}) collective-permute-start(bf16[1,96,768]{2,1,0:T(8,128)(2,1)S(1)} %constant_dynamic-slice_fusion.11), channel_id=1, source_target_pairs={{0,16},{4,20},{8,24},{12,28},{16,0},{20,4},{24,8},{28,12},{1,17},{... | collective-permute-start | bytes 442376 | tf_op jit(solution)/shard_map/ppermute | solution.py:288
  361.1 12.8 %collective-permute-start.60 = (bf16[4,96,384]{2,1,0:T(8,128)(2,1)S(1)}, bf16[4,96,384]{2,1,0:T(8,128)(2,1)S(1)}, u32[]{:S(2)}, u32[]{:S(2)}) collective-permute-start(bf16[4,96,384]{2,1,0:T(8,128)(2,1)S(1)} %dynamic-slice_bitcast_fusion.15), channel_id=1, source_target_pairs={{0,1},{1,0},{2,3},{3,2},{4,5},{5,4},{6,7},{7,6},{8,9},{9,8},{10,11... | collective-permute-start | bytes 884744 | tf_op jit(solution)/shard_map/ppermute | solution.py:288
  362.2 11.7 %collective-permute-start.59 = (bf16[4,96,384]{2,1,0:T(8,128)(2,1)S(1)}, bf16[4,96,384]{2,1,0:T(8,128)(2,1)S(1)}, u32[]{:S(2)}, u32[]{:S(2)}) collective-permute-start(bf16[4,96,384]{2,1,0:T(8,128)(2,1)S(1)} %dynamic-slice_bitcast_fusion.16), channel_id=1, source_target_pairs={{0,4},{4,0},{8,12},{12,8},{16,20},{20,16},{24,28},{28,24},{1,5},{5... | collective-permute-start | bytes 884744 | tf_op jit(solution)/shard_map/ppermute | solution.py:288
  363.5 10.4 %collective-permute-start.58 = (bf16[2,1536,384]{2,1,0:T(8,128)(2,1)S(1)}, bf16[2,1536,384]{2,1,0:T(8,128)(2,1)S(1)}, u32[]{:S(2)}, u32[]{:S(2)}) collective-permute-start(bf16[2,1536,384]{2,1,0:T(8,128)(2,1)S(1)} %pad_maximum_fusion.6), channel_id=1, source_target_pairs={{0,2},{2,0},{1,3},{3,1},{4,6},{6,4},{5,7},{7,5},{8,10},{10,8},{9,1... | collective-permute-start | bytes 7077896 | tf_op jit(solution)/shard_map/ppermute | solution.py:288
  373.9 14.7 %collective-permute-start.69 = (bf16[96,768]{1,0:T(8,128)(2,1)S(1)}, bf16[96,768]{1,0:T(8,128)(2,1)S(1)}, u32[]{:S(2)}, u32[]{:S(2)}) collective-permute-start(bf16[96,768]{1,0:T(8,128)(2,1)S(1)} %fusion.436), channel_id=1, source_target_pairs={{0,3},{1,2},{2,1},{3,0},{4,7},{5,6},{6,5},{7,4},{8,11},{9,10},{10,... | collective-permute-start | bytes 442376 | tf_op jit(solution)/shard_map/ppermute | solution.py:288
  375.2 14.0 %collective-permute-start.68 = (bf16[96,768]{1,0:T(8,128)(2,1)S(1)}, bf16[96,768]{1,0:T(8,128)(2,1)S(1)}, u32[]{:S(2)}, u32[]{:S(2)}) collective-permute-start(bf16[96,768]{1,0:T(8,128)(2,1)S(1)} %fusion.436), channel_id=1, source_target_pairs={{0,2},{2,0},{1,3},{3,1},{4,6},{6,4},{5,7},{7,5},{8,10},{10,8},{9,1... | collective-permute-start | bytes 442376 | tf_op jit(solution)/shard_map/ppermute | solution.py:288
  375.2 14.5 %collective-permute-start.67 = (bf16[96,768]{1,0:T(8,128)(2,1)S(1)}, bf16[96,768]{1,0:T(8,128)(2,1)S(1)}, u32[]{:S(2)}, u32[]{:S(2)}) collective-permute-start(bf16[96,768]{1,0:T(8,128)(2,1)S(1)} %fusion.436), channel_id=1, source_target_pairs={{0,1},{1,0},{2,3},{3,2},{4,5},{5,4},{6,7},{7,6},{8,9},{9,8},{10,11... | collective-permute-start | bytes 442376 | tf_op jit(solution)/shard_map/ppermute | solution.py:288
  376.3 28.2 %collective-permute-start.70 = (bf16[384,384]{1,0:T(8,128)(2,1)S(1)}, bf16[384,384]{1,0:T(8,128)(2,1)S(1)}, u32[]{:S(2)}, u32[]{:S(2)}) collective-permute-start(bf16[384,384]{1,0:T(8,128)(2,1)S(1)} %fusion.422), channel_id=1, source_target_pairs={{0,1},{1,0},{2,3},{3,2},{4,5},{5,4},{6,7},{7,6},{8,9},{9,8},{10,11... | collective-permute-start | bytes 884744 | tf_op jit(solution)/shard_map/ppermute | solution.py:288
  386.2 18.3 %collective-permute-start.63 = (bf16[2,768,768]{2,1,0:T(8,128)(2,1)S(1)}, bf16[2,768,768]{2,1,0:T(8,128)(2,1)S(1)}, u32[]{:S(2)}, u32[]{:S(2)}) collective-permute-start(bf16[2,768,768]{2,1,0:T(8,128)(2,1)S(1)} %pad_maximum_fusion.7), channel_id=1, source_target_pairs={{0,2},{2,0},{1,3},{3,1},{4,6},{6,4},{5,7},{7,5},{8,10},{10,8},{9,1... | collective-permute-start | bytes 7077896 | tf_op jit(solution)/shard_map/ppermute | solution.py:288
  389.2 10.7 %collective-permute-start.64 = (bf16[2,96,384]{2,1,0:T(8,128)(2,1)S(1)}, bf16[2,96,384]{2,1,0:T(8,128)(2,1)S(1)}, u32[]{:S(2)}, u32[]{:S(2)}) collective-permute-start(bf16[2,96,384]{2,1,0:T(8,128)(2,1)S(1)} %get-tuple-element.623), channel_id=1, source_target_pairs={{0,8},{4,12},{8,0},{12,4},{16,24},{20,28},{24,16},{28,20},{1,9},{5... | collective-permute-start | bytes 442376 | tf_op jit(solution)/shard_map/ppermute | solution.py:288
  389.8 14.7 %collective-permute-start.65 = (bf16[2,96,384]{2,1,0:T(8,128)(2,1)S(1)}, bf16[2,96,384]{2,1,0:T(8,128)(2,1)S(1)}, u32[]{:S(2)}, u32[]{:S(2)}) collective-permute-start(bf16[2,96,384]{2,1,0:T(8,128)(2,1)S(1)} %get-tuple-element.624), channel_id=1, source_target_pairs={{0,16},{4,20},{8,24},{12,28},{16,0},{20,4},{24,8},{28,12},{1,17},{... | collective-permute-start | bytes 442376 | tf_op jit(solution)/shard_map/ppermute | solution.py:288
  413.7 28.1 %collective-permute-start.76 = (bf16[4,384,384]{2,1,0:T(8,128)(2,1)S(1)}, bf16[4,384,384]{2,1,0:T(8,128)(2,1)S(1)}, u32[]{:S(2)}, u32[]{:S(2)}) collective-permute-start(bf16[4,384,384]{2,1,0:T(8,128)(2,1)S(1)} %dynamic-slice_bitcast_fusion.1), channel_id=1, source_target_pairs={{0,4},{4,0},{8,12},{12,8},{16,20},{20,16},{24,28},{28,24},{1,5},{5... | collective-permute-start | bytes 3538952 | tf_op jit(solution)/shard_map/ppermute | solution.py:288
  414.4 27.7 %collective-permute-start.77 = (bf16[768,768]{1,0:T(8,128)(2,1)S(1)}, bf16[768,768]{1,0:T(8,128)(2,1)S(1)}, u32[]{:S(2)}, u32[]{:S(2)}) collective-permute-start(bf16[768,768]{1,0:T(8,128)(2,1)S(1)} %dynamic-slice_bitcast_fusion), channel_id=1, source_target_pairs={{0,1},{1,0},{2,3},{3,2},{4,5},{5,4},{6,7},{7,6},{8,9},{9,8},{10,11... | collective-permute-start | bytes 3538952 | tf_op jit(solution)/shard_map/ppermute | solution.py:288
  442.5 22.5 %collective-permute-start.84 = (bf16[4,96,768]{2,1,0:T(8,128)(2,1)S(1)}, bf16[4,96,768]{2,1,0:T(8,128)(2,1)S(1)}, u32[]{:S(2)}, u32[]{:S(2)}) collective-permute-start(bf16[4,96,768]{2,1,0:T(8,128)(2,1)S(1)} %dynamic-slice_bitcast_fusion.4), channel_id=1, source_target_pairs={{0,4},{4,0},{8,12},{12,8},{16,20},{20,16},{24,28},{28,24},{1,5},{5... | collective-permute-start | bytes 1769480 | tf_op jit(solution)/shard_map/ppermute | solution.py:288
  444.3 15.5 %collective-permute-start.81 = (bf16[2,384,384]{2,1,0:T(8,128)(2,1)S(1)}, bf16[2,384,384]{2,1,0:T(8,128)(2,1)S(1)}, u32[]{:S(2)}, u32[]{:S(2)}) collective-permute-start(bf16[2,384,384]{2,1,0:T(8,128)(2,1)S(1)} %dynamic-slice_bitcast_fusion.7), channel_id=1, source_target_pairs={{0,8},{4,12},{8,0},{12,4},{16,24},{20,28},{24,16},{28,20},{1,9},{5... | collective-permute-start | bytes 1769480 | tf_op jit(solution)/shard_map/ppermute | solution.py:288
  460.9 15.6 %collective-permute-start.85 = (bf16[1,384,384]{2,1,0:T(8,128)(2,1)S(1)}, bf16[1,384,384]{2,1,0:T(8,128)(2,1)S(1)}, u32[]{:S(2)}, u32[]{:S(2)}) collective-permute-start(bf16[1,384,384]{2,1,0:T(8,128)(2,1)S(1)} %constant_dynamic-slice_fusion.7), channel_id=1, source_target_pairs={{0,16},{4,20},{8,24},{12,28},{16,0},{20,4},{24,8},{28,12},{1,17},{... | collective-permute-start | bytes 884744 | tf_op jit(solution)/shard_map/ppermute | solution.py:288
  462.6 15.1 %collective-permute-start.82 = (bf16[8,96,384]{2,1,0:T(8,128)(2,1)S(1)}, bf16[8,96,384]{2,1,0:T(8,128)(2,1)S(1)}, u32[]{:S(2)}, u32[]{:S(2)}) collective-permute-start(bf16[8,96,384]{2,1,0:T(8,128)(2,1)S(1)} %dynamic-slice_bitcast_fusion.6), channel_id=1, source_target_pairs={{0,1},{1,0},{2,3},{3,2},{4,5},{5,4},{6,7},{7,6},{8,9},{9,8},{10,11... | collective-permute-start | bytes 1769480 | tf_op jit(solution)/shard_map/ppermute | solution.py:288
  463.6 14.7 %collective-permute-start.83 = (bf16[2,4,96,384]{3,2,1,0:T(8,128)(2,1)S(1)}, bf16[2,4,96,384]{3,2,1,0:T(8,128)(2,1)S(1)}, u32[]{:S(2)}, u32[]{:S(2)}) collective-permute-start(bf16[2,4,96,384]{3,2,1,0:T(8,128)(2,1)S(1)} %dynamic-slice_bitcast_fusion.5), channel_id=1, source_target_pairs={{0,4},{4,0},{8,12},{12,8},{16,20},{20,16},{24,28},{28,24},{1,5},{5... | collective-permute-start | bytes 1769480 | tf_op jit(solution)/shard_map/ppermute | solution.py:288
  484.3 11.7 %collective-permute-start.88 = (bf16[384,384]{1,0:T(8,128)(2,1)}, bf16[384,384]{1,0:T(8,128)(2,1)}, u32[]{:S(2)}, u32[]{:S(2)}) collective-permute-start(bf16[384,384]{1,0:T(8,128)(2,1)} %fusion.423), channel_id=1, source_target_pairs={{0,1},{1,0},{2,3},{3,2},{4,5},{5,4},{6,7},{7,6},{8,9},{9,8},{10,11... | collective-permute-start | bytes 884744 | tf_op jit(solution)/shard_map/ppermute | solution.py:288
  501.5 13.6 %collective-permute-start.93 = (bf16[1,96,768]{2,1,0:T(8,128)(2,1)S(1)}, bf16[1,96,768]{2,1,0:T(8,128)(2,1)S(1)}, u32[]{:S(2)}, u32[]{:S(2)}) collective-permute-start(bf16[1,96,768]{2,1,0:T(8,128)(2,1)S(1)} %constant_dynamic-slice_fusion.6), channel_id=1, source_target_pairs={{0,16},{4,20},{8,24},{12,28},{16,0},{20,4},{24,8},{28,12},{1,17},{... | collective-permute-start | bytes 442376 | tf_op jit(solution)/shard_map/ppermute | solution.py:288
  502.3 12.8 %collective-permute-start.92 = (bf16[2,96,384]{2,1,0:T(8,128)(2,1)S(1)}, bf16[2,96,384]{2,1,0:T(8,128)(2,1)S(1)}, u32[]{:S(2)}, u32[]{:S(2)}) collective-permute-start(bf16[2,96,384]{2,1,0:T(8,128)(2,1)S(1)} %get-tuple-element.619), channel_id=1, source_target_pairs={{0,24},{4,28},{8,16},{12,20},{16,8},{20,12},{24,0},{28,4},{1,25},{... | collective-permute-start | bytes 442376 | tf_op jit(solution)/shard_map/ppermute | solution.py:288
  504.1 12.1 %collective-permute-start.90 = (bf16[2,96,384]{2,1,0:T(8,128)(2,1)S(1)}, bf16[2,96,384]{2,1,0:T(8,128)(2,1)S(1)}, u32[]{:S(2)}, u32[]{:S(2)}) collective-permute-start(bf16[2,96,384]{2,1,0:T(8,128)(2,1)S(1)} %get-tuple-element.620), channel_id=1, source_target_pairs={{0,8},{4,12},{8,0},{12,4},{16,24},{20,28},{24,16},{28,20},{1,9},{5... | collective-permute-start | bytes 442376 | tf_op jit(solution)/shard_map/ppermute | solution.py:288
  505.2 18.7 %collective-permute-start.91 = (bf16[2,96,384]{2,1,0:T(8,128)(2,1)S(1)}, bf16[2,96,384]{2,1,0:T(8,128)(2,1)S(1)}, u32[]{:S(2)}, u32[]{:S(2)}) collective-permute-start(bf16[2,96,384]{2,1,0:T(8,128)(2,1)S(1)} %get-tuple-element.621), channel_id=1, source_target_pairs={{0,16},{4,20},{8,24},{12,28},{16,0},{20,4},{24,8},{28,12},{1,17},{... | collective-permute-start | bytes 442376 | tf_op jit(solution)/shard_map/ppermute | solution.py:288
  508.1 17.4 %collective-permute-start.106 = (bf16[1,256,768]{2,1,0:T(8,128)(2,1)S(1)}, bf16[1,256,768]{2,1,0:T(8,128)(2,1)S(1)}, u32[]{:S(2)}, u32[]{:S(2)}) collective-permute-start(bf16[1,256,768]{2,1,0:T(8,128)(2,1)S(1)} %copy-done.139), channel_id=1, source_target_pairs={{0,1},{1,0},{2,3},{3,2},{4,5},{5,4},{6,7},{7,6},{8,9},{9,8},{10,11... | collective-permute-start | bytes 1179656 | tf_op jit(solution)/shard_map/ppermute | solution.py:288
  515.1 15.7 %collective-permute-start.103 = (bf16[384,384]{1,0:T(8,128)(2,1)S(1)}, bf16[384,384]{1,0:T(8,128)(2,1)S(1)}, u32[]{:S(2)}, u32[]{:S(2)}) collective-permute-start(bf16[384,384]{1,0:T(8,128)(2,1)S(1)} %add_convert_fusion.14), channel_id=1, source_target_pairs={{0,2},{2,0},{1,3},{3,1},{4,6},{6,4},{5,7},{7,5},{8,10},{10,8},{9,1... | collective-permute-start | bytes 884744 | tf_op jit(solution)/shard_map/ppermute | solution.py:288
  515.1 26.3 %collective-permute-start.104 = (bf16[1,256,768]{2,1,0:T(8,128)(2,1)S(1)}, bf16[1,256,768]{2,1,0:T(8,128)(2,1)S(1)}, u32[]{:S(2)}, u32[]{:S(2)}) collective-permute-start(bf16[1,256,768]{2,1,0:T(8,128)(2,1)S(1)} %fusion.351), channel_id=1, source_target_pairs={{0,1},{1,0},{2,3},{3,2},{4,5},{5,4},{6,7},{7,6},{8,9},{9,8},{10,11... | collective-permute-start | bytes 1179656 | tf_op jit(solution)/shard_map/ppermute | solution.py:288
  541.4 13.9 %collective-permute-start.109 = (f32[24,768]{1,0:T(8,128)S(1)}, f32[24,768]{1,0:T(8,128)S(1)}, u32[]{:S(2)}, u32[]{:S(2)}) collective-permute-start(f32[24,768]{1,0:T(8,128)S(1)} %add.1030), channel_id=1, source_target_pairs={{0,24},{4,28},{8,16},{12,20},{16,8},{20,12},{24,0},{28,4},{1,25},{... | collective-permute-start | bytes 221192 | tf_op jit(solution)/shard_map/ppermute | solution.py:288
  543.3 12.0 %collective-permute-start.108 = (f32[24,768]{1,0:T(8,128)S(1)}, f32[24,768]{1,0:T(8,128)S(1)}, u32[]{:S(2)}, u32[]{:S(2)}) collective-permute-start(f32[24,768]{1,0:T(8,128)S(1)} %add.1030), channel_id=1, source_target_pairs={{0,16},{4,20},{8,24},{12,28},{16,0},{20,4},{24,8},{28,12},{1,17},{... | collective-permute-start | bytes 221192 | tf_op jit(solution)/shard_map/ppermute | solution.py:288
  (230 other events, 1447.8 us)

commit v6 on v5

--- a/solution.py
+++ b/solution.py
@@ -669,13 +669,14 @@
     grads_mine, grads_theirs = attend_back(
         core, mine, away, logsum, (mixed_mine, mixed_theirs), (slope_own, slope_away)
     )
-    grads_mine, grads_theirs, middle_slope = cut(
-        (grads_mine, grads_theirs, middle_slope), down_flow, up_flow, *before
-    )
     grads_away = swap(grads_theirs, "blk")
+    slopes_mine = [contract(normed, grads_mine[i]) for i in range(3)]
+    grads_mine, grads_away, slopes_mine, middle_slope = cut(
+        (grads_mine, grads_away, slopes_mine, middle_slope), down_flow, up_flow, *before
+    )
+    slopes_away = [contract(normed, grads_away[i]) for i in range(3)]
     first, second = [], []
-    for grads, out_slope in zip((grads_mine, grads_away), out_slopes):
-        slopes = [contract(normed, grads[i]) for i in range(3)]
+    for slopes, out_slope in zip((slopes_mine, slopes_away), out_slopes):
         first.append(jnp.stack(slopes[:2]))
         second.append(jnp.stack([slopes[2], out_slope]))
     attention_flow = Flow(reduce_attention((first[0], second[0]), (first[1], second[1])))

time: 563 us -> 579 us (1.028)
  waiting for transfers between devices: 139 us -> 148 us
    ppermute x110, waiting for transfers between devices: 139 us -> 148 us  [swap(): return lax.ppermute(item, axis, [(i, i ^ mask) for i in range(count)])]
    unnamed x380 -> x400, local copies, waits for them, and re-layouts: 27.2 us -> 26.5 us
  transfers between devices with their start and end apart: 110 -> 110, of which waited for: 41 -> 43; matrix products, arithmetic and copies ran while one was open for 32% -> 30% of each run, Pallas kernels for 10% -> 10%
where the time goes in v6:
time: 579 us; the launch traced here: 569 us
  waiting for transfers between devices  148 us (26%)
  starting transfers between devices  102 us (18%)
  matrix products  102 us (18%)
  other arithmetic  94.3 us (16%)
  local copies, waits for them, and re-layouts  61.7 us (11%)
  Pallas kernels  55.4 us (10%)
    ppermute x110, waiting for transfers between devices, swap(): return lax.ppermute(item, axis, [(i, i ^ mask) for i in range(count)])  148 us
    ppermute x110, starting transfers between devices, swap(): return lax.ppermute(item, axis, [(i, i ^ mask) for i in range(count)])  102 us
    dot_general x32, matrix products, matmul(): return jnp.dot(left, right, preferred_element_type=FULL)  42.7 us
    dot_general x32, matrix products, transposed(): return jnp.einsum('ste,de->std', left, right, preferred_element_type=FULL)  34.4 us
    pallas_call x2, Pallas kernels, attend_back(): pl.pallas_call(attend_back_kernel, grid_spec=pltpu.PrefetchScalarGridSpec...  32.2 us
    unnamed x400, local copies, waits for them, and re-layouts  26.5 us
    another operation x64, other arithmetic, ordered(): return jnp.stack([low, high], axis=axis)  26 us
    dot_general x32, matrix products, contract(): jnp.einsum('std,ste->de', left, right, preferred_element_type=FULL)  24.6 us
  transfers between devices with their start and end apart: 110, of which 43 were waited for; matrix products, arithmetic and copies ran while one was open for 30% of the time, Pallas kernels for 10%

profile of v6, /device:TPU:0, one launch (start us, length us, event | category | flops | bytes accessed | tf_op | source)
XLA Modules:
  0.0 568.9 jit_solution(9473391023243047308)
XLA Ops:
  3.8 1.7 slice_bitcast_fusion.10
  8.1 4.0 collective-permute-start.4
  14.0 2.5 collective-permute-start.2
  23.3 3.8 collective-permute-done.1
  27.2 2.8 collective-permute-start.7
  36.7 2.1 collective-permute-done.8
  43.8 2.2 collective-permute-start.13
  50.6 6.0 %collective-permute-done.12 = bf16[2,96,768]{2,1,0:T(8,128)(2,1)} collective-permute-done((bf16[2,96,768]{2,1,0:T(8,128)(2,1)}, bf16[2,96,768]{2,1,0:T(8,128)(2,1)}, u32[]{:S(2)}, u32[]{:S(2)}) %collective-permute-start.12) | collective-permute-done | bytes 294944 | tf_op jit(solution)/shard_map/ppermute | solution.py:288
  56.6 2.8 collective-permute-done.11
  61.9 1.8 select_bitcast_fusion.22
  65.9 1.8 fusion.476
  74.5 1.9 fusion.172
  79.9 5.8 %collective-permute-done.17 = bf16[2,384,384]{2,1,0:T(8,128)(2,1)} collective-permute-done((bf16[2,384,384]{2,1,0:T(8,128)(2,1)}, bf16[2,384,384]{2,1,0:T(8,128)(2,1)}, u32[]{:S(2)}, u32[]{:S(2)}) %collective-permute-start.17) | collective-permute-done | bytes 589856 | tf_op jit(solution)/shard_map/ppermute | solution.py:288
  85.7 3.0 collective-permute-done.16
  98.7 3.0 collective-permute-start.23
  102.3 11.6 %attend.2 = (bf16[1,512,384]{2,1,0:T(8,128)(2,1)S(1)}, bf16[1,512,384]{2,1,0:T(8,128)(2,1)S(1)}, f32[1,3,8,1024]{3,2,1,0:T(8,128)S(1)}) custom-call(s32[1]{0:T(128)} %bitcast.core_ref, bf16[3,1,512,384]{3,2,1,0:T(8,128)(2,1)S(1)} %pad_maximum_fusion.16.mine_ref, bf16[3,1,512,384]{3,2,1,0:T(8,128)(2,1)S(1)} %collective-permute-done.18.theirs_ref), custom_call_target="tpu_custom_call" | custom-call | tf_op jit(solution)/shard_map/attend/pallas_call | solution.py:100
  114.0 6.2 %collective-permute-done.20 = bf16[4,384,384]{2,1,0:T(8,128)(2,1)S(1)} collective-permute-done((bf16[4,384,384]{2,1,0:T(8,128)(2,1)S(1)}, bf16[4,384,384]{2,1,0:T(8,128)(2,1)S(1)}, u32[]{:S(2)}, u32[]{:S(2)}) %collective-permute-start.20) | collective-permute-done | bytes 1179680 | tf_op jit(solution)/shard_map/ppermute | solution.py:288
  133.9 3.3 collective-permute-done.28
  140.1 2.6 collective-permute-start.33
  154.2 2.6 collective-permute-done.31
  167.6 9.2 %fusion.120 = f32[512,384]{1,0:T(8,128)S(1)} fusion(bf16[1,512,1536]{2,1,0:T(8,128)(2,1)S(1)} %copy-done.99, bf16[2,1536,384]{2,1,0:T(8,128)(2,1)S(1)} %copy-done.57), kind=kOutput, calls=%fused_computation.219 | convolution fusion | flops 603979776 | bytes 3538944 | tf_op jit(solution)/shard_map/dot_general | solution.py:275
  184.1 1.9 fusion.174
  201.8 11.6 %attend.3 = (bf16[1,512,384]{2,1,0:T(8,128)(2,1)S(1)}, bf16[1,512,384]{2,1,0:T(8,128)(2,1)S(1)}, f32[1,3,8,1024]{3,2,1,0:T(8,128)S(1)}) custom-call(s32[1]{0:T(128)} %bitcast.core_ref, bf16[3,1,512,384]{3,2,1,0:T(8,128)(2,1)S(1)} %pad_maximum_fusion.21.mine_ref, bf16[3,1,512,384]{3,2,1,0:T(8,128)(2,1)S(1)} %collective-permute-done.38.theirs_ref), custom_call_target="tpu_custom_call" | custom-call | tf_op jit(solution)/shard_map/attend/pallas_call | solution.py:100
  213.4 11.0 %collective-permute-done.39 = bf16[768,768]{1,0:T(8,128)(2,1)} collective-permute-done((bf16[768,768]{1,0:T(8,128)(2,1)}, bf16[768,768]{1,0:T(8,128)(2,1)}, u32[]{:S(2)}, u32[]{:S(2)}) %collective-permute-start.39) | collective-permute-done | bytes 1179680 | tf_op jit(solution)/shard_map/ppermute | solution.py:288
  225.6 1.8 broadcast_select_fusion.1
  227.5 2.6 select_bitcast_fusion.1
  235.3 1.8 select_bitcast_fusion.7
  250.2 2.9 fusion.106
  271.3 2.3 fusion.503
  273.6 2.5 fusion.501
  290.6 1.7 fusion.148
  295.8 16.2 %attend_back.2 = (bf16[3,1,512,384]{3,2,1,0:T(8,128)(2,1)S(1)}, bf16[3,1,512,384]{3,2,1,0:T(8,128)(2,1)S(1)}) custom-call(s32[1]{0:T(128)} %bitcast.core_ref, bf16[3,1,512,384]{3,2,1,0:T(8,128)(2,1)S(1)} %pad_maximum_fusion.21.mine_ref, bf16[3,1,512,384]{3,2,1,0:T(8,128)(2,1)S(1)} %collective-permute-done.38.theirs_ref, ...), custom_call_target="tpu_custom_call" | custom-call | tf_op jit(solution)/shard_map/attend_back/pallas_call | solution.py:190
  315.3 6.3 %collective-permute-done.50 = bf16[768,768]{1,0:T(8,128)(2,1)S(1)} collective-permute-done((bf16[768,768]{1,0:T(8,128)(2,1)S(1)}, bf16[768,768]{1,0:T(8,128)(2,1)S(1)}, u32[]{:S(2)}, u32[]{:S(2)}) %collective-permute-start.50) | collective-permute-done | bytes 1179680 | tf_op jit(solution)/shard_map/ppermute | solution.py:288
  333.1 2.4 fusion.77
  338.6 7.3 %collective-permute-done.54 = bf16[2,384,384]{2,1,0:T(8,128)(2,1)S(1)} collective-permute-done((bf16[2,384,384]{2,1,0:T(8,128)(2,1)S(1)}, bf16[2,384,384]{2,1,0:T(8,128)(2,1)S(1)}, u32[]{:S(2)}, u32[]{:S(2)}) %collective-permute-start.54) | collective-permute-done | bytes 589856 | tf_op jit(solution)/shard_map/ppermute | solution.py:288
  356.6 4.3 collective-permute-done.57
  361.0 4.1 collective-permute-done.55
  365.7 2.4 collective-permute-start.61
  368.2 1.7 collective-permute-start.60
  375.4 2.3 fusion.511
  377.7 2.5 fusion.509
  397.4 3.2 collective-permute-start.65
  402.2 2.6 collective-permute-done.66
  404.7 2.9 collective-permute-done.64
  407.6 4.4 collective-permute-done.65
  416.2 1.7 fusion.149
  425.7 16.0 %attend_back.3 = (bf16[3,1,512,384]{3,2,1,0:T(8,128)(2,1)S(1)}, bf16[3,1,512,384]{3,2,1,0:T(8,128)(2,1)S(1)}) custom-call(s32[1]{0:T(128)} %bitcast.core_ref, bf16[3,1,512,384]{3,2,1,0:T(8,128)(2,1)S(1)} %copy-done.1, bf16[3,1,512,384]{3,2,1,0:T(8,128)(2,1)S(1)} %copy-done.3, f32[1,3,8,1024]{3,2,1,0:T(8,128)S(1)} %get-tuple-element.267.logsum_ref, ...), custom_call_target="tpu_custom_call" | custom-call | tf_op jit(solution)/shard_map/attend_back/pallas_call | solution.py:190
  444.5 4.7 collective-permute-done.77
  461.3 1.8 add_bitcast_fusion
  463.1 9.0 %collective-permute-done.81 = bf16[2,384,384]{2,1,0:T(8,128)(2,1)S(1)} collective-permute-done((bf16[2,384,384]{2,1,0:T(8,128)(2,1)S(1)}, bf16[2,384,384]{2,1,0:T(8,128)(2,1)S(1)}, u32[]{:S(2)}, u32[]{:S(2)}) %collective-permute-start.81) | collective-permute-done | bytes 589856 | tf_op jit(solution)/shard_map/ppermute | solution.py:288
  477.5 11.1 %collective-permute-done.85 = bf16[1,384,384]{2,1,0:T(8,128)(2,1)S(1)} collective-permute-done((bf16[1,384,384]{2,1,0:T(8,128)(2,1)S(1)}, bf16[1,384,384]{2,1,0:T(8,128)(2,1)S(1)}, u32[]{:S(2)}, u32[]{:S(2)}) %collective-permute-start.85) | collective-permute-done | bytes 294944 | tf_op jit(solution)/shard_map/ppermute | solution.py:288
  498.4 1.9 concatenate.282
  500.4 3.6 collective-permute-done.87
  504.0 3.8 collective-permute-done.88
  513.2 1.7 collective-permute-start.93
  517.1 2.3 collective-permute-start.91
  521.2 6.2 %collective-permute-done.93 = bf16[1,96,768]{2,1,0:T(8,128)(2,1)S(1)} collective-permute-done((bf16[1,96,768]{2,1,0:T(8,128)(2,1)S(1)}, bf16[1,96,768]{2,1,0:T(8,128)(2,1)S(1)}, u32[]{:S(2)}, u32[]{:S(2)}) %collective-permute-start.93) | collective-permute-done | bytes 147488 | tf_op jit(solution)/shard_map/ppermute | solution.py:288
  527.9 7.8 %collective-permute-done.91 = bf16[2,96,384]{2,1,0:T(8,128)(2,1)S(1)} collective-permute-done((bf16[2,96,384]{2,1,0:T(8,128)(2,1)S(1)}, bf16[2,96,384]{2,1,0:T(8,128)(2,1)S(1)}, u32[]{:S(2)}, u32[]{:S(2)}) %collective-permute-start.91) | collective-permute-done | bytes 147488 | tf_op jit(solution)/shard_map/ppermute | solution.py:288
  539.1 3.2 collective-permute-done.105
  545.9 2.3 collective-permute-done.97
  548.3 2.7 collective-permute-done.102
  551.0 2.8 collective-permute-done.100
  553.8 2.4 collective-permute-start.109
  556.2 2.1 collective-permute-start.108
  (1016 shorter events, 292.5 us)
Async XLA Ops:
  8.1 15.3 %collective-permute-start.4 = (bf16[1,24,96]{2,1,0:T(8,128)(2,1)S(1)}, bf16[1,24,96]{2,1,0:T(8,128)(2,1)S(1)}, u32[]{:S(2)}, u32[]{:S(2)}) collective-permute-start(bf16[1,24,96]{2,1,0:T(8,128)(2,1)S(1)} %broadcast_in_dim_reshape.3), channel_id=1, source_target_pairs={{0,16},{4,20},{8,24},{12,28},{16,0},{20,4},{24,8},{28,12},{1,17},{... | collective-permute-start | bytes 13832 | tf_op jit(solution)/shard_map/ppermute | solution.py:288
  12.1 11.2 %collective-permute-start = (bf16[2,1,96,384]{3,2,0,1:T(8,128)(2,1)}, bf16[2,1,96,384]{3,2,0,1:T(8,128)(2,1)}, u32[]{:S(2)}, u32[]{:S(2)}) collective-permute-start(bf16[2,1,96,384]{3,2,0,1:T(8,128)(2,1)} %maximum_bitcast_fusion.12), channel_id=1, source_target_pairs={{0,8},{4,12},{8,0},{12,4},{16,24},{20,28},{24,16},{28,20},{1,9},{5... | collective-permute-start | bytes 442376 | tf_op jit(solution)/shard_map/ppermute | solution.py:288
  13.7 13.5 %collective-permute-start.1 = (bf16[2,1,96,384]{3,2,0,1:T(8,128)(2,1)}, bf16[2,1,96,384]{3,2,0,1:T(8,128)(2,1)}, u32[]{:S(2)}, u32[]{:S(2)}) collective-permute-start(bf16[2,1,96,384]{3,2,0,1:T(8,128)(2,1)} %maximum_bitcast_fusion.12), channel_id=1, source_target_pairs={{0,16},{4,20},{8,24},{12,28},{16,0},{20,4},{24,8},{28,12},{1,17},{... | collective-permute-start | bytes 442376 | tf_op jit(solution)/shard_map/ppermute | solution.py:288
  14.0 13.1 %collective-permute-start.2 = (bf16[2,1,96,384]{3,2,0,1:T(8,128)(2,1)}, bf16[2,1,96,384]{3,2,0,1:T(8,128)(2,1)}, u32[]{:S(2)}, u32[]{:S(2)}) collective-permute-start(bf16[2,1,96,384]{3,2,0,1:T(8,128)(2,1)} %maximum_bitcast_fusion.12), channel_id=1, source_target_pairs={{0,24},{4,28},{8,16},{12,20},{16,8},{20,12},{24,0},{28,4},{1,25},{... | collective-permute-start | bytes 442376 | tf_op jit(solution)/shard_map/ppermute | solution.py:288
  43.0 13.6 %collective-permute-start.12 = (bf16[2,96,768]{2,1,0:T(8,128)(2,1)}, bf16[2,96,768]{2,1,0:T(8,128)(2,1)}, u32[]{:S(2)}, u32[]{:S(2)}) collective-permute-start(bf16[2,96,768]{2,1,0:T(8,128)(2,1)} %maximum_bitcast_fusion.10), channel_id=1, source_target_pairs={{0,8},{4,12},{8,0},{12,4},{16,24},{20,28},{24,16},{28,20},{1,9},{5... | collective-permute-start | bytes 884744 | tf_op jit(solution)/shard_map/ppermute | solution.py:288
  43.8 12.8 %collective-permute-start.13 = (bf16[1,384,384]{2,1,0:T(8,128)(2,1)}, bf16[1,384,384]{2,1,0:T(8,128)(2,1)}, u32[]{:S(2)}, u32[]{:S(2)}) collective-permute-start(bf16[1,384,384]{2,1,0:T(8,128)(2,1)} %constant_dynamic-slice_fusion.15), channel_id=1, source_target_pairs={{0,16},{4,20},{8,24},{12,28},{16,0},{20,4},{24,8},{28,12},{1,17},{... | collective-permute-start | bytes 884744 | tf_op jit(solution)/shard_map/ppermute | solution.py:288
  46.9 12.5 %collective-permute-start.11 = (bf16[2,4,96,384]{3,2,1,0:T(8,128)(2,1)}, bf16[2,4,96,384]{3,2,1,0:T(8,128)(2,1)}, u32[]{:S(2)}, u32[]{:S(2)}) collective-permute-start(bf16[2,4,96,384]{3,2,1,0:T(8,128)(2,1)} %pad_maximum_fusion.31), channel_id=1, source_target_pairs={{0,4},{4,0},{8,12},{12,8},{16,20},{20,16},{24,28},{28,24},{1,5},{5... | collective-permute-start | bytes 1769480 | tf_op jit(solution)/shard_map/ppermute | solution.py:288
  48.7 12.0 %collective-permute-start.10 = (bf16[8,96,384]{2,1,0:T(8,128)(2,1)S(1)}, bf16[8,96,384]{2,1,0:T(8,128)(2,1)}, u32[]{:S(2)}, u32[]{:S(2)}) collective-permute-start(bf16[8,96,384]{2,1,0:T(8,128)(2,1)S(1)} %bitcast.1545), channel_id=1, source_target_pairs={{0,1},{1,0},{2,3},{3,2},{4,5},{5,4},{6,7},{7,6},{8,9},{9,8},{10,11... | collective-permute-start | bytes 1769480 | tf_op jit(solution)/shard_map/ppermute | solution.py:288
  69.8 15.9 %collective-permute-start.17 = (bf16[2,384,384]{2,1,0:T(8,128)(2,1)}, bf16[2,384,384]{2,1,0:T(8,128)(2,1)}, u32[]{:S(2)}, u32[]{:S(2)}) collective-permute-start(bf16[2,384,384]{2,1,0:T(8,128)(2,1)} %maximum_bitcast_fusion.4), channel_id=1, source_target_pairs={{0,8},{4,12},{8,0},{12,4},{16,24},{20,28},{24,16},{28,20},{1,9},{5... | collective-permute-start | bytes 1769480 | tf_op jit(solution)/shard_map/ppermute | solution.py:288
  73.1 15.6 %collective-permute-start.16 = (bf16[4,96,768]{2,1,0:T(8,128)(2,1)}, bf16[4,96,768]{2,1,0:T(8,128)(2,1)}, u32[]{:S(2)}, u32[]{:S(2)}) collective-permute-start(bf16[4,96,768]{2,1,0:T(8,128)(2,1)} %bitcast.64), channel_id=1, source_target_pairs={{0,4},{4,0},{8,12},{12,8},{16,20},{20,16},{24,28},{28,24},{1,5},{5... | collective-permute-start | bytes 1769480 | tf_op jit(solution)/shard_map/ppermute | solution.py:288
  91.7 28.4 %collective-permute-start.20 = (bf16[4,384,384]{2,1,0:T(8,128)(2,1)S(1)}, bf16[4,384,384]{2,1,0:T(8,128)(2,1)S(1)}, u32[]{:S(2)}, u32[]{:S(2)}) collective-permute-start(bf16[4,384,384]{2,1,0:T(8,128)(2,1)S(1)} %bitcast.1514), channel_id=1, source_target_pairs={{0,4},{4,0},{8,12},{12,8},{16,20},{20,16},{24,28},{28,24},{1,5},{5... | collective-permute-start | bytes 3538952 | tf_op jit(solution)/shard_map/ppermute | solution.py:288
  92.4 28.1 %collective-permute-start.19 = (bf16[768,768]{1,0:T(8,128)(2,1)S(1)}, bf16[768,768]{1,0:T(8,128)(2,1)S(1)}, u32[]{:S(2)}, u32[]{:S(2)}) collective-permute-start(bf16[768,768]{1,0:T(8,128)(2,1)S(1)} %bitcast.1515), channel_id=1, source_target_pairs={{0,1},{1,0},{2,3},{3,2},{4,5},{5,4},{6,7},{7,6},{8,9},{9,8},{10,11... | collective-permute-start | bytes 3538952 | tf_op jit(solution)/shard_map/ppermute | solution.py:288
  97.3 23.1 %collective-permute-start.21 = (bf16[2,1,96,384]{3,2,0,1:T(8,128)(2,1)S(1)}, bf16[2,1,96,384]{3,2,0,1:T(8,128)(2,1)S(1)}, u32[]{:S(2)}, u32[]{:S(2)}) collective-permute-start(bf16[2,1,96,384]{3,2,0,1:T(8,128)(2,1)S(1)} %copy-done.145), channel_id=1, source_target_pairs={{0,8},{4,12},{8,0},{12,4},{16,24},{20,28},{24,16},{28,20},{1,9},{5... | collective-permute-start | bytes 442376 | tf_op jit(solution)/shard_map/ppermute | solution.py:288
  97.9 22.5 %collective-permute-start.22 = (bf16[2,1,96,384]{3,2,0,1:T(8,128)(2,1)S(1)}, bf16[2,1,96,384]{3,2,0,1:T(8,128)(2,1)S(1)}, u32[]{:S(2)}, u32[]{:S(2)}) collective-permute-start(bf16[2,1,96,384]{3,2,0,1:T(8,128)(2,1)S(1)} %copy-done.145), channel_id=1, source_target_pairs={{0,16},{4,20},{8,24},{12,28},{16,0},{20,4},{24,8},{28,12},{1,17},{... | collective-permute-start | bytes 442376 | tf_op jit(solution)/shard_map/ppermute | solution.py:288
  98.7 21.8 %collective-permute-start.23 = (bf16[2,1,96,384]{3,2,0,1:T(8,128)(2,1)S(1)}, bf16[2,1,96,384]{3,2,0,1:T(8,128)(2,1)S(1)}, u32[]{:S(2)}, u32[]{:S(2)}) collective-permute-start(bf16[2,1,96,384]{3,2,0,1:T(8,128)(2,1)S(1)} %copy-done.145), channel_id=1, source_target_pairs={{0,24},{4,28},{8,16},{12,20},{16,8},{20,12},{24,0},{28,4},{1,25},{... | collective-permute-start | bytes 442376 | tf_op jit(solution)/shard_map/ppermute | solution.py:288
  121.4 11.6 %collective-permute-start.29 = (bf16[1,96,768]{2,1,0:T(8,128)(2,1)S(1)}, bf16[1,96,768]{2,1,0:T(8,128)(2,1)S(1)}, u32[]{:S(2)}, u32[]{:S(2)}) collective-permute-start(bf16[1,96,768]{2,1,0:T(8,128)(2,1)S(1)} %copy-done.144), channel_id=1, source_target_pairs={{0,16},{4,20},{8,24},{12,28},{16,0},{20,4},{24,8},{28,12},{1,17},{... | collective-permute-start | bytes 442376 | tf_op jit(solution)/shard_map/ppermute | solution.py:288
  123.6 13.6 %collective-permute-start.25 = (bf16[2,768,768]{2,1,0:T(8,128)(2,1)S(1)}, bf16[2,768,768]{2,1,0:T(8,128)(2,1)S(1)}, u32[]{:S(2)}, u32[]{:S(2)}) collective-permute-start(bf16[2,768,768]{2,1,0:T(8,128)(2,1)S(1)} %pad_maximum_fusion.2), channel_id=1, source_target_pairs={{0,2},{2,0},{1,3},{3,1},{4,6},{6,4},{5,7},{7,5},{8,10},{10,8},{9,1... | collective-permute-start | bytes 7077896 | tf_op jit(solution)/shard_map/ppermute | solution.py:288
  124.2 13.0 %collective-permute-start.26 = (bf16[2,1536,384]{2,1,0:T(8,128)(2,1)S(1)}, bf16[2,1536,384]{2,1,0:T(8,128)(2,1)S(1)}, u32[]{:S(2)}, u32[]{:S(2)}) collective-permute-start(bf16[2,1536,384]{2,1,0:T(8,128)(2,1)S(1)} %bitcast.1546), channel_id=1, source_target_pairs={{0,2},{2,0},{1,3},{3,1},{4,6},{6,4},{5,7},{7,5},{8,10},{10,8},{9,1... | collective-permute-start | bytes 7077896 | tf_op jit(solution)/shard_map/ppermute | solution.py:288
  139.6 14.6 %collective-permute-start.32 = (bf16[2,96,768]{2,1,0:T(8,128)(2,1)S(1)}, bf16[2,96,768]{2,1,0:T(8,128)(2,1)S(1)}, u32[]{:S(2)}, u32[]{:S(2)}) collective-permute-start(bf16[2,96,768]{2,1,0:T(8,128)(2,1)S(1)} %maximum_bitcast_fusion.11), channel_id=1, source_target_pairs={{0,8},{4,12},{8,0},{12,4},{16,24},{20,28},{24,16},{28,20},{1,9},{5... | collective-permute-start | bytes 884744 | tf_op jit(solution)/shard_map/ppermute | solution.py:288
  140.1 14.1 %collective-permute-start.33 = (bf16[1,384,384]{2,1,0:T(8,128)(2,1)S(1)}, bf16[1,384,384]{2,1,0:T(8,128)(2,1)S(1)}, u32[]{:S(2)}, u32[]{:S(2)}) collective-permute-start(bf16[1,384,384]{2,1,0:T(8,128)(2,1)S(1)} %copy-done.140), channel_id=1, source_target_pairs={{0,16},{4,20},{8,24},{12,28},{16,0},{20,4},{24,8},{28,12},{1,17},{... | collective-permute-start | bytes 884744 | tf_op jit(solution)/shard_map/ppermute | solution.py:288
  142.7 14.1 %collective-permute-start.31 = (bf16[2,4,96,384]{3,2,1,0:T(8,128)(2,1)S(1)}, bf16[2,4,96,384]{3,2,1,0:T(8,128)(2,1)S(1)}, u32[]{:S(2)}, u32[]{:S(2)}) collective-permute-start(bf16[2,4,96,384]{3,2,1,0:T(8,128)(2,1)S(1)} %pad_maximum_fusion.34), channel_id=1, source_target_pairs={{0,4},{4,0},{8,12},{12,8},{16,20},{20,16},{24,28},{28,24},{1,5},{5... | collective-permute-start | bytes 1769480 | tf_op jit(solution)/shard_map/ppermute | solution.py:288
  143.3 13.7 %collective-permute-start.30 = (bf16[8,96,384]{2,1,0:T(8,128)(2,1)S(1)}, bf16[8,96,384]{2,1,0:T(8,128)(2,1)S(1)}, u32[]{:S(2)}, u32[]{:S(2)}) collective-permute-start(bf16[8,96,384]{2,1,0:T(8,128)(2,1)S(1)} %bitcast.1544), channel_id=1, source_target_pairs={{0,1},{1,0},{2,3},{3,2},{4,5},{5,4},{6,7},{7,6},{8,9},{9,8},{10,11... | collective-permute-start | bytes 1769480 | tf_op jit(solution)/shard_map/ppermute | solution.py:288
  163.1 27.5 %collective-permute-start.37 = (bf16[2,384,384]{2,1,0:T(8,128)(2,1)}, bf16[2,384,384]{2,1,0:T(8,128)(2,1)}, u32[]{:S(2)}, u32[]{:S(2)}) collective-permute-start(bf16[2,384,384]{2,1,0:T(8,128)(2,1)} %maximum_bitcast_fusion.5), channel_id=1, source_target_pairs={{0,8},{4,12},{8,0},{12,4},{16,24},{20,28},{24,16},{28,20},{1,9},{5... | collective-permute-start | bytes 1769480 | tf_op jit(solution)/shard_map/ppermute | solution.py:288
  164.5 26.1 %collective-permute-start.36 = (bf16[4,96,768]{2,1,0:T(8,128)(2,1)}, bf16[4,96,768]{2,1,0:T(8,128)(2,1)}, u32[]{:S(2)}, u32[]{:S(2)}) collective-permute-start(bf16[4,96,768]{2,1,0:T(8,128)(2,1)} %bitcast.143), channel_id=1, source_target_pairs={{0,4},{4,0},{8,12},{12,8},{16,20},{20,16},{24,28},{28,24},{1,5},{5... | collective-permute-start | bytes 1769480 | tf_op jit(solution)/shard_map/ppermute | solution.py:288
  195.8 28.6 %collective-permute-start.39 = (bf16[768,768]{1,0:T(8,128)(2,1)}, bf16[768,768]{1,0:T(8,128)(2,1)}, u32[]{:S(2)}, u32[]{:S(2)}) collective-permute-start(bf16[768,768]{1,0:T(8,128)(2,1)} %bitcast.156), channel_id=1, source_target_pairs={{0,1},{1,0},{2,3},{3,2},{4,5},{5,4},{6,7},{7,6},{8,9},{9,8},{10,11... | collective-permute-start | bytes 3538952 | tf_op jit(solution)/shard_map/ppermute | solution.py:288
  197.3 28.3 %collective-permute-start.40 = (bf16[4,384,384]{2,1,0:T(8,128)(2,1)}, bf16[4,384,384]{2,1,0:T(8,128)(2,1)}, u32[]{:S(2)}, u32[]{:S(2)}) collective-permute-start(bf16[4,384,384]{2,1,0:T(8,128)(2,1)} %bitcast.159), channel_id=1, source_target_pairs={{0,4},{4,0},{8,12},{12,8},{16,20},{20,16},{24,28},{28,24},{1,5},{5... | collective-permute-start | bytes 3538952 | tf_op jit(solution)/shard_map/ppermute | solution.py:288
  231.5 26.3 %collective-permute-start.44 = (bf16[1,256,768]{2,1,0:T(8,128)(2,1)}, bf16[1,256,768]{2,1,0:T(8,128)(2,1)}, u32[]{:S(2)}, u32[]{:S(2)}) collective-permute-start(bf16[1,256,768]{2,1,0:T(8,128)(2,1)} %get-tuple-element.322), channel_id=1, source_target_pairs={{0,1},{1,0},{2,3},{3,2},{4,5},{5,4},{6,7},{7,6},{8,9},{9,8},{10,11... | collective-permute-start | bytes 1179656 | tf_op jit(solution)/shard_map/ppermute | solution.py:288
  281.7 33.6 %collective-permute-start.49 = (bf16[4,384,384]{2,1,0:T(8,128)(2,1)S(1)}, bf16[4,384,384]{2,1,0:T(8,128)(2,1)S(1)}, u32[]{:S(2)}, u32[]{:S(2)}) collective-permute-start(bf16[4,384,384]{2,1,0:T(8,128)(2,1)S(1)} %dynamic-slice_bitcast_fusion.3), channel_id=1, source_target_pairs={{0,4},{4,0},{8,12},{12,8},{16,20},{20,16},{24,28},{28,24},{1,5},{5... | collective-permute-start | bytes 3538952 | tf_op jit(solution)/shard_map/ppermute | solution.py:288
  293.4 28.2 %collective-permute-start.50 = (bf16[768,768]{1,0:T(8,128)(2,1)S(1)}, bf16[768,768]{1,0:T(8,128)(2,1)S(1)}, u32[]{:S(2)}, u32[]{:S(2)}) collective-permute-start(bf16[768,768]{1,0:T(8,128)(2,1)S(1)} %dynamic-slice_bitcast_fusion.2), channel_id=1, source_target_pairs={{0,1},{1,0},{2,3},{3,2},{4,5},{5,4},{6,7},{7,6},{8,9},{9,8},{10,11... | collective-permute-start | bytes 3538952 | tf_op jit(solution)/shard_map/ppermute | solution.py:288
  331.2 14.8 %collective-permute-start.54 = (bf16[2,384,384]{2,1,0:T(8,128)(2,1)S(1)}, bf16[2,384,384]{2,1,0:T(8,128)(2,1)S(1)}, u32[]{:S(2)}, u32[]{:S(2)}) collective-permute-start(bf16[2,384,384]{2,1,0:T(8,128)(2,1)S(1)} %dynamic-slice_bitcast_fusion.10), channel_id=1, source_target_pairs={{0,8},{4,12},{8,0},{12,4},{16,24},{20,28},{24,16},{28,20},{1,9},{5... | collective-permute-start | bytes 1769480 | tf_op jit(solution)/shard_map/ppermute | solution.py:288
  331.9 14.4 %collective-permute-start.53 = (bf16[4,96,768]{2,1,0:T(8,128)(2,1)S(1)}, bf16[4,96,768]{2,1,0:T(8,128)(2,1)S(1)}, u32[]{:S(2)}, u32[]{:S(2)}) collective-permute-start(bf16[4,96,768]{2,1,0:T(8,128)(2,1)S(1)} %dynamic-slice_bitcast_fusion.11), channel_id=1, source_target_pairs={{0,4},{4,0},{8,12},{12,8},{16,20},{20,16},{24,28},{28,24},{1,5},{5... | collective-permute-start | bytes 1769480 | tf_op jit(solution)/shard_map/ppermute | solution.py:288
  332.6 13.7 %collective-permute-start.51 = (bf16[2,768,384]{2,1,0:T(8,128)(2,1)S(1)}, bf16[2,768,384]{2,1,0:T(8,128)(2,1)S(1)}, u32[]{:S(2)}, u32[]{:S(2)}) collective-permute-start(bf16[2,768,384]{2,1,0:T(8,128)(2,1)S(1)} %pad_maximum_fusion.24), channel_id=1, source_target_pairs={{0,2},{2,0},{1,3},{3,1},{4,6},{6,4},{5,7},{7,5},{8,10},{10,8},{9,1... | collective-permute-start | bytes 3538952 | tf_op jit(solution)/shard_map/ppermute | solution.py:288
  332.6 13.7 %collective-permute-start.52 = (bf16[2,768,384]{2,1,0:T(8,128)(2,1)S(1)}, bf16[2,768,384]{2,1,0:T(8,128)(2,1)S(1)}, u32[]{:S(2)}, u32[]{:S(2)}) collective-permute-start(bf16[2,768,384]{2,1,0:T(8,128)(2,1)S(1)} %pad_maximum_fusion.25), channel_id=1, source_target_pairs={{0,2},{2,0},{1,3},{3,1},{4,6},{6,4},{5,7},{7,5},{8,10},{10,8},{9,1... | collective-permute-start | bytes 3538952 | tf_op jit(solution)/shard_map/ppermute | solution.py:288
  349.3 32.1 %collective-permute-start.62 = (bf16[1,384,384]{2,1,0:T(8,128)(2,1)S(1)}, bf16[1,384,384]{2,1,0:T(8,128)(2,1)S(1)}, u32[]{:S(2)}, u32[]{:S(2)}) collective-permute-start(bf16[1,384,384]{2,1,0:T(8,128)(2,1)S(1)} %constant_dynamic-slice_fusion.10), channel_id=1, source_target_pairs={{0,16},{4,20},{8,24},{12,28},{16,0},{20,4},{24,8},{28,12},{1,17},{... | collective-permute-start | bytes 884744 | tf_op jit(solution)/shard_map/ppermute | solution.py:288
  349.8 11.2 %collective-permute-start.57 = (bf16[2,96,768]{2,1,0:T(8,128)(2,1)S(1)}, bf16[2,96,768]{2,1,0:T(8,128)(2,1)S(1)}, u32[]{:S(2)}, u32[]{:S(2)}) collective-permute-start(bf16[2,96,768]{2,1,0:T(8,128)(2,1)S(1)} %dynamic-slice_bitcast_fusion.17), channel_id=1, source_target_pairs={{0,8},{4,12},{8,0},{12,4},{16,24},{20,28},{24,16},{28,20},{1,9},{5... | collective-permute-start | bytes 884744 | tf_op jit(solution)/shard_map/ppermute | solution.py:288
  352.1 13.0 %collective-permute-start.55 = (bf16[8,96,384]{2,1,0:T(8,128)(2,1)S(1)}, bf16[8,96,384]{2,1,0:T(8,128)(2,1)S(1)}, u32[]{:S(2)}, u32[]{:S(2)}) collective-permute-start(bf16[8,96,384]{2,1,0:T(8,128)(2,1)S(1)} %dynamic-slice_bitcast_fusion.9), channel_id=1, source_target_pairs={{0,1},{1,0},{2,3},{3,2},{4,5},{5,4},{6,7},{7,6},{8,9},{9,8},{10,11... | collective-permute-start | bytes 1769480 | tf_op jit(solution)/shard_map/ppermute | solution.py:288
  352.8 12.4 %collective-permute-start.56 = (bf16[2,4,96,384]{3,2,1,0:T(8,128)(2,1)S(1)}, bf16[2,4,96,384]{3,2,1,0:T(8,128)(2,1)S(1)}, u32[]{:S(2)}, u32[]{:S(2)}) collective-permute-start(bf16[2,4,96,384]{3,2,1,0:T(8,128)(2,1)S(1)} %dynamic-slice_bitcast_fusion.8), channel_id=1, source_target_pairs={{0,4},{4,0},{8,12},{12,8},{16,20},{20,16},{24,28},{28,24},{1,5},{5... | collective-permute-start | bytes 1769480 | tf_op jit(solution)/shard_map/ppermute | solution.py:288
  365.7 15.8 %collective-permute-start.61 = (bf16[1,96,768]{2,1,0:T(8,128)(2,1)S(1)}, bf16[1,96,768]{2,1,0:T(8,128)(2,1)S(1)}, u32[]{:S(2)}, u32[]{:S(2)}) collective-permute-start(bf16[1,96,768]{2,1,0:T(8,128)(2,1)S(1)} %constant_dynamic-slice_fusion.11), channel_id=1, source_target_pairs={{0,16},{4,20},{8,24},{12,28},{16,0},{20,4},{24,8},{28,12},{1,17},{... | collective-permute-start | bytes 442376 | tf_op jit(solution)/shard_map/ppermute | solution.py:288
  368.2 13.3 %collective-permute-start.60 = (bf16[4,96,384]{2,1,0:T(8,128)(2,1)S(1)}, bf16[4,96,384]{2,1,0:T(8,128)(2,1)S(1)}, u32[]{:S(2)}, u32[]{:S(2)}) collective-permute-start(bf16[4,96,384]{2,1,0:T(8,128)(2,1)S(1)} %dynamic-slice_bitcast_fusion.15), channel_id=1, source_target_pairs={{0,1},{1,0},{2,3},{3,2},{4,5},{5,4},{6,7},{7,6},{8,9},{9,8},{10,11... | collective-permute-start | bytes 884744 | tf_op jit(solution)/shard_map/ppermute | solution.py:288
  369.9 11.5 %collective-permute-start.59 = (bf16[4,96,384]{2,1,0:T(8,128)(2,1)S(1)}, bf16[4,96,384]{2,1,0:T(8,128)(2,1)S(1)}, u32[]{:S(2)}, u32[]{:S(2)}) collective-permute-start(bf16[4,96,384]{2,1,0:T(8,128)(2,1)S(1)} %dynamic-slice_bitcast_fusion.16), channel_id=1, source_target_pairs={{0,4},{4,0},{8,12},{12,8},{16,20},{20,16},{24,28},{28,24},{1,5},{5... | collective-permute-start | bytes 884744 | tf_op jit(solution)/shard_map/ppermute | solution.py:288
  370.2 11.3 %collective-permute-start.58 = (bf16[2,1536,384]{2,1,0:T(8,128)(2,1)S(1)}, bf16[2,1536,384]{2,1,0:T(8,128)(2,1)S(1)}, u32[]{:S(2)}, u32[]{:S(2)}) collective-permute-start(bf16[2,1536,384]{2,1,0:T(8,128)(2,1)S(1)} %pad_maximum_fusion.6), channel_id=1, source_target_pairs={{0,2},{2,0},{1,3},{3,1},{4,6},{6,4},{5,7},{7,5},{8,10},{10,8},{9,1... | collective-permute-start | bytes 7077896 | tf_op jit(solution)/shard_map/ppermute | solution.py:288
  381.5 14.7 %collective-permute-start.69 = (bf16[96,768]{1,0:T(8,128)(2,1)S(1)}, bf16[96,768]{1,0:T(8,128)(2,1)S(1)}, u32[]{:S(2)}, u32[]{:S(2)}) collective-permute-start(bf16[96,768]{1,0:T(8,128)(2,1)S(1)} %fusion.442), channel_id=1, source_target_pairs={{0,3},{1,2},{2,1},{3,0},{4,7},{5,6},{6,5},{7,4},{8,11},{9,10},{10,... | collective-permute-start | bytes 442376 | tf_op jit(solution)/shard_map/ppermute | solution.py:288
  382.9 13.9 %collective-permute-start.68 = (bf16[96,768]{1,0:T(8,128)(2,1)S(1)}, bf16[96,768]{1,0:T(8,128)(2,1)S(1)}, u32[]{:S(2)}, u32[]{:S(2)}) collective-permute-start(bf16[96,768]{1,0:T(8,128)(2,1)S(1)} %fusion.442), channel_id=1, source_target_pairs={{0,2},{2,0},{1,3},{3,1},{4,6},{6,4},{5,7},{7,5},{8,10},{10,8},{9,1... | collective-permute-start | bytes 442376 | tf_op jit(solution)/shard_map/ppermute | solution.py:288
  382.9 14.5 %collective-permute-start.67 = (bf16[96,768]{1,0:T(8,128)(2,1)S(1)}, bf16[96,768]{1,0:T(8,128)(2,1)S(1)}, u32[]{:S(2)}, u32[]{:S(2)}) collective-permute-start(bf16[96,768]{1,0:T(8,128)(2,1)S(1)} %fusion.442), channel_id=1, source_target_pairs={{0,1},{1,0},{2,3},{3,2},{4,5},{5,4},{6,7},{7,6},{8,9},{9,8},{10,11... | collective-permute-start | bytes 442376 | tf_op jit(solution)/shard_map/ppermute | solution.py:288
  383.9 28.1 %collective-permute-start.70 = (bf16[384,384]{1,0:T(8,128)(2,1)S(1)}, bf16[384,384]{1,0:T(8,128)(2,1)S(1)}, u32[]{:S(2)}, u32[]{:S(2)}) collective-permute-start(bf16[384,384]{1,0:T(8,128)(2,1)S(1)} %fusion.428), channel_id=1, source_target_pairs={{0,1},{1,0},{2,3},{3,2},{4,5},{5,4},{6,7},{7,6},{8,9},{9,8},{10,11... | collective-permute-start | bytes 884744 | tf_op jit(solution)/shard_map/ppermute | solution.py:288
  393.8 18.3 %collective-permute-start.63 = (bf16[2,768,768]{2,1,0:T(8,128)(2,1)S(1)}, bf16[2,768,768]{2,1,0:T(8,128)(2,1)S(1)}, u32[]{:S(2)}, u32[]{:S(2)}) collective-permute-start(bf16[2,768,768]{2,1,0:T(8,128)(2,1)S(1)} %pad_maximum_fusion.7), channel_id=1, source_target_pairs={{0,2},{2,0},{1,3},{3,1},{4,6},{6,4},{5,7},{7,5},{8,10},{10,8},{9,1... | collective-permute-start | bytes 7077896 | tf_op jit(solution)/shard_map/ppermute | solution.py:288
  397.4 14.6 %collective-permute-start.65 = (bf16[2,96,384]{2,1,0:T(8,128)(2,1)S(1)}, bf16[2,96,384]{2,1,0:T(8,128)(2,1)S(1)}, u32[]{:S(2)}, u32[]{:S(2)}) collective-permute-start(bf16[2,96,384]{2,1,0:T(8,128)(2,1)S(1)} %get-tuple-element.636), channel_id=1, source_target_pairs={{0,16},{4,20},{8,24},{12,28},{16,0},{20,4},{24,8},{28,12},{1,17},{... | collective-permute-start | bytes 442376 | tf_op jit(solution)/shard_map/ppermute | solution.py:288
  421.2 28.1 %collective-permute-start.77 = (bf16[4,384,384]{2,1,0:T(8,128)(2,1)S(1)}, bf16[4,384,384]{2,1,0:T(8,128)(2,1)S(1)}, u32[]{:S(2)}, u32[]{:S(2)}) collective-permute-start(bf16[4,384,384]{2,1,0:T(8,128)(2,1)S(1)} %dynamic-slice_bitcast_fusion.1), channel_id=1, source_target_pairs={{0,4},{4,0},{8,12},{12,8},{16,20},{20,16},{24,28},{28,24},{1,5},{5... | collective-permute-start | bytes 3538952 | tf_op jit(solution)/shard_map/ppermute | solution.py:288
  422.2 27.7 %collective-permute-start.78 = (bf16[768,768]{1,0:T(8,128)(2,1)S(1)}, bf16[768,768]{1,0:T(8,128)(2,1)S(1)}, u32[]{:S(2)}, u32[]{:S(2)}) collective-permute-start(bf16[768,768]{1,0:T(8,128)(2,1)S(1)} %dynamic-slice_bitcast_fusion), channel_id=1, source_target_pairs={{0,1},{1,0},{2,3},{3,2},{4,5},{5,4},{6,7},{7,6},{8,9},{9,8},{10,11... | collective-permute-start | bytes 3538952 | tf_op jit(solution)/shard_map/ppermute | solution.py:288
  456.0 16.1 %collective-permute-start.79 = (bf16[2,768,384]{2,1,0:T(8,128)(2,1)S(1)}, bf16[2,768,384]{2,1,0:T(8,128)(2,1)S(1)}, u32[]{:S(2)}, u32[]{:S(2)}) collective-permute-start(bf16[2,768,384]{2,1,0:T(8,128)(2,1)S(1)} %pad_maximum_fusion.26), channel_id=1, source_target_pairs={{0,2},{2,0},{1,3},{3,1},{4,6},{6,4},{5,7},{7,5},{8,10},{10,8},{9,1... | collective-permute-start | bytes 3538952 | tf_op jit(solution)/shard_map/ppermute | solution.py:288
  456.1 16.0 %collective-permute-start.80 = (bf16[2,768,384]{2,1,0:T(8,128)(2,1)S(1)}, bf16[2,768,384]{2,1,0:T(8,128)(2,1)S(1)}, u32[]{:S(2)}, u32[]{:S(2)}) collective-permute-start(bf16[2,768,384]{2,1,0:T(8,128)(2,1)S(1)} %pad_maximum_fusion.27), channel_id=1, source_target_pairs={{0,2},{2,0},{1,3},{3,1},{4,6},{6,4},{5,7},{7,5},{8,10},{10,8},{9,1... | collective-permute-start | bytes 3538952 | tf_op jit(solution)/shard_map/ppermute | solution.py:288
  456.7 15.4 %collective-permute-start.81 = (bf16[2,384,384]{2,1,0:T(8,128)(2,1)S(1)}, bf16[2,384,384]{2,1,0:T(8,128)(2,1)S(1)}, u32[]{:S(2)}, u32[]{:S(2)}) collective-permute-start(bf16[2,384,384]{2,1,0:T(8,128)(2,1)S(1)} %dynamic-slice_bitcast_fusion.7), channel_id=1, source_target_pairs={{0,8},{4,12},{8,0},{12,4},{16,24},{20,28},{24,16},{28,20},{1,9},{5... | collective-permute-start | bytes 1769480 | tf_op jit(solution)/shard_map/ppermute | solution.py:288
  460.1 17.3 %collective-permute-start.84 = (bf16[4,96,768]{2,1,0:T(8,128)(2,1)S(1)}, bf16[4,96,768]{2,1,0:T(8,128)(2,1)S(1)}, u32[]{:S(2)}, u32[]{:S(2)}) collective-permute-start(bf16[4,96,768]{2,1,0:T(8,128)(2,1)S(1)} %dynamic-slice_bitcast_fusion.4), channel_id=1, source_target_pairs={{0,4},{4,0},{8,12},{12,8},{16,20},{20,16},{24,28},{28,24},{1,5},{5... | collective-permute-start | bytes 1769480 | tf_op jit(solution)/shard_map/ppermute | solution.py:288
  473.1 15.4 %collective-permute-start.85 = (bf16[1,384,384]{2,1,0:T(8,128)(2,1)S(1)}, bf16[1,384,384]{2,1,0:T(8,128)(2,1)S(1)}, u32[]{:S(2)}, u32[]{:S(2)}) collective-permute-start(bf16[1,384,384]{2,1,0:T(8,128)(2,1)S(1)} %constant_dynamic-slice_fusion.7), channel_id=1, source_target_pairs={{0,16},{4,20},{8,24},{12,28},{16,0},{20,4},{24,8},{28,12},{1,17},{... | collective-permute-start | bytes 884744 | tf_op jit(solution)/shard_map/ppermute | solution.py:288
  474.2 14.6 %collective-permute-start.82 = (bf16[8,96,384]{2,1,0:T(8,128)(2,1)S(1)}, bf16[8,96,384]{2,1,0:T(8,128)(2,1)S(1)}, u32[]{:S(2)}, u32[]{:S(2)}) collective-permute-start(bf16[8,96,384]{2,1,0:T(8,128)(2,1)S(1)} %dynamic-slice_bitcast_fusion.6), channel_id=1, source_target_pairs={{0,1},{1,0},{2,3},{3,2},{4,5},{5,4},{6,7},{7,6},{8,9},{9,8},{10,11... | collective-permute-start | bytes 1769480 | tf_op jit(solution)/shard_map/ppermute | solution.py:288
  475.8 14.2 %collective-permute-start.83 = (bf16[2,4,96,384]{3,2,1,0:T(8,128)(2,1)S(1)}, bf16[2,4,96,384]{3,2,1,0:T(8,128)(2,1)S(1)}, u32[]{:S(2)}, u32[]{:S(2)}) collective-permute-start(bf16[2,4,96,384]{3,2,1,0:T(8,128)(2,1)S(1)} %dynamic-slice_bitcast_fusion.5), channel_id=1, source_target_pairs={{0,4},{4,0},{8,12},{12,8},{16,20},{20,16},{24,28},{28,24},{1,5},{5... | collective-permute-start | bytes 1769480 | tf_op jit(solution)/shard_map/ppermute | solution.py:288
  513.2 14.2 %collective-permute-start.93 = (bf16[1,96,768]{2,1,0:T(8,128)(2,1)S(1)}, bf16[1,96,768]{2,1,0:T(8,128)(2,1)S(1)}, u32[]{:S(2)}, u32[]{:S(2)}) collective-permute-start(bf16[1,96,768]{2,1,0:T(8,128)(2,1)S(1)} %constant_dynamic-slice_fusion.6), channel_id=1, source_target_pairs={{0,16},{4,20},{8,24},{12,28},{16,0},{20,4},{24,8},{28,12},{1,17},{... | collective-permute-start | bytes 442376 | tf_op jit(solution)/shard_map/ppermute | solution.py:288
  515.0 12.5 %collective-permute-start.92 = (bf16[2,96,384]{2,1,0:T(8,128)(2,1)S(1)}, bf16[2,96,384]{2,1,0:T(8,128)(2,1)S(1)}, u32[]{:S(2)}, u32[]{:S(2)}) collective-permute-start(bf16[2,96,384]{2,1,0:T(8,128)(2,1)S(1)} %get-tuple-element.631), channel_id=1, source_target_pairs={{0,24},{4,28},{8,16},{12,20},{16,8},{20,12},{24,0},{28,4},{1,25},{... | collective-permute-start | bytes 442376 | tf_op jit(solution)/shard_map/ppermute | solution.py:288
  516.4 11.5 %collective-permute-start.90 = (bf16[2,96,384]{2,1,0:T(8,128)(2,1)S(1)}, bf16[2,96,384]{2,1,0:T(8,128)(2,1)S(1)}, u32[]{:S(2)}, u32[]{:S(2)}) collective-permute-start(bf16[2,96,384]{2,1,0:T(8,128)(2,1)S(1)} %get-tuple-element.632), channel_id=1, source_target_pairs={{0,8},{4,12},{8,0},{12,4},{16,24},{20,28},{24,16},{28,20},{1,9},{5... | collective-permute-start | bytes 442376 | tf_op jit(solution)/shard_map/ppermute | solution.py:288
  517.1 18.7 %collective-permute-start.91 = (bf16[2,96,384]{2,1,0:T(8,128)(2,1)S(1)}, bf16[2,96,384]{2,1,0:T(8,128)(2,1)S(1)}, u32[]{:S(2)}, u32[]{:S(2)}) collective-permute-start(bf16[2,96,384]{2,1,0:T(8,128)(2,1)S(1)} %get-tuple-element.633), channel_id=1, source_target_pairs={{0,16},{4,20},{8,24},{12,28},{16,0},{20,4},{24,8},{28,12},{1,17},{... | collective-permute-start | bytes 442376 | tf_op jit(solution)/shard_map/ppermute | solution.py:288
  520.6 17.3 %collective-permute-start.106 = (bf16[1,256,768]{2,1,0:T(8,128)(2,1)S(1)}, bf16[1,256,768]{2,1,0:T(8,128)(2,1)S(1)}, u32[]{:S(2)}, u32[]{:S(2)}) collective-permute-start(bf16[1,256,768]{2,1,0:T(8,128)(2,1)S(1)} %copy-done.139), channel_id=1, source_target_pairs={{0,1},{1,0},{2,3},{3,2},{4,5},{5,4},{6,7},{7,6},{8,9},{9,8},{10,11... | collective-permute-start | bytes 1179656 | tf_op jit(solution)/shard_map/ppermute | solution.py:288
  527.4 16.2 %collective-permute-start.103 = (bf16[384,384]{1,0:T(8,128)(2,1)S(1)}, bf16[384,384]{1,0:T(8,128)(2,1)S(1)}, u32[]{:S(2)}, u32[]{:S(2)}) collective-permute-start(bf16[384,384]{1,0:T(8,128)(2,1)S(1)} %add_convert_fusion.14), channel_id=1, source_target_pairs={{0,2},{2,0},{1,3},{3,1},{4,6},{6,4},{5,7},{7,5},{8,10},{10,8},{9,1... | collective-permute-start | bytes 884744 | tf_op jit(solution)/shard_map/ppermute | solution.py:288
  527.4 26.3 %collective-permute-start.104 = (bf16[1,256,768]{2,1,0:T(8,128)(2,1)S(1)}, bf16[1,256,768]{2,1,0:T(8,128)(2,1)S(1)}, u32[]{:S(2)}, u32[]{:S(2)}) collective-permute-start(bf16[1,256,768]{2,1,0:T(8,128)(2,1)S(1)} %fusion.345), channel_id=1, source_target_pairs={{0,1},{1,0},{2,3},{3,2},{4,5},{5,4},{6,7},{7,6},{8,9},{9,8},{10,11... | collective-permute-start | bytes 1179656 | tf_op jit(solution)/shard_map/ppermute | solution.py:288
  553.8 13.3 %collective-permute-start.109 = (f32[24,768]{1,0:T(8,128)S(1)}, f32[24,768]{1,0:T(8,128)S(1)}, u32[]{:S(2)}, u32[]{:S(2)}) collective-permute-start(f32[24,768]{1,0:T(8,128)S(1)} %add.1030), channel_id=1, source_target_pairs={{0,24},{4,28},{8,16},{12,20},{16,8},{20,12},{24,0},{28,4},{1,25},{... | collective-permute-start | bytes 221192 | tf_op jit(solution)/shard_map/ppermute | solution.py:288
  (240 other events, 1647.7 us)
